TPU v7x, 32 devices: a whole 2x2x4 slice. The times are simulated.
32 devices in a mesh: panel: 2 (over y), dom: 4 (over z), blk: 2 (over x), dir: 2 (over core).
Axes of the slice: x: 2, y: 2, z: 4, core: 2. Of those that a mesh axis runs over, the one named last changes fastest.
Arguments:
- panel_vectors: bfloat16 [3072, 2048], P('dom', ('panel', 'blk')), parts along dimension 1, may hold values from -6 to 6
- force_blocks: float32 [16, 9, 1024], P(None, None, 'dom'), may hold values from -1 to 1
- bond_vectors: float32 [2, 16, 1024], P('dir', None, 'dom'), may hold values from -4 to 4
- neighbours: int32 [16, 1024], P(None, 'dom'), may hold values from 0 to 511
- boundary_low: int32 [512], P('dom'), may hold values from 0 to 255
- boundary_high: int32 [512], P('dom'), may hold values from 0 to 255
Outputs:
- coupling: float32 [2, 2048, 1024], P('dir', ('panel', 'dom'), 'blk'), parts along dimension 1
There are 2 independent parts, one for each index of `panel`. A program takes and returns all parts, laid end to end along the dimension named above; an argument that names none is the same for every part. Nothing has to cross between parts.
Inputs may be any that keep to these rules, and one draw needn't show every extreme that they name: `neighbours`: an entry below 256 names an atom of the same domain; from 256 to 383 the listed boundary atoms of the domain below; from 384 on those of the domain above. `boundary_low`: local atom numbers within the domain that owns the block; repeats may occur. `boundary_high`: local atom numbers within the domain that owns the block; repeats may occur.
All inputs are finite; a program needn't handle non-finite values.
Results may differ from a plain program's by a relative error of at most 0.0029.
Values may be sent and summed in bfloat16 or wider, within the bound.
No kernel may reach another device: no remote copies, remote signals or barrier semaphores. Data moves between devices by JAX's collectives and lax.ppermute only.
A program may use at most 64 MiB of HBM per device.

v0:
```python
import jax
import jax.numpy as jnp
from jax import lax
from jax.sharding import PartitionSpec as P

K = 16


def from_behind(value, axis, by):
    length = lax.axis_size(axis)
    return lax.ppermute(value, axis, [(i, (i + by) % length) for i in range(length)])


def per_device(panel_vectors, force_blocks, bond_vectors, neighbours, boundary_low, boundary_high):
    rows, cols = panel_vectors.shape
    atoms = rows // 3
    own = panel_vectors.reshape(atoms, 3, cols)
    send_low = own[boundary_low]
    send_high = own[boundary_high]
    below = from_behind(send_high, "dom", 1)
    above = from_behind(send_low, "dom", -1)
    extended = jnp.concatenate([own, below, above], axis=0)
    weights = force_blocks * bond_vectors[0][:, None, :]
    flux = jnp.zeros((atoms, 3, cols), jnp.float32)
    for k in range(K):
        gathered = extended[neighbours[k]]
        blocks = weights[k].reshape(3, 3, atoms).transpose(2, 0, 1)
        flux = flux + jnp.sum(blocks[:, :, :, None] * gathered[:, None, :, :], axis=2)
    flux_rows = flux.astype(jnp.bfloat16).reshape(rows, cols)
    partial_sum = jnp.dot(
        lax.all_gather(panel_vectors, "blk", axis=1, tiled=True).T,
        flux_rows,
        preferred_element_type=jnp.float32,
    )
    domains = lax.axis_size("dom")
    scale = (3.0 * atoms * domains) ** (-0.5)
    result = lax.psum_scatter(partial_sum, "dom", scatter_dimension=0, tiled=True)
    return (result * scale)[None, :, :]


def solution(mesh):
    in_specs = (
        P("dom", ("panel", "blk")),
        P(None, None, "dom"),
        P("dir", None, "dom"),
        P(None, "dom"),
        P("dom"),
        P("dom"),
    )
    out_specs = P("dir", ("panel", "dom"), "blk")
    return jax.shard_map(
        per_device, mesh=mesh, in_specs=in_specs, out_specs=out_specs, check_vma=False
    )
```

profile of v0, /device:TPU:0, one launch (start us, length us, event | category | flops | bytes accessed | tf_op | source)
XLA Modules:
  0.0 185.1 jit_solution(13326271073689447377)
XLA Ops:
  7.3 2.5 %reshape.553 = bf16[256,3,512]{2,1,0:T(4,128)(2,1)S(1)} reshape(bf16[768,512]{1,0:T(8,128)(2,1)} %param.6) | data formatting | bytes 1572864 | tf_op jit(solution)/shard_map/reshape | solution.py:17
  9.9 1.8 gather_fusion
  11.7 3.0 %collective-permute-start = (bf16[128,3,512]{2,1,0:T(4,128)(2,1)}, bf16[128,3,512]{2,1,0:T(4,128)(2,1)}, u32[]{:S(2)}, u32[]{:S(2)}) collective-permute-start(bf16[128,3,512]{2,1,0:T(4,128)(2,1)} %gather_fusion), channel_id=1, source_target_pairs={{0,4},{4,8},{8,12},{12,0},{1,5},{5,9},{9,13},{13,1},{2,6},{6,10},{... | collective-permute-start | bytes 1179656 | tf_op jit(solution)/shard_map/ppermute | solution.py:11
  14.7 1.8 gather_fusion.1
  16.5 2.0 %collective-permute-start.1 = (bf16[128,3,512]{2,1,0:T(4,128)(2,1)}, bf16[128,3,512]{2,1,0:T(4,128)(2,1)}, u32[]{:S(2)}, u32[]{:S(2)}) collective-permute-start(bf16[128,3,512]{2,1,0:T(4,128)(2,1)} %gather_fusion.1), channel_id=1, source_target_pairs={{0,12},{4,0},{8,4},{12,8},{1,13},{5,1},{9,5},{13,9},{2,14},{6,2},{... | collective-permute-start | bytes 1179656 | tf_op jit(solution)/shard_map/ppermute | solution.py:11
  19.7 10.1 %collective-permute-done = bf16[128,3,512]{2,1,0:T(4,128)(2,1)} collective-permute-done((bf16[128,3,512]{2,1,0:T(4,128)(2,1)}, bf16[128,3,512]{2,1,0:T(4,128)(2,1)}, u32[]{:S(2)}, u32[]{:S(2)}) %collective-permute-start) | collective-permute-done | bytes 393248 | tf_op jit(solution)/shard_map/ppermute | solution.py:11
  31.1 9.1 %collective-permute-done.1 = bf16[128,3,512]{2,1,0:T(4,128)(2,1)} collective-permute-done((bf16[128,3,512]{2,1,0:T(4,128)(2,1)}, bf16[128,3,512]{2,1,0:T(4,128)(2,1)}, u32[]{:S(2)}, u32[]{:S(2)}) %collective-permute-start.1) | collective-permute-done | bytes 393248 | tf_op jit(solution)/shard_map/ppermute | solution.py:11
  41.5 1.5 gather_fusion.16
  44.4 1.5 gather_fusion.7
  47.3 1.5 gather_fusion.6
  48.9 1.4 copy_convert_fusion.11
  50.3 1.5 gather_fusion.5
  51.8 1.5 copy_convert_fusion.12
  53.3 1.5 gather_fusion.4
  56.2 1.5 gather_fusion.3
  59.1 1.5 gather_fusion.2
  60.7 1.4 copy_convert_fusion.15
  62.1 1.5 gather_fusion.15
  65.1 1.7 gather_fusion.14
  66.8 1.5 copy_convert_fusion.3
  68.3 1.5 gather_fusion.13
  71.2 1.5 gather_fusion.12
  74.2 1.5 gather_fusion.11
  75.7 1.4 copy_convert_fusion.6
  77.1 1.5 gather_fusion.10
  80.1 1.5 gather_fusion.9
  83.0 1.5 gather_fusion.8
  86.0 1.5 multiply_reduce_fusion.1
  87.6 1.5 multiply_reduce_fusion.10
  89.2 1.6 multiply_reduce_fusion.11
  90.8 1.6 multiply_reduce_fusion.12
  92.4 1.5 multiply_reduce_fusion.13
  94.0 1.5 multiply_reduce_fusion.14
  95.6 1.6 multiply_reduce_fusion.15
  97.2 1.5 multiply_reduce_fusion.2
  98.8 1.6 multiply_reduce_fusion.3
  100.4 1.6 multiply_reduce_fusion.4
  102.0 1.7 multiply_reduce_fusion.5
  103.7 1.6 multiply_reduce_fusion.6
  105.3 1.5 multiply_reduce_fusion.7
  106.9 1.5 multiply_reduce_fusion.8
  108.5 1.6 multiply_reduce_fusion.9
  110.1 1.5 gather_fusion.17
  111.9 1.5 multiply_reduce_fusion
  114.3 10.8 %add_convert_fusion = bf16[256,3,512]{2,0,1:T(8,128)(2,1)} fusion(f32[256,3,512]{2,0,1:T(8,128)} %multiply_reduce_fusion, f32[256,3,512]{2,0,1:T(8,128)S(1)} %copy-done.9, f32[256,3,512]{2,0,1:T(8,128)} %multiply_reduce_fusion.2, f32[256,3,512]{2,0,1:T(8,128)} %multiply_reduce_fusion.3, f32[256,3,512]{2,0,1:T(8,128)} %multiply_reduce_fusion.4, ...), kind=kLoop, calls=%fused_computation.35 | loop fusion | flops 6291456 | bytes 25952256 | tf_op jit(solution)/shard_map/convert_element_type | solution.py:29
  125.2 1.8 copy.77
  127.7 3.7 %convolution_bitcast_fusion = f32[1024,512]{0,1:T(8,128)} fusion(bf16[768,512]{1,0:T(8,128)(2,1)S(1)} %reshape.711, bf16[768,1024]{1,0:T(8,128)(2,1)} %all-gather.2.cloned.1.call-done), kind=kOutput, calls=%fused_computation.34 | convolution fusion | flops 805306368 | bytes 4456448 | tf_op jit(solution)/shard_map/dot_general | solution.py:30
  131.4 44.7 %reduce-scatter.2.cloned.1.call-done = f32[256,512]{0,1:T(8,128)} async-done(((f32[1024,512]{0,1:T(8,128)}), f32[256,512]{0,1:T(8,128)}) %reduce-scatter.2.cloned.1.call-update) | async-done | bytes 524304 | tf_op jit(solution)/shard_map/reduce_scatter | solution.py:37
  (94 shorter events, 22.9 us)
Async XLA Ops:
  6.5 3.3 %copy-start.19 = (s32[128]{0:T(128)S(1)}, s32[128]{0:T(128)}, u32[]{:S(2)}) copy-start(s32[128]{0:T(128)} %param.10) | copy-start | bytes 1540
  6.5 3.3 %copy-start.20 = (s32[128]{0:T(128)S(1)}, s32[128]{0:T(128)}, u32[]{:S(2)}) copy-start(s32[128]{0:T(128)} %param.11) | copy-start | bytes 1540
  6.5 121.2 %all-gather.2.cloned.1.call-start = ((), (), s32[]{:S(2)}) async-start(), calls=%async_computation.1 | async-start | bytes 2359296 | tf_op jit(solution)/shard_map/all_gather | solution.py:31
  7.3 11.3 %copy-start.18 = (s32[16,256]{1,0:T(8,128)S(1)}, s32[16,256]{1,0:T(8,128)}, u32[]{:S(2)}) copy-start(s32[16,256]{1,0:T(8,128)} %param.9) | copy-start | bytes 49156
  7.3 11.3 %copy-start.16 = (f32[16,9,256]{2,0,1:T(8,128)S(1)}, f32[16,9,256]{2,0,1:T(8,128)}, u32[]{:S(2)}) copy-start(f32[16,9,256]{2,0,1:T(8,128)} %param.7) | copy-start | bytes 442372
  7.3 11.3 %copy-start.17 = (f32[1,16,256]{2,1,0:T(8,128)S(1)}, f32[1,16,256]{2,1,0:T(8,128)}, u32[]{:S(2)}) copy-start(f32[1,16,256]{2,1,0:T(8,128)} %param.8) | copy-start | bytes 49156
  7.3 168.8 %reduce-scatter.2.cloned.1.call-start = ((), (), s32[]{:S(2)}) async-start(), calls=%async_computation.2 | async-start | bytes 2621440 | tf_op jit(solution)/shard_map/reduce_scatter | solution.py:37
  11.7 18.2 %collective-permute-start = (bf16[128,3,512]{2,1,0:T(4,128)(2,1)}, bf16[128,3,512]{2,1,0:T(4,128)(2,1)}, u32[]{:S(2)}, u32[]{:S(2)}) collective-permute-start(bf16[128,3,512]{2,1,0:T(4,128)(2,1)} %gather_fusion), channel_id=1, source_target_pairs={{0,4},{4,8},{8,12},{12,0},{1,5},{5,9},{9,13},{13,1},{2,6},{6,10},{... | collective-permute-start | bytes 1179656 | tf_op jit(solution)/shard_map/ppermute | solution.py:11
  16.5 23.7 %collective-permute-start.1 = (bf16[128,3,512]{2,1,0:T(4,128)(2,1)}, bf16[128,3,512]{2,1,0:T(4,128)(2,1)}, u32[]{:S(2)}, u32[]{:S(2)}) collective-permute-start(bf16[128,3,512]{2,1,0:T(4,128)(2,1)} %gather_fusion.1), channel_id=1, source_target_pairs={{0,12},{4,0},{8,4},{12,8},{1,13},{5,1},{9,5},{13,9},{2,14},{6,2},{... | collective-permute-start | bytes 1179656 | tf_op jit(solution)/shard_map/ppermute | solution.py:11
  84.6 1.4 copy-start
  86.0 1.6 copy-start.1
  87.6 1.6 copy-start.2
  89.2 1.6 copy-start.3
  90.8 1.6 copy-start.4
  92.4 1.6 copy-start.5
  94.0 1.6 copy-start.6
  95.6 1.6 copy-start.7
  97.2 1.6 copy-start.8
  98.8 1.6 copy-start.10
  100.4 1.6 copy-start.12
  102.0 1.8 copy-start.13
  103.7 1.6 copy-start.14
  105.3 1.6 copy-start.15
  111.9 1.6 copy-start.9
  111.9 2.4 %copy-start.11 = (f32[256,3,512]{2,0,1:T(8,128)S(1)}, f32[256,3,512]{2,0,1:T(8,128)}, u32[]{:S(2)}) copy-start(f32[256,3,512]{2,0,1:T(8,128)} %multiply_reduce_fusion.10) | copy-start | bytes 4718596
Sparse Core Ops, SparseCore 0:
  8.9 29.8 all-gather.1
  131.6 44.5 reduce-scatter.1
where the time goes:
time: 186 us; the launch traced here: 185 us
  waiting for transfers between devices  64.7 us (35%)
  other arithmetic  57.4 us (31%)
  local copies, waits for them, and re-layouts  40.3 us (22%)
  between operations  13.9 us (7%)
  starting transfers between devices  5.09 us (3%)
  matrix products  3.71 us (2%)
    reduce_scatter x1, waiting for transfers between devices, per_device(): lax.psum_scatter(partial_sum, 'dom', scatter_dimension=0, tiled=True)  44.7 us
    reduce_sum x16, other arithmetic, per_device(): jnp.sum(blocks[:, :, :, None] * gathered[:, None, :, :], axis=2)  25 us
    gather x16, local copies, waits for them, and re-layouts, per_device(): gathered = extended[neighbours[k]]  24.7 us
    convert_element_type x16, other arithmetic, per_device(): blocks[:, :, :, None] * gathered[:, None, :, :]  20.4 us
    ppermute x2, waiting for transfers between devices, from_behind(): lax.ppermute(value, axis, [(i, (i + by) % length) for i in range(length)])  19.2 us
    convert_element_type x1, other arithmetic, per_device(): flux_rows = flux.astype(jnp.bfloat16).reshape(rows, cols)  10.8 us
    ppermute x2, starting transfers between devices, from_behind(): lax.ppermute(value, axis, [(i, (i + by) % length) for i in range(length)])  5.05 us
    unnamed x44, local copies, waits for them, and re-layouts  4.28 us
  transfers between devices with their start and end apart: 4, of which 3 were waited for; matrix products, arithmetic and copies ran while one was open for 50% of the time, Pallas kernels for 0%

commit v1 on v0

v1 whole, which is shorter than its diff:
```python
import jax
import jax.numpy as jnp
from jax import lax
from jax.experimental import pallas as pl
from jax.experimental.pallas import tpu as pltpu
from jax.sharding import PartitionSpec as P

GROUP = 16
BF16 = jnp.bfloat16
F32 = jnp.float32


def params(mib=24):
    return pltpu.CompilerParams(vmem_limit_bytes=mib * 1024 * 1024)


def dot(a, b, contract=((1,), (0,))):
    return lax.dot_general(a, b, (contract, ((), ())), preferred_element_type=F32)


def one_hot(mask):
    return jnp.where(mask, 1.0, 0.0).astype(BF16)


def prep_kernel(half_ref, v_ref, low_ref, high_ref, own_ref, send_low_ref, send_high_ref, turned_ref):
    rows, cols = v_ref.shape
    atoms = rows // 3
    half = cols // 2
    v = v_ref[:, pl.ds(pl.multiple_of(half_ref[0] * half, 128), half)]
    lane = lax.broadcasted_iota(jnp.int32, (atoms, rows), 1)
    atom = lax.broadcasted_iota(jnp.int32, (atoms, rows), 0)
    for b in range(3):
        picked = dot(one_hot(lane == 3 * atom + b), v)
        own_ref[b * atoms : (b + 1) * atoms, :] = picked.astype(BF16)
        turned_ref[:, b * atoms : (b + 1) * atoms] = picked.T.astype(BF16)
    for list_ref, out_ref in ((low_ref, send_low_ref), (high_ref, send_high_ref)):
        count = list_ref.shape[1]
        named = jnp.broadcast_to(list_ref[...], (128, count)).T
        lane = lax.broadcasted_iota(jnp.int32, (count, 128), 1)
        for b in range(3):
            wanted = 3 * named + b
            hot = jnp.concatenate(
                [one_hot(lane + t * 128 == wanted) for t in range(rows // 128)], axis=1
            )
            out_ref[b * count : (b + 1) * count, :] = dot(hot, v).astype(BF16)


def weights_kernel(force_ref, bond_ref, near_ref, hi_ref, lo_ref, table_ref):
    steps, nine, atoms = force_ref.shape
    groups = atoms // GROUP
    extent = hi_ref.shape[1] // 3
    lane = lax.broadcasted_iota(jnp.int32, (24, atoms), 1)
    rows = []
    for k in range(steps):
        force = force_ref[k]
        near = near_ref[k : k + 1, :].astype(F32)
        rows.append(
            jnp.concatenate(
                [
                    force * bond_ref[0, k : k + 1, :],
                    force * bond_ref[1, k : k + 1, :],
                    jnp.broadcast_to(near, (6, atoms)),
                ],
                axis=0,
            )
        )
    bit = 1
    while bit < steps:
        taken = ((lane // GROUP) & bit) != 0
        turned = list(rows)
        for p in range(steps):
            if p & bit:
                continue
            q = p | bit
            turned[p] = jnp.where(taken, pltpu.roll(rows[q], GROUP * bit, 1), rows[p])
            turned[q] = jnp.where(taken, rows[q], pltpu.roll(rows[p], atoms - GROUP * bit, 1))
        rows = turned
        bit *= 2
    for g in range(groups):
        table_ref[g] = rows[g]

    mask = (
        lax.broadcasted_iota(jnp.int32, (GROUP, atoms), 1) % GROUP
        == lax.broadcasted_iota(jnp.int32, (GROUP, atoms), 0)
    )
    target = lax.broadcasted_iota(jnp.int32, (extent, atoms), 0).astype(F32)

    def group(g, carry):
        table = table_ref[g]
        hot = one_hot(target == table[18:19, :])
        spread = jnp.concatenate(
            [jnp.where(mask, table[r : r + 1, :], 0.0) for r in range(18)], axis=0
        )
        top = spread.astype(BF16)
        rest = (spread - top.astype(F32)).astype(BF16)
        both = ((1,), (1,))
        dense = dot(top, hot, both) + dot(rest, hot, both)
        hi = dense.astype(BF16)
        lo = (dense - hi.astype(F32)).astype(BF16)
        for e in range(2):
            for a in range(3):
                at = pl.ds(pl.multiple_of((e * 3 + a) * atoms + g * GROUP, GROUP), GROUP)
                for b in range(3):
                    r = (e * 9 + 3 * a + b) * GROUP
                    span = slice(b * extent, (b + 1) * extent)
                    hi_ref[at, span] = hi[r : r + GROUP]
                    lo_ref[at, span] = lo[r : r + GROUP]
        return carry

    lax.fori_loop(0, groups, group, 0)


def couple_kernel(hi_ref, lo_ref, own_ref, below_ref, above_ref, turned_ref, out_ref, ext_ref, flux_ref):
    rows, half = own_ref.shape
    atoms = rows // 3
    count = below_ref.shape[0] // 3
    extent = atoms + 2 * count
    for b in range(3):
        at = b * extent
        ext_ref[at : at + atoms] = own_ref[b * atoms : (b + 1) * atoms]
        ext_ref[at + atoms : at + atoms + count] = below_ref[b * count : (b + 1) * count]
        ext_ref[at + atoms + count : at + extent] = above_ref[b * count : (b + 1) * count]
    ext = ext_ref[...]
    for e in range(2):
        for a in range(3):
            at = (e * 3 + a) * atoms
            flux = dot(hi_ref[at : at + atoms, :], ext) + dot(lo_ref[at : at + atoms, :], ext)
            flux_ref[a * atoms : (a + 1) * atoms, e * half : (e + 1) * half] = flux.astype(BF16)
    flux = flux_ref[...]
    modes = turned_ref.shape[0]
    block = out_ref.shape[1]
    chunk = max(block, min(256, modes))
    for at in range(0, modes, chunk):
        term = dot(turned_ref[at : at + chunk, :], flux).astype(BF16)
        for s in range(chunk // block):
            for e in range(2):
                out_ref[2 * (at // block + s) + e] = term[
                    s * block : (s + 1) * block, e * half : (e + 1) * half
                ]


def sum_kernel(scale, terms_ref, out_ref):
    pairs, block, half = terms_ref.shape
    for c in range(2):
        total = terms_ref[c].astype(F32)
        for d in range(1, pairs // 2):
            total = total + terms_ref[2 * d + c].astype(F32)
        out_ref[0, :, c * half : (c + 1) * half] = total * scale


def shift(value, axis, by):
    length = lax.axis_size(axis)
    return lax.ppermute(value, axis, [(i, (i + by) % length) for i in range(length)])


def shape(dims, dtype):
    return jax.ShapeDtypeStruct(dims, dtype)


def per_device(panel_vectors, force_blocks, bond_vectors, neighbours, boundary_low, boundary_high):
    rows, cols = panel_vectors.shape
    atoms = rows // 3
    half = cols // 2
    count = boundary_low.shape[0]
    extent = atoms + 2 * count
    domains = lax.axis_size("dom")
    modes = cols * lax.axis_size("blk")
    block = modes // domains
    vmem = pl.BlockSpec(memory_space=pltpu.VMEM)
    smem = pl.BlockSpec(memory_space=pltpu.SMEM)

    own, send_low, send_high, turned = pl.pallas_call(
        prep_kernel,
        out_shape=(
            shape((rows, half), BF16),
            shape((3 * count, half), BF16),
            shape((3 * count, half), BF16),
            shape((half, rows), BF16),
        ),
        in_specs=[smem, vmem, vmem, vmem],
        out_specs=(vmem,) * 4,
        compiler_params=params(),
        name="prep",
    )(
        lax.axis_index("dir").reshape(1),
        panel_vectors,
        boundary_low.reshape(1, count),
        boundary_high.reshape(1, count),
    )
    below = shift(send_high, "dom", 1)
    above = shift(send_low, "dom", -1)
    turned_all = lax.all_gather(turned, ("blk", "dir"), axis=0, tiled=True)
    bonds = lax.all_gather(bond_vectors, "dir", axis=0, tiled=True)

    hi, lo = pl.pallas_call(
        weights_kernel,
        out_shape=(shape((2 * rows, 3 * extent), BF16),) * 2,
        in_specs=[vmem] * 3,
        out_specs=(vmem,) * 2,
        scratch_shapes=[pltpu.VMEM((atoms // GROUP, 24, atoms), F32)],
        compiler_params=params(32),
        cost_estimate=pl.CostEstimate(
            flops=8 * 10**9, bytes_accessed=10**7, transcendentals=0
        ),
        name="weights",
    )(force_blocks, bonds, neighbours)

    terms = pl.pallas_call(
        couple_kernel,
        out_shape=shape((2 * domains, block, half), BF16),
        in_specs=[vmem] * 6,
        out_specs=vmem,
        scratch_shapes=[
            pltpu.VMEM((3 * extent, half), BF16),
            pltpu.VMEM((rows, 2 * half), BF16),
        ],
        compiler_params=params(32),
        name="couple",
    )(hi, lo, own, below, above, turned_all)

    terms = lax.all_to_all(terms, ("dom", "dir"), split_axis=0, concat_axis=0, tiled=True)

    scale = (3.0 * atoms * domains) ** (-0.5)
    return pl.pallas_call(
        lambda *refs: sum_kernel(scale, *refs),
        out_shape=shape((1, block, cols), F32),
        in_specs=[vmem],
        out_specs=vmem,
        compiler_params=params(),
        name="total",
    )(terms)


def solution(mesh):
    in_specs = (
        P("dom", ("panel", "blk")),
        P(None, None, "dom"),
        P("dir", None, "dom"),
        P(None, "dom"),
        P("dom"),
        P("dom"),
    )
    out_specs = P("dir", ("panel", "dom"), "blk")
    return jax.shard_map(
        per_device, mesh=mesh, in_specs=in_specs, out_specs=out_specs, check_vma=False
    )
```

time: 186 us -> 81.9 us (0.44)
  waiting for transfers between devices: 64.7 us -> 3.07 us
  other arithmetic: 57.4 us -> 0 us
  blocking collectives: 0 us -> 33 us
  local copies, waits for them, and re-layouts: 40.3 us -> 14.5 us
  Pallas kernels: 0 us -> 12.3 us
  matrix products: 3.71 us -> 0 us
    reduce_scatter x1 -> x0, waiting for transfers between devices: 44.7 us -> none  [per_device(): lax.psum_scatter(partial_sum, 'dom', scatter_dimension=0, tiled=True)]
    convert_element_type x17 -> x0, other arithmetic: 31.2 us -> none  [the longest x16 20.4 us: per_device(): blocks[:, :, :, None] * gathered[:, None, :, :]]
    all_to_all x0 -> x1, blocking collectives: none -> 31 us  [per_device(): lax.all_to_all(terms, ('dom', 'dir'), split_axis=0, concat_axis=0, tiled=...]
    gather x18 -> x0, local copies, waits for them, and re-layouts: 28.3 us -> none  [the longest x16 24.7 us: per_device(): gathered = extended[neighbours[k]]]
    reduce_sum x16 -> x0, other arithmetic: 25 us -> none  [per_device(): jnp.sum(blocks[:, :, :, None] * gathered[:, None, :, :], axis=2)]
    ppermute x2, waiting for transfers between devices: 19.2 us -> 0.01 us  [shift(): lax.ppermute(value, axis, [(i, (i + by) % length) for i in range(length)])]
    pallas_call x0 -> x4, Pallas kernels: none -> 12.3 us  [the longest x1 6.23 us: per_device(): pl.pallas_call(weights_kernel, out_shape=(shape((2 * rows, 3 * extent), B...]
    unnamed x44 -> x19, local copies, waits for them, and re-layouts: 4.28 us -> 14.5 us
  transfers between devices with their start and end apart: 4 -> 3, of which waited for: 3 -> 1; matrix products, arithmetic and copies ran while one was open for 50% -> 1% of each run, Pallas kernels for 0% -> 8%
where the time goes in v1:
time: 81.9 us; the launch traced here: 81.5 us
  blocking collectives  33 us (40%)
  local copies, waits for them, and re-layouts  14.5 us (18%)
  between operations  13.4 us (16%)
  Pallas kernels  12.3 us (15%)
  starting transfers between devices  5.17 us (6%)
  waiting for transfers between devices  3.07 us (4%)
    all_to_all x1, blocking collectives, per_device(): lax.all_to_all(terms, ('dom', 'dir'), split_axis=0, concat_axis=0, tiled=...  31 us
    unnamed x19, local copies, waits for them, and re-layouts  14.5 us
    pallas_call x1, Pallas kernels, per_device(): pl.pallas_call(weights_kernel, out_shape=(shape((2 * rows, 3 * extent), B...  6.23 us
    ppermute x2, starting transfers between devices, shift(): lax.ppermute(value, axis, [(i, (i + by) % length) for i in range(length)])  5.17 us
    pallas_call x1, Pallas kernels, per_device(): pl.pallas_call(couple_kernel, out_shape=shape((2 * domains, block, half),...  3.45 us
    all_gather x1, waiting for transfers between devices, per_device(): turned_all = lax.all_gather(turned, ('blk', 'dir'), axis=0, tiled=True)  3.05 us
    all_gather x1, blocking collectives, per_device(): bonds = lax.all_gather(bond_vectors, 'dir', axis=0, tiled=True)  2.04 us
    pallas_call x1, Pallas kernels, per_device(): pl.pallas_call(prep_kernel, out_shape=(shape((rows, half), BF16), shape((...  1.7 us
  transfers between devices with their start and end apart: 3, of which 1 were waited for; matrix products, arithmetic and copies ran while one was open for 1% of the time, Pallas kernels for 8%

profile of v1, /device:TPU:0, one launch (start us, length us, event | category | flops | bytes accessed | tf_op | source)
XLA Modules:
  0.0 81.5 jit_solution(16474166980986256473)
XLA Ops:
  6.5 0.0 all-gather.2.cloned.1.call-start
  6.5 0.0 copy-start.5
  6.5 1.1 %copy-done.5 = bf16[768,512]{1,0:T(8,128)(2,1)S(1)} copy-done((bf16[768,512]{1,0:T(8,128)(2,1)S(1)}, bf16[768,512]{1,0:T(8,128)(2,1)}, u32[]{:S(2)}) %copy-start.5) | copy-done | bytes 786456
  7.7 0.0 copy-start.6
  7.7 0.7 copy-done.6
  8.3 0.0 copy-start.7
  8.3 0.7 copy-done.7
  9.0 1.7 %prep.1 = (bf16[768,256]{1,0:T(8,128)(2,1)S(1)}, bf16[384,256]{1,0:T(8,128)(2,1)S(1)}, bf16[384,256]{1,0:T(8,128)(2,1)S(1)}, bf16[256,768]{1,0:T(8,128)(2,1)}) custom-call(s32[1]{0:T(128)} %bitcast.half_ref, bf16[768,512]{1,0:T(8,128)(2,1)S(1)} %copy-done.5, s32[1,128]{1,0:T(1,128)S(1)} %bitcast.3, s32[1,128]{1,0:T(1,128)S(1)} %bitcast.4), custom_call_target="tpu_custom_call" | custom-call | tf_op jit(solution)/shard_map/prep/pallas_call | solution.py:172
  10.7 0.0 all-gather.2.cloned.1.call-update
  10.7 3.1 %collective-permute-start = (bf16[384,256]{1,0:T(8,128)(2,1)S(1)}, bf16[384,256]{1,0:T(8,128)(2,1)S(1)}, u32[]{:S(2)}, u32[]{:S(2)}) collective-permute-start(bf16[384,256]{1,0:T(8,128)(2,1)S(1)} %get-tuple-element.14), channel_id=1, source_target_pairs={{0,4},{4,8},{8,12},{12,0},{1,5},{5,9},{9,13},{13,1},{2,6},{6,10},{... | collective-permute-start | bytes 589832 | tf_op jit(solution)/shard_map/ppermute | solution.py:153
  13.8 2.1 %collective-permute-start.1 = (bf16[384,256]{1,0:T(8,128)(2,1)S(1)}, bf16[384,256]{1,0:T(8,128)(2,1)S(1)}, u32[]{:S(2)}, u32[]{:S(2)}) collective-permute-start(bf16[384,256]{1,0:T(8,128)(2,1)S(1)} %get-tuple-element.15), channel_id=1, source_target_pairs={{0,12},{4,0},{8,4},{12,8},{1,13},{5,1},{9,5},{13,9},{2,14},{6,2},{... | collective-permute-start | bytes 589832 | tf_op jit(solution)/shard_map/ppermute | solution.py:153
  15.9 1.0 %copy.8.force_ref = f32[16,9,256]{2,1,0:T(8,128)S(1)} copy(f32[16,9,256]{2,0,1:T(8,128)} %param.7) | data formatting | bytes 294912 | tf_op args[1]
  16.9 2.0 %all_gather.6.bond_ref = f32[2,16,256]{2,1,0:T(8,128)S(1)} all-gather(f32[1,16,256]{2,1,0:T(8,128)} %param.8), channel_id=1, replica_groups=mesh['panel'=2,'dom'=4,'blk'=2,'dir'=2] {'dir'}, dimensions={0}, use_global_device_ids=true | all-gather | bytes 49152 | tf_op jit(solution)/shard_map/all_gather | solution.py:193
  18.9 0.0 copy-start.8
  18.9 0.7 copy-done.8
  19.6 6.2 %weights.1 = (bf16[1536,1536]{1,0:T(8,128)(2,1)S(1)}, bf16[1536,1536]{1,0:T(8,128)(2,1)S(1)}) custom-call(f32[16,9,256]{2,1,0:T(8,128)S(1)} %copy.8.force_ref, f32[2,16,256]{2,1,0:T(8,128)S(1)} %all_gather.6.bond_ref, s32[16,256]{1,0:T(8,128)S(1)} %copy-done.8), custom_call_target="tpu_custom_call" | custom-call | flops 8000000000 | bytes 10000000 | tf_op jit(solution)/shard_map/weights/pallas_call | solution.py:195
  25.9 0.0 copy-start
  25.9 2.1 %copy-done = bf16[1536,1536]{1,0:T(8,128)(2,1)} copy-done((bf16[1536,1536]{1,0:T(8,128)(2,1)}, bf16[1536,1536]{1,0:T(8,128)(2,1)S(1)}, u32[]{:S(2)}) %copy-start) | copy-done | bytes 4718616
  28.0 0.0 copy-start.2
  28.0 2.2 %copy-done.2 = bf16[1536,1536]{1,0:T(8,128)(2,1)} copy-done((bf16[1536,1536]{1,0:T(8,128)(2,1)}, bf16[1536,1536]{1,0:T(8,128)(2,1)S(1)}, u32[]{:S(2)}) %copy-start.2) | copy-done | bytes 4718616
  30.2 0.0 collective-permute-done.below_ref
  30.2 0.0 collective-permute-done.1.above_ref
  30.2 3.0 %all-gather.2.cloned.1.call-done.turned_ref = bf16[1024,768]{1,0:T(8,128)(2,1)} async-done(((bf16[256,768]{1,0:T(8,128)(2,1)}), bf16[1024,768]{1,0:T(8,128)(2,1)}) %all-gather.2.cloned.1.call-update) | async-done | bytes 1572880 | tf_op jit(solution)/shard_map/all_gather | solution.py:192
  33.2 0.0 copy-start.1
  33.2 2.3 %copy-done.1 = bf16[1536,1536]{1,0:T(8,128)(2,1)S(1)} copy-done((bf16[1536,1536]{1,0:T(8,128)(2,1)S(1)}, bf16[1536,1536]{1,0:T(8,128)(2,1)}, u32[]{:S(2)}) %copy-start.1) | copy-done | bytes 4718616
  35.6 0.0 copy-start.3
  35.6 2.3 %copy-done.3 = bf16[1536,1536]{1,0:T(8,128)(2,1)S(1)} copy-done((bf16[1536,1536]{1,0:T(8,128)(2,1)S(1)}, bf16[1536,1536]{1,0:T(8,128)(2,1)}, u32[]{:S(2)}) %copy-start.3) | copy-done | bytes 4718616
  37.9 0.0 copy-start.4
  37.9 1.4 %copy-done.4 = bf16[1024,768]{1,0:T(8,128)(2,1)S(1)} copy-done((bf16[1024,768]{1,0:T(8,128)(2,1)S(1)}, bf16[1024,768]{1,0:T(8,128)(2,1)}, u32[]{:S(2)}) %copy-start.4) | copy-done | bytes 1572888
  39.3 3.5 %couple.1 = bf16[8,256,256]{2,1,0:T(8,128)(2,1)S(1)} custom-call(bf16[1536,1536]{1,0:T(8,128)(2,1)S(1)} %copy-done.1, bf16[1536,1536]{1,0:T(8,128)(2,1)S(1)} %copy-done.3, bf16[768,256]{1,0:T(8,128)(2,1)S(1)} %get-tuple-element.13.own_ref, bf16[384,256]{1,0:T(8,128)(2,1)S(1)} %collective-permute-done.below_ref, ...), custom_call_target="tpu_custom_call" | custom-call | tf_op jit(solution)/shard_map/couple/pallas_call | solution.py:208
  42.8 31.0 %all_to_all.5.refs_0_ = bf16[8,256,256]{2,1,0:T(8,128)(2,1)S(1)} all-to-all(bf16[8,256,256]{2,1,0:T(8,128)(2,1)S(1)} %couple.1), channel_id=1, replica_groups=mesh['panel'=2,'dom'=4,'blk'=2,'dir'=2] {'dom','dir'}, dimensions={0} | all-to-all | bytes 2097152 | tf_op jit(solution)/shard_map/all_to_all | solution.py:221
  73.8 0.9 %total.1 = f32[1,256,512]{2,1,0:T(8,128)} custom-call(bf16[8,256,256]{2,1,0:T(8,128)(2,1)S(1)} %all_to_all.5.refs_0_), custom_call_target="tpu_custom_call" | custom-call | tf_op jit(solution)/shard_map/total/pallas_call | solution.py:224
Async XLA Ops:
  6.5 26.7 %all-gather.2.cloned.1.call-start = ((), (), s32[]{:S(2)}) async-start(), calls=%async_computation.1 | async-start | bytes 1966080 | tf_op jit(solution)/shard_map/all_gather | solution.py:192
  6.5 1.1 %copy-start.5 = (bf16[768,512]{1,0:T(8,128)(2,1)S(1)}, bf16[768,512]{1,0:T(8,128)(2,1)}, u32[]{:S(2)}) copy-start(bf16[768,512]{1,0:T(8,128)(2,1)} %v_ref.1) | copy-start | bytes 2359300
  7.7 0.7 copy-start.6
  8.3 0.7 copy-start.7
  10.7 19.5 %collective-permute-start = (bf16[384,256]{1,0:T(8,128)(2,1)S(1)}, bf16[384,256]{1,0:T(8,128)(2,1)S(1)}, u32[]{:S(2)}, u32[]{:S(2)}) collective-permute-start(bf16[384,256]{1,0:T(8,128)(2,1)S(1)} %get-tuple-element.14), channel_id=1, source_target_pairs={{0,4},{4,8},{8,12},{12,0},{1,5},{5,9},{9,13},{13,1},{2,6},{6,10},{... | collective-permute-start | bytes 589832 | tf_op jit(solution)/shard_map/ppermute | solution.py:153
  13.8 16.4 %collective-permute-start.1 = (bf16[384,256]{1,0:T(8,128)(2,1)S(1)}, bf16[384,256]{1,0:T(8,128)(2,1)S(1)}, u32[]{:S(2)}, u32[]{:S(2)}) collective-permute-start(bf16[384,256]{1,0:T(8,128)(2,1)S(1)} %get-tuple-element.15), channel_id=1, source_target_pairs={{0,12},{4,0},{8,4},{12,8},{1,13},{5,1},{9,5},{13,9},{2,14},{6,2},{... | collective-permute-start | bytes 589832 | tf_op jit(solution)/shard_map/ppermute | solution.py:153
  18.9 0.7 copy-start.8
  25.9 2.1 %copy-start = (bf16[1536,1536]{1,0:T(8,128)(2,1)}, bf16[1536,1536]{1,0:T(8,128)(2,1)S(1)}, u32[]{:S(2)}) copy-start(bf16[1536,1536]{1,0:T(8,128)(2,1)S(1)} %get-tuple-element.11.hi_ref) | copy-start | bytes 14155780
  28.0 2.2 %copy-start.2 = (bf16[1536,1536]{1,0:T(8,128)(2,1)}, bf16[1536,1536]{1,0:T(8,128)(2,1)S(1)}, u32[]{:S(2)}) copy-start(bf16[1536,1536]{1,0:T(8,128)(2,1)S(1)} %get-tuple-element.12.lo_ref) | copy-start | bytes 14155780
  33.2 2.3 %copy-start.1 = (bf16[1536,1536]{1,0:T(8,128)(2,1)S(1)}, bf16[1536,1536]{1,0:T(8,128)(2,1)}, u32[]{:S(2)}) copy-start(bf16[1536,1536]{1,0:T(8,128)(2,1)} %copy-done) | copy-start | bytes 14155780
  35.6 2.3 %copy-start.3 = (bf16[1536,1536]{1,0:T(8,128)(2,1)S(1)}, bf16[1536,1536]{1,0:T(8,128)(2,1)}, u32[]{:S(2)}) copy-start(bf16[1536,1536]{1,0:T(8,128)(2,1)} %copy-done.2) | copy-start | bytes 14155780
  37.9 1.4 %copy-start.4 = (bf16[1024,768]{1,0:T(8,128)(2,1)S(1)}, bf16[1024,768]{1,0:T(8,128)(2,1)}, u32[]{:S(2)}) copy-start(bf16[1024,768]{1,0:T(8,128)(2,1)} %all-gather.2.cloned.1.call-done.turned_ref) | copy-start | bytes 4718596
Sparse Core Ops, SparseCore 0:
  10.8 22.3 all-gather.1

commit v2 on v1

--- a/solution.py
+++ b/solution.py
@@ -22,11 +22,32 @@
     return jnp.where(mask, 1.0, 0.0).astype(BF16)
 
 
-def prep_kernel(half_ref, v_ref, low_ref, high_ref, own_ref, send_low_ref, send_high_ref, turned_ref):
-    rows, cols = v_ref.shape
+def fetch(sources, targets, sems):
+    copies = [
+        pltpu.make_async_copy(source, target, sems.at[i])
+        for i, (source, target) in enumerate(zip(sources, targets))
+    ]
+    for copy in copies:
+        copy.start()
+    for copy in copies:
+        copy.wait()
+
+
+def prep_kernel(
+    v_hbm, low_hbm, high_hbm, force_hbm, bond_hbm, near_hbm,
+    own_ref, send_low_ref, send_high_ref, turned_ref, source_ref,
+    v_ref, low_ref, high_ref, near_ref, sems,
+):
+    rows, half = v_ref.shape
     atoms = rows // 3
-    half = cols // 2
-    v = v_ref[:, pl.ds(pl.multiple_of(half_ref[0] * half, 128), half)]
+    columns = pl.ds(pl.multiple_of(lax.axis_index("dir") * half, 128), half)
+    fetch(
+        (v_hbm.at[:, columns], low_hbm, high_hbm, force_hbm, bond_hbm, near_hbm),
+        (v_ref, low_ref, high_ref, source_ref.at[0:9], source_ref.at[9:10], near_ref),
+        sems,
+    )
+    source_ref[10] = near_ref[...].astype(F32)
+    v = v_ref[...]
     lane = lax.broadcasted_iota(jnp.int32, (atoms, rows), 1)
     atom = lax.broadcasted_iota(jnp.int32, (atoms, rows), 0)
     for b in range(3):
@@ -45,22 +66,26 @@
             out_ref[b * count : (b + 1) * count, :] = dot(hot, v).astype(BF16)
 
 
-def weights_kernel(force_ref, bond_ref, near_ref, hi_ref, lo_ref, table_ref):
-    steps, nine, atoms = force_ref.shape
+def weights_kernel(
+    source_ref, other_ref,
+    own_hi_ref, own_lo_ref, hi_ref, lo_ref, table_ref,
+):
+    _, steps, atoms = source_ref.shape
     groups = atoms // GROUP
-    extent = hi_ref.shape[1] // 3
+    halo = hi_ref.shape[1] // 3
+    extent = atoms + halo
+    first = lax.axis_index("dir") == 0
+    mine, other = source_ref[9], other_ref[0]
+    bonds = (jnp.where(first, mine, other), jnp.where(first, other, mine))
     lane = lax.broadcasted_iota(jnp.int32, (24, atoms), 1)
     rows = []
     for k in range(steps):
-        force = force_ref[k]
-        near = near_ref[k : k + 1, :].astype(F32)
+        force = source_ref[0:9, k, :]
+        near = source_ref[10, k : k + 1, :]
         rows.append(
             jnp.concatenate(
-                [
-                    force * bond_ref[0, k : k + 1, :],
-                    force * bond_ref[1, k : k + 1, :],
-                    jnp.broadcast_to(near, (6, atoms)),
-                ],
+                [force * bonds[0][k : k + 1, :], force * bonds[1][k : k + 1, :]]
+                + [jnp.broadcast_to(near, (6, atoms))],
                 axis=0,
             )
         )
@@ -102,41 +127,60 @@
                 at = pl.ds(pl.multiple_of((e * 3 + a) * atoms + g * GROUP, GROUP), GROUP)
                 for b in range(3):
                     r = (e * 9 + 3 * a + b) * GROUP
-                    span = slice(b * extent, (b + 1) * extent)
-                    hi_ref[at, span] = hi[r : r + GROUP]
-                    lo_ref[at, span] = lo[r : r + GROUP]
+                    near, far = slice(b * atoms, (b + 1) * atoms), slice(b * halo, (b + 1) * halo)
+                    own_hi_ref[at, near] = hi[r : r + GROUP, :atoms]
+                    own_lo_ref[at, near] = lo[r : r + GROUP, :atoms]
+                    hi_ref[at, far] = hi[r : r + GROUP, atoms:]
+                    lo_ref[at, far] = lo[r : r + GROUP, atoms:]
         return carry
 
     lax.fori_loop(0, groups, group, 0)
 
 
-def couple_kernel(hi_ref, lo_ref, own_ref, below_ref, above_ref, turned_ref, out_ref, ext_ref, flux_ref):
-    rows, half = own_ref.shape
-    atoms = rows // 3
+def own_kernel(hi_ref, lo_ref, own_ref, below_ref, above_ref, *refs):
+    quarters = len(refs) // 2 - 1
+    flux_ref, halo_ref = refs[quarters : quarters + 2]
+    own = own_ref[...]
+    part = own.shape[0] // 3
+    for at in range(0, hi_ref.shape[0], part):
+        rows = slice(at, at + part)
+        flux_ref[rows, :] = dot(hi_ref[rows, :], own) + dot(lo_ref[rows, :], own)
     count = below_ref.shape[0] // 3
-    extent = atoms + 2 * count
     for b in range(3):
-        at = b * extent
-        ext_ref[at : at + atoms] = own_ref[b * atoms : (b + 1) * atoms]
-        ext_ref[at + atoms : at + atoms + count] = below_ref[b * count : (b + 1) * count]
-        ext_ref[at + atoms + count : at + extent] = above_ref[b * count : (b + 1) * count]
-    ext = ext_ref[...]
+        at = 2 * b * count
+        halo_ref[at : at + count] = below_ref[b * count : (b + 1) * count]
+        halo_ref[at + count : at + 2 * count] = above_ref[b * count : (b + 1) * count]
+    for got_ref, given_ref in zip(refs[:quarters], refs[quarters + 2 :]):
+        given_ref[...] = got_ref[...]
+
+
+def flux_kernel(part_ref, hi_ref, lo_ref, halo_ref, flux_ref):
+    half = part_ref.shape[1]
+    atoms = flux_ref.shape[0] // 3
+    halo = halo_ref[...]
     for e in range(2):
         for a in range(3):
-            at = (e * 3 + a) * atoms
-            flux = dot(hi_ref[at : at + atoms, :], ext) + dot(lo_ref[at : at + atoms, :], ext)
+            at = slice((e * 3 + a) * atoms, (e * 3 + a + 1) * atoms)
+            flux = part_ref[at, :] + (dot(hi_ref[at, :], halo) + dot(lo_ref[at, :], halo))
             flux_ref[a * atoms : (a + 1) * atoms, e * half : (e + 1) * half] = flux.astype(BF16)
+
+
+def couple_kernel(flux_ref, *refs):
+    *quarter_refs, out_ref = refs
+    half = quarter_refs[0].shape[0]
+    block = out_ref.shape[1]
+    tiles = len(quarter_refs) // 2
+    me, core = lax.axis_index("blk"), lax.axis_index("dir")
     flux = flux_ref[...]
-    modes = turned_ref.shape[0]
-    block = out_ref.shape[1]
-    chunk = max(block, min(256, modes))
-    for at in range(0, modes, chunk):
-        term = dot(turned_ref[at : at + chunk, :], flux).astype(BF16)
-        for s in range(chunk // block):
-            for e in range(2):
-                out_ref[2 * (at // block + s) + e] = term[
-                    s * block : (s + 1) * block, e * half : (e + 1) * half
-                ]
+    for j in range(tiles):
+        tile = lax.rem(me - j + tiles, tiles)
+        for s in range(2):
+            quarter = 2 * tile + (core if s == 0 else 1 - core)
+            term = dot(quarter_refs[2 * j + s][...], flux).astype(BF16)
+            for t in range(half // block):
+                for e in range(2):
+                    at = 2 * (quarter * (half // block) + t) + e
+                    out_ref[at] = term[t * block : (t + 1) * block, e * half : (e + 1) * half]
 
 
 def sum_kernel(scale, terms_ref, out_ref):
@@ -162,61 +206,94 @@
     atoms = rows // 3
     half = cols // 2
     count = boundary_low.shape[0]
-    extent = atoms + 2 * count
-    domains = lax.axis_size("dom")
-    modes = cols * lax.axis_size("blk")
-    block = modes // domains
+    domains, tiles = lax.axis_size("dom"), lax.axis_size("blk")
+    block = cols * tiles // domains
     vmem = pl.BlockSpec(memory_space=pltpu.VMEM)
-    smem = pl.BlockSpec(memory_space=pltpu.SMEM)
-
-    own, send_low, send_high, turned = pl.pallas_call(
+    hbm = pl.BlockSpec(memory_space=pltpu.HBM)
+
+    other_bonds = shift(bond_vectors, "dir", 1)
+    lists = [boundary_low.reshape(1, count), boundary_high.reshape(1, count)]
+    forces = force_blocks.transpose(1, 0, 2)
+    own, send_low, send_high, turned, sources = pl.pallas_call(
         prep_kernel,
         out_shape=(
             shape((rows, half), BF16),
             shape((3 * count, half), BF16),
             shape((3 * count, half), BF16),
             shape((half, rows), BF16),
-        ),
-        in_specs=[smem, vmem, vmem, vmem],
-        out_specs=(vmem,) * 4,
-        compiler_params=params(),
+            shape((11, *neighbours.shape), F32),
+        ),
+        in_specs=[hbm] * 6,
+        out_specs=(vmem,) * 5,
+        scratch_shapes=[
+            pltpu.VMEM((rows, half), BF16),
+            pltpu.VMEM((1, count), jnp.int32),
+            pltpu.VMEM((1, count), jnp.int32),
+            pltpu.VMEM(neighbours.shape, jnp.int32),
+            pltpu.SemaphoreType.DMA((6,)),
+        ],
+        compiler_params=params(58),
         name="prep",
-    )(
-        lax.axis_index("dir").reshape(1),
-        panel_vectors,
-        boundary_low.reshape(1, count),
-        boundary_high.reshape(1, count),
-    )
+    )(panel_vectors, *lists, forces, bond_vectors, neighbours)
     below = shift(send_high, "dom", 1)
     above = shift(send_low, "dom", -1)
-    turned_all = lax.all_gather(turned, ("blk", "dir"), axis=0, tiled=True)
-    bonds = lax.all_gather(bond_vectors, "dir", axis=0, tiled=True)
-
-    hi, lo = pl.pallas_call(
+    quarters = [shift(turned, "blk", j) for j in range(1, tiles)]
+    turned_other = shift(turned, "dir", 1)
+
+    *own_weights, hi, lo = pl.pallas_call(
         weights_kernel,
-        out_shape=(shape((2 * rows, 3 * extent), BF16),) * 2,
-        in_specs=[vmem] * 3,
-        out_specs=(vmem,) * 2,
+        out_shape=(
+            shape((2 * rows, rows), BF16),
+            shape((2 * rows, rows), BF16),
+            shape((2 * rows, 6 * count), BF16),
+            shape((2 * rows, 6 * count), BF16),
+        ),
+        in_specs=[vmem] * 2,
+        out_specs=(vmem,) * 4,
         scratch_shapes=[pltpu.VMEM((atoms // GROUP, 24, atoms), F32)],
         compiler_params=params(32),
         cost_estimate=pl.CostEstimate(
-            flops=8 * 10**9, bytes_accessed=10**7, transcendentals=0
+            flops=7 * 10**9, bytes_accessed=10**7, transcendentals=0
         ),
         name="weights",
-    )(force_blocks, bonds, neighbours)
+    )(sources, other_bonds)
+
+    partial_flux, halo, *quarters = pl.pallas_call(
+        own_kernel,
+        out_shape=[shape((2 * rows, half), F32), shape((6 * count, half), BF16)]
+        + [shape(turned.shape, BF16)] * len(quarters),
+        in_specs=[vmem] * (5 + len(quarters)),
+        out_specs=[vmem] * (2 + len(quarters)),
+        compiler_params=params(16),
+        cost_estimate=pl.CostEstimate(
+            flops=2 * 10**9, bytes_accessed=10**6, transcendentals=0
+        ),
+        name="own",
+    )(*own_weights, own, below, above, *quarters)
+    given = [turned, turned_other]
+    for quarter in quarters:
+        given += [quarter, shift(quarter, "dir", 1)]
+
+    flux = pl.pallas_call(
+        flux_kernel,
+        out_shape=shape((rows, 2 * half), BF16),
+        in_specs=[vmem] * 4,
+        out_specs=vmem,
+        compiler_params=params(16),
+        cost_estimate=pl.CostEstimate(
+            flops=2 * 10**9, bytes_accessed=10**6, transcendentals=0
+        ),
+        name="flux",
+    )(partial_flux, hi, lo, halo)
 
     terms = pl.pallas_call(
         couple_kernel,
         out_shape=shape((2 * domains, block, half), BF16),
-        in_specs=[vmem] * 6,
+        in_specs=[vmem] * (1 + len(given)),
         out_specs=vmem,
-        scratch_shapes=[
-            pltpu.VMEM((3 * extent, half), BF16),
-            pltpu.VMEM((rows, 2 * half), BF16),
-        ],
-        compiler_params=params(32),
+        compiler_params=params(16),
         name="couple",
-    )(hi, lo, own, below, above, turned_all)
+    )(flux, *given)
 
     terms = lax.all_to_all(terms, ("dom", "dir"), split_axis=0, concat_axis=0, tiled=True)
 

time: 81.9 us -> 54.3 us (0.66)
  local copies, waits for them, and re-layouts: 14.5 us -> 0.93 us
  between operations: 13.4 us -> 0.07 us
  blocking collectives: 33 us -> 30 us
  starting transfers between devices: 5.17 us -> 7.13 us
  Pallas kernels: 12.3 us -> 13.9 us
  waiting for transfers between devices: 3.07 us -> 2.08 us
    unnamed x19 -> x6, local copies, waits for them, and re-layouts: 14.5 us -> 0.93 us
    all_gather x1 -> x0, waiting for transfers between devices: 3.05 us -> none  [per_device(): turned_all = lax.all_gather(turned, ('blk', 'dir'), axis=0, tiled=True)]
    pallas_call x1 -> x3, Pallas kernels: 6.23 us -> 9.03 us  [the longest x1 6.26 us: per_device(): pl.pallas_call(weights_kernel, out_shape=(shape((2 * rows, rows), BF16),...]
    pallas_call x1, Pallas kernels: 3.45 us -> 0.97 us  [per_device(): pl.pallas_call(couple_kernel, out_shape=shape((2 * domains, block, half),...]
    ppermute x2 -> x6, waiting for transfers between devices: 0.01 us -> 2.08 us  [shift(): lax.ppermute(value, axis, [(i, (i + by) % length) for i in range(length)])]
    all_gather x1 -> x0, blocking collectives: 2.04 us -> none  [per_device(): bonds = lax.all_gather(bond_vectors, 'dir', axis=0, tiled=True)]
    ppermute x2 -> x6, starting transfers between devices: 5.17 us -> 7.13 us  [shift(): lax.ppermute(value, axis, [(i, (i + by) % length) for i in range(length)])]
    pallas_call x1, Pallas kernels: 1.7 us -> 2.95 us  [per_device(): pl.pallas_call(prep_kernel, out_shape=(shape((rows, half), BF16), shape((...]
  transfers between devices with their start and end apart: 3 -> 6, of which waited for: 1 -> 2; matrix products, arithmetic and copies ran while one was open for 1% -> 0% of each run, Pallas kernels for 8% -> 22%
where the time goes in v2:
time: 54.3 us; the launch traced here: 54.1 us
  blocking collectives  30 us (55%)
  Pallas kernels  13.9 us (26%)
  starting transfers between devices  7.13 us (13%)
  waiting for transfers between devices  2.08 us (4%)
  local copies, waits for them, and re-layouts  0.93 us (2%)
    all_to_all x1, blocking collectives, per_device(): lax.all_to_all(terms, ('dom', 'dir'), split_axis=0, concat_axis=0, tiled=...  30 us
    ppermute x6, starting transfers between devices, shift(): lax.ppermute(value, axis, [(i, (i + by) % length) for i in range(length)])  7.13 us
    pallas_call x1, Pallas kernels, per_device(): pl.pallas_call(weights_kernel, out_shape=(shape((2 * rows, rows), BF16),...  6.26 us
    pallas_call x1, Pallas kernels, per_device(): pl.pallas_call(prep_kernel, out_shape=(shape((rows, half), BF16), shape((...  2.95 us
    ppermute x6, waiting for transfers between devices, shift(): lax.ppermute(value, axis, [(i, (i + by) % length) for i in range(length)])  2.08 us
    pallas_call x1, Pallas kernels, per_device(): pl.pallas_call(flux_kernel, out_shape=shape((rows, 2 * half), BF16), in_s...  1.38 us
    pallas_call x1, Pallas kernels, per_device(): pl.pallas_call(own_kernel, out_shape=[shape((2 * rows, half), F32), shape...  1.38 us
  transfers between devices with their start and end apart: 6, of which 2 were waited for; matrix products, arithmetic and copies ran while one was open for 0% of the time, Pallas kernels for 22%

profile of v2, /device:TPU:0, one launch (start us, length us, event | category | flops | bytes accessed | tf_op | source)
XLA Modules:
  0.0 54.1 jit_solution(13933500635164582032)
XLA Ops:
  0.0 0.5 collective-permute-start
  0.5 2.9 %prep.1 = (bf16[768,256]{1,0:T(8,128)(2,1)}, bf16[384,256]{1,0:T(8,128)(2,1)}, bf16[384,256]{1,0:T(8,128)(2,1)}, bf16[256,768]{1,0:T(8,128)(2,1)}, f32[11,16,256]{2,1,0:T(8,128)}) custom-call(bf16[768,512]{1,0:T(8,128)(2,1)} %v_hbm.1, s32[1,128]{1,0:T(1,128)} %bitcast.4, s32[1,128]{1,0:T(1,128)} %bitcast.5, f32[9,16,256]{2,1,0:T(8,128)} %bitcast.3, ...), custom_call_target="tpu_custom_call" | custom-call | tf_op jit(solution)/shard_map/prep/pallas_call | solution.py:217
  3.4 2.6 %collective-permute-start.3 = (bf16[256,768]{1,0:T(8,128)(2,1)}, bf16[256,768]{1,0:T(8,128)(2,1)S(1)}, u32[]{:S(2)}, u32[]{:S(2)}) collective-permute-start(bf16[256,768]{1,0:T(8,128)(2,1)} %get-tuple-element.23.refs_0_), channel_id=1, source_target_pairs={{0,2},{2,0},{1,3},{3,1},{4,6},{6,4},{5,7},{7,5},{8,10},{10,8},{9,1... | collective-permute-start | bytes 1179656 | tf_op jit(solution)/shard_map/ppermute | solution.py:197
  6.0 0.2 collective-permute-start.4
  6.2 1.6 %collective-permute-start.1 = (bf16[384,256]{1,0:T(8,128)(2,1)}, bf16[384,256]{1,0:T(8,128)(2,1)S(1)}, u32[]{:S(2)}, u32[]{:S(2)}) collective-permute-start(bf16[384,256]{1,0:T(8,128)(2,1)} %get-tuple-element.21), channel_id=1, source_target_pairs={{0,4},{4,8},{8,12},{12,0},{1,5},{5,9},{9,13},{13,1},{2,6},{6,10},{... | collective-permute-start | bytes 589832 | tf_op jit(solution)/shard_map/ppermute | solution.py:197
  7.8 2.2 %collective-permute-start.2 = (bf16[384,256]{1,0:T(8,128)(2,1)}, bf16[384,256]{1,0:T(8,128)(2,1)S(1)}, u32[]{:S(2)}, u32[]{:S(2)}) collective-permute-start(bf16[384,256]{1,0:T(8,128)(2,1)} %get-tuple-element.22), channel_id=1, source_target_pairs={{0,12},{4,0},{8,4},{12,8},{1,13},{5,1},{9,5},{13,9},{2,14},{6,2},{... | collective-permute-start | bytes 589832 | tf_op jit(solution)/shard_map/ppermute | solution.py:197
  10.0 0.0 collective-permute-done.other_ref
  10.0 0.0 copy-start.2
  10.0 0.9 %copy-done.2 = f32[11,16,256]{2,1,0:T(8,128)S(1)} copy-done((f32[11,16,256]{2,1,0:T(8,128)S(1)}, f32[11,16,256]{2,1,0:T(8,128)}, u32[]{:S(2)}) %copy-start.2) | copy-done | bytes 180248
  10.9 0.0 copy-start.1
  10.9 6.3 %weights.1 = (bf16[1536,768]{1,0:T(8,128)(2,1)S(1)}, bf16[1536,768]{1,0:T(8,128)(2,1)S(1)}, bf16[1536,768]{1,0:T(8,128)(2,1)S(1)}, bf16[1536,768]{1,0:T(8,128)(2,1)S(1)}) custom-call(f32[11,16,256]{2,1,0:T(8,128)S(1)} %copy-done.2, f32[1,16,256]{2,1,0:T(8,128)S(1)} %collective-permute-done.other_ref), custom_call_target="tpu_custom_call" | custom-call | flops 7000000000 | bytes 10000000 | tf_op jit(solution)/shard_map/weights/pallas_call | solution.py:243
  17.2 0.0 collective-permute-done.1.below_ref
  17.2 1.8 %collective-permute-done.2.above_ref = bf16[384,256]{1,0:T(8,128)(2,1)S(1)} collective-permute-done((bf16[384,256]{1,0:T(8,128)(2,1)}, bf16[384,256]{1,0:T(8,128)(2,1)S(1)}, u32[]{:S(2)}, u32[]{:S(2)}) %collective-permute-start.2) | collective-permute-done | bytes 196640 | tf_op jit(solution)/shard_map/ppermute | solution.py:197
  19.0 0.0 collective-permute-done.3.refs_0_
  19.0 0.0 copy-done.1
  19.0 1.4 %own.1 = (f32[1536,256]{1,0:T(8,128)S(1)}, bf16[768,256]{1,0:T(8,128)(2,1)S(1)}, bf16[256,768]{1,0:T(8,128)(2,1)S(1)}) custom-call(bf16[1536,768]{1,0:T(8,128)(2,1)S(1)} %get-tuple-element.18.hi_ref, bf16[1536,768]{1,0:T(8,128)(2,1)S(1)} %get-tuple-element.19.lo_ref, bf16[768,256]{1,0:T(8,128)(2,1)S(1)} %copy-done.1, ...), custom_call_target="tpu_custom_call" | custom-call | flops 2000000000 | bytes 1000000 | tf_op jit(solution)/shard_map/own/pallas_call | solution.py:261
  20.4 0.1 collective-permute-start.5
  20.5 0.0 copy-start
  20.5 1.4 %flux.1.flux_ref = bf16[768,512]{1,0:T(8,128)(2,1)S(1)} custom-call(f32[1536,256]{1,0:T(8,128)S(1)} %get-tuple-element.24.part_ref, bf16[1536,768]{1,0:T(8,128)(2,1)S(1)} %get-tuple-element.25.hi_ref, bf16[1536,768]{1,0:T(8,128)(2,1)S(1)} %get-tuple-element.26.lo_ref, bf16[768,256]{1,0:T(8,128)(2,1)S(1)} %get-tuple-element.27.halo_ref), custom_call_target="tpu_custom_call" | custom-call | flops 2000000000 | bytes 1000000 | tf_op jit(solution)/shard_map/flux/pallas_call | solution.py:277
  21.9 0.0 collective-permute-done.4.refs_1_
  21.9 0.3 collective-permute-done.5.refs_3_
  22.2 0.0 copy-done
  22.2 1.0 %couple.1 = bf16[8,256,256]{2,1,0:T(8,128)(2,1)S(1)} custom-call(bf16[768,512]{1,0:T(8,128)(2,1)S(1)} %flux.1.flux_ref, bf16[256,768]{1,0:T(8,128)(2,1)S(1)} %copy-done, bf16[256,768]{1,0:T(8,128)(2,1)S(1)} %collective-permute-done.4.refs_1_, bf16[256,768]{1,0:T(8,128)(2,1)S(1)} %get-tuple-element.28.refs_2_, bf16[256,768]{1,0:T(8,128)(2,1)S(1)} %collective-permute-done.5.refs_3_), custom_call_target="tpu_custom_call" | custom-call | tf_op jit(solution)/shard_map/couple/pallas_call | solution.py:289
  23.2 30.0 %all_to_all.5.refs_0_ = bf16[8,256,256]{2,1,0:T(8,128)(2,1)S(1)} all-to-all(bf16[8,256,256]{2,1,0:T(8,128)(2,1)S(1)} %couple.1), channel_id=1, replica_groups=mesh['panel'=2,'dom'=4,'blk'=2,'dir'=2] {'dom','dir'}, dimensions={0} | all-to-all | bytes 2097152 | tf_op jit(solution)/shard_map/all_to_all | solution.py:298
  53.1 0.9 %total.1 = f32[1,256,512]{2,1,0:T(8,128)} custom-call(bf16[8,256,256]{2,1,0:T(8,128)(2,1)S(1)} %all_to_all.5.refs_0_), custom_call_target="tpu_custom_call" | custom-call | tf_op jit(solution)/shard_map/total/pallas_call | solution.py:301
Async XLA Ops:
  0.0 10.0 %collective-permute-start = (f32[1,16,256]{2,1,0:T(8,128)}, f32[1,16,256]{2,1,0:T(8,128)S(1)}, u32[]{:S(2)}, u32[]{:S(2)}) collective-permute-start(f32[1,16,256]{2,1,0:T(8,128)} %bond_hbm.1), channel_id=1, source_target_pairs={{0,1},{1,0},{2,3},{3,2},{4,5},{5,4},{6,7},{7,6},{8,9},{9,8},{10,11... | collective-permute-start | bytes 49160 | tf_op jit(solution)/shard_map/ppermute | solution.py:197
  3.4 15.6 %collective-permute-start.3 = (bf16[256,768]{1,0:T(8,128)(2,1)}, bf16[256,768]{1,0:T(8,128)(2,1)S(1)}, u32[]{:S(2)}, u32[]{:S(2)}) collective-permute-start(bf16[256,768]{1,0:T(8,128)(2,1)} %get-tuple-element.23.refs_0_), channel_id=1, source_target_pairs={{0,2},{2,0},{1,3},{3,1},{4,6},{6,4},{5,7},{7,5},{8,10},{10,8},{9,1... | collective-permute-start | bytes 1179656 | tf_op jit(solution)/shard_map/ppermute | solution.py:197
  6.0 15.9 %collective-permute-start.4 = (bf16[256,768]{1,0:T(8,128)(2,1)}, bf16[256,768]{1,0:T(8,128)(2,1)S(1)}, u32[]{:S(2)}, u32[]{:S(2)}) collective-permute-start(bf16[256,768]{1,0:T(8,128)(2,1)} %get-tuple-element.23.refs_0_), channel_id=1, source_target_pairs={{0,1},{1,0},{2,3},{3,2},{4,5},{5,4},{6,7},{7,6},{8,9},{9,8},{10,11... | collective-permute-start | bytes 1179656 | tf_op jit(solution)/shard_map/ppermute | solution.py:197
  6.2 11.0 %collective-permute-start.1 = (bf16[384,256]{1,0:T(8,128)(2,1)}, bf16[384,256]{1,0:T(8,128)(2,1)S(1)}, u32[]{:S(2)}, u32[]{:S(2)}) collective-permute-start(bf16[384,256]{1,0:T(8,128)(2,1)} %get-tuple-element.21), channel_id=1, source_target_pairs={{0,4},{4,8},{8,12},{12,0},{1,5},{5,9},{9,13},{13,1},{2,6},{6,10},{... | collective-permute-start | bytes 589832 | tf_op jit(solution)/shard_map/ppermute | solution.py:197
  7.8 11.2 %collective-permute-start.2 = (bf16[384,256]{1,0:T(8,128)(2,1)}, bf16[384,256]{1,0:T(8,128)(2,1)S(1)}, u32[]{:S(2)}, u32[]{:S(2)}) collective-permute-start(bf16[384,256]{1,0:T(8,128)(2,1)} %get-tuple-element.22), channel_id=1, source_target_pairs={{0,12},{4,0},{8,4},{12,8},{1,13},{5,1},{9,5},{13,9},{2,14},{6,2},{... | collective-permute-start | bytes 589832 | tf_op jit(solution)/shard_map/ppermute | solution.py:197
  10.0 0.9 %copy-start.2 = (f32[11,16,256]{2,1,0:T(8,128)S(1)}, f32[11,16,256]{2,1,0:T(8,128)}, u32[]{:S(2)}) copy-start(f32[11,16,256]{2,1,0:T(8,128)} %get-tuple-element.17.source_ref) | copy-start | bytes 540676
  10.9 8.1 %copy-start.1 = (bf16[768,256]{1,0:T(8,128)(2,1)S(1)}, bf16[768,256]{1,0:T(8,128)(2,1)}, u32[]{:S(2)}) copy-start(bf16[768,256]{1,0:T(8,128)(2,1)} %get-tuple-element.20.own_ref) | copy-start | bytes 1179652
  20.4 1.8 %collective-permute-start.5 = (bf16[256,768]{1,0:T(8,128)(2,1)S(1)}, bf16[256,768]{1,0:T(8,128)(2,1)S(1)}, u32[]{:S(2)}, u32[]{:S(2)}) collective-permute-start(bf16[256,768]{1,0:T(8,128)(2,1)S(1)} %get-tuple-element.28.refs_2_), channel_id=1, source_target_pairs={{0,1},{1,0},{2,3},{3,2},{4,5},{5,4},{6,7},{7,6},{8,9},{9,8},{10,11... | collective-permute-start | bytes 1179656 | tf_op jit(solution)/shard_map/ppermute | solution.py:197
  20.5 1.7 %copy-start = (bf16[256,768]{1,0:T(8,128)(2,1)S(1)}, bf16[256,768]{1,0:T(8,128)(2,1)}, u32[]{:S(2)}) copy-start(bf16[256,768]{1,0:T(8,128)(2,1)} %get-tuple-element.23.refs_0_) | copy-start | bytes 1179652

commit v3 on v2

--- a/solution.py
+++ b/solution.py
@@ -74,9 +74,7 @@
     groups = atoms // GROUP
     halo = hi_ref.shape[1] // 3
     extent = atoms + halo
-    first = lax.axis_index("dir") == 0
-    mine, other = source_ref[9], other_ref[0]
-    bonds = (jnp.where(first, mine, other), jnp.where(first, other, mine))
+    bonds = (source_ref[9], other_ref[0])
     lane = lax.broadcasted_iota(jnp.int32, (24, atoms), 1)
     rows = []
     for k in range(steps):
@@ -165,22 +163,32 @@
             flux_ref[a * atoms : (a + 1) * atoms, e * half : (e + 1) * half] = flux.astype(BF16)
 
 
+def terms_of(flux_ref, quarter_refs, store, wanted=lambda tile: True):
+    tiles = len(quarter_refs) // 2
+    me, core = lax.axis_index("blk"), lax.axis_index("dir")
+    for j in range(tiles):
+        tile = lax.rem(me - j + tiles, tiles)
+
+        @pl.when(wanted(tile))
+        def _():
+            for s in range(2):
+                quarter = 2 * tile + (core if s == 0 else 1 - core)
+                store(quarter, dot(quarter_refs[2 * j + s][...], flux_ref[...]))
+
+
 def couple_kernel(flux_ref, *refs):
     *quarter_refs, out_ref = refs
     half = quarter_refs[0].shape[0]
     block = out_ref.shape[1]
-    tiles = len(quarter_refs) // 2
-    me, core = lax.axis_index("blk"), lax.axis_index("dir")
-    flux = flux_ref[...]
-    for j in range(tiles):
-        tile = lax.rem(me - j + tiles, tiles)
-        for s in range(2):
-            quarter = 2 * tile + (core if s == 0 else 1 - core)
-            term = dot(quarter_refs[2 * j + s][...], flux).astype(BF16)
-            for t in range(half // block):
-                for e in range(2):
-                    at = 2 * (quarter * (half // block) + t) + e
-                    out_ref[at] = term[t * block : (t + 1) * block, e * half : (e + 1) * half]
+    core = lax.axis_index("dir")
+
+    def store(quarter, term):
+        for t in range(half // block):
+            for e in range(2):
+                at = 2 * (quarter * (half // block) + t) + (core if e == 0 else 1 - core)
+                out_ref[at] = term[t * block : (t + 1) * block, e * half : (e + 1) * half].astype(BF16)
+
+    terms_of(flux_ref, quarter_refs, store)
 
 
 def sum_kernel(scale, terms_ref, out_ref):
@@ -192,9 +200,79 @@
         out_ref[0, :, c * half : (c + 1) * half] = total * scale
 
 
+def far_kernel(flux_ref, *refs):
+    *quarter_refs, far_ref, add_ref = refs
+    half = quarter_refs[0].shape[0]
+    home = lax.axis_index("dom")
+
+    def store(quarter, term):
+        away = quarter ^ home
+        for e in range(2):
+            part = term[:, e * half : (e + 1) * half]
+
+            @pl.when(away == 3)
+            def _():
+                far_ref[e] = part.astype(BF16)
+
+            @pl.when(away == 2)
+            def _():
+                add_ref[e] = part
+
+    terms_of(flux_ref, quarter_refs, store, lambda tile: (tile ^ (home // 2)) == 1)
+
+
+def near_kernel(flux_ref, *refs):
+    *quarter_refs, near_ref, keep_ref, give_ref = refs
+    half = quarter_refs[0].shape[0]
+    home = lax.axis_index("dom")
+
+    def store(quarter, term):
+        away = quarter ^ home
+
+        @pl.when(away == 1)
+        def _():
+            near_ref[0] = term[:, :half].astype(BF16)
+            near_ref[1] = term[:, half:].astype(BF16)
+
+        @pl.when(away == 0)
+        def _():
+            keep_ref[...] = term[:, :half]
+            give_ref[...] = term[:, half:].astype(BF16)
+
+    terms_of(flux_ref, quarter_refs, store, lambda tile: (tile ^ (home // 2)) == 0)
+
+
+def add_kernel(far_ref, add_ref, near_ref, sum0_ref, sum1_ref, near0_ref, near1_ref):
+    sum0_ref[...] = (add_ref[0] + far_ref[0].astype(F32)).astype(BF16)
+    sum1_ref[...] = (add_ref[1] + far_ref[1].astype(F32)).astype(BF16)
+    near0_ref[...] = near_ref[0]
+    near1_ref[...] = near_ref[1]
+
+
+def halving_sum_kernel(scale, keep_ref, give_ref, near0_ref, near1_ref, sum0_ref, sum1_ref, out_ref):
+    half = keep_ref.shape[1]
+    core = lax.axis_index("dir")
+    mine = pl.ds(pl.multiple_of(core * half, 128), half)
+    other = pl.ds(pl.multiple_of((1 - core) * half, 128), half)
+    for at, first, near, far in (
+        (mine, keep_ref, near0_ref, sum0_ref),
+        (other, give_ref, near1_ref, sum1_ref),
+    ):
+        total = first[...].astype(F32) + near[...].astype(F32) + far[...].astype(F32)
+        out_ref[0, :, at] = total * scale
+
+
 def shift(value, axis, by):
     length = lax.axis_size(axis)
     return lax.ppermute(value, axis, [(i, (i + by) % length) for i in range(length)])
+
+
+def swap(value, away, other_core):
+    domains = lax.axis_size("dom")
+    pairs = [
+        (2 * d + c, 2 * (d ^ away) + (c ^ other_core)) for d in range(domains) for c in range(2)
+    ]
+    return lax.ppermute(value, ("dom", "dir"), pairs)
 
 
 def shape(dims, dtype):
@@ -286,6 +364,51 @@
         name="flux",
     )(partial_flux, hi, lo, halo)
 
+    scale = (3.0 * atoms * domains) ** (-0.5)
+    result = shape((1, block, cols), F32)
+    if domains == 4 and block == half:
+        sent, kept = shape((block, half), BF16), shape((block, half), F32)
+        pair = shape((2, block, half), BF16)
+        cost = pl.CostEstimate(flops=8 * 10**8, bytes_accessed=10**6, transcendentals=0)
+        far, add = pl.pallas_call(
+            far_kernel,
+            out_shape=(pair, shape((2, block, half), F32)),
+            in_specs=[vmem] * (1 + len(given)),
+            out_specs=(vmem,) * 2,
+            compiler_params=params(16),
+            cost_estimate=cost,
+            name="far",
+        )(flux, *given)
+        far = swap(far, 1, 0)
+        near, keep, give = pl.pallas_call(
+            near_kernel,
+            out_shape=(pair, kept, sent),
+            in_specs=[vmem] * (1 + len(given)),
+            out_specs=(vmem,) * 3,
+            compiler_params=params(16),
+            cost_estimate=cost,
+            name="near",
+        )(flux, *given)
+        give = swap(give, 0, 1)
+        sum0, sum1, near0, near1 = pl.pallas_call(
+            add_kernel,
+            out_shape=(sent,) * 4,
+            in_specs=[vmem] * 3,
+            out_specs=(vmem,) * 4,
+            compiler_params=params(16),
+            name="add",
+        )(far, add, near)
+        sum0, sum1 = swap(sum0, 2, 0), swap(sum1, 2, 1)
+        near0, near1 = swap(near0, 1, 0), swap(near1, 1, 1)
+        return pl.pallas_call(
+            lambda *refs: halving_sum_kernel(scale, *refs),
+            out_shape=result,
+            in_specs=[vmem] * 6,
+            out_specs=vmem,
+            compiler_params=params(16),
+            name="total",
+        )(keep, give, near0, near1, sum0, sum1)
+
     terms = pl.pallas_call(
         couple_kernel,
         out_shape=shape((2 * domains, block, half), BF16),
@@ -294,13 +417,10 @@
         compiler_params=params(16),
         name="couple",
     )(flux, *given)
-
     terms = lax.all_to_all(terms, ("dom", "dir"), split_axis=0, concat_axis=0, tiled=True)
-
-    scale = (3.0 * atoms * domains) ** (-0.5)
     return pl.pallas_call(
         lambda *refs: sum_kernel(scale, *refs),
-        out_shape=shape((1, block, cols), F32),
+        out_shape=result,
         in_specs=[vmem],
         out_specs=vmem,
         compiler_params=params(),

time: 54.3 us -> 48.4 us (0.89)
  blocking collectives: 30 us -> 0 us
  waiting for transfers between devices: 2.08 us -> 19.9 us
  starting transfers between devices: 7.13 us -> 12.8 us
  Pallas kernels: 13.9 us -> 14.5 us
    all_to_all x1 -> x0, blocking collectives: 30 us -> none  [per_device(): lax.all_to_all(terms, ('dom', 'dir'), split_axis=0, concat_axis=0, tiled=...]
    ppermute x0 -> x6, waiting for transfers between devices: none -> 17.8 us  [swap(): return lax.ppermute(value, ('dom', 'dir'), pairs)]
    ppermute x0 -> x6, starting transfers between devices: none -> 5.72 us  [swap(): return lax.ppermute(value, ('dom', 'dir'), pairs)]
    pallas_call x2 -> x4, Pallas kernels: 1.91 us -> 2.54 us  [the longest x1 0.89 us: per_device(): pl.pallas_call(lambda *refs: halving_sum_kernel(scale, *refs), out_shape=...]
  transfers between devices with their start and end apart: 6 -> 12, of which waited for: 2 -> 6; matrix products, arithmetic and copies ran while one was open for 0% -> 0% of each run, Pallas kernels for 22% -> 27%
where the time goes in v3:
time: 48.4 us; the launch traced here: 48.3 us
  waiting for transfers between devices  19.9 us (41%)
  Pallas kernels  14.5 us (30%)
  starting transfers between devices  12.8 us (26%)
  local copies, waits for them, and re-layouts  0.93 us (2%)
    ppermute x6, waiting for transfers between devices, swap(): return lax.ppermute(value, ('dom', 'dir'), pairs)  17.8 us
    ppermute x6, starting transfers between devices, shift(): lax.ppermute(value, axis, [(i, (i + by) % length) for i in range(length)])  7.13 us
    pallas_call x1, Pallas kernels, per_device(): pl.pallas_call(weights_kernel, out_shape=(shape((2 * rows, rows), BF16),...  6.26 us
    ppermute x6, starting transfers between devices, swap(): return lax.ppermute(value, ('dom', 'dir'), pairs)  5.72 us
    pallas_call x1, Pallas kernels, per_device(): pl.pallas_call(prep_kernel, out_shape=(shape((rows, half), BF16), shape((...  2.96 us
    ppermute x6, waiting for transfers between devices, shift(): lax.ppermute(value, axis, [(i, (i + by) % length) for i in range(length)])  2.09 us
    pallas_call x1, Pallas kernels, per_device(): pl.pallas_call(flux_kernel, out_shape=shape((rows, 2 * half), BF16), in_s...  1.38 us
    pallas_call x1, Pallas kernels, per_device(): pl.pallas_call(own_kernel, out_shape=[shape((2 * rows, half), F32), shape...  1.38 us
  transfers between devices with their start and end apart: 12, of which 6 were waited for; matrix products, arithmetic and copies ran while one was open for 0% of the time, Pallas kernels for 27%

profile of v3, /device:TPU:0, one launch (start us, length us, event | category | flops | bytes accessed | tf_op | source)
XLA Modules:
  0.0 48.3 jit_solution(6595076189391365045)
XLA Ops:
  0.0 0.5 collective-permute-start
  0.5 3.0 %prep.1 = (bf16[768,256]{1,0:T(8,128)(2,1)}, bf16[384,256]{1,0:T(8,128)(2,1)}, bf16[384,256]{1,0:T(8,128)(2,1)}, bf16[256,768]{1,0:T(8,128)(2,1)}, f32[11,16,256]{2,1,0:T(8,128)}) custom-call(bf16[768,512]{1,0:T(8,128)(2,1)} %v_hbm.1, s32[1,128]{1,0:T(1,128)} %bitcast.4, s32[1,128]{1,0:T(1,128)} %bitcast.5, f32[9,16,256]{2,1,0:T(8,128)} %bitcast.3, ...), custom_call_target="tpu_custom_call" | custom-call | tf_op jit(solution)/shard_map/prep/pallas_call | solution.py:295
  3.4 2.6 %collective-permute-start.3 = (bf16[256,768]{1,0:T(8,128)(2,1)}, bf16[256,768]{1,0:T(8,128)(2,1)S(1)}, u32[]{:S(2)}, u32[]{:S(2)}) collective-permute-start(bf16[256,768]{1,0:T(8,128)(2,1)} %get-tuple-element.32.refs_0_), channel_id=1, source_target_pairs={{0,2},{2,0},{1,3},{3,1},{4,6},{6,4},{5,7},{7,5},{8,10},{10,8},{9,1... | collective-permute-start | bytes 1179656 | tf_op jit(solution)/shard_map/ppermute | solution.py:267
  6.0 0.2 collective-permute-start.4
  6.2 1.6 %collective-permute-start.1 = (bf16[384,256]{1,0:T(8,128)(2,1)}, bf16[384,256]{1,0:T(8,128)(2,1)S(1)}, u32[]{:S(2)}, u32[]{:S(2)}) collective-permute-start(bf16[384,256]{1,0:T(8,128)(2,1)} %get-tuple-element.30), channel_id=1, source_target_pairs={{0,4},{4,8},{8,12},{12,0},{1,5},{5,9},{9,13},{13,1},{2,6},{6,10},{... | collective-permute-start | bytes 589832 | tf_op jit(solution)/shard_map/ppermute | solution.py:267
  7.8 2.2 %collective-permute-start.2 = (bf16[384,256]{1,0:T(8,128)(2,1)}, bf16[384,256]{1,0:T(8,128)(2,1)S(1)}, u32[]{:S(2)}, u32[]{:S(2)}) collective-permute-start(bf16[384,256]{1,0:T(8,128)(2,1)} %get-tuple-element.31), channel_id=1, source_target_pairs={{0,12},{4,0},{8,4},{12,8},{1,13},{5,1},{9,5},{13,9},{2,14},{6,2},{... | collective-permute-start | bytes 589832 | tf_op jit(solution)/shard_map/ppermute | solution.py:267
  10.0 0.0 collective-permute-done.other_ref
  10.0 0.0 copy-start.2
  10.0 0.9 %copy-done.2 = f32[11,16,256]{2,1,0:T(8,128)S(1)} copy-done((f32[11,16,256]{2,1,0:T(8,128)S(1)}, f32[11,16,256]{2,1,0:T(8,128)}, u32[]{:S(2)}) %copy-start.2) | copy-done | bytes 180248
  10.9 0.0 copy-start.1
  11.0 6.3 %weights.1 = (bf16[1536,768]{1,0:T(8,128)(2,1)S(1)}, bf16[1536,768]{1,0:T(8,128)(2,1)S(1)}, bf16[1536,768]{1,0:T(8,128)(2,1)S(1)}, bf16[1536,768]{1,0:T(8,128)(2,1)S(1)}) custom-call(f32[11,16,256]{2,1,0:T(8,128)S(1)} %copy-done.2, f32[1,16,256]{2,1,0:T(8,128)S(1)} %collective-permute-done.other_ref), custom_call_target="tpu_custom_call" | custom-call | flops 7000000000 | bytes 10000000 | tf_op jit(solution)/shard_map/weights/pallas_call | solution.py:321
  17.2 0.0 collective-permute-done.1.below_ref
  17.2 1.8 %collective-permute-done.2.above_ref = bf16[384,256]{1,0:T(8,128)(2,1)S(1)} collective-permute-done((bf16[384,256]{1,0:T(8,128)(2,1)}, bf16[384,256]{1,0:T(8,128)(2,1)S(1)}, u32[]{:S(2)}, u32[]{:S(2)}) %collective-permute-start.2) | collective-permute-done | bytes 196640 | tf_op jit(solution)/shard_map/ppermute | solution.py:267
  19.0 0.0 collective-permute-done.3.refs_0_
  19.0 0.0 copy-done.1
  19.0 1.4 %own.1 = (f32[1536,256]{1,0:T(8,128)S(1)}, bf16[768,256]{1,0:T(8,128)(2,1)S(1)}, bf16[256,768]{1,0:T(8,128)(2,1)S(1)}) custom-call(bf16[1536,768]{1,0:T(8,128)(2,1)S(1)} %get-tuple-element.27.hi_ref, bf16[1536,768]{1,0:T(8,128)(2,1)S(1)} %get-tuple-element.28.lo_ref, bf16[768,256]{1,0:T(8,128)(2,1)S(1)} %copy-done.1, ...), custom_call_target="tpu_custom_call" | custom-call | flops 2000000000 | bytes 1000000 | tf_op jit(solution)/shard_map/own/pallas_call | solution.py:339
  20.4 0.1 collective-permute-start.5
  20.5 0.0 copy-start
  20.5 1.4 %flux.1.flux_ref = bf16[768,512]{1,0:T(8,128)(2,1)S(1)} custom-call(f32[1536,256]{1,0:T(8,128)S(1)} %get-tuple-element.33.part_ref, bf16[1536,768]{1,0:T(8,128)(2,1)S(1)} %get-tuple-element.34.hi_ref, bf16[1536,768]{1,0:T(8,128)(2,1)S(1)} %get-tuple-element.35.lo_ref, bf16[768,256]{1,0:T(8,128)(2,1)S(1)} %get-tuple-element.36.halo_ref), custom_call_target="tpu_custom_call" | custom-call | flops 2000000000 | bytes 1000000 | tf_op jit(solution)/shard_map/flux/pallas_call | solution.py:355
  21.9 0.0 collective-permute-done.4.refs_1_
  21.9 0.3 collective-permute-done.5.refs_3_
  22.2 0.0 copy-done
  22.2 0.8 %far.1 = (bf16[2,256,256]{2,1,0:T(8,128)(2,1)S(1)}, f32[2,256,256]{2,1,0:T(8,128)S(1)}) custom-call(bf16[768,512]{1,0:T(8,128)(2,1)S(1)} %flux.1.flux_ref, bf16[256,768]{1,0:T(8,128)(2,1)S(1)} %copy-done, bf16[256,768]{1,0:T(8,128)(2,1)S(1)} %collective-permute-done.4.refs_1_, bf16[256,768]{1,0:T(8,128)(2,1)S(1)} %get-tuple-element.37.refs_2_, ...), custom_call_target="tpu_custom_call" | custom-call | flops 800000000 | bytes 1000000 | tf_op jit(solution)/shard_map/far/pallas_call | solution.py:373
  23.0 1.2 %collective-permute-start.7 = (bf16[2,256,256]{2,1,0:T(8,128)(2,1)S(1)}, bf16[2,256,256]{2,1,0:T(8,128)(2,1)S(1)}, u32[]{:S(2)}, u32[]{:S(2)}) collective-permute-start(bf16[2,256,256]{2,1,0:T(8,128)(2,1)S(1)} %get-tuple-element.40), channel_id=1, source_target_pairs={{0,4},{1,5},{4,0},{5,1},{8,12},{9,13},{12,8},{13,9},{2,6},{3,7},{6... | collective-permute-start | bytes 786440 | tf_op jit(solution)/shard_map/ppermute | solution.py:275
  24.2 0.8 %near.1 = (bf16[2,256,256]{2,1,0:T(8,128)(2,1)S(1)}, f32[256,256]{1,0:T(8,128)S(1)}, bf16[256,256]{1,0:T(8,128)(2,1)S(1)}) custom-call(bf16[768,512]{1,0:T(8,128)(2,1)S(1)} %flux.1.flux_ref, bf16[256,768]{1,0:T(8,128)(2,1)S(1)} %copy-done, bf16[256,768]{1,0:T(8,128)(2,1)S(1)} %collective-permute-done.4.refs_1_, ...), custom_call_target="tpu_custom_call" | custom-call | flops 800000000 | bytes 1000000 | tf_op jit(solution)/shard_map/near/pallas_call | solution.py:383
  25.0 0.1 collective-permute-start.6
  25.1 6.4 %collective-permute-done.7.far_ref = bf16[2,256,256]{2,1,0:T(8,128)(2,1)S(1)} collective-permute-done((bf16[2,256,256]{2,1,0:T(8,128)(2,1)S(1)}, bf16[2,256,256]{2,1,0:T(8,128)(2,1)S(1)}, u32[]{:S(2)}, u32[]{:S(2)}) %collective-permute-start.7) | collective-permute-done | bytes 262176 | tf_op jit(solution)/shard_map/ppermute | solution.py:275
  31.5 0.1 add.1
  31.6 1.4 %collective-permute-start.10 = (bf16[256,256]{1,0:T(8,128)(2,1)S(1)}, bf16[256,256]{1,0:T(8,128)(2,1)S(1)}, u32[]{:S(2)}, u32[]{:S(2)}) collective-permute-start(bf16[256,256]{1,0:T(8,128)(2,1)S(1)} %get-tuple-element.45), channel_id=1, source_target_pairs={{0,8},{1,9},{4,12},{5,13},{8,0},{9,1},{12,4},{13,5},{2,10},{3,11},... | collective-permute-start | bytes 393224 | tf_op jit(solution)/shard_map/ppermute | solution.py:275
  32.9 0.4 collective-permute-start.11
  33.3 1.2 %collective-permute-start.8 = (bf16[256,256]{1,0:T(8,128)(2,1)S(1)}, bf16[256,256]{1,0:T(8,128)(2,1)S(1)}, u32[]{:S(2)}, u32[]{:S(2)}) collective-permute-start(bf16[256,256]{1,0:T(8,128)(2,1)S(1)} %get-tuple-element.43), channel_id=1, source_target_pairs={{0,4},{1,5},{4,0},{5,1},{8,12},{9,13},{12,8},{13,9},{2,6},{3,7},{6... | collective-permute-start | bytes 393224 | tf_op jit(solution)/shard_map/ppermute | solution.py:275
  34.5 1.5 %collective-permute-start.9 = (bf16[256,256]{1,0:T(8,128)(2,1)S(1)}, bf16[256,256]{1,0:T(8,128)(2,1)S(1)}, u32[]{:S(2)}, u32[]{:S(2)}) collective-permute-start(bf16[256,256]{1,0:T(8,128)(2,1)S(1)} %get-tuple-element.44), channel_id=1, source_target_pairs={{0,5},{1,4},{4,1},{5,0},{8,13},{9,12},{12,9},{13,8},{2,7},{3,6},{6... | collective-permute-start | bytes 393224 | tf_op jit(solution)/shard_map/ppermute | solution.py:275
  36.0 0.0 collective-permute-done.6.refs_1_
  36.0 7.8 %collective-permute-done.10.refs_4_ = bf16[256,256]{1,0:T(8,128)(2,1)S(1)} collective-permute-done((bf16[256,256]{1,0:T(8,128)(2,1)S(1)}, bf16[256,256]{1,0:T(8,128)(2,1)S(1)}, u32[]{:S(2)}, u32[]{:S(2)}) %collective-permute-start.10) | collective-permute-done | bytes 131104 | tf_op jit(solution)/shard_map/ppermute | solution.py:275
  43.8 1.4 %collective-permute-done.11.refs_5_ = bf16[256,256]{1,0:T(8,128)(2,1)S(1)} collective-permute-done((bf16[256,256]{1,0:T(8,128)(2,1)S(1)}, bf16[256,256]{1,0:T(8,128)(2,1)S(1)}, u32[]{:S(2)}, u32[]{:S(2)}) %collective-permute-start.11) | collective-permute-done | bytes 131104 | tf_op jit(solution)/shard_map/ppermute | solution.py:275
  45.1 0.0 collective-permute-done.8.refs_2_
  45.1 2.2 %collective-permute-done.9.refs_3_ = bf16[256,256]{1,0:T(8,128)(2,1)S(1)} collective-permute-done((bf16[256,256]{1,0:T(8,128)(2,1)S(1)}, bf16[256,256]{1,0:T(8,128)(2,1)S(1)}, u32[]{:S(2)}, u32[]{:S(2)}) %collective-permute-start.9) | collective-permute-done | bytes 131104 | tf_op jit(solution)/shard_map/ppermute | solution.py:275
  47.4 0.9 %total.1 = f32[1,256,512]{2,1,0:T(8,128)} custom-call(f32[256,256]{1,0:T(8,128)S(1)} %get-tuple-element.38.refs_0_, bf16[256,256]{1,0:T(8,128)(2,1)S(1)} %collective-permute-done.6.refs_1_, bf16[256,256]{1,0:T(8,128)(2,1)S(1)} %collective-permute-done.8.refs_2_, bf16[256,256]{1,0:T(8,128)(2,1)S(1)} %collective-permute-done.9.refs_3_, ...), custom_call_target="tpu_custom_call" | custom-call | tf_op jit(solution)/shard_map/total/pallas_call | solution.py:403
Async XLA Ops:
  0.0 10.0 %collective-permute-start = (f32[1,16,256]{2,1,0:T(8,128)}, f32[1,16,256]{2,1,0:T(8,128)S(1)}, u32[]{:S(2)}, u32[]{:S(2)}) collective-permute-start(f32[1,16,256]{2,1,0:T(8,128)} %bond_hbm.1), channel_id=1, source_target_pairs={{0,1},{1,0},{2,3},{3,2},{4,5},{5,4},{6,7},{7,6},{8,9},{9,8},{10,11... | collective-permute-start | bytes 49160 | tf_op jit(solution)/shard_map/ppermute | solution.py:267
  3.4 15.6 %collective-permute-start.3 = (bf16[256,768]{1,0:T(8,128)(2,1)}, bf16[256,768]{1,0:T(8,128)(2,1)S(1)}, u32[]{:S(2)}, u32[]{:S(2)}) collective-permute-start(bf16[256,768]{1,0:T(8,128)(2,1)} %get-tuple-element.32.refs_0_), channel_id=1, source_target_pairs={{0,2},{2,0},{1,3},{3,1},{4,6},{6,4},{5,7},{7,5},{8,10},{10,8},{9,1... | collective-permute-start | bytes 1179656 | tf_op jit(solution)/shard_map/ppermute | solution.py:267
  6.0 15.9 %collective-permute-start.4 = (bf16[256,768]{1,0:T(8,128)(2,1)}, bf16[256,768]{1,0:T(8,128)(2,1)S(1)}, u32[]{:S(2)}, u32[]{:S(2)}) collective-permute-start(bf16[256,768]{1,0:T(8,128)(2,1)} %get-tuple-element.32.refs_0_), channel_id=1, source_target_pairs={{0,1},{1,0},{2,3},{3,2},{4,5},{5,4},{6,7},{7,6},{8,9},{9,8},{10,11... | collective-permute-start | bytes 1179656 | tf_op jit(solution)/shard_map/ppermute | solution.py:267
  6.2 11.0 %collective-permute-start.1 = (bf16[384,256]{1,0:T(8,128)(2,1)}, bf16[384,256]{1,0:T(8,128)(2,1)S(1)}, u32[]{:S(2)}, u32[]{:S(2)}) collective-permute-start(bf16[384,256]{1,0:T(8,128)(2,1)} %get-tuple-element.30), channel_id=1, source_target_pairs={{0,4},{4,8},{8,12},{12,0},{1,5},{5,9},{9,13},{13,1},{2,6},{6,10},{... | collective-permute-start | bytes 589832 | tf_op jit(solution)/shard_map/ppermute | solution.py:267
  7.8 11.2 %collective-permute-start.2 = (bf16[384,256]{1,0:T(8,128)(2,1)}, bf16[384,256]{1,0:T(8,128)(2,1)S(1)}, u32[]{:S(2)}, u32[]{:S(2)}) collective-permute-start(bf16[384,256]{1,0:T(8,128)(2,1)} %get-tuple-element.31), channel_id=1, source_target_pairs={{0,12},{4,0},{8,4},{12,8},{1,13},{5,1},{9,5},{13,9},{2,14},{6,2},{... | collective-permute-start | bytes 589832 | tf_op jit(solution)/shard_map/ppermute | solution.py:267
  10.0 0.9 %copy-start.2 = (f32[11,16,256]{2,1,0:T(8,128)S(1)}, f32[11,16,256]{2,1,0:T(8,128)}, u32[]{:S(2)}) copy-start(f32[11,16,256]{2,1,0:T(8,128)} %get-tuple-element.26.source_ref) | copy-start | bytes 540676
  10.9 8.1 %copy-start.1 = (bf16[768,256]{1,0:T(8,128)(2,1)S(1)}, bf16[768,256]{1,0:T(8,128)(2,1)}, u32[]{:S(2)}) copy-start(bf16[768,256]{1,0:T(8,128)(2,1)} %get-tuple-element.29.own_ref) | copy-start | bytes 1179652
  20.4 1.8 %collective-permute-start.5 = (bf16[256,768]{1,0:T(8,128)(2,1)S(1)}, bf16[256,768]{1,0:T(8,128)(2,1)S(1)}, u32[]{:S(2)}, u32[]{:S(2)}) collective-permute-start(bf16[256,768]{1,0:T(8,128)(2,1)S(1)} %get-tuple-element.37.refs_2_), channel_id=1, source_target_pairs={{0,1},{1,0},{2,3},{3,2},{4,5},{5,4},{6,7},{7,6},{8,9},{9,8},{10,11... | collective-permute-start | bytes 1179656 | tf_op jit(solution)/shard_map/ppermute | solution.py:267
  20.5 1.7 %copy-start = (bf16[256,768]{1,0:T(8,128)(2,1)S(1)}, bf16[256,768]{1,0:T(8,128)(2,1)}, u32[]{:S(2)}) copy-start(bf16[256,768]{1,0:T(8,128)(2,1)} %get-tuple-element.32.refs_0_) | copy-start | bytes 1179652
  23.0 8.5 %collective-permute-start.7 = (bf16[2,256,256]{2,1,0:T(8,128)(2,1)S(1)}, bf16[2,256,256]{2,1,0:T(8,128)(2,1)S(1)}, u32[]{:S(2)}, u32[]{:S(2)}) collective-permute-start(bf16[2,256,256]{2,1,0:T(8,128)(2,1)S(1)} %get-tuple-element.40), channel_id=1, source_target_pairs={{0,4},{1,5},{4,0},{5,1},{8,12},{9,13},{12,8},{13,9},{2,6},{3,7},{6... | collective-permute-start | bytes 786440 | tf_op jit(solution)/shard_map/ppermute | solution.py:275
  25.0 11.0 %collective-permute-start.6 = (bf16[256,256]{1,0:T(8,128)(2,1)S(1)}, bf16[256,256]{1,0:T(8,128)(2,1)S(1)}, u32[]{:S(2)}, u32[]{:S(2)}) collective-permute-start(bf16[256,256]{1,0:T(8,128)(2,1)S(1)} %get-tuple-element.39), channel_id=1, source_target_pairs={{0,1},{1,0},{4,5},{5,4},{8,9},{9,8},{12,13},{13,12},{2,3},{3,2},{6... | collective-permute-start | bytes 393224 | tf_op jit(solution)/shard_map/ppermute | solution.py:275
  31.6 12.2 %collective-permute-start.10 = (bf16[256,256]{1,0:T(8,128)(2,1)S(1)}, bf16[256,256]{1,0:T(8,128)(2,1)S(1)}, u32[]{:S(2)}, u32[]{:S(2)}) collective-permute-start(bf16[256,256]{1,0:T(8,128)(2,1)S(1)} %get-tuple-element.45), channel_id=1, source_target_pairs={{0,8},{1,9},{4,12},{5,13},{8,0},{9,1},{12,4},{13,5},{2,10},{3,11},... | collective-permute-start | bytes 393224 | tf_op jit(solution)/shard_map/ppermute | solution.py:275
  32.9 12.2 %collective-permute-start.11 = (bf16[256,256]{1,0:T(8,128)(2,1)S(1)}, bf16[256,256]{1,0:T(8,128)(2,1)S(1)}, u32[]{:S(2)}, u32[]{:S(2)}) collective-permute-start(bf16[256,256]{1,0:T(8,128)(2,1)S(1)} %get-tuple-element.46), channel_id=1, source_target_pairs={{0,9},{1,8},{4,13},{5,12},{8,1},{9,0},{12,5},{13,4},{2,11},{3,10},... | collective-permute-start | bytes 393224 | tf_op jit(solution)/shard_map/ppermute | solution.py:275
  33.3 11.9 %collective-permute-start.8 = (bf16[256,256]{1,0:T(8,128)(2,1)S(1)}, bf16[256,256]{1,0:T(8,128)(2,1)S(1)}, u32[]{:S(2)}, u32[]{:S(2)}) collective-permute-start(bf16[256,256]{1,0:T(8,128)(2,1)S(1)} %get-tuple-element.43), channel_id=1, source_target_pairs={{0,4},{1,5},{4,0},{5,1},{8,12},{9,13},{12,8},{13,9},{2,6},{3,7},{6... | collective-permute-start | bytes 393224 | tf_op jit(solution)/shard_map/ppermute | solution.py:275
  34.5 12.9 %collective-permute-start.9 = (bf16[256,256]{1,0:T(8,128)(2,1)S(1)}, bf16[256,256]{1,0:T(8,128)(2,1)S(1)}, u32[]{:S(2)}, u32[]{:S(2)}) collective-permute-start(bf16[256,256]{1,0:T(8,128)(2,1)S(1)} %get-tuple-element.44), channel_id=1, source_target_pairs={{0,5},{1,4},{4,1},{5,0},{8,13},{9,12},{12,9},{13,8},{2,7},{3,6},{6... | collective-permute-start | bytes 393224 | tf_op jit(solution)/shard_map/ppermute | solution.py:275

commit v4 on v3

--- a/solution.py
+++ b/solution.py
@@ -33,17 +33,37 @@
         copy.wait()
 
 
+def my_columns(half):
+    return pl.ds(pl.multiple_of(lax.axis_index("dir") * half, 128), half)
+
+
+def boundary_kernel(
+    v_hbm, low_hbm, high_hbm, send_low_ref, send_high_ref, v_ref, low_ref, high_ref, sems
+):
+    rows, half = v_ref.shape
+    fetch((v_hbm.at[:, my_columns(half)], low_hbm, high_hbm), (v_ref, low_ref, high_ref), sems)
+    v = v_ref[...]
+    for list_ref, out_ref in ((low_ref, send_low_ref), (high_ref, send_high_ref)):
+        count = list_ref.shape[1]
+        named = jnp.broadcast_to(list_ref[...], (128, count)).T
+        lane = lax.broadcasted_iota(jnp.int32, (count, 128), 1)
+        for b in range(3):
+            wanted = 3 * named + b
+            hot = jnp.concatenate(
+                [one_hot(lane + t * 128 == wanted) for t in range(rows // 128)], axis=1
+            )
+            out_ref[b * count : (b + 1) * count, :] = dot(hot, v).astype(BF16)
+
+
 def prep_kernel(
-    v_hbm, low_hbm, high_hbm, force_hbm, bond_hbm, near_hbm,
-    own_ref, send_low_ref, send_high_ref, turned_ref, source_ref,
-    v_ref, low_ref, high_ref, near_ref, sems,
+    v_hbm, force_hbm, bond_hbm, near_hbm, sent0_hbm, sent1_hbm,
+    own_ref, turned_ref, source_ref, v_ref, near_ref, sems,
 ):
     rows, half = v_ref.shape
     atoms = rows // 3
-    columns = pl.ds(pl.multiple_of(lax.axis_index("dir") * half, 128), half)
     fetch(
-        (v_hbm.at[:, columns], low_hbm, high_hbm, force_hbm, bond_hbm, near_hbm),
-        (v_ref, low_ref, high_ref, source_ref.at[0:9], source_ref.at[9:10], near_ref),
+        (v_hbm.at[:, my_columns(half)], force_hbm, bond_hbm, near_hbm),
+        (v_ref, source_ref.at[0:9], source_ref.at[9:10], near_ref),
         sems,
     )
     source_ref[10] = near_ref[...].astype(F32)
@@ -54,21 +74,11 @@
         picked = dot(one_hot(lane == 3 * atom + b), v)
         own_ref[b * atoms : (b + 1) * atoms, :] = picked.astype(BF16)
         turned_ref[:, b * atoms : (b + 1) * atoms] = picked.T.astype(BF16)
-    for list_ref, out_ref in ((low_ref, send_low_ref), (high_ref, send_high_ref)):
-        count = list_ref.shape[1]
-        named = jnp.broadcast_to(list_ref[...], (128, count)).T
-        lane = lax.broadcasted_iota(jnp.int32, (count, 128), 1)
-        for b in range(3):
-            wanted = 3 * named + b
-            hot = jnp.concatenate(
-                [one_hot(lane + t * 128 == wanted) for t in range(rows // 128)], axis=1
-            )
-            out_ref[b * count : (b + 1) * count, :] = dot(hot, v).astype(BF16)
 
 
 def weights_kernel(
-    source_ref, other_ref,
-    own_hi_ref, own_lo_ref, hi_ref, lo_ref, table_ref,
+    source_ref, other_ref, own_ref,
+    flux_ref, hi_ref, lo_ref, table_ref, own_hi_ref, own_lo_ref,
 ):
     _, steps, atoms = source_ref.shape
     groups = atoms // GROUP
@@ -106,11 +116,14 @@
         lax.broadcasted_iota(jnp.int32, (GROUP, atoms), 1) % GROUP
         == lax.broadcasted_iota(jnp.int32, (GROUP, atoms), 0)
     )
-    target = lax.broadcasted_iota(jnp.int32, (extent, atoms), 0).astype(F32)
-
-    def group(g, carry):
+    target = lax.broadcasted_iota(jnp.int32, (256, atoms), 0).astype(F32).astype(BF16)
+
+    def group(g):
         table = table_ref[g]
-        hot = one_hot(target == table[18:19, :])
+        named = [(table[18:19, :] - at).astype(BF16) for at in range(0, extent, 256)]
+        hot = jnp.concatenate(
+            [jnp.where(target == name, BF16(1), BF16(0)) for name in named], axis=0
+        )
         spread = jnp.concatenate(
             [jnp.where(mask, table[r : r + 1, :], 0.0) for r in range(18)], axis=0
         )
@@ -130,25 +143,28 @@
                     own_lo_ref[at, near] = lo[r : r + GROUP, :atoms]
                     hi_ref[at, far] = hi[r : r + GROUP, atoms:]
                     lo_ref[at, far] = lo[r : r + GROUP, atoms:]
+
+    def several(step, carry):
+        for g in range(4):
+            group(4 * step + g)
         return carry
 
-    lax.fori_loop(0, groups, group, 0)
-
-
-def own_kernel(hi_ref, lo_ref, own_ref, below_ref, above_ref, *refs):
-    quarters = len(refs) // 2 - 1
-    flux_ref, halo_ref = refs[quarters : quarters + 2]
+    lax.fori_loop(0, groups // 4, several, 0)
     own = own_ref[...]
-    part = own.shape[0] // 3
-    for at in range(0, hi_ref.shape[0], part):
-        rows = slice(at, at + part)
-        flux_ref[rows, :] = dot(hi_ref[rows, :], own) + dot(lo_ref[rows, :], own)
+    for part in range(6):
+        at = slice(part * atoms, (part + 1) * atoms)
+        flux_ref[at, :] = dot(own_hi_ref[at, :], own) + dot(own_lo_ref[at, :], own)
+
+
+def relay_kernel(below_ref, above_ref, part_hbm, *refs):
+    quarters = len(refs) // 2
+    halo_ref = refs[quarters]
     count = below_ref.shape[0] // 3
     for b in range(3):
         at = 2 * b * count
         halo_ref[at : at + count] = below_ref[b * count : (b + 1) * count]
         halo_ref[at + count : at + 2 * count] = above_ref[b * count : (b + 1) * count]
-    for got_ref, given_ref in zip(refs[:quarters], refs[quarters + 2 :]):
+    for got_ref, given_ref in zip(refs[:quarters], refs[quarters + 1 :]):
         given_ref[...] = got_ref[...]
 
 
@@ -289,65 +305,78 @@
     vmem = pl.BlockSpec(memory_space=pltpu.VMEM)
     hbm = pl.BlockSpec(memory_space=pltpu.HBM)
 
+    lists = [boundary_low.reshape(1, count), boundary_high.reshape(1, count)]
+    send_low, send_high = pl.pallas_call(
+        boundary_kernel,
+        out_shape=(shape((3 * count, half), BF16),) * 2,
+        in_specs=[hbm] * 3,
+        out_specs=(vmem,) * 2,
+        scratch_shapes=[
+            pltpu.VMEM((rows, half), BF16),
+            pltpu.VMEM((1, count), jnp.int32),
+            pltpu.VMEM((1, count), jnp.int32),
+            pltpu.SemaphoreType.DMA((3,)),
+        ],
+        compiler_params=params(58),
+        name="boundary",
+    )(panel_vectors, *lists)
+    below = shift(send_high, "dom", 1)
+    above = shift(send_low, "dom", -1)
+
     other_bonds = shift(bond_vectors, "dir", 1)
-    lists = [boundary_low.reshape(1, count), boundary_high.reshape(1, count)]
     forces = force_blocks.transpose(1, 0, 2)
-    own, send_low, send_high, turned, sources = pl.pallas_call(
+    own, turned, sources = pl.pallas_call(
         prep_kernel,
         out_shape=(
             shape((rows, half), BF16),
-            shape((3 * count, half), BF16),
-            shape((3 * count, half), BF16),
             shape((half, rows), BF16),
             shape((11, *neighbours.shape), F32),
         ),
         in_specs=[hbm] * 6,
-        out_specs=(vmem,) * 5,
+        out_specs=(vmem,) * 3,
         scratch_shapes=[
             pltpu.VMEM((rows, half), BF16),
-            pltpu.VMEM((1, count), jnp.int32),
-            pltpu.VMEM((1, count), jnp.int32),
             pltpu.VMEM(neighbours.shape, jnp.int32),
-            pltpu.SemaphoreType.DMA((6,)),
+            pltpu.SemaphoreType.DMA((4,)),
         ],
         compiler_params=params(58),
+        cost_estimate=pl.CostEstimate(
+            flops=10**9, bytes_accessed=10**6, transcendentals=0
+        ),
         name="prep",
-    )(panel_vectors, *lists, forces, bond_vectors, neighbours)
-    below = shift(send_high, "dom", 1)
-    above = shift(send_low, "dom", -1)
+    )(panel_vectors, forces, bond_vectors, neighbours, send_high, send_low)
     quarters = [shift(turned, "blk", j) for j in range(1, tiles)]
     turned_other = shift(turned, "dir", 1)
 
-    *own_weights, hi, lo = pl.pallas_call(
+    partial_flux, hi, lo = pl.pallas_call(
         weights_kernel,
         out_shape=(
-            shape((2 * rows, rows), BF16),
-            shape((2 * rows, rows), BF16),
+            shape((2 * rows, half), F32),
             shape((2 * rows, 6 * count), BF16),
             shape((2 * rows, 6 * count), BF16),
         ),
-        in_specs=[vmem] * 2,
-        out_specs=(vmem,) * 4,
-        scratch_shapes=[pltpu.VMEM((atoms // GROUP, 24, atoms), F32)],
+        in_specs=[vmem] * 3,
+        out_specs=(vmem,) * 3,
+        scratch_shapes=[
+            pltpu.VMEM((atoms // GROUP, 24, atoms), F32),
+            pltpu.VMEM((2 * rows, rows), BF16),
+            pltpu.VMEM((2 * rows, rows), BF16),
+        ],
         compiler_params=params(32),
         cost_estimate=pl.CostEstimate(
-            flops=7 * 10**9, bytes_accessed=10**7, transcendentals=0
+            flops=8*10**9, bytes_accessed=10**7, transcendentals=0
         ),
         name="weights",
-    )(sources, other_bonds)
-
-    partial_flux, halo, *quarters = pl.pallas_call(
-        own_kernel,
-        out_shape=[shape((2 * rows, half), F32), shape((6 * count, half), BF16)]
-        + [shape(turned.shape, BF16)] * len(quarters),
-        in_specs=[vmem] * (5 + len(quarters)),
-        out_specs=[vmem] * (2 + len(quarters)),
+    )(sources, other_bonds, own)
+
+    halo, *quarters = pl.pallas_call(
+        relay_kernel,
+        out_shape=[shape((6 * count, half), BF16)] + [shape(turned.shape, BF16)] * (tiles - 1),
+        in_specs=[vmem, vmem, pl.BlockSpec(memory_space=pl.ANY)] + [vmem] * len(quarters),
+        out_specs=[vmem] * tiles,
         compiler_params=params(16),
-        cost_estimate=pl.CostEstimate(
-            flops=2 * 10**9, bytes_accessed=10**6, transcendentals=0
-        ),
-        name="own",
-    )(*own_weights, own, below, above, *quarters)
+        name="relay",
+    )(below, above, partial_flux, *quarters)
     given = [turned, turned_other]
     for quarter in quarters:
         given += [quarter, shift(quarter, "dir", 1)]

time: 48.4 us -> 50.4 us (1.041)
  waiting for transfers between devices: 19.9 us -> 22.5 us
  starting transfers between devices: 12.8 us -> 11.8 us
  local copies, waits for them, and re-layouts: 0.93 us -> 1.92 us
  Pallas kernels: 14.5 us -> 13.9 us
    ppermute x6, waiting for transfers between devices: 17.8 us -> 19.4 us  [swap(): return lax.ppermute(value, ('dom', 'dir'), pairs)]
    unnamed x6, local copies, waits for them, and re-layouts: 0.93 us -> 1.92 us
    ppermute x6, waiting for transfers between devices: 2.09 us -> 3.08 us  [shift(): lax.ppermute(value, axis, [(i, (i + by) % length) for i in range(length)])]
    ppermute x6, starting transfers between devices: 5.72 us -> 4.82 us  [swap(): return lax.ppermute(value, ('dom', 'dir'), pairs)]
    pallas_call x2 -> x3, Pallas kernels: 7.64 us -> 7.45 us  [the longest x1 5.09 us: per_device(): pl.pallas_call(weights_kernel, out_shape=(shape((2 * rows, half), F32), s...]
  transfers between devices with their start and end apart: 12 -> 12, of which waited for: 6 -> 5; matrix products, arithmetic and copies ran while one was open for 0% -> 0% of each run, Pallas kernels for 27% -> 24%
where the time goes in v4:
time: 50.4 us; the launch traced here: 50.2 us
  waiting for transfers between devices  22.5 us (45%)
  Pallas kernels  13.9 us (28%)
  starting transfers between devices  11.8 us (23%)
  local copies, waits for them, and re-layouts  1.92 us (4%)
    ppermute x6, waiting for transfers between devices, swap(): return lax.ppermute(value, ('dom', 'dir'), pairs)  19.4 us
    ppermute x6, starting transfers between devices, shift(): lax.ppermute(value, axis, [(i, (i + by) % length) for i in range(length)])  6.96 us
    pallas_call x1, Pallas kernels, per_device(): pl.pallas_call(weights_kernel, out_shape=(shape((2 * rows, half), F32), s...  5.09 us
    ppermute x6, starting transfers between devices, swap(): return lax.ppermute(value, ('dom', 'dir'), pairs)  4.82 us
    ppermute x6, waiting for transfers between devices, shift(): lax.ppermute(value, axis, [(i, (i + by) % length) for i in range(length)])  3.08 us
    pallas_call x1, Pallas kernels, per_device(): pl.pallas_call(prep_kernel, out_shape=(shape((rows, half), BF16), shape((...  2.48 us
    pallas_call x1, Pallas kernels, per_device(): pl.pallas_call(boundary_kernel, out_shape=(shape((3 * count, half), BF16)...  2.31 us
    unnamed x6, local copies, waits for them, and re-layouts  1.92 us
  transfers between devices with their start and end apart: 12, of which 5 were waited for; matrix products, arithmetic and copies ran while one was open for 0% of the time, Pallas kernels for 24%

profile of v4, /device:TPU:0, one launch (start us, length us, event | category | flops | bytes accessed | tf_op | source)
XLA Modules:
  0.0 50.2 jit_solution(15002927372102670884)
XLA Ops:
  0.0 0.5 collective-permute-start
  0.5 2.3 %boundary.1 = (bf16[384,256]{1,0:T(8,128)(2,1)}, bf16[384,256]{1,0:T(8,128)(2,1)}) custom-call(bf16[768,512]{1,0:T(8,128)(2,1)} %v_hbm.3, s32[1,128]{1,0:T(1,128)} %bitcast.3, s32[1,128]{1,0:T(1,128)} %bitcast.4), custom_call_target="tpu_custom_call" | custom-call | tf_op jit(solution)/shard_map/boundary/pallas_call | solution.py:309
  2.8 2.6 %collective-permute-start.1 = (bf16[384,256]{1,0:T(8,128)(2,1)}, bf16[384,256]{1,0:T(8,128)(2,1)S(1)}, u32[]{:S(2)}, u32[]{:S(2)}) collective-permute-start(bf16[384,256]{1,0:T(8,128)(2,1)} %get-tuple-element.24.sent0_hbm), channel_id=1, source_target_pairs={{0,4},{4,8},{8,12},{12,0},{1,5},{5,9},{9,13},{13,1},{2,6},{6,10},{... | collective-permute-start | bytes 589832 | tf_op jit(solution)/shard_map/ppermute | solution.py:283
  5.4 2.1 %collective-permute-start.2 = (bf16[384,256]{1,0:T(8,128)(2,1)}, bf16[384,256]{1,0:T(8,128)(2,1)S(1)}, u32[]{:S(2)}, u32[]{:S(2)}) collective-permute-start(bf16[384,256]{1,0:T(8,128)(2,1)} %get-tuple-element.25.sent1_hbm), channel_id=1, source_target_pairs={{0,12},{4,0},{8,4},{12,8},{1,13},{5,1},{9,5},{13,9},{2,14},{6,2},{... | collective-permute-start | bytes 589832 | tf_op jit(solution)/shard_map/ppermute | solution.py:283
  7.5 2.5 %prep.1 = (bf16[768,256]{1,0:T(8,128)(2,1)}, bf16[256,768]{1,0:T(8,128)(2,1)}, f32[11,16,256]{2,1,0:T(8,128)}) custom-call(bf16[768,512]{1,0:T(8,128)(2,1)} %v_hbm.3, f32[9,16,256]{2,1,0:T(8,128)} %bitcast.5, f32[1,16,256]{2,1,0:T(8,128)} %bond_hbm.1, s32[16,256]{1,0:T(8,128)} %near_hbm.1, bf16[384,256]{1,0:T(8,128)(2,1)} %get-tuple-element.24.sent0_hbm, ...), custom_call_target="tpu_custom_call" | custom-call | flops 1000000000 | bytes 1000000 | tf_op jit(solution)/shard_map/prep/pallas_call | solution.py:328
  10.0 1.7 %collective-permute-start.3 = (bf16[256,768]{1,0:T(8,128)(2,1)}, bf16[256,768]{1,0:T(8,128)(2,1)S(1)}, u32[]{:S(2)}, u32[]{:S(2)}) collective-permute-start(bf16[256,768]{1,0:T(8,128)(2,1)} %get-tuple-element.31.refs_0_), channel_id=1, source_target_pairs={{0,2},{2,0},{1,3},{3,1},{4,6},{6,4},{5,7},{7,5},{8,10},{10,8},{9,1... | collective-permute-start | bytes 1179656 | tf_op jit(solution)/shard_map/ppermute | solution.py:283
  11.7 0.0 collective-permute-start.4
  11.7 0.0 collective-permute-done.other_ref
  11.7 0.0 copy-start.1
  11.7 1.0 %copy-done.1 = bf16[768,256]{1,0:T(8,128)(2,1)S(1)} copy-done((bf16[768,256]{1,0:T(8,128)(2,1)S(1)}, bf16[768,256]{1,0:T(8,128)(2,1)}, u32[]{:S(2)}) %copy-start.1) | copy-done | bytes 393240
  12.7 0.0 copy-start.2
  12.7 0.9 %copy-done.2 = f32[11,16,256]{2,1,0:T(8,128)S(1)} copy-done((f32[11,16,256]{2,1,0:T(8,128)S(1)}, f32[11,16,256]{2,1,0:T(8,128)}, u32[]{:S(2)}) %copy-start.2) | copy-done | bytes 180248
  13.6 5.1 %weights.1 = (f32[1536,256]{1,0:T(8,128)S(1)}, bf16[1536,768]{1,0:T(8,128)(2,1)S(1)}, bf16[1536,768]{1,0:T(8,128)(2,1)S(1)}) custom-call(f32[11,16,256]{2,1,0:T(8,128)S(1)} %copy-done.2, f32[1,16,256]{2,1,0:T(8,128)S(1)} %collective-permute-done.other_ref, bf16[768,256]{1,0:T(8,128)(2,1)S(1)} %copy-done.1), custom_call_target="tpu_custom_call" | custom-call | flops 8000000000 | bytes 10000000 | tf_op jit(solution)/shard_map/weights/pallas_call | solution.py:351
  18.7 0.0 collective-permute-done.1.below_ref
  18.7 0.0 collective-permute-done.2.above_ref
  18.7 2.8 %collective-permute-done.3.refs_0_ = bf16[256,768]{1,0:T(8,128)(2,1)S(1)} collective-permute-done((bf16[256,768]{1,0:T(8,128)(2,1)}, bf16[256,768]{1,0:T(8,128)(2,1)S(1)}, u32[]{:S(2)}, u32[]{:S(2)}) %collective-permute-start.3) | collective-permute-done | bytes 393248 | tf_op jit(solution)/shard_map/ppermute | solution.py:283
  21.5 0.1 relay.1
  21.6 0.1 collective-permute-start.5
  21.6 0.0 copy-start
  21.6 1.4 %flux.1.flux_ref = bf16[768,512]{1,0:T(8,128)(2,1)S(1)} custom-call(f32[1536,256]{1,0:T(8,128)S(1)} %get-tuple-element.28.part_hbm.part_ref, bf16[1536,768]{1,0:T(8,128)(2,1)S(1)} %get-tuple-element.29.hi_ref, bf16[1536,768]{1,0:T(8,128)(2,1)S(1)} %get-tuple-element.30.lo_ref, bf16[768,256]{1,0:T(8,128)(2,1)S(1)} %get-tuple-element.32.halo_ref), custom_call_target="tpu_custom_call" | custom-call | flops 2000000000 | bytes 1000000 | tf_op jit(solution)/shard_map/flux/pallas_call | solution.py:384
  23.0 0.0 collective-permute-done.4.refs_1_
  23.0 0.3 collective-permute-done.5.refs_3_
  23.3 0.0 copy-done
  23.3 0.8 %far.1 = (bf16[2,256,256]{2,1,0:T(8,128)(2,1)S(1)}, f32[2,256,256]{2,1,0:T(8,128)S(1)}) custom-call(bf16[768,512]{1,0:T(8,128)(2,1)S(1)} %flux.1.flux_ref, bf16[256,768]{1,0:T(8,128)(2,1)S(1)} %copy-done, bf16[256,768]{1,0:T(8,128)(2,1)S(1)} %collective-permute-done.4.refs_1_, bf16[256,768]{1,0:T(8,128)(2,1)S(1)} %get-tuple-element.33.refs_2_, ...), custom_call_target="tpu_custom_call" | custom-call | flops 800000000 | bytes 1000000 | tf_op jit(solution)/shard_map/far/pallas_call | solution.py:402
  24.2 0.1 collective-permute-start.7
  24.2 0.8 %near.1 = (bf16[2,256,256]{2,1,0:T(8,128)(2,1)S(1)}, f32[256,256]{1,0:T(8,128)S(1)}, bf16[256,256]{1,0:T(8,128)(2,1)S(1)}) custom-call(bf16[768,512]{1,0:T(8,128)(2,1)S(1)} %flux.1.flux_ref, bf16[256,768]{1,0:T(8,128)(2,1)S(1)} %copy-done, bf16[256,768]{1,0:T(8,128)(2,1)S(1)} %collective-permute-done.4.refs_1_, ...), custom_call_target="tpu_custom_call" | custom-call | flops 800000000 | bytes 1000000 | tf_op jit(solution)/shard_map/near/pallas_call | solution.py:412
  25.1 0.3 collective-permute-start.6
  25.3 7.3 %collective-permute-done.7.far_ref = bf16[2,256,256]{2,1,0:T(8,128)(2,1)S(1)} collective-permute-done((bf16[2,256,256]{2,1,0:T(8,128)(2,1)S(1)}, bf16[2,256,256]{2,1,0:T(8,128)(2,1)S(1)}, u32[]{:S(2)}, u32[]{:S(2)}) %collective-permute-start.7) | collective-permute-done | bytes 262176 | tf_op jit(solution)/shard_map/ppermute | solution.py:291
  32.7 0.1 add.1
  32.7 0.4 collective-permute-start.8
  33.1 0.5 collective-permute-start.9
  33.6 1.5 %collective-permute-start.10 = (bf16[256,256]{1,0:T(8,128)(2,1)S(1)}, bf16[256,256]{1,0:T(8,128)(2,1)S(1)}, u32[]{:S(2)}, u32[]{:S(2)}) collective-permute-start(bf16[256,256]{1,0:T(8,128)(2,1)S(1)} %get-tuple-element.41), channel_id=1, source_target_pairs={{0,8},{1,9},{4,12},{5,13},{8,0},{9,1},{12,4},{13,5},{2,10},{3,11},... | collective-permute-start | bytes 393224 | tf_op jit(solution)/shard_map/ppermute | solution.py:291
  35.0 2.1 %collective-permute-start.11 = (bf16[256,256]{1,0:T(8,128)(2,1)S(1)}, bf16[256,256]{1,0:T(8,128)(2,1)S(1)}, u32[]{:S(2)}, u32[]{:S(2)}) collective-permute-start(bf16[256,256]{1,0:T(8,128)(2,1)S(1)} %get-tuple-element.42), channel_id=1, source_target_pairs={{0,9},{1,8},{4,13},{5,12},{8,1},{9,0},{12,5},{13,4},{2,11},{3,10},... | collective-permute-start | bytes 393224 | tf_op jit(solution)/shard_map/ppermute | solution.py:291
  37.2 0.0 collective-permute-done.6.refs_1_
  37.2 4.5 %collective-permute-done.8.refs_2_ = bf16[256,256]{1,0:T(8,128)(2,1)S(1)} collective-permute-done((bf16[256,256]{1,0:T(8,128)(2,1)S(1)}, bf16[256,256]{1,0:T(8,128)(2,1)S(1)}, u32[]{:S(2)}, u32[]{:S(2)}) %collective-permute-start.8) | collective-permute-done | bytes 131104 | tf_op jit(solution)/shard_map/ppermute | solution.py:291
  41.7 0.0 collective-permute-done.9.refs_3_
  41.7 0.0 collective-permute-done.10.refs_4_
  41.8 7.5 %collective-permute-done.11.refs_5_ = bf16[256,256]{1,0:T(8,128)(2,1)S(1)} collective-permute-done((bf16[256,256]{1,0:T(8,128)(2,1)S(1)}, bf16[256,256]{1,0:T(8,128)(2,1)S(1)}, u32[]{:S(2)}, u32[]{:S(2)}) %collective-permute-start.11) | collective-permute-done | bytes 131104 | tf_op jit(solution)/shard_map/ppermute | solution.py:291
  49.3 0.9 %total.1 = f32[1,256,512]{2,1,0:T(8,128)} custom-call(f32[256,256]{1,0:T(8,128)S(1)} %get-tuple-element.34.refs_0_, bf16[256,256]{1,0:T(8,128)(2,1)S(1)} %collective-permute-done.6.refs_1_, bf16[256,256]{1,0:T(8,128)(2,1)S(1)} %collective-permute-done.8.refs_2_, bf16[256,256]{1,0:T(8,128)(2,1)S(1)} %collective-permute-done.9.refs_3_, ...), custom_call_target="tpu_custom_call" | custom-call | tf_op jit(solution)/shard_map/total/pallas_call | solution.py:432
Async XLA Ops:
  0.0 11.7 %collective-permute-start = (f32[1,16,256]{2,1,0:T(8,128)}, f32[1,16,256]{2,1,0:T(8,128)S(1)}, u32[]{:S(2)}, u32[]{:S(2)}) collective-permute-start(f32[1,16,256]{2,1,0:T(8,128)} %bond_hbm.1), channel_id=1, source_target_pairs={{0,1},{1,0},{2,3},{3,2},{4,5},{5,4},{6,7},{7,6},{8,9},{9,8},{10,11... | collective-permute-start | bytes 49160 | tf_op jit(solution)/shard_map/ppermute | solution.py:283
  2.8 15.9 %collective-permute-start.1 = (bf16[384,256]{1,0:T(8,128)(2,1)}, bf16[384,256]{1,0:T(8,128)(2,1)S(1)}, u32[]{:S(2)}, u32[]{:S(2)}) collective-permute-start(bf16[384,256]{1,0:T(8,128)(2,1)} %get-tuple-element.24.sent0_hbm), channel_id=1, source_target_pairs={{0,4},{4,8},{8,12},{12,0},{1,5},{5,9},{9,13},{13,1},{2,6},{6,10},{... | collective-permute-start | bytes 589832 | tf_op jit(solution)/shard_map/ppermute | solution.py:283
  5.4 13.3 %collective-permute-start.2 = (bf16[384,256]{1,0:T(8,128)(2,1)}, bf16[384,256]{1,0:T(8,128)(2,1)S(1)}, u32[]{:S(2)}, u32[]{:S(2)}) collective-permute-start(bf16[384,256]{1,0:T(8,128)(2,1)} %get-tuple-element.25.sent1_hbm), channel_id=1, source_target_pairs={{0,12},{4,0},{8,4},{12,8},{1,13},{5,1},{9,5},{13,9},{2,14},{6,2},{... | collective-permute-start | bytes 589832 | tf_op jit(solution)/shard_map/ppermute | solution.py:283
  10.0 11.5 %collective-permute-start.3 = (bf16[256,768]{1,0:T(8,128)(2,1)}, bf16[256,768]{1,0:T(8,128)(2,1)S(1)}, u32[]{:S(2)}, u32[]{:S(2)}) collective-permute-start(bf16[256,768]{1,0:T(8,128)(2,1)} %get-tuple-element.31.refs_0_), channel_id=1, source_target_pairs={{0,2},{2,0},{1,3},{3,1},{4,6},{6,4},{5,7},{7,5},{8,10},{10,8},{9,1... | collective-permute-start | bytes 1179656 | tf_op jit(solution)/shard_map/ppermute | solution.py:283
  11.7 11.3 %collective-permute-start.4 = (bf16[256,768]{1,0:T(8,128)(2,1)}, bf16[256,768]{1,0:T(8,128)(2,1)S(1)}, u32[]{:S(2)}, u32[]{:S(2)}) collective-permute-start(bf16[256,768]{1,0:T(8,128)(2,1)} %get-tuple-element.31.refs_0_), channel_id=1, source_target_pairs={{0,1},{1,0},{2,3},{3,2},{4,5},{5,4},{6,7},{7,6},{8,9},{9,8},{10,11... | collective-permute-start | bytes 1179656 | tf_op jit(solution)/shard_map/ppermute | solution.py:283
  11.7 1.0 %copy-start.1 = (bf16[768,256]{1,0:T(8,128)(2,1)S(1)}, bf16[768,256]{1,0:T(8,128)(2,1)}, u32[]{:S(2)}) copy-start(bf16[768,256]{1,0:T(8,128)(2,1)} %get-tuple-element.27.own_ref) | copy-start | bytes 1179652
  12.7 0.9 %copy-start.2 = (f32[11,16,256]{2,1,0:T(8,128)S(1)}, f32[11,16,256]{2,1,0:T(8,128)}, u32[]{:S(2)}) copy-start(f32[11,16,256]{2,1,0:T(8,128)} %get-tuple-element.26.source_ref) | copy-start | bytes 540676
  21.6 1.8 %collective-permute-start.5 = (bf16[256,768]{1,0:T(8,128)(2,1)S(1)}, bf16[256,768]{1,0:T(8,128)(2,1)S(1)}, u32[]{:S(2)}, u32[]{:S(2)}) collective-permute-start(bf16[256,768]{1,0:T(8,128)(2,1)S(1)} %get-tuple-element.33.refs_2_), channel_id=1, source_target_pairs={{0,1},{1,0},{2,3},{3,2},{4,5},{5,4},{6,7},{7,6},{8,9},{9,8},{10,11... | collective-permute-start | bytes 1179656 | tf_op jit(solution)/shard_map/ppermute | solution.py:283
  21.6 1.7 %copy-start = (bf16[256,768]{1,0:T(8,128)(2,1)S(1)}, bf16[256,768]{1,0:T(8,128)(2,1)}, u32[]{:S(2)}) copy-start(bf16[256,768]{1,0:T(8,128)(2,1)} %get-tuple-element.31.refs_0_) | copy-start | bytes 1179652
  24.2 8.5 %collective-permute-start.7 = (bf16[2,256,256]{2,1,0:T(8,128)(2,1)S(1)}, bf16[2,256,256]{2,1,0:T(8,128)(2,1)S(1)}, u32[]{:S(2)}, u32[]{:S(2)}) collective-permute-start(bf16[2,256,256]{2,1,0:T(8,128)(2,1)S(1)} %get-tuple-element.36), channel_id=1, source_target_pairs={{0,4},{1,5},{4,0},{5,1},{8,12},{9,13},{12,8},{13,9},{2,6},{3,7},{6... | collective-permute-start | bytes 786440 | tf_op jit(solution)/shard_map/ppermute | solution.py:291
  25.1 12.1 %collective-permute-start.6 = (bf16[256,256]{1,0:T(8,128)(2,1)S(1)}, bf16[256,256]{1,0:T(8,128)(2,1)S(1)}, u32[]{:S(2)}, u32[]{:S(2)}) collective-permute-start(bf16[256,256]{1,0:T(8,128)(2,1)S(1)} %get-tuple-element.35), channel_id=1, source_target_pairs={{0,1},{1,0},{4,5},{5,4},{8,9},{9,8},{12,13},{13,12},{2,3},{3,2},{6... | collective-permute-start | bytes 393224 | tf_op jit(solution)/shard_map/ppermute | solution.py:291
  32.7 9.0 %collective-permute-start.8 = (bf16[256,256]{1,0:T(8,128)(2,1)S(1)}, bf16[256,256]{1,0:T(8,128)(2,1)S(1)}, u32[]{:S(2)}, u32[]{:S(2)}) collective-permute-start(bf16[256,256]{1,0:T(8,128)(2,1)S(1)} %get-tuple-element.39), channel_id=1, source_target_pairs={{0,4},{1,5},{4,0},{5,1},{8,12},{9,13},{12,8},{13,9},{2,6},{3,7},{6... | collective-permute-start | bytes 393224 | tf_op jit(solution)/shard_map/ppermute | solution.py:291
  33.1 8.6 %collective-permute-start.9 = (bf16[256,256]{1,0:T(8,128)(2,1)S(1)}, bf16[256,256]{1,0:T(8,128)(2,1)S(1)}, u32[]{:S(2)}, u32[]{:S(2)}) collective-permute-start(bf16[256,256]{1,0:T(8,128)(2,1)S(1)} %get-tuple-element.40), channel_id=1, source_target_pairs={{0,5},{1,4},{4,1},{5,0},{8,13},{9,12},{12,9},{13,8},{2,7},{3,6},{6... | collective-permute-start | bytes 393224 | tf_op jit(solution)/shard_map/ppermute | solution.py:291
  33.6 8.2 %collective-permute-start.10 = (bf16[256,256]{1,0:T(8,128)(2,1)S(1)}, bf16[256,256]{1,0:T(8,128)(2,1)S(1)}, u32[]{:S(2)}, u32[]{:S(2)}) collective-permute-start(bf16[256,256]{1,0:T(8,128)(2,1)S(1)} %get-tuple-element.41), channel_id=1, source_target_pairs={{0,8},{1,9},{4,12},{5,13},{8,0},{9,1},{12,4},{13,5},{2,10},{3,11},... | collective-permute-start | bytes 393224 | tf_op jit(solution)/shard_map/ppermute | solution.py:291
  35.0 14.3 %collective-permute-start.11 = (bf16[256,256]{1,0:T(8,128)(2,1)S(1)}, bf16[256,256]{1,0:T(8,128)(2,1)S(1)}, u32[]{:S(2)}, u32[]{:S(2)}) collective-permute-start(bf16[256,256]{1,0:T(8,128)(2,1)S(1)} %get-tuple-element.42), channel_id=1, source_target_pairs={{0,9},{1,8},{4,13},{5,12},{8,1},{9,0},{12,5},{13,4},{2,11},{3,10},... | collective-permute-start | bytes 393224 | tf_op jit(solution)/shard_map/ppermute | solution.py:291

commit v5 on v4

v5 whole, which is shorter than its diff:
```python
import functools

import jax
import jax.numpy as jnp
from jax import lax
from jax.experimental import pallas as pl
from jax.experimental.pallas import tpu as pltpu
from jax.sharding import PartitionSpec as P

GROUP = 16
BF16 = jnp.bfloat16
F32 = jnp.float32


def params(mib=24):
    return pltpu.CompilerParams(vmem_limit_bytes=mib * 1024 * 1024)


def dot(a, b, contract=((1,), (0,))):
    return lax.dot_general(a, b, (contract, ((), ())), preferred_element_type=F32)


def one_hot(mask):
    return jnp.where(mask, 1.0, 0.0).astype(BF16)


def my_columns(half):
    return pl.ds(pl.multiple_of(lax.axis_index("dir") * half, 128), half)


def prep_kernel(
    v_hbm, low_hbm, high_hbm, force_hbm, bond_hbm, near_hbm,
    turned_hbm, send_low_hbm, send_high_hbm, own_hbm, source_hbm,
    v_ref, low_ref, high_ref, near_ref, turned_ref, send_low_ref, send_high_ref, own_ref,
    name_ref, in_sems, out_sems,
):
    rows, half = v_ref.shape
    atoms = rows // 3
    v_in = pltpu.make_async_copy(v_hbm.at[:, my_columns(half)], v_ref, in_sems.at[0])
    v_in.start()
    lists_in = [
        pltpu.make_async_copy(low_hbm, low_ref, in_sems.at[1]),
        pltpu.make_async_copy(high_hbm, high_ref, in_sems.at[2]),
        pltpu.make_async_copy(near_hbm, near_ref, in_sems.at[3]),
    ]
    for copy in lists_in:
        copy.start()
    out = [
        pltpu.make_async_copy(force_hbm, source_hbm.at[0:9], out_sems.at[0]),
        pltpu.make_async_copy(bond_hbm, source_hbm.at[9:10], out_sems.at[1]),
    ]
    for copy in out:
        copy.start()

    def leave(ref, hbm):
        copy = pltpu.make_async_copy(ref, hbm, out_sems.at[len(out)])
        copy.start()
        out.append(copy)

    lane = lax.broadcasted_iota(jnp.int32, (atoms, rows), 1)
    atom = lax.broadcasted_iota(jnp.int32, (atoms, rows), 0)
    hot = [one_hot(lane == 3 * atom + b) for b in range(3)]
    v_in.wait()
    v = v_ref[...]
    for b in range(3):
        picked = dot(hot[b], v)
        turned_ref[:, b * atoms : (b + 1) * atoms] = picked.T.astype(BF16)
        own_ref[b * atoms : (b + 1) * atoms, :] = picked.astype(BF16)
    leave(turned_ref, turned_hbm)
    for copy in lists_in:
        copy.wait()
    name_ref[0] = near_ref[...].astype(F32)
    for list_ref, send_ref, send_hbm in (
        (high_ref, send_high_ref, send_high_hbm),
        (low_ref, send_low_ref, send_low_hbm),
    ):
        count = list_ref.shape[1]
        named = jnp.broadcast_to(list_ref[...], (128, count)).T
        lane = lax.broadcasted_iota(jnp.int32, (count, 128), 1)
        for b in range(3):
            wanted = 3 * named + b
            picks = jnp.concatenate(
                [one_hot(lane + t * 128 == wanted) for t in range(rows // 128)], axis=1
            )
            send_ref[b * count : (b + 1) * count, :] = dot(picks, v).astype(BF16)
        leave(send_ref, send_hbm)
    leave(own_ref, own_hbm)
    leave(name_ref, source_hbm.at[10:11])
    for copy in out:
        copy.wait()


def weights_kernel(
    source_ref, other_ref, own_ref,
    flux_ref, hi_ref, lo_ref, table_ref, own_hi_ref, own_lo_ref,
):
    _, steps, atoms = source_ref.shape
    groups = atoms // GROUP
    halo = hi_ref.shape[1] // 3
    extent = atoms + halo
    bonds = (source_ref[9], other_ref[0])
    lane = lax.broadcasted_iota(jnp.int32, (24, atoms), 1)
    rows = []
    for k in range(steps):
        force = source_ref[0:9, k, :]
        near = source_ref[10, k : k + 1, :]
        rows.append(
            jnp.concatenate(
                [force * bonds[0][k : k + 1, :], force * bonds[1][k : k + 1, :]]
                + [jnp.broadcast_to(near, (6, atoms))],
                axis=0,
            )
        )
    bit = 1
    while bit < steps:
        taken = ((lane // GROUP) & bit) != 0
        turned = list(rows)
        for p in range(steps):
            if p & bit:
                continue
            q = p | bit
            turned[p] = jnp.where(taken, pltpu.roll(rows[q], GROUP * bit, 1), rows[p])
            turned[q] = jnp.where(taken, rows[q], pltpu.roll(rows[p], atoms - GROUP * bit, 1))
        rows = turned
        bit *= 2
    for g in range(groups):
        table_ref[g] = rows[g]

    mask = (
        lax.broadcasted_iota(jnp.int32, (GROUP, atoms), 1) % GROUP
        == lax.broadcasted_iota(jnp.int32, (GROUP, atoms), 0)
    )
    target = lax.broadcasted_iota(jnp.int32, (256, atoms), 0).astype(F32).astype(BF16)

    def group(g):
        table = table_ref[g]
        named = [(table[18:19, :] - at).astype(BF16) for at in range(0, extent, 256)]
        hot = jnp.concatenate(
            [jnp.where(target == name, BF16(1), BF16(0)) for name in named], axis=0
        )
        spread = jnp.concatenate(
            [jnp.where(mask, table[r : r + 1, :], 0.0) for r in range(18)], axis=0
        )
        top = spread.astype(BF16)
        rest = (spread - top.astype(F32)).astype(BF16)
        both = ((1,), (1,))
        dense = dot(top, hot, both) + dot(rest, hot, both)
        hi = dense.astype(BF16)
        lo = (dense - hi.astype(F32)).astype(BF16)
        for e in range(2):
            for a in range(3):
                at = pl.ds(pl.multiple_of((e * 3 + a) * atoms + g * GROUP, GROUP), GROUP)
                for b in range(3):
                    r = (e * 9 + 3 * a + b) * GROUP
                    near, far = slice(b * atoms, (b + 1) * atoms), slice(b * halo, (b + 1) * halo)
                    own_hi_ref[at, near] = hi[r : r + GROUP, :atoms]
                    own_lo_ref[at, near] = lo[r : r + GROUP, :atoms]
                    hi_ref[at, far] = hi[r : r + GROUP, atoms:]
                    lo_ref[at, far] = lo[r : r + GROUP, atoms:]

    def several(step, carry):
        for g in range(4):
            group(4 * step + g)
        return carry

    lax.fori_loop(0, groups // 4, several, 0)
    own = own_ref[...]
    for part in range(6):
        at = slice(part * atoms, (part + 1) * atoms)
        flux_ref[at, :] = dot(own_hi_ref[at, :], own) + dot(own_lo_ref[at, :], own)


def relay_kernel(part_hbm, below_hbm, above_hbm, *refs):
    for got_ref, given_ref in zip(refs[: len(refs) // 2], refs[len(refs) // 2 :]):
        given_ref[...] = got_ref[...]


def flux_kernel(e, part_ref, hi_ref, lo_ref, below_ref, above_ref, flux_ref, halo_ref):
    count = below_ref.shape[0] // 3
    for b in range(3):
        at = 2 * b * count
        halo_ref[at : at + count] = below_ref[b * count : (b + 1) * count]
        halo_ref[at + count : at + 2 * count] = above_ref[b * count : (b + 1) * count]
    atoms = flux_ref.shape[0] // 3
    halo = halo_ref[...]
    for a in range(3):
        at = slice((e * 3 + a) * atoms, (e * 3 + a + 1) * atoms)
        flux = part_ref[at, :] + (dot(hi_ref[at, :], halo) + dot(lo_ref[at, :], halo))
        flux_ref[a * atoms : (a + 1) * atoms, :] = flux.astype(BF16)


def terms_of(quarter_refs, store, wanted=lambda tile: True):
    tiles = len(quarter_refs) // 2
    me, core = lax.axis_index("blk"), lax.axis_index("dir")
    for j in range(tiles):
        tile = lax.rem(me - j + tiles, tiles)

        @pl.when(wanted(tile))
        def _():
            for s in range(2):
                store(2 * tile + (core if s == 0 else 1 - core), quarter_refs[2 * j + s])


def couple_kernel(flux0_ref, flux1_ref, *refs):
    *quarter_refs, out_ref = refs
    half = quarter_refs[0].shape[0]
    block = out_ref.shape[1]
    core = lax.axis_index("dir")

    def store(quarter, turned_ref):
        for e, flux_ref in enumerate((flux0_ref, flux1_ref)):
            term = dot(turned_ref[...], flux_ref[...]).astype(BF16)
            for t in range(half // block):
                at = 2 * (quarter * (half // block) + t) + (core if e == 0 else 1 - core)
                out_ref[at] = term[t * block : (t + 1) * block]

    terms_of(quarter_refs, store)


def sum_kernel(scale, terms_ref, out_ref):
    pairs, block, half = terms_ref.shape
    for c in range(2):
        total = terms_ref[c].astype(F32)
        for d in range(1, pairs // 2):
            total = total + terms_ref[2 * d + c].astype(F32)
        out_ref[0, :, c * half : (c + 1) * half] = total * scale


def far_kernel(flux_ref, *refs):
    *quarter_refs, far_ref, add_ref = refs
    home = lax.axis_index("dom")

    def store(quarter, turned_ref):
        term = dot(turned_ref[...], flux_ref[...])

        @pl.when((quarter ^ home) == 3)
        def _():
            far_ref[...] = term.astype(BF16)

        @pl.when((quarter ^ home) == 2)
        def _():
            add_ref[...] = term

    terms_of(quarter_refs, store, lambda tile: (tile ^ (home // 2)) == 1)


def near_kernel(flux0_ref, flux1_ref, *refs):
    *quarter_refs, near0_ref, near1_ref, keep_ref, give_ref = refs
    home = lax.axis_index("dom")

    def store(quarter, turned_ref):
        terms = [dot(turned_ref[...], ref[...]) for ref in (flux0_ref, flux1_ref)]

        @pl.when((quarter ^ home) == 1)
        def _():
            near0_ref[...] = terms[0].astype(BF16)
            near1_ref[...] = terms[1].astype(BF16)

        @pl.when((quarter ^ home) == 0)
        def _():
            keep_ref[...] = terms[0]
            give_ref[...] = terms[1].astype(BF16)

    terms_of(quarter_refs, store, lambda tile: (tile ^ (home // 2)) == 0)


def add_kernel(far_ref, add_ref, sum_ref):
    sum_ref[...] = (add_ref[...] + far_ref[...].astype(F32)).astype(BF16)


def halving_sum_kernel(scale, keep_ref, give_ref, near0_ref, near1_ref, sum0_ref, sum1_ref, out_ref):
    half = keep_ref.shape[1]
    core = lax.axis_index("dir")
    mine = pl.ds(pl.multiple_of(core * half, 128), half)
    other = pl.ds(pl.multiple_of((1 - core) * half, 128), half)
    for at, first, near, far in (
        (mine, keep_ref, near0_ref, sum0_ref),
        (other, give_ref, near1_ref, sum1_ref),
    ):
        total = first[...].astype(F32) + near[...].astype(F32) + far[...].astype(F32)
        out_ref[0, :, at] = total * scale


def shift(value, axis, by):
    length = lax.axis_size(axis)
    return lax.ppermute(value, axis, [(i, (i + by) % length) for i in range(length)])


def swap(value, away, other_core):
    domains = lax.axis_size("dom")
    pairs = [
        (2 * d + c, 2 * (d ^ away) + (c ^ other_core)) for d in range(domains) for c in range(2)
    ]
    return lax.ppermute(value, ("dom", "dir"), pairs)


def shape(dims, dtype):
    return jax.ShapeDtypeStruct(dims, dtype)


def per_device(panel_vectors, force_blocks, bond_vectors, neighbours, boundary_low, boundary_high):
    rows, cols = panel_vectors.shape
    atoms = rows // 3
    half = cols // 2
    count = boundary_low.shape[0]
    domains, tiles = lax.axis_size("dom"), lax.axis_size("blk")
    block = cols * tiles // domains
    vmem = pl.BlockSpec(memory_space=pltpu.VMEM)
    hbm = pl.BlockSpec(memory_space=pltpu.HBM)
    anywhere = pl.BlockSpec(memory_space=pl.ANY)

    other_bonds = shift(bond_vectors, "dir", 1)
    lists = [boundary_low.reshape(1, count), boundary_high.reshape(1, count)]
    forces = force_blocks.transpose(1, 0, 2)
    prepared = (
        shape((half, rows), BF16),
        shape((3 * count, half), BF16),
        shape((3 * count, half), BF16),
        shape((rows, half), BF16),
    )
    turned, send_low, send_high, own, sources = pl.pallas_call(
        prep_kernel,
        out_shape=(*prepared, shape((11, *neighbours.shape), F32)),
        in_specs=[hbm] * 6,
        out_specs=(hbm,) * 5,
        scratch_shapes=[
            pltpu.VMEM((rows, half), BF16),
            pltpu.VMEM((1, count), jnp.int32),
            pltpu.VMEM((1, count), jnp.int32),
            pltpu.VMEM(neighbours.shape, jnp.int32),
            *[pltpu.VMEM(like.shape, like.dtype) for like in prepared],
            pltpu.VMEM((1, *neighbours.shape), F32),
            pltpu.SemaphoreType.DMA((4,)),
            pltpu.SemaphoreType.DMA((7,)),
        ],
        compiler_params=params(58),
        name="prep",
    )(panel_vectors, *lists, forces, bond_vectors, neighbours)
    quarters = [shift(turned, "blk", j) for j in range(1, tiles)]
    turned_other = shift(turned, "dir", 1)
    below = shift(send_high, "dom", 1)
    above = shift(send_low, "dom", -1)

    partial_flux, hi, lo = pl.pallas_call(
        weights_kernel,
        out_shape=(
            shape((2 * rows, half), F32),
            shape((2 * rows, 6 * count), BF16),
            shape((2 * rows, 6 * count), BF16),
        ),
        in_specs=[vmem] * 3,
        out_specs=(vmem,) * 3,
        scratch_shapes=[
            pltpu.VMEM((atoms // GROUP, 24, atoms), F32),
            pltpu.VMEM((2 * rows, rows), BF16),
            pltpu.VMEM((2 * rows, rows), BF16),
        ],
        compiler_params=params(32),
        cost_estimate=pl.CostEstimate(
            flops=8*10**9, bytes_accessed=10**7, transcendentals=0
        ),
        name="weights",
    )(sources, other_bonds, own)

    quarters = pl.pallas_call(
        relay_kernel,
        out_shape=[shape(turned.shape, BF16)] * (tiles - 1),
        in_specs=[anywhere] * 3 + [vmem] * len(quarters),
        out_specs=[vmem] * (tiles - 1),
        compiler_params=params(16),
        name="relay",
    )(partial_flux, below, above, *quarters)
    given = [turned, turned_other]
    for quarter in quarters:
        given += [quarter, shift(quarter, "dir", 1)]

    def flux_of(e):
        return pl.pallas_call(
            functools.partial(flux_kernel, e),
            out_shape=shape((rows, half), BF16),
            in_specs=[vmem] * 5,
            out_specs=vmem,
            scratch_shapes=[pltpu.VMEM((6 * count, half), BF16)],
            compiler_params=params(16),
            cost_estimate=pl.CostEstimate(
                flops=10**9, bytes_accessed=10**6, transcendentals=0
            ),
            name="flux",
        )(partial_flux, hi, lo, below, above)

    scale = (3.0 * atoms * domains) ** (-0.5)
    result = shape((1, block, cols), F32)
    if domains == 4 and block == half:
        sent, kept = shape((block, half), BF16), shape((block, half), F32)
        cost = pl.CostEstimate(flops=4 * 10**8, bytes_accessed=10**6, transcendentals=0)

        def far_of(flux):
            far, add = pl.pallas_call(
                far_kernel,
                out_shape=(sent, kept),
                in_specs=[vmem] * (1 + len(given)),
                out_specs=(vmem,) * 2,
                compiler_params=params(16),
                cost_estimate=cost,
                name="far",
            )(flux, *given)
            return far, add

        flux0, flux1 = flux_of(0), flux_of(1)
        far0, add0 = far_of(flux0)
        far1, add1 = far_of(flux1)
        far0, far1 = swap(far0, 1, 0), swap(far1, 1, 0)
        near0, near1, keep, give = pl.pallas_call(
            near_kernel,
            out_shape=(sent, sent, kept, sent),
            in_specs=[vmem] * (2 + len(given)),
            out_specs=(vmem,) * 4,
            compiler_params=params(16),
            cost_estimate=cost,
            name="near",
        )(flux0, flux1, *given)
        give, near0, near1 = swap(give, 0, 1), swap(near0, 1, 0), swap(near1, 1, 1)

        def sum_of(far, add):
            return pl.pallas_call(
                add_kernel,
                out_shape=sent,
                in_specs=[vmem] * 2,
                out_specs=vmem,
                compiler_params=params(16),
                name="add",
            )(far, add)

        sum0, sum1 = swap(sum_of(far0, add0), 2, 0), swap(sum_of(far1, add1), 2, 1)
        return pl.pallas_call(
            lambda *refs: halving_sum_kernel(scale, *refs),
            out_shape=result,
            in_specs=[vmem] * 6,
            out_specs=vmem,
            compiler_params=params(16),
            name="total",
        )(keep, give, near0, near1, sum0, sum1)

    terms = pl.pallas_call(
        couple_kernel,
        out_shape=shape((2 * domains, block, half), BF16),
        in_specs=[vmem] * (2 + len(given)),
        out_specs=vmem,
        compiler_params=params(16),
        name="couple",
    )(flux_of(0), flux_of(1), *given)
    terms = lax.all_to_all(terms, ("dom", "dir"), split_axis=0, concat_axis=0, tiled=True)
    return pl.pallas_call(
        lambda *refs: sum_kernel(scale, *refs),
        out_shape=result,
        in_specs=[vmem],
        out_specs=vmem,
        compiler_params=params(),
        name="total",
    )(terms)


def solution(mesh):
    in_specs = (
        P("dom", ("panel", "blk")),
        P(None, None, "dom"),
        P("dir", None, "dom"),
        P(None, "dom"),
        P("dom"),
        P("dom"),
    )
    out_specs = P("dir", ("panel", "dom"), "blk")
    return jax.shard_map(
        per_device, mesh=mesh, in_specs=in_specs, out_specs=out_specs, check_vma=False
    )
```

time: 50.4 us -> 46.8 us (0.929)
  waiting for transfers between devices: 22.5 us -> 15.3 us
  Pallas kernels: 13.9 us -> 16 us
  starting transfers between devices: 11.8 us -> 13.2 us
    ppermute x6 -> x7, waiting for transfers between devices: 19.4 us -> 13.7 us  [swap(): return lax.ppermute(value, ('dom', 'dir'), pairs)]
    pallas_call x7 -> x9, Pallas kernels: 7.9 us -> 10.1 us  [the longest x1 6.18 us: per_device(): pl.pallas_call(prep_kernel, out_shape=(*prepared, shape((11, *neighbours....]
    ppermute x6, waiting for transfers between devices: 3.08 us -> 1.61 us  [shift(): lax.ppermute(value, axis, [(i, (i + by) % length) for i in range(length)])]
    ppermute x6 -> x7, starting transfers between devices: 4.82 us -> 5.75 us  [swap(): return lax.ppermute(value, ('dom', 'dir'), pairs)]
  transfers between devices with their start and end apart: 12 -> 13, of which waited for: 5 -> 7; matrix products, arithmetic and copies ran while one was open for 0% -> 0% of each run, Pallas kernels for 24% -> 31%
where the time goes in v5:
time: 46.8 us; the launch traced here: 46.6 us
  Pallas kernels  16 us (34%)
  waiting for transfers between devices  15.3 us (33%)
  starting transfers between devices  13.2 us (28%)
  local copies, waits for them, and re-layouts  1.99 us (4%)
    ppermute x7, waiting for transfers between devices, swap(): return lax.ppermute(value, ('dom', 'dir'), pairs)  13.7 us
    ppermute x6, starting transfers between devices, shift(): lax.ppermute(value, axis, [(i, (i + by) % length) for i in range(length)])  7.41 us
    pallas_call x1, Pallas kernels, per_device(): pl.pallas_call(prep_kernel, out_shape=(*prepared, shape((11, *neighbours....  6.18 us
    ppermute x7, starting transfers between devices, swap(): return lax.ppermute(value, ('dom', 'dir'), pairs)  5.75 us
    pallas_call x1, Pallas kernels, per_device(): pl.pallas_call(weights_kernel, out_shape=(shape((2 * rows, half), F32), s...  5.09 us
    unnamed x6, local copies, waits for them, and re-layouts  1.99 us
    ppermute x6, waiting for transfers between devices, shift(): lax.ppermute(value, axis, [(i, (i + by) % length) for i in range(length)])  1.61 us
    pallas_call x2, Pallas kernels, flux_of(): pl.pallas_call(functools.partial(flux_kernel, e), out_shape=shape((rows,...  1.55 us
  transfers between devices with their start and end apart: 13, of which 7 were waited for; matrix products, arithmetic and copies ran while one was open for 0% of the time, Pallas kernels for 31%

profile of v5, /device:TPU:0, one launch (start us, length us, event | category | flops | bytes accessed | tf_op | source)
XLA Modules:
  0.0 46.6 jit_solution(3117750155693827656)
XLA Ops:
  0.0 0.5 collective-permute-start
  0.5 6.2 %prep.1 = (bf16[256,768]{1,0:T(8,128)(2,1)}, bf16[384,256]{1,0:T(8,128)(2,1)}, bf16[384,256]{1,0:T(8,128)(2,1)}, bf16[768,256]{1,0:T(8,128)(2,1)}, f32[11,16,256]{2,1,0:T(8,128)}) custom-call(bf16[768,512]{1,0:T(8,128)(2,1)} %v_hbm.1, s32[1,128]{1,0:T(1,128)} %bitcast.4, s32[1,128]{1,0:T(1,128)} %bitcast.5, f32[9,16,256]{2,1,0:T(8,128)} %bitcast.3, ...), custom_call_target="tpu_custom_call" | custom-call | tf_op jit(solution)/shard_map/prep/pallas_call | solution.py:321
  6.6 0.1 collective-permute-start.3
  6.8 2.9 %collective-permute-start.4 = (bf16[256,768]{1,0:T(8,128)(2,1)}, bf16[256,768]{1,0:T(8,128)(2,1)S(1)}, u32[]{:S(2)}, u32[]{:S(2)}) collective-permute-start(bf16[256,768]{1,0:T(8,128)(2,1)} %get-tuple-element.28.refs_0_), channel_id=1, source_target_pairs={{0,2},{2,0},{1,3},{3,1},{4,6},{6,4},{5,7},{7,5},{8,10},{10,8},{9,1... | collective-permute-start | bytes 1179656 | tf_op jit(solution)/shard_map/ppermute | solution.py:286
  9.7 1.6 %collective-permute-start.1 = (bf16[384,256]{1,0:T(8,128)(2,1)}, bf16[384,256]{1,0:T(8,128)(2,1)S(1)}, u32[]{:S(2)}, u32[]{:S(2)}) collective-permute-start(bf16[384,256]{1,0:T(8,128)(2,1)} %get-tuple-element.26), channel_id=1, source_target_pairs={{0,4},{4,8},{8,12},{12,0},{1,5},{5,9},{9,13},{13,1},{2,6},{6,10},{... | collective-permute-start | bytes 589832 | tf_op jit(solution)/shard_map/ppermute | solution.py:286
  11.3 2.2 %collective-permute-start.2 = (bf16[384,256]{1,0:T(8,128)(2,1)}, bf16[384,256]{1,0:T(8,128)(2,1)S(1)}, u32[]{:S(2)}, u32[]{:S(2)}) collective-permute-start(bf16[384,256]{1,0:T(8,128)(2,1)} %get-tuple-element.27), channel_id=1, source_target_pairs={{0,12},{4,0},{8,4},{12,8},{1,13},{5,1},{9,5},{13,9},{2,14},{6,2},{... | collective-permute-start | bytes 589832 | tf_op jit(solution)/shard_map/ppermute | solution.py:286
  13.5 0.0 collective-permute-done.other_ref
  13.5 0.0 copy-start.1
  13.5 1.0 %copy-done.1 = bf16[768,256]{1,0:T(8,128)(2,1)S(1)} copy-done((bf16[768,256]{1,0:T(8,128)(2,1)S(1)}, bf16[768,256]{1,0:T(8,128)(2,1)}, u32[]{:S(2)}) %copy-start.1) | copy-done | bytes 393240
  14.5 0.0 copy-start.2
  14.5 0.9 %copy-done.2 = f32[11,16,256]{2,1,0:T(8,128)S(1)} copy-done((f32[11,16,256]{2,1,0:T(8,128)S(1)}, f32[11,16,256]{2,1,0:T(8,128)}, u32[]{:S(2)}) %copy-start.2) | copy-done | bytes 180248
  15.5 5.1 %weights.1 = (f32[1536,256]{1,0:T(8,128)S(1)}, bf16[1536,768]{1,0:T(8,128)(2,1)S(1)}, bf16[1536,768]{1,0:T(8,128)(2,1)S(1)}) custom-call(f32[11,16,256]{2,1,0:T(8,128)S(1)} %copy-done.2, f32[1,16,256]{2,1,0:T(8,128)S(1)} %collective-permute-done.other_ref, bf16[768,256]{1,0:T(8,128)(2,1)S(1)} %copy-done.1), custom_call_target="tpu_custom_call" | custom-call | flops 8000000000 | bytes 10000000 | tf_op jit(solution)/shard_map/weights/pallas_call | solution.py:344
  20.6 0.0 collective-permute-done.1.below_ref.below_hbm
  20.6 1.5 %collective-permute-done.2.above_ref.above_hbm = bf16[384,256]{1,0:T(8,128)(2,1)S(1)} collective-permute-done((bf16[384,256]{1,0:T(8,128)(2,1)}, bf16[384,256]{1,0:T(8,128)(2,1)S(1)}, u32[]{:S(2)}, u32[]{:S(2)}) %collective-permute-start.2) | collective-permute-done | bytes 196640 | tf_op jit(solution)/shard_map/ppermute | solution.py:286
  22.0 0.0 collective-permute-done.4.refs_0_
  22.1 0.1 collective-permute-start.5
  22.1 0.8 %flux.2.flux0_ref.flux_ref = bf16[768,256]{1,0:T(8,128)(2,1)S(1)} custom-call(f32[1536,256]{1,0:T(8,128)S(1)} %get-tuple-element.23.part_ref.part_hbm, bf16[1536,768]{1,0:T(8,128)(2,1)S(1)} %get-tuple-element.24.hi_ref, bf16[1536,768]{1,0:T(8,128)(2,1)S(1)} %get-tuple-element.25.lo_ref, bf16[384,256]{1,0:T(8,128)(2,1)S(1)} %collective-permute-done.1.below_ref.below_hbm, ...), custom_call_target="tpu_custom_call" | custom-call | flops 1000000000 | bytes 1000000 | tf_op jit(solution)/shard_map/flux/pallas_call | solution.py:378
  22.9 0.0 copy-start
  22.9 0.8 %flux.3.flux1_ref.flux_ref = bf16[768,256]{1,0:T(8,128)(2,1)S(1)} custom-call(f32[1536,256]{1,0:T(8,128)S(1)} %get-tuple-element.23.part_ref.part_hbm, bf16[1536,768]{1,0:T(8,128)(2,1)S(1)} %get-tuple-element.24.hi_ref, bf16[1536,768]{1,0:T(8,128)(2,1)S(1)} %get-tuple-element.25.lo_ref, bf16[384,256]{1,0:T(8,128)(2,1)S(1)} %collective-permute-done.1.below_ref.below_hbm, ...), custom_call_target="tpu_custom_call" | custom-call | flops 1000000000 | bytes 1000000 | tf_op jit(solution)/shard_map/flux/pallas_call | solution.py:378
  23.7 0.0 collective-permute-done.3.refs_1_
  23.7 0.1 collective-permute-done.5.refs_3_
  23.9 0.1 copy-done
  23.9 0.7 %far.2 = (bf16[256,256]{1,0:T(8,128)(2,1)S(1)}, f32[256,256]{1,0:T(8,128)S(1)}) custom-call(bf16[768,256]{1,0:T(8,128)(2,1)S(1)} %flux.2.flux0_ref.flux_ref, bf16[256,768]{1,0:T(8,128)(2,1)S(1)} %copy-done, bf16[256,768]{1,0:T(8,128)(2,1)S(1)} %collective-permute-done.3.refs_1_, bf16[256,768]{1,0:T(8,128)(2,1)S(1)} %relay.1.refs_2_, ...), custom_call_target="tpu_custom_call" | custom-call | flops 400000000 | bytes 1000000 | tf_op jit(solution)/shard_map/far/pallas_call | solution.py:398
  24.7 1.2 %collective-permute-start.9 = (bf16[256,256]{1,0:T(8,128)(2,1)S(1)}, bf16[256,256]{1,0:T(8,128)(2,1)S(1)}, u32[]{:S(2)}, u32[]{:S(2)}) collective-permute-start(bf16[256,256]{1,0:T(8,128)(2,1)S(1)} %get-tuple-element.33), channel_id=1, source_target_pairs={{0,4},{1,5},{4,0},{5,1},{8,12},{9,13},{12,8},{13,9},{2,6},{3,7},{6... | collective-permute-start | bytes 393224 | tf_op jit(solution)/shard_map/ppermute | solution.py:294
  25.8 0.7 %far.3 = (bf16[256,256]{1,0:T(8,128)(2,1)S(1)}, f32[256,256]{1,0:T(8,128)S(1)}) custom-call(bf16[768,256]{1,0:T(8,128)(2,1)S(1)} %flux.3.flux1_ref.flux_ref, bf16[256,768]{1,0:T(8,128)(2,1)S(1)} %copy-done, bf16[256,768]{1,0:T(8,128)(2,1)S(1)} %collective-permute-done.3.refs_1_, bf16[256,768]{1,0:T(8,128)(2,1)S(1)} %relay.1.refs_2_, ...), custom_call_target="tpu_custom_call" | custom-call | flops 400000000 | bytes 1000000 | tf_op jit(solution)/shard_map/far/pallas_call | solution.py:398
  26.6 1.0 %collective-permute-start.11 = (bf16[256,256]{1,0:T(8,128)(2,1)S(1)}, bf16[256,256]{1,0:T(8,128)(2,1)S(1)}, u32[]{:S(2)}, u32[]{:S(2)}) collective-permute-start(bf16[256,256]{1,0:T(8,128)(2,1)S(1)} %get-tuple-element.35), channel_id=1, source_target_pairs={{0,4},{1,5},{4,0},{5,1},{8,12},{9,13},{12,8},{13,9},{2,6},{3,7},{6... | collective-permute-start | bytes 393224 | tf_op jit(solution)/shard_map/ppermute | solution.py:294
  27.5 0.8 %near.1 = (bf16[256,256]{1,0:T(8,128)(2,1)S(1)}, bf16[256,256]{1,0:T(8,128)(2,1)S(1)}, f32[256,256]{1,0:T(8,128)S(1)}, bf16[256,256]{1,0:T(8,128)(2,1)S(1)}) custom-call(bf16[768,256]{1,0:T(8,128)(2,1)S(1)} %flux.2.flux0_ref.flux_ref, bf16[768,256]{1,0:T(8,128)(2,1)S(1)} %flux.3.flux1_ref.flux_ref, bf16[256,768]{1,0:T(8,128)(2,1)S(1)} %copy-done, ...), custom_call_target="tpu_custom_call" | custom-call | flops 400000000 | bytes 1000000 | tf_op jit(solution)/shard_map/near/pallas_call | solution.py:413
  28.3 0.1 collective-permute-start.6
  28.4 1.2 %collective-permute-start.7 = (bf16[256,256]{1,0:T(8,128)(2,1)S(1)}, bf16[256,256]{1,0:T(8,128)(2,1)S(1)}, u32[]{:S(2)}, u32[]{:S(2)}) collective-permute-start(bf16[256,256]{1,0:T(8,128)(2,1)S(1)} %get-tuple-element.31), channel_id=1, source_target_pairs={{0,4},{1,5},{4,0},{5,1},{8,12},{9,13},{12,8},{13,9},{2,6},{3,7},{6... | collective-permute-start | bytes 393224 | tf_op jit(solution)/shard_map/ppermute | solution.py:294
  29.6 0.7 %collective-permute-start.8 = (bf16[256,256]{1,0:T(8,128)(2,1)S(1)}, bf16[256,256]{1,0:T(8,128)(2,1)S(1)}, u32[]{:S(2)}, u32[]{:S(2)}) collective-permute-start(bf16[256,256]{1,0:T(8,128)(2,1)S(1)} %get-tuple-element.32), channel_id=1, source_target_pairs={{0,5},{1,4},{4,1},{5,0},{8,13},{9,12},{12,9},{13,8},{2,7},{3,6},{6... | collective-permute-start | bytes 393224 | tf_op jit(solution)/shard_map/ppermute | solution.py:294
  30.3 0.7 %collective-permute-done.9.far_ref = bf16[256,256]{1,0:T(8,128)(2,1)S(1)} collective-permute-done((bf16[256,256]{1,0:T(8,128)(2,1)S(1)}, bf16[256,256]{1,0:T(8,128)(2,1)S(1)}, u32[]{:S(2)}, u32[]{:S(2)}) %collective-permute-start.9) | collective-permute-done | bytes 131104 | tf_op jit(solution)/shard_map/ppermute | solution.py:294
  31.0 1.4 %collective-permute-start.10 = (bf16[256,256]{1,0:T(8,128)(2,1)S(1)}, bf16[256,256]{1,0:T(8,128)(2,1)S(1)}, u32[]{:S(2)}, u32[]{:S(2)}) collective-permute-start(bf16[256,256]{1,0:T(8,128)(2,1)S(1)} %add.2), channel_id=1, source_target_pairs={{0,8},{1,9},{4,12},{5,13},{8,0},{9,1},{12,4},{13,5},{2,10},{3,11},... | collective-permute-start | bytes 393224 | tf_op jit(solution)/shard_map/ppermute | solution.py:294
  32.4 1.4 %collective-permute-done.11.far_ref = bf16[256,256]{1,0:T(8,128)(2,1)S(1)} collective-permute-done((bf16[256,256]{1,0:T(8,128)(2,1)S(1)}, bf16[256,256]{1,0:T(8,128)(2,1)S(1)}, u32[]{:S(2)}, u32[]{:S(2)}) %collective-permute-start.11) | collective-permute-done | bytes 131104 | tf_op jit(solution)/shard_map/ppermute | solution.py:294
  33.8 0.3 collective-permute-start.12
  34.1 0.0 collective-permute-done.6.refs_1_
  34.1 7.9 %collective-permute-done.7.refs_2_ = bf16[256,256]{1,0:T(8,128)(2,1)S(1)} collective-permute-done((bf16[256,256]{1,0:T(8,128)(2,1)S(1)}, bf16[256,256]{1,0:T(8,128)(2,1)S(1)}, u32[]{:S(2)}, u32[]{:S(2)}) %collective-permute-start.7) | collective-permute-done | bytes 131104 | tf_op jit(solution)/shard_map/ppermute | solution.py:294
  42.0 2.0 %collective-permute-done.8.refs_3_ = bf16[256,256]{1,0:T(8,128)(2,1)S(1)} collective-permute-done((bf16[256,256]{1,0:T(8,128)(2,1)S(1)}, bf16[256,256]{1,0:T(8,128)(2,1)S(1)}, u32[]{:S(2)}, u32[]{:S(2)}) %collective-permute-start.8) | collective-permute-done | bytes 131104 | tf_op jit(solution)/shard_map/ppermute | solution.py:294
  44.0 0.0 collective-permute-done.10.refs_4_
  44.0 1.7 %collective-permute-done.12.refs_5_ = bf16[256,256]{1,0:T(8,128)(2,1)S(1)} collective-permute-done((bf16[256,256]{1,0:T(8,128)(2,1)S(1)}, bf16[256,256]{1,0:T(8,128)(2,1)S(1)}, u32[]{:S(2)}, u32[]{:S(2)}) %collective-permute-start.12) | collective-permute-done | bytes 131104 | tf_op jit(solution)/shard_map/ppermute | solution.py:294
  45.7 0.9 %total.1 = f32[1,256,512]{2,1,0:T(8,128)} custom-call(f32[256,256]{1,0:T(8,128)S(1)} %get-tuple-element.29.refs_0_, bf16[256,256]{1,0:T(8,128)(2,1)S(1)} %collective-permute-done.6.refs_1_, bf16[256,256]{1,0:T(8,128)(2,1)S(1)} %collective-permute-done.7.refs_2_, bf16[256,256]{1,0:T(8,128)(2,1)S(1)} %collective-permute-done.8.refs_3_, ...), custom_call_target="tpu_custom_call" | custom-call | tf_op jit(solution)/shard_map/total/pallas_call | solution.py:435
  (3 shorter events, 0.1 us)
Async XLA Ops:
  0.0 13.5 %collective-permute-start = (f32[1,16,256]{2,1,0:T(8,128)}, f32[1,16,256]{2,1,0:T(8,128)S(1)}, u32[]{:S(2)}, u32[]{:S(2)}) collective-permute-start(f32[1,16,256]{2,1,0:T(8,128)} %bond_hbm.1), channel_id=1, source_target_pairs={{0,1},{1,0},{2,3},{3,2},{4,5},{5,4},{6,7},{7,6},{8,9},{9,8},{10,11... | collective-permute-start | bytes 49160 | tf_op jit(solution)/shard_map/ppermute | solution.py:286
  6.6 17.1 %collective-permute-start.3 = (bf16[256,768]{1,0:T(8,128)(2,1)}, bf16[256,768]{1,0:T(8,128)(2,1)S(1)}, u32[]{:S(2)}, u32[]{:S(2)}) collective-permute-start(bf16[256,768]{1,0:T(8,128)(2,1)} %get-tuple-element.28.refs_0_), channel_id=1, source_target_pairs={{0,1},{1,0},{2,3},{3,2},{4,5},{5,4},{6,7},{7,6},{8,9},{9,8},{10,11... | collective-permute-start | bytes 1179656 | tf_op jit(solution)/shard_map/ppermute | solution.py:286
  6.8 15.3 %collective-permute-start.4 = (bf16[256,768]{1,0:T(8,128)(2,1)}, bf16[256,768]{1,0:T(8,128)(2,1)S(1)}, u32[]{:S(2)}, u32[]{:S(2)}) collective-permute-start(bf16[256,768]{1,0:T(8,128)(2,1)} %get-tuple-element.28.refs_0_), channel_id=1, source_target_pairs={{0,2},{2,0},{1,3},{3,1},{4,6},{6,4},{5,7},{7,5},{8,10},{10,8},{9,1... | collective-permute-start | bytes 1179656 | tf_op jit(solution)/shard_map/ppermute | solution.py:286
  9.7 10.8 %collective-permute-start.1 = (bf16[384,256]{1,0:T(8,128)(2,1)}, bf16[384,256]{1,0:T(8,128)(2,1)S(1)}, u32[]{:S(2)}, u32[]{:S(2)}) collective-permute-start(bf16[384,256]{1,0:T(8,128)(2,1)} %get-tuple-element.26), channel_id=1, source_target_pairs={{0,4},{4,8},{8,12},{12,0},{1,5},{5,9},{9,13},{13,1},{2,6},{6,10},{... | collective-permute-start | bytes 589832 | tf_op jit(solution)/shard_map/ppermute | solution.py:286
  11.3 10.7 %collective-permute-start.2 = (bf16[384,256]{1,0:T(8,128)(2,1)}, bf16[384,256]{1,0:T(8,128)(2,1)S(1)}, u32[]{:S(2)}, u32[]{:S(2)}) collective-permute-start(bf16[384,256]{1,0:T(8,128)(2,1)} %get-tuple-element.27), channel_id=1, source_target_pairs={{0,12},{4,0},{8,4},{12,8},{1,13},{5,1},{9,5},{13,9},{2,14},{6,2},{... | collective-permute-start | bytes 589832 | tf_op jit(solution)/shard_map/ppermute | solution.py:286
  13.5 1.0 %copy-start.1 = (bf16[768,256]{1,0:T(8,128)(2,1)S(1)}, bf16[768,256]{1,0:T(8,128)(2,1)}, u32[]{:S(2)}) copy-start(bf16[768,256]{1,0:T(8,128)(2,1)} %get-tuple-element.22.own_ref) | copy-start | bytes 1179652
  14.5 0.9 %copy-start.2 = (f32[11,16,256]{2,1,0:T(8,128)S(1)}, f32[11,16,256]{2,1,0:T(8,128)}, u32[]{:S(2)}) copy-start(f32[11,16,256]{2,1,0:T(8,128)} %get-tuple-element.21.source_ref) | copy-start | bytes 540676
  22.1 1.8 %collective-permute-start.5 = (bf16[256,768]{1,0:T(8,128)(2,1)S(1)}, bf16[256,768]{1,0:T(8,128)(2,1)S(1)}, u32[]{:S(2)}, u32[]{:S(2)}) collective-permute-start(bf16[256,768]{1,0:T(8,128)(2,1)S(1)} %relay.1.refs_2_), channel_id=1, source_target_pairs={{0,1},{1,0},{2,3},{3,2},{4,5},{5,4},{6,7},{7,6},{8,9},{9,8},{10,11... | collective-permute-start | bytes 1179656 | tf_op jit(solution)/shard_map/ppermute | solution.py:286
  22.9 1.0 %copy-start = (bf16[256,768]{1,0:T(8,128)(2,1)S(1)}, bf16[256,768]{1,0:T(8,128)(2,1)}, u32[]{:S(2)}) copy-start(bf16[256,768]{1,0:T(8,128)(2,1)} %get-tuple-element.28.refs_0_) | copy-start | bytes 1179652
  24.7 6.4 %collective-permute-start.9 = (bf16[256,256]{1,0:T(8,128)(2,1)S(1)}, bf16[256,256]{1,0:T(8,128)(2,1)S(1)}, u32[]{:S(2)}, u32[]{:S(2)}) collective-permute-start(bf16[256,256]{1,0:T(8,128)(2,1)S(1)} %get-tuple-element.33), channel_id=1, source_target_pairs={{0,4},{1,5},{4,0},{5,1},{8,12},{9,13},{12,8},{13,9},{2,6},{3,7},{6... | collective-permute-start | bytes 393224 | tf_op jit(solution)/shard_map/ppermute | solution.py:294
  26.6 7.2 %collective-permute-start.11 = (bf16[256,256]{1,0:T(8,128)(2,1)S(1)}, bf16[256,256]{1,0:T(8,128)(2,1)S(1)}, u32[]{:S(2)}, u32[]{:S(2)}) collective-permute-start(bf16[256,256]{1,0:T(8,128)(2,1)S(1)} %get-tuple-element.35), channel_id=1, source_target_pairs={{0,4},{1,5},{4,0},{5,1},{8,12},{9,13},{12,8},{13,9},{2,6},{3,7},{6... | collective-permute-start | bytes 393224 | tf_op jit(solution)/shard_map/ppermute | solution.py:294
  28.3 5.8 %collective-permute-start.6 = (bf16[256,256]{1,0:T(8,128)(2,1)S(1)}, bf16[256,256]{1,0:T(8,128)(2,1)S(1)}, u32[]{:S(2)}, u32[]{:S(2)}) collective-permute-start(bf16[256,256]{1,0:T(8,128)(2,1)S(1)} %get-tuple-element.30), channel_id=1, source_target_pairs={{0,1},{1,0},{4,5},{5,4},{8,9},{9,8},{12,13},{13,12},{2,3},{3,2},{6... | collective-permute-start | bytes 393224 | tf_op jit(solution)/shard_map/ppermute | solution.py:294
  28.4 13.6 %collective-permute-start.7 = (bf16[256,256]{1,0:T(8,128)(2,1)S(1)}, bf16[256,256]{1,0:T(8,128)(2,1)S(1)}, u32[]{:S(2)}, u32[]{:S(2)}) collective-permute-start(bf16[256,256]{1,0:T(8,128)(2,1)S(1)} %get-tuple-element.31), channel_id=1, source_target_pairs={{0,4},{1,5},{4,0},{5,1},{8,12},{9,13},{12,8},{13,9},{2,6},{3,7},{6... | collective-permute-start | bytes 393224 | tf_op jit(solution)/shard_map/ppermute | solution.py:294
  29.6 14.4 %collective-permute-start.8 = (bf16[256,256]{1,0:T(8,128)(2,1)S(1)}, bf16[256,256]{1,0:T(8,128)(2,1)S(1)}, u32[]{:S(2)}, u32[]{:S(2)}) collective-permute-start(bf16[256,256]{1,0:T(8,128)(2,1)S(1)} %get-tuple-element.32), channel_id=1, source_target_pairs={{0,5},{1,4},{4,1},{5,0},{8,13},{9,12},{12,9},{13,8},{2,7},{3,6},{6... | collective-permute-start | bytes 393224 | tf_op jit(solution)/shard_map/ppermute | solution.py:294
  31.0 13.0 %collective-permute-start.10 = (bf16[256,256]{1,0:T(8,128)(2,1)S(1)}, bf16[256,256]{1,0:T(8,128)(2,1)S(1)}, u32[]{:S(2)}, u32[]{:S(2)}) collective-permute-start(bf16[256,256]{1,0:T(8,128)(2,1)S(1)} %add.2), channel_id=1, source_target_pairs={{0,8},{1,9},{4,12},{5,13},{8,0},{9,1},{12,4},{13,5},{2,10},{3,11},... | collective-permute-start | bytes 393224 | tf_op jit(solution)/shard_map/ppermute | solution.py:294
  33.8 11.9 %collective-permute-start.12 = (bf16[256,256]{1,0:T(8,128)(2,1)S(1)}, bf16[256,256]{1,0:T(8,128)(2,1)S(1)}, u32[]{:S(2)}, u32[]{:S(2)}) collective-permute-start(bf16[256,256]{1,0:T(8,128)(2,1)S(1)} %add.3), channel_id=1, source_target_pairs={{0,9},{1,8},{4,13},{5,12},{8,1},{9,0},{12,5},{13,4},{2,11},{3,10},... | collective-permute-start | bytes 393224 | tf_op jit(solution)/shard_map/ppermute | solution.py:294

commit v6 on v5

--- a/solution.py
+++ b/solution.py
@@ -30,46 +30,49 @@
 
 def prep_kernel(
     v_hbm, low_hbm, high_hbm, force_hbm, bond_hbm, near_hbm,
-    turned_hbm, send_low_hbm, send_high_hbm, own_hbm, source_hbm,
+    turned_hbm, send_low_hbm, send_high_hbm, own_hbm, source_hbm, bond_out_hbm,
     v_ref, low_ref, high_ref, near_ref, turned_ref, send_low_ref, send_high_ref, own_ref,
-    name_ref, in_sems, out_sems,
+    source_ref, in_sems, out_sems,
 ):
     rows, half = v_ref.shape
     atoms = rows // 3
-    v_in = pltpu.make_async_copy(v_hbm.at[:, my_columns(half)], v_ref, in_sems.at[0])
-    v_in.start()
-    lists_in = [
-        pltpu.make_async_copy(low_hbm, low_ref, in_sems.at[1]),
-        pltpu.make_async_copy(high_hbm, high_ref, in_sems.at[2]),
-        pltpu.make_async_copy(near_hbm, near_ref, in_sems.at[3]),
+    arriving = [
+        pltpu.make_async_copy(source, target, in_sems.at[i])
+        for i, (source, target) in enumerate(
+            (
+                (v_hbm.at[:, my_columns(half)], v_ref),
+                (low_hbm, low_ref),
+                (high_hbm, high_ref),
+                (near_hbm, near_ref),
+                (force_hbm, source_ref.at[0:9]),
+                (bond_hbm, source_ref.at[9:10]),
+            )
+        )
     ]
-    for copy in lists_in:
+    for copy in arriving:
         copy.start()
-    out = [
-        pltpu.make_async_copy(force_hbm, source_hbm.at[0:9], out_sems.at[0]),
-        pltpu.make_async_copy(bond_hbm, source_hbm.at[9:10], out_sems.at[1]),
-    ]
-    for copy in out:
+    leaving = []
+
+    def leave(ref, hbm):
+        copy = pltpu.make_async_copy(ref, hbm, out_sems.at[len(leaving)])
         copy.start()
-
-    def leave(ref, hbm):
-        copy = pltpu.make_async_copy(ref, hbm, out_sems.at[len(out)])
-        copy.start()
-        out.append(copy)
+        leaving.append(copy)
 
     lane = lax.broadcasted_iota(jnp.int32, (atoms, rows), 1)
     atom = lax.broadcasted_iota(jnp.int32, (atoms, rows), 0)
     hot = [one_hot(lane == 3 * atom + b) for b in range(3)]
-    v_in.wait()
+    for copy in arriving:
+        copy.wait()
+    source_ref[10] = near_ref[...].astype(F32)
+    leave(source_ref.at[9:10], bond_out_hbm)
+    leave(source_ref, source_hbm)
     v = v_ref[...]
     for b in range(3):
         picked = dot(hot[b], v)
         turned_ref[:, b * atoms : (b + 1) * atoms] = picked.T.astype(BF16)
         own_ref[b * atoms : (b + 1) * atoms, :] = picked.astype(BF16)
     leave(turned_ref, turned_hbm)
-    for copy in lists_in:
-        copy.wait()
-    name_ref[0] = near_ref[...].astype(F32)
+    leave(own_ref, own_hbm)
     for list_ref, send_ref, send_hbm in (
         (high_ref, send_high_ref, send_high_hbm),
         (low_ref, send_low_ref, send_low_hbm),
@@ -84,9 +87,7 @@
             )
             send_ref[b * count : (b + 1) * count, :] = dot(picks, v).astype(BF16)
         leave(send_ref, send_hbm)
-    leave(own_ref, own_hbm)
-    leave(name_ref, source_hbm.at[10:11])
-    for copy in out:
+    for copy in leaving:
         copy.wait()
 
 
@@ -309,7 +310,6 @@
     hbm = pl.BlockSpec(memory_space=pltpu.HBM)
     anywhere = pl.BlockSpec(memory_space=pl.ANY)
 
-    other_bonds = shift(bond_vectors, "dir", 1)
     lists = [boundary_low.reshape(1, count), boundary_high.reshape(1, count)]
     forces = force_blocks.transpose(1, 0, 2)
     prepared = (
@@ -318,26 +318,31 @@
         shape((3 * count, half), BF16),
         shape((rows, half), BF16),
     )
-    turned, send_low, send_high, own, sources = pl.pallas_call(
+    turned, send_low, send_high, own, sources, bonds = pl.pallas_call(
         prep_kernel,
-        out_shape=(*prepared, shape((11, *neighbours.shape), F32)),
+        out_shape=(
+            *prepared,
+            shape((11, *neighbours.shape), F32),
+            shape(bond_vectors.shape, F32),
+        ),
         in_specs=[hbm] * 6,
-        out_specs=(hbm,) * 5,
+        out_specs=(hbm,) * 6,
         scratch_shapes=[
             pltpu.VMEM((rows, half), BF16),
             pltpu.VMEM((1, count), jnp.int32),
             pltpu.VMEM((1, count), jnp.int32),
             pltpu.VMEM(neighbours.shape, jnp.int32),
             *[pltpu.VMEM(like.shape, like.dtype) for like in prepared],
-            pltpu.VMEM((1, *neighbours.shape), F32),
-            pltpu.SemaphoreType.DMA((4,)),
-            pltpu.SemaphoreType.DMA((7,)),
+            pltpu.VMEM((11, *neighbours.shape), F32),
+            pltpu.SemaphoreType.DMA((6,)),
+            pltpu.SemaphoreType.DMA((6,)),
         ],
         compiler_params=params(58),
         name="prep",
     )(panel_vectors, *lists, forces, bond_vectors, neighbours)
     quarters = [shift(turned, "blk", j) for j in range(1, tiles)]
     turned_other = shift(turned, "dir", 1)
+    other_bonds = shift(bonds, "dir", 1)
     below = shift(send_high, "dom", 1)
     above = shift(send_low, "dom", -1)
 

time: 46.8 us -> 43.7 us (0.934)
  Pallas kernels: 16 us -> 12.9 us
    pallas_call x1, Pallas kernels: 6.18 us -> 3.08 us  [per_device(): pl.pallas_call(prep_kernel, out_shape=(*prepared, shape((11, *neighbours....]
  transfers between devices with their start and end apart: 13 -> 13, of which waited for: 7 -> 7; matrix products, arithmetic and copies ran while one was open for 0% -> 0% of each run, Pallas kernels for 31% -> 19%
where the time goes in v6:
time: 43.7 us; the launch traced here: 43.5 us
  waiting for transfers between devices  15.3 us (35%)
  starting transfers between devices  13.1 us (30%)
  Pallas kernels  12.9 us (30%)
  local copies, waits for them, and re-layouts  1.99 us (5%)
    ppermute x7, waiting for transfers between devices, swap(): return lax.ppermute(value, ('dom', 'dir'), pairs)  13.7 us
    ppermute x6, starting transfers between devices, shift(): lax.ppermute(value, axis, [(i, (i + by) % length) for i in range(length)])  7.41 us
    ppermute x7, starting transfers between devices, swap(): return lax.ppermute(value, ('dom', 'dir'), pairs)  5.74 us
    pallas_call x1, Pallas kernels, per_device(): pl.pallas_call(weights_kernel, out_shape=(shape((2 * rows, half), F32), s...  5.09 us
    pallas_call x1, Pallas kernels, per_device(): pl.pallas_call(prep_kernel, out_shape=(*prepared, shape((11, *neighbours....  3.08 us
    unnamed x6, local copies, waits for them, and re-layouts  1.99 us
    ppermute x6, waiting for transfers between devices, shift(): lax.ppermute(value, axis, [(i, (i + by) % length) for i in range(length)])  1.61 us
    pallas_call x2, Pallas kernels, flux_of(): pl.pallas_call(functools.partial(flux_kernel, e), out_shape=shape((rows,...  1.55 us
  transfers between devices with their start and end apart: 13, of which 7 were waited for; matrix products, arithmetic and copies ran while one was open for 0% of the time, Pallas kernels for 19%

profile of v6, /device:TPU:0, one launch (start us, length us, event | category | flops | bytes accessed | tf_op | source)
XLA Modules:
  0.0 43.5 jit_solution(9772978006779412952)
XLA Ops:
  0.0 3.1 %prep.1 = (bf16[256,768]{1,0:T(8,128)(2,1)}, bf16[384,256]{1,0:T(8,128)(2,1)}, bf16[384,256]{1,0:T(8,128)(2,1)}, bf16[768,256]{1,0:T(8,128)(2,1)}, f32[11,16,256]{2,1,0:T(8,128)}, /*index=5*/f32[1,16,256]{2,1,0:T(8,128)}) custom-call(bf16[768,512]{1,0:T(8,128)(2,1)} %v_hbm.1, s32[1,128]{1,0:T(1,128)} %bitcast.4, s32[1,128]{1,0:T(1,128)} %bitcast.5, ...), custom_call_target="tpu_custom_call" | custom-call | tf_op jit(solution)/shard_map/prep/pallas_call | solution.py:321
  3.1 0.5 %collective-permute-start = (f32[1,16,256]{2,1,0:T(8,128)}, f32[1,16,256]{2,1,0:T(8,128)S(1)}, u32[]{:S(2)}, u32[]{:S(2)}) collective-permute-start(f32[1,16,256]{2,1,0:T(8,128)} %get-tuple-element.23), channel_id=1, source_target_pairs={{0,1},{1,0},{2,3},{3,2},{4,5},{5,4},{6,7},{7,6},{8,9},{9,8},{10,11... | collective-permute-start | bytes 49160 | tf_op jit(solution)/shard_map/ppermute | solution.py:287
  3.6 0.1 collective-permute-start.3
  3.7 2.9 %collective-permute-start.4 = (bf16[256,768]{1,0:T(8,128)(2,1)}, bf16[256,768]{1,0:T(8,128)(2,1)S(1)}, u32[]{:S(2)}, u32[]{:S(2)}) collective-permute-start(bf16[256,768]{1,0:T(8,128)(2,1)} %get-tuple-element.30.refs_0_), channel_id=1, source_target_pairs={{0,2},{2,0},{1,3},{3,1},{4,6},{6,4},{5,7},{7,5},{8,10},{10,8},{9,1... | collective-permute-start | bytes 1179656 | tf_op jit(solution)/shard_map/ppermute | solution.py:287
  6.6 1.6 %collective-permute-start.1 = (bf16[384,256]{1,0:T(8,128)(2,1)}, bf16[384,256]{1,0:T(8,128)(2,1)S(1)}, u32[]{:S(2)}, u32[]{:S(2)}) collective-permute-start(bf16[384,256]{1,0:T(8,128)(2,1)} %get-tuple-element.28), channel_id=1, source_target_pairs={{0,4},{4,8},{8,12},{12,0},{1,5},{5,9},{9,13},{13,1},{2,6},{6,10},{... | collective-permute-start | bytes 589832 | tf_op jit(solution)/shard_map/ppermute | solution.py:287
  8.2 2.2 %collective-permute-start.2 = (bf16[384,256]{1,0:T(8,128)(2,1)}, bf16[384,256]{1,0:T(8,128)(2,1)S(1)}, u32[]{:S(2)}, u32[]{:S(2)}) collective-permute-start(bf16[384,256]{1,0:T(8,128)(2,1)} %get-tuple-element.29), channel_id=1, source_target_pairs={{0,12},{4,0},{8,4},{12,8},{1,13},{5,1},{9,5},{13,9},{2,14},{6,2},{... | collective-permute-start | bytes 589832 | tf_op jit(solution)/shard_map/ppermute | solution.py:287
  10.4 0.0 collective-permute-done.other_ref
  10.4 0.0 copy-start.1
  10.4 1.0 %copy-done.1 = bf16[768,256]{1,0:T(8,128)(2,1)S(1)} copy-done((bf16[768,256]{1,0:T(8,128)(2,1)S(1)}, bf16[768,256]{1,0:T(8,128)(2,1)}, u32[]{:S(2)}) %copy-start.1) | copy-done | bytes 393240
  11.4 0.0 copy-start.2
  11.4 0.9 %copy-done.2 = f32[11,16,256]{2,1,0:T(8,128)S(1)} copy-done((f32[11,16,256]{2,1,0:T(8,128)S(1)}, f32[11,16,256]{2,1,0:T(8,128)}, u32[]{:S(2)}) %copy-start.2) | copy-done | bytes 180248
  12.4 5.1 %weights.1 = (f32[1536,256]{1,0:T(8,128)S(1)}, bf16[1536,768]{1,0:T(8,128)(2,1)S(1)}, bf16[1536,768]{1,0:T(8,128)(2,1)S(1)}) custom-call(f32[11,16,256]{2,1,0:T(8,128)S(1)} %copy-done.2, f32[1,16,256]{2,1,0:T(8,128)S(1)} %collective-permute-done.other_ref, bf16[768,256]{1,0:T(8,128)(2,1)S(1)} %copy-done.1), custom_call_target="tpu_custom_call" | custom-call | flops 8000000000 | bytes 10000000 | tf_op jit(solution)/shard_map/weights/pallas_call | solution.py:349
  17.5 0.0 collective-permute-done.1.below_ref.below_hbm
  17.5 1.5 %collective-permute-done.2.above_ref.above_hbm = bf16[384,256]{1,0:T(8,128)(2,1)S(1)} collective-permute-done((bf16[384,256]{1,0:T(8,128)(2,1)}, bf16[384,256]{1,0:T(8,128)(2,1)S(1)}, u32[]{:S(2)}, u32[]{:S(2)}) %collective-permute-start.2) | collective-permute-done | bytes 196640 | tf_op jit(solution)/shard_map/ppermute | solution.py:287
  18.9 0.0 collective-permute-done.4.refs_0_
  19.0 0.1 collective-permute-start.5
  19.0 0.8 %flux.2.flux0_ref.flux_ref = bf16[768,256]{1,0:T(8,128)(2,1)S(1)} custom-call(f32[1536,256]{1,0:T(8,128)S(1)} %get-tuple-element.25.part_ref.part_hbm, bf16[1536,768]{1,0:T(8,128)(2,1)S(1)} %get-tuple-element.26.hi_ref, bf16[1536,768]{1,0:T(8,128)(2,1)S(1)} %get-tuple-element.27.lo_ref, bf16[384,256]{1,0:T(8,128)(2,1)S(1)} %collective-permute-done.1.below_ref.below_hbm, ...), custom_call_target="tpu_custom_call" | custom-call | flops 1000000000 | bytes 1000000 | tf_op jit(solution)/shard_map/flux/pallas_call | solution.py:383
  19.8 0.0 copy-start
  19.8 0.8 %flux.3.flux1_ref.flux_ref = bf16[768,256]{1,0:T(8,128)(2,1)S(1)} custom-call(f32[1536,256]{1,0:T(8,128)S(1)} %get-tuple-element.25.part_ref.part_hbm, bf16[1536,768]{1,0:T(8,128)(2,1)S(1)} %get-tuple-element.26.hi_ref, bf16[1536,768]{1,0:T(8,128)(2,1)S(1)} %get-tuple-element.27.lo_ref, bf16[384,256]{1,0:T(8,128)(2,1)S(1)} %collective-permute-done.1.below_ref.below_hbm, ...), custom_call_target="tpu_custom_call" | custom-call | flops 1000000000 | bytes 1000000 | tf_op jit(solution)/shard_map/flux/pallas_call | solution.py:383
  20.6 0.0 collective-permute-done.3.refs_1_
  20.6 0.1 collective-permute-done.5.refs_3_
  20.8 0.1 copy-done
  20.8 0.7 %far.2 = (bf16[256,256]{1,0:T(8,128)(2,1)S(1)}, f32[256,256]{1,0:T(8,128)S(1)}) custom-call(bf16[768,256]{1,0:T(8,128)(2,1)S(1)} %flux.2.flux0_ref.flux_ref, bf16[256,768]{1,0:T(8,128)(2,1)S(1)} %copy-done, bf16[256,768]{1,0:T(8,128)(2,1)S(1)} %collective-permute-done.3.refs_1_, bf16[256,768]{1,0:T(8,128)(2,1)S(1)} %relay.1.refs_2_, ...), custom_call_target="tpu_custom_call" | custom-call | flops 400000000 | bytes 1000000 | tf_op jit(solution)/shard_map/far/pallas_call | solution.py:403
  21.6 1.2 %collective-permute-start.9 = (bf16[256,256]{1,0:T(8,128)(2,1)S(1)}, bf16[256,256]{1,0:T(8,128)(2,1)S(1)}, u32[]{:S(2)}, u32[]{:S(2)}) collective-permute-start(bf16[256,256]{1,0:T(8,128)(2,1)S(1)} %get-tuple-element.35), channel_id=1, source_target_pairs={{0,4},{1,5},{4,0},{5,1},{8,12},{9,13},{12,8},{13,9},{2,6},{3,7},{6... | collective-permute-start | bytes 393224 | tf_op jit(solution)/shard_map/ppermute | solution.py:295
  22.7 0.7 %far.3 = (bf16[256,256]{1,0:T(8,128)(2,1)S(1)}, f32[256,256]{1,0:T(8,128)S(1)}) custom-call(bf16[768,256]{1,0:T(8,128)(2,1)S(1)} %flux.3.flux1_ref.flux_ref, bf16[256,768]{1,0:T(8,128)(2,1)S(1)} %copy-done, bf16[256,768]{1,0:T(8,128)(2,1)S(1)} %collective-permute-done.3.refs_1_, bf16[256,768]{1,0:T(8,128)(2,1)S(1)} %relay.1.refs_2_, ...), custom_call_target="tpu_custom_call" | custom-call | flops 400000000 | bytes 1000000 | tf_op jit(solution)/shard_map/far/pallas_call | solution.py:403
  23.5 1.0 %collective-permute-start.11 = (bf16[256,256]{1,0:T(8,128)(2,1)S(1)}, bf16[256,256]{1,0:T(8,128)(2,1)S(1)}, u32[]{:S(2)}, u32[]{:S(2)}) collective-permute-start(bf16[256,256]{1,0:T(8,128)(2,1)S(1)} %get-tuple-element.37), channel_id=1, source_target_pairs={{0,4},{1,5},{4,0},{5,1},{8,12},{9,13},{12,8},{13,9},{2,6},{3,7},{6... | collective-permute-start | bytes 393224 | tf_op jit(solution)/shard_map/ppermute | solution.py:295
  24.4 0.8 %near.1 = (bf16[256,256]{1,0:T(8,128)(2,1)S(1)}, bf16[256,256]{1,0:T(8,128)(2,1)S(1)}, f32[256,256]{1,0:T(8,128)S(1)}, bf16[256,256]{1,0:T(8,128)(2,1)S(1)}) custom-call(bf16[768,256]{1,0:T(8,128)(2,1)S(1)} %flux.2.flux0_ref.flux_ref, bf16[768,256]{1,0:T(8,128)(2,1)S(1)} %flux.3.flux1_ref.flux_ref, bf16[256,768]{1,0:T(8,128)(2,1)S(1)} %copy-done, ...), custom_call_target="tpu_custom_call" | custom-call | flops 400000000 | bytes 1000000 | tf_op jit(solution)/shard_map/near/pallas_call | solution.py:418
  25.3 0.1 collective-permute-start.6
  25.3 1.2 %collective-permute-start.7 = (bf16[256,256]{1,0:T(8,128)(2,1)S(1)}, bf16[256,256]{1,0:T(8,128)(2,1)S(1)}, u32[]{:S(2)}, u32[]{:S(2)}) collective-permute-start(bf16[256,256]{1,0:T(8,128)(2,1)S(1)} %get-tuple-element.33), channel_id=1, source_target_pairs={{0,4},{1,5},{4,0},{5,1},{8,12},{9,13},{12,8},{13,9},{2,6},{3,7},{6... | collective-permute-start | bytes 393224 | tf_op jit(solution)/shard_map/ppermute | solution.py:295
  26.5 0.7 %collective-permute-start.8 = (bf16[256,256]{1,0:T(8,128)(2,1)S(1)}, bf16[256,256]{1,0:T(8,128)(2,1)S(1)}, u32[]{:S(2)}, u32[]{:S(2)}) collective-permute-start(bf16[256,256]{1,0:T(8,128)(2,1)S(1)} %get-tuple-element.34), channel_id=1, source_target_pairs={{0,5},{1,4},{4,1},{5,0},{8,13},{9,12},{12,9},{13,8},{2,7},{3,6},{6... | collective-permute-start | bytes 393224 | tf_op jit(solution)/shard_map/ppermute | solution.py:295
  27.2 0.7 %collective-permute-done.9.far_ref = bf16[256,256]{1,0:T(8,128)(2,1)S(1)} collective-permute-done((bf16[256,256]{1,0:T(8,128)(2,1)S(1)}, bf16[256,256]{1,0:T(8,128)(2,1)S(1)}, u32[]{:S(2)}, u32[]{:S(2)}) %collective-permute-start.9) | collective-permute-done | bytes 131104 | tf_op jit(solution)/shard_map/ppermute | solution.py:295
  27.9 1.4 %collective-permute-start.10 = (bf16[256,256]{1,0:T(8,128)(2,1)S(1)}, bf16[256,256]{1,0:T(8,128)(2,1)S(1)}, u32[]{:S(2)}, u32[]{:S(2)}) collective-permute-start(bf16[256,256]{1,0:T(8,128)(2,1)S(1)} %add.2), channel_id=1, source_target_pairs={{0,8},{1,9},{4,12},{5,13},{8,0},{9,1},{12,4},{13,5},{2,10},{3,11},... | collective-permute-start | bytes 393224 | tf_op jit(solution)/shard_map/ppermute | solution.py:295
  29.3 1.4 %collective-permute-done.11.far_ref = bf16[256,256]{1,0:T(8,128)(2,1)S(1)} collective-permute-done((bf16[256,256]{1,0:T(8,128)(2,1)S(1)}, bf16[256,256]{1,0:T(8,128)(2,1)S(1)}, u32[]{:S(2)}, u32[]{:S(2)}) %collective-permute-start.11) | collective-permute-done | bytes 131104 | tf_op jit(solution)/shard_map/ppermute | solution.py:295
  30.8 0.3 collective-permute-start.12
  31.0 0.0 collective-permute-done.6.refs_1_
  31.0 7.9 %collective-permute-done.7.refs_2_ = bf16[256,256]{1,0:T(8,128)(2,1)S(1)} collective-permute-done((bf16[256,256]{1,0:T(8,128)(2,1)S(1)}, bf16[256,256]{1,0:T(8,128)(2,1)S(1)}, u32[]{:S(2)}, u32[]{:S(2)}) %collective-permute-start.7) | collective-permute-done | bytes 131104 | tf_op jit(solution)/shard_map/ppermute | solution.py:295
  38.9 2.0 %collective-permute-done.8.refs_3_ = bf16[256,256]{1,0:T(8,128)(2,1)S(1)} collective-permute-done((bf16[256,256]{1,0:T(8,128)(2,1)S(1)}, bf16[256,256]{1,0:T(8,128)(2,1)S(1)}, u32[]{:S(2)}, u32[]{:S(2)}) %collective-permute-start.8) | collective-permute-done | bytes 131104 | tf_op jit(solution)/shard_map/ppermute | solution.py:295
  40.9 0.0 collective-permute-done.10.refs_4_
  40.9 1.7 %collective-permute-done.12.refs_5_ = bf16[256,256]{1,0:T(8,128)(2,1)S(1)} collective-permute-done((bf16[256,256]{1,0:T(8,128)(2,1)S(1)}, bf16[256,256]{1,0:T(8,128)(2,1)S(1)}, u32[]{:S(2)}, u32[]{:S(2)}) %collective-permute-start.12) | collective-permute-done | bytes 131104 | tf_op jit(solution)/shard_map/ppermute | solution.py:295
  42.6 0.9 %total.1 = f32[1,256,512]{2,1,0:T(8,128)} custom-call(f32[256,256]{1,0:T(8,128)S(1)} %get-tuple-element.31.refs_0_, bf16[256,256]{1,0:T(8,128)(2,1)S(1)} %collective-permute-done.6.refs_1_, bf16[256,256]{1,0:T(8,128)(2,1)S(1)} %collective-permute-done.7.refs_2_, bf16[256,256]{1,0:T(8,128)(2,1)S(1)} %collective-permute-done.8.refs_3_, ...), custom_call_target="tpu_custom_call" | custom-call | tf_op jit(solution)/shard_map/total/pallas_call | solution.py:440
  (3 shorter events, 0.1 us)
Async XLA Ops:
  3.1 7.3 %collective-permute-start = (f32[1,16,256]{2,1,0:T(8,128)}, f32[1,16,256]{2,1,0:T(8,128)S(1)}, u32[]{:S(2)}, u32[]{:S(2)}) collective-permute-start(f32[1,16,256]{2,1,0:T(8,128)} %get-tuple-element.23), channel_id=1, source_target_pairs={{0,1},{1,0},{2,3},{3,2},{4,5},{5,4},{6,7},{7,6},{8,9},{9,8},{10,11... | collective-permute-start | bytes 49160 | tf_op jit(solution)/shard_map/ppermute | solution.py:287
  3.6 17.0 %collective-permute-start.3 = (bf16[256,768]{1,0:T(8,128)(2,1)}, bf16[256,768]{1,0:T(8,128)(2,1)S(1)}, u32[]{:S(2)}, u32[]{:S(2)}) collective-permute-start(bf16[256,768]{1,0:T(8,128)(2,1)} %get-tuple-element.30.refs_0_), channel_id=1, source_target_pairs={{0,1},{1,0},{2,3},{3,2},{4,5},{5,4},{6,7},{7,6},{8,9},{9,8},{10,11... | collective-permute-start | bytes 1179656 | tf_op jit(solution)/shard_map/ppermute | solution.py:287
  3.7 15.2 %collective-permute-start.4 = (bf16[256,768]{1,0:T(8,128)(2,1)}, bf16[256,768]{1,0:T(8,128)(2,1)S(1)}, u32[]{:S(2)}, u32[]{:S(2)}) collective-permute-start(bf16[256,768]{1,0:T(8,128)(2,1)} %get-tuple-element.30.refs_0_), channel_id=1, source_target_pairs={{0,2},{2,0},{1,3},{3,1},{4,6},{6,4},{5,7},{7,5},{8,10},{10,8},{9,1... | collective-permute-start | bytes 1179656 | tf_op jit(solution)/shard_map/ppermute | solution.py:287
  6.6 10.8 %collective-permute-start.1 = (bf16[384,256]{1,0:T(8,128)(2,1)}, bf16[384,256]{1,0:T(8,128)(2,1)S(1)}, u32[]{:S(2)}, u32[]{:S(2)}) collective-permute-start(bf16[384,256]{1,0:T(8,128)(2,1)} %get-tuple-element.28), channel_id=1, source_target_pairs={{0,4},{4,8},{8,12},{12,0},{1,5},{5,9},{9,13},{13,1},{2,6},{6,10},{... | collective-permute-start | bytes 589832 | tf_op jit(solution)/shard_map/ppermute | solution.py:287
  8.2 10.7 %collective-permute-start.2 = (bf16[384,256]{1,0:T(8,128)(2,1)}, bf16[384,256]{1,0:T(8,128)(2,1)S(1)}, u32[]{:S(2)}, u32[]{:S(2)}) collective-permute-start(bf16[384,256]{1,0:T(8,128)(2,1)} %get-tuple-element.29), channel_id=1, source_target_pairs={{0,12},{4,0},{8,4},{12,8},{1,13},{5,1},{9,5},{13,9},{2,14},{6,2},{... | collective-permute-start | bytes 589832 | tf_op jit(solution)/shard_map/ppermute | solution.py:287
  10.4 1.0 %copy-start.1 = (bf16[768,256]{1,0:T(8,128)(2,1)S(1)}, bf16[768,256]{1,0:T(8,128)(2,1)}, u32[]{:S(2)}) copy-start(bf16[768,256]{1,0:T(8,128)(2,1)} %get-tuple-element.24.own_ref) | copy-start | bytes 1179652
  11.4 0.9 %copy-start.2 = (f32[11,16,256]{2,1,0:T(8,128)S(1)}, f32[11,16,256]{2,1,0:T(8,128)}, u32[]{:S(2)}) copy-start(f32[11,16,256]{2,1,0:T(8,128)} %get-tuple-element.22.source_ref) | copy-start | bytes 540676
  19.0 1.8 %collective-permute-start.5 = (bf16[256,768]{1,0:T(8,128)(2,1)S(1)}, bf16[256,768]{1,0:T(8,128)(2,1)S(1)}, u32[]{:S(2)}, u32[]{:S(2)}) collective-permute-start(bf16[256,768]{1,0:T(8,128)(2,1)S(1)} %relay.1.refs_2_), channel_id=1, source_target_pairs={{0,1},{1,0},{2,3},{3,2},{4,5},{5,4},{6,7},{7,6},{8,9},{9,8},{10,11... | collective-permute-start | bytes 1179656 | tf_op jit(solution)/shard_map/ppermute | solution.py:287
  19.8 1.0 %copy-start = (bf16[256,768]{1,0:T(8,128)(2,1)S(1)}, bf16[256,768]{1,0:T(8,128)(2,1)}, u32[]{:S(2)}) copy-start(bf16[256,768]{1,0:T(8,128)(2,1)} %get-tuple-element.30.refs_0_) | copy-start | bytes 1179652
  21.6 6.4 %collective-permute-start.9 = (bf16[256,256]{1,0:T(8,128)(2,1)S(1)}, bf16[256,256]{1,0:T(8,128)(2,1)S(1)}, u32[]{:S(2)}, u32[]{:S(2)}) collective-permute-start(bf16[256,256]{1,0:T(8,128)(2,1)S(1)} %get-tuple-element.35), channel_id=1, source_target_pairs={{0,4},{1,5},{4,0},{5,1},{8,12},{9,13},{12,8},{13,9},{2,6},{3,7},{6... | collective-permute-start | bytes 393224 | tf_op jit(solution)/shard_map/ppermute | solution.py:295
  23.5 7.2 %collective-permute-start.11 = (bf16[256,256]{1,0:T(8,128)(2,1)S(1)}, bf16[256,256]{1,0:T(8,128)(2,1)S(1)}, u32[]{:S(2)}, u32[]{:S(2)}) collective-permute-start(bf16[256,256]{1,0:T(8,128)(2,1)S(1)} %get-tuple-element.37), channel_id=1, source_target_pairs={{0,4},{1,5},{4,0},{5,1},{8,12},{9,13},{12,8},{13,9},{2,6},{3,7},{6... | collective-permute-start | bytes 393224 | tf_op jit(solution)/shard_map/ppermute | solution.py:295
  25.3 5.8 %collective-permute-start.6 = (bf16[256,256]{1,0:T(8,128)(2,1)S(1)}, bf16[256,256]{1,0:T(8,128)(2,1)S(1)}, u32[]{:S(2)}, u32[]{:S(2)}) collective-permute-start(bf16[256,256]{1,0:T(8,128)(2,1)S(1)} %get-tuple-element.32), channel_id=1, source_target_pairs={{0,1},{1,0},{4,5},{5,4},{8,9},{9,8},{12,13},{13,12},{2,3},{3,2},{6... | collective-permute-start | bytes 393224 | tf_op jit(solution)/shard_map/ppermute | solution.py:295
  25.3 13.6 %collective-permute-start.7 = (bf16[256,256]{1,0:T(8,128)(2,1)S(1)}, bf16[256,256]{1,0:T(8,128)(2,1)S(1)}, u32[]{:S(2)}, u32[]{:S(2)}) collective-permute-start(bf16[256,256]{1,0:T(8,128)(2,1)S(1)} %get-tuple-element.33), channel_id=1, source_target_pairs={{0,4},{1,5},{4,0},{5,1},{8,12},{9,13},{12,8},{13,9},{2,6},{3,7},{6... | collective-permute-start | bytes 393224 | tf_op jit(solution)/shard_map/ppermute | solution.py:295
  26.5 14.4 %collective-permute-start.8 = (bf16[256,256]{1,0:T(8,128)(2,1)S(1)}, bf16[256,256]{1,0:T(8,128)(2,1)S(1)}, u32[]{:S(2)}, u32[]{:S(2)}) collective-permute-start(bf16[256,256]{1,0:T(8,128)(2,1)S(1)} %get-tuple-element.34), channel_id=1, source_target_pairs={{0,5},{1,4},{4,1},{5,0},{8,13},{9,12},{12,9},{13,8},{2,7},{3,6},{6... | collective-permute-start | bytes 393224 | tf_op jit(solution)/shard_map/ppermute | solution.py:295
  27.9 13.0 %collective-permute-start.10 = (bf16[256,256]{1,0:T(8,128)(2,1)S(1)}, bf16[256,256]{1,0:T(8,128)(2,1)S(1)}, u32[]{:S(2)}, u32[]{:S(2)}) collective-permute-start(bf16[256,256]{1,0:T(8,128)(2,1)S(1)} %add.2), channel_id=1, source_target_pairs={{0,8},{1,9},{4,12},{5,13},{8,0},{9,1},{12,4},{13,5},{2,10},{3,11},... | collective-permute-start | bytes 393224 | tf_op jit(solution)/shard_map/ppermute | solution.py:295
  30.8 11.9 %collective-permute-start.12 = (bf16[256,256]{1,0:T(8,128)(2,1)S(1)}, bf16[256,256]{1,0:T(8,128)(2,1)S(1)}, u32[]{:S(2)}, u32[]{:S(2)}) collective-permute-start(bf16[256,256]{1,0:T(8,128)(2,1)S(1)} %add.3), channel_id=1, source_target_pairs={{0,9},{1,8},{4,13},{5,12},{8,1},{9,0},{12,5},{13,4},{2,11},{3,10},... | collective-permute-start | bytes 393224 | tf_op jit(solution)/shard_map/ppermute | solution.py:295

commit v7 on v6

--- a/solution.py
+++ b/solution.py
@@ -30,8 +30,8 @@
 
 def prep_kernel(
     v_hbm, low_hbm, high_hbm, force_hbm, bond_hbm, near_hbm,
-    turned_hbm, send_low_hbm, send_high_hbm, own_hbm, source_hbm, bond_out_hbm,
-    v_ref, low_ref, high_ref, near_ref, turned_ref, send_low_ref, send_high_ref, own_ref,
+    turned_hbm, send_low_hbm, send_high_hbm, source_hbm, bond_out_hbm,
+    v_ref, low_ref, high_ref, near_ref, turned_ref, send_low_ref, send_high_ref,
     source_ref, in_sems, out_sems,
 ):
     rows, half = v_ref.shape
@@ -61,38 +61,40 @@
     lane = lax.broadcasted_iota(jnp.int32, (atoms, rows), 1)
     atom = lax.broadcasted_iota(jnp.int32, (atoms, rows), 0)
     hot = [one_hot(lane == 3 * atom + b) for b in range(3)]
-    for copy in arriving:
+    for copy in arriving[1:]:
         copy.wait()
     source_ref[10] = near_ref[...].astype(F32)
     leave(source_ref.at[9:10], bond_out_hbm)
     leave(source_ref, source_hbm)
-    v = v_ref[...]
-    for b in range(3):
-        picked = dot(hot[b], v)
-        turned_ref[:, b * atoms : (b + 1) * atoms] = picked.T.astype(BF16)
-        own_ref[b * atoms : (b + 1) * atoms, :] = picked.astype(BF16)
-    leave(turned_ref, turned_hbm)
-    leave(own_ref, own_hbm)
-    for list_ref, send_ref, send_hbm in (
-        (high_ref, send_high_ref, send_high_hbm),
-        (low_ref, send_low_ref, send_low_hbm),
-    ):
+    picks = []
+    for list_ref in (high_ref, low_ref):
         count = list_ref.shape[1]
         named = jnp.broadcast_to(list_ref[...], (128, count)).T
         lane = lax.broadcasted_iota(jnp.int32, (count, 128), 1)
         for b in range(3):
             wanted = 3 * named + b
-            picks = jnp.concatenate(
-                [one_hot(lane + t * 128 == wanted) for t in range(rows // 128)], axis=1
+            picks.append(
+                jnp.concatenate(
+                    [one_hot(lane + t * 128 == wanted) for t in range(rows // 128)], axis=1
+                )
             )
-            send_ref[b * count : (b + 1) * count, :] = dot(picks, v).astype(BF16)
+    arriving[0].wait()
+    v = v_ref[...]
+    for b in range(3):
+        turned_ref[:, b * atoms : (b + 1) * atoms] = dot(hot[b], v).T.astype(BF16)
+    leave(turned_ref, turned_hbm)
+    for i, (send_ref, send_hbm) in enumerate(
+        ((send_high_ref, send_high_hbm), (send_low_ref, send_low_hbm))
+    ):
+        for b in range(3):
+            send_ref[b * count : (b + 1) * count, :] = dot(picks[3 * i + b], v).astype(BF16)
         leave(send_ref, send_hbm)
     for copy in leaving:
         copy.wait()
 
 
 def weights_kernel(
-    source_ref, other_ref, own_ref,
+    source_ref, other_ref, turned_ref,
     flux_ref, hi_ref, lo_ref, table_ref, own_hi_ref, own_lo_ref,
 ):
     _, steps, atoms = source_ref.shape
@@ -165,10 +167,11 @@
         return carry
 
     lax.fori_loop(0, groups // 4, several, 0)
-    own = own_ref[...]
+    turned = turned_ref[...]
     for part in range(6):
         at = slice(part * atoms, (part + 1) * atoms)
-        flux_ref[at, :] = dot(own_hi_ref[at, :], own) + dot(own_lo_ref[at, :], own)
+        hi, lo = own_hi_ref[at, :], own_lo_ref[at, :]
+        flux_ref[at, :] = dot(hi, turned, ((1,), (1,))) + dot(lo, turned, ((1,), (1,)))
 
 
 def relay_kernel(part_hbm, below_hbm, above_hbm, *refs):
@@ -227,7 +230,7 @@
         out_ref[0, :, c * half : (c + 1) * half] = total * scale
 
 
-def far_kernel(flux_ref, *refs):
+def far_kernel(after, flux_ref, *refs):
     *quarter_refs, far_ref, add_ref = refs
     home = lax.axis_index("dom")
 
@@ -265,8 +268,11 @@
     terms_of(quarter_refs, store, lambda tile: (tile ^ (home // 2)) == 0)
 
 
-def add_kernel(far_ref, add_ref, sum_ref):
+def add_kernel(far_ref, add_ref, *refs):
+    held_refs, (sum_ref, *given_refs) = refs[: len(refs) // 2], refs[len(refs) // 2 :]
     sum_ref[...] = (add_ref[...] + far_ref[...].astype(F32)).astype(BF16)
+    for held_ref, given_ref in zip(held_refs, given_refs):
+        given_ref[...] = held_ref[...]
 
 
 def halving_sum_kernel(scale, keep_ref, give_ref, near0_ref, near1_ref, sum0_ref, sum1_ref, out_ref):
@@ -316,9 +322,8 @@
         shape((half, rows), BF16),
         shape((3 * count, half), BF16),
         shape((3 * count, half), BF16),
-        shape((rows, half), BF16),
     )
-    turned, send_low, send_high, own, sources, bonds = pl.pallas_call(
+    turned, send_low, send_high, sources, bonds = pl.pallas_call(
         prep_kernel,
         out_shape=(
             *prepared,
@@ -326,7 +331,7 @@
             shape(bond_vectors.shape, F32),
         ),
         in_specs=[hbm] * 6,
-        out_specs=(hbm,) * 6,
+        out_specs=(hbm,) * 5,
         scratch_shapes=[
             pltpu.VMEM((rows, half), BF16),
             pltpu.VMEM((1, count), jnp.int32),
@@ -335,7 +340,7 @@
             *[pltpu.VMEM(like.shape, like.dtype) for like in prepared],
             pltpu.VMEM((11, *neighbours.shape), F32),
             pltpu.SemaphoreType.DMA((6,)),
-            pltpu.SemaphoreType.DMA((6,)),
+            pltpu.SemaphoreType.DMA((5,)),
         ],
         compiler_params=params(58),
         name="prep",
@@ -365,7 +370,7 @@
             flops=8*10**9, bytes_accessed=10**7, transcendentals=0
         ),
         name="weights",
-    )(sources, other_bonds, own)
+    )(sources, other_bonds, turned)
 
     quarters = pl.pallas_call(
         relay_kernel,
@@ -399,21 +404,21 @@
         sent, kept = shape((block, half), BF16), shape((block, half), F32)
         cost = pl.CostEstimate(flops=4 * 10**8, bytes_accessed=10**6, transcendentals=0)
 
-        def far_of(flux):
+        def far_of(flux, after):
             far, add = pl.pallas_call(
                 far_kernel,
                 out_shape=(sent, kept),
-                in_specs=[vmem] * (1 + len(given)),
+                in_specs=[anywhere] + [vmem] * (1 + len(given)),
                 out_specs=(vmem,) * 2,
                 compiler_params=params(16),
                 cost_estimate=cost,
                 name="far",
-            )(flux, *given)
+            )(after, flux, *given)
             return far, add
 
         flux0, flux1 = flux_of(0), flux_of(1)
-        far0, add0 = far_of(flux0)
-        far1, add1 = far_of(flux1)
+        far0, add0 = far_of(flux0, flux1)
+        far1, add1 = far_of(flux1, far0)
         far0, far1 = swap(far0, 1, 0), swap(far1, 1, 0)
         near0, near1, keep, give = pl.pallas_call(
             near_kernel,
@@ -424,19 +429,21 @@
             cost_estimate=cost,
             name="near",
         )(flux0, flux1, *given)
-        give, near0, near1 = swap(give, 0, 1), swap(near0, 1, 0), swap(near1, 1, 1)
-
-        def sum_of(far, add):
+
+        def sum_of(far, add, *handed_on):
             return pl.pallas_call(
                 add_kernel,
-                out_shape=sent,
-                in_specs=[vmem] * 2,
-                out_specs=vmem,
+                out_shape=[sent] * (1 + len(handed_on)),
+                in_specs=[vmem] * (2 + len(handed_on)),
+                out_specs=[vmem] * (1 + len(handed_on)),
                 compiler_params=params(16),
                 name="add",
-            )(far, add)
-
-        sum0, sum1 = swap(sum_of(far0, add0), 2, 0), swap(sum_of(far1, add1), 2, 1)
+            )(far, add, *handed_on)
+
+        near0 = swap(near0, 1, 0)
+        sum0 = swap(sum_of(far0, add0)[0], 2, 0)
+        sum1, near1, give = sum_of(far1, add1, near1, give)
+        sum1, near1, give = swap(sum1, 2, 1), swap(near1, 1, 1), swap(give, 0, 1)
         return pl.pallas_call(
             lambda *refs: halving_sum_kernel(scale, *refs),
             out_shape=result,

time: 43.7 us -> 43.7 us (level)
  starting transfers between devices: 13.1 us -> 14.5 us
  waiting for transfers between devices: 15.3 us -> 14 us
    ppermute x7, waiting for transfers between devices: 13.7 us -> 11.8 us  [swap(): return lax.ppermute(value, ('dom', 'dir'), pairs)]
    ppermute x7, starting transfers between devices: 5.74 us -> 7.35 us  [swap(): return lax.ppermute(value, ('dom', 'dir'), pairs)]
    ppermute x6, waiting for transfers between devices: 1.61 us -> 2.14 us  [shift(): lax.ppermute(value, axis, [(i, (i + by) % length) for i in range(length)])]
    unnamed x6 -> x4, local copies, waits for them, and re-layouts: 1.99 us -> 1.92 us
where the time goes in v7:
time: 43.7 us; the launch traced here: 43.5 us
  starting transfers between devices  14.5 us (33%)
  waiting for transfers between devices  14 us (32%)
  Pallas kernels  13 us (30%)
  local copies, waits for them, and re-layouts  1.92 us (4%)
    ppermute x7, waiting for transfers between devices, swap(): return lax.ppermute(value, ('dom', 'dir'), pairs)  11.8 us
    ppermute x7, starting transfers between devices, swap(): return lax.ppermute(value, ('dom', 'dir'), pairs)  7.35 us
    ppermute x6, starting transfers between devices, shift(): lax.ppermute(value, axis, [(i, (i + by) % length) for i in range(length)])  7.14 us
    pallas_call x1, Pallas kernels, per_device(): pl.pallas_call(weights_kernel, out_shape=(shape((2 * rows, half), F32), s...  5.12 us
    pallas_call x1, Pallas kernels, per_device(): pl.pallas_call(prep_kernel, out_shape=(*prepared, shape((11, *neighbours....  3.11 us
    ppermute x6, waiting for transfers between devices, shift(): lax.ppermute(value, axis, [(i, (i + by) % length) for i in range(length)])  2.14 us
    unnamed x4, local copies, waits for them, and re-layouts  1.92 us
    pallas_call x2, Pallas kernels, flux_of(): pl.pallas_call(functools.partial(flux_kernel, e), out_shape=shape((rows,...  1.55 us
  transfers between devices with their start and end apart: 13, of which 7 were waited for; matrix products, arithmetic and copies ran while one was open for 0% of the time, Pallas kernels for 19%

profile of v7, /device:TPU:0, one launch (start us, length us, event | category | flops | bytes accessed | tf_op | source)
XLA Modules:
  0.0 43.5 jit_solution(6284874556935160734)
XLA Ops:
  0.0 3.1 %prep.1 = (bf16[256,768]{1,0:T(8,128)(2,1)}, bf16[384,256]{1,0:T(8,128)(2,1)}, bf16[384,256]{1,0:T(8,128)(2,1)}, f32[11,16,256]{2,1,0:T(8,128)}, f32[1,16,256]{2,1,0:T(8,128)}) custom-call(bf16[768,512]{1,0:T(8,128)(2,1)} %v_hbm.1, s32[1,128]{1,0:T(1,128)} %bitcast.4, s32[1,128]{1,0:T(1,128)} %bitcast.5, f32[9,16,256]{2,1,0:T(8,128)} %bitcast.3, ...), custom_call_target="tpu_custom_call" | custom-call | tf_op jit(solution)/shard_map/prep/pallas_call | solution.py:326
  3.1 0.5 %collective-permute-start = (f32[1,16,256]{2,1,0:T(8,128)}, f32[1,16,256]{2,1,0:T(8,128)S(1)}, u32[]{:S(2)}, u32[]{:S(2)}) collective-permute-start(f32[1,16,256]{2,1,0:T(8,128)} %get-tuple-element.25), channel_id=1, source_target_pairs={{0,1},{1,0},{2,3},{3,2},{4,5},{5,4},{6,7},{7,6},{8,9},{9,8},{10,11... | collective-permute-start | bytes 49160 | tf_op jit(solution)/shard_map/ppermute | solution.py:293
  3.6 2.6 %collective-permute-start.4 = (bf16[256,768]{1,0:T(8,128)(2,1)}, bf16[256,768]{1,0:T(8,128)(2,1)S(1)}, u32[]{:S(2)}, u32[]{:S(2)}) collective-permute-start(bf16[256,768]{1,0:T(8,128)(2,1)} %get-tuple-element.26.turned_ref.refs_0_), channel_id=1, source_target_pairs={{0,2},{2,0},{1,3},{3,1},{4,6},{6,4},{5,7},{7,5},{8,10},{10,8},{9,1... | collective-permute-start | bytes 1179656 | tf_op jit(solution)/shard_map/ppermute | solution.py:293
  6.2 0.2 collective-permute-start.3
  6.4 1.6 %collective-permute-start.1 = (bf16[384,256]{1,0:T(8,128)(2,1)}, bf16[384,256]{1,0:T(8,128)(2,1)S(1)}, u32[]{:S(2)}, u32[]{:S(2)}) collective-permute-start(bf16[384,256]{1,0:T(8,128)(2,1)} %get-tuple-element.30), channel_id=1, source_target_pairs={{0,4},{4,8},{8,12},{12,0},{1,5},{5,9},{9,13},{13,1},{2,6},{6,10},{... | collective-permute-start | bytes 589832 | tf_op jit(solution)/shard_map/ppermute | solution.py:293
  7.9 2.2 %collective-permute-start.2 = (bf16[384,256]{1,0:T(8,128)(2,1)}, bf16[384,256]{1,0:T(8,128)(2,1)S(1)}, u32[]{:S(2)}, u32[]{:S(2)}) collective-permute-start(bf16[384,256]{1,0:T(8,128)(2,1)} %get-tuple-element.31), channel_id=1, source_target_pairs={{0,12},{4,0},{8,4},{12,8},{1,13},{5,1},{9,5},{13,9},{2,14},{6,2},{... | collective-permute-start | bytes 589832 | tf_op jit(solution)/shard_map/ppermute | solution.py:293
  10.2 0.0 collective-permute-done.other_ref
  10.2 0.0 copy-start
  10.2 1.0 %copy-done = bf16[256,768]{1,0:T(8,128)(2,1)S(1)} copy-done((bf16[256,768]{1,0:T(8,128)(2,1)S(1)}, bf16[256,768]{1,0:T(8,128)(2,1)}, u32[]{:S(2)}) %copy-start) | copy-done | bytes 393240
  11.2 0.0 copy-start.1
  11.2 0.9 %copy-done.1 = f32[11,16,256]{2,1,0:T(8,128)S(1)} copy-done((f32[11,16,256]{2,1,0:T(8,128)S(1)}, f32[11,16,256]{2,1,0:T(8,128)}, u32[]{:S(2)}) %copy-start.1) | copy-done | bytes 180248
  12.1 5.1 %weights.1 = (f32[1536,256]{1,0:T(8,128)S(1)}, bf16[1536,768]{1,0:T(8,128)(2,1)S(1)}, bf16[1536,768]{1,0:T(8,128)(2,1)S(1)}) custom-call(f32[11,16,256]{2,1,0:T(8,128)S(1)} %copy-done.1, f32[1,16,256]{2,1,0:T(8,128)S(1)} %collective-permute-done.other_ref, bf16[256,768]{1,0:T(8,128)(2,1)S(1)} %copy-done), custom_call_target="tpu_custom_call" | custom-call | flops 8000000000 | bytes 10000000 | tf_op jit(solution)/shard_map/weights/pallas_call | solution.py:354
  17.2 0.0 collective-permute-done.1.below_ref.below_hbm
  17.3 2.0 %collective-permute-done.2.above_ref.above_hbm = bf16[384,256]{1,0:T(8,128)(2,1)S(1)} collective-permute-done((bf16[384,256]{1,0:T(8,128)(2,1)}, bf16[384,256]{1,0:T(8,128)(2,1)S(1)}, u32[]{:S(2)}, u32[]{:S(2)}) %collective-permute-start.2) | collective-permute-done | bytes 196640 | tf_op jit(solution)/shard_map/ppermute | solution.py:293
  19.2 0.0 collective-permute-done.4.refs_0_
  19.3 0.1 collective-permute-start.5
  19.4 0.8 %flux.3.flux1_ref.after.flux_ref = bf16[768,256]{1,0:T(8,128)(2,1)S(1)} custom-call(f32[1536,256]{1,0:T(8,128)S(1)} %get-tuple-element.27.part_ref.part_hbm, bf16[1536,768]{1,0:T(8,128)(2,1)S(1)} %get-tuple-element.28.hi_ref, bf16[1536,768]{1,0:T(8,128)(2,1)S(1)} %get-tuple-element.29.lo_ref, ...), custom_call_target="tpu_custom_call" | custom-call | flops 1000000000 | bytes 1000000 | tf_op jit(solution)/shard_map/flux/pallas_call | solution.py:388
  20.1 0.8 %flux.2.flux0_ref.flux_ref = bf16[768,256]{1,0:T(8,128)(2,1)S(1)} custom-call(f32[1536,256]{1,0:T(8,128)S(1)} %get-tuple-element.27.part_ref.part_hbm, bf16[1536,768]{1,0:T(8,128)(2,1)S(1)} %get-tuple-element.28.hi_ref, bf16[1536,768]{1,0:T(8,128)(2,1)S(1)} %get-tuple-element.29.lo_ref, bf16[384,256]{1,0:T(8,128)(2,1)S(1)} %collective-permute-done.1.below_ref.below_hbm, ...), custom_call_target="tpu_custom_call" | custom-call | flops 1000000000 | bytes 1000000 | tf_op jit(solution)/shard_map/flux/pallas_call | solution.py:388
  20.9 0.0 collective-permute-done.3.refs_1_
  20.9 0.1 collective-permute-done.5.refs_3_
  21.1 0.7 %far.2 = (bf16[256,256]{1,0:T(8,128)(2,1)S(1)}, f32[256,256]{1,0:T(8,128)S(1)}) custom-call(bf16[768,256]{1,0:T(8,128)(2,1)S(1)} %flux.3.flux1_ref.after.flux_ref, bf16[768,256]{1,0:T(8,128)(2,1)S(1)} %flux.2.flux0_ref.flux_ref, bf16[256,768]{1,0:T(8,128)(2,1)S(1)} %copy-done, bf16[256,768]{1,0:T(8,128)(2,1)S(1)} %collective-permute-done.3.refs_1_, ...), custom_call_target="tpu_custom_call" | custom-call | flops 400000000 | bytes 1000000 | tf_op jit(solution)/shard_map/far/pallas_call | solution.py:408
  21.8 1.2 %collective-permute-start.10 = (bf16[256,256]{1,0:T(8,128)(2,1)S(1)}, bf16[256,256]{1,0:T(8,128)(2,1)S(1)}, u32[]{:S(2)}, u32[]{:S(2)}) collective-permute-start(bf16[256,256]{1,0:T(8,128)(2,1)S(1)} %get-tuple-element.33.after), channel_id=1, source_target_pairs={{0,4},{1,5},{4,0},{5,1},{8,12},{9,13},{12,8},{13,9},{2,6},{3,7},{6... | collective-permute-start | bytes 393224 | tf_op jit(solution)/shard_map/ppermute | solution.py:301
  23.0 0.7 %far.3 = (bf16[256,256]{1,0:T(8,128)(2,1)S(1)}, f32[256,256]{1,0:T(8,128)S(1)}) custom-call(bf16[256,256]{1,0:T(8,128)(2,1)S(1)} %get-tuple-element.33.after, bf16[768,256]{1,0:T(8,128)(2,1)S(1)} %flux.3.flux1_ref.after.flux_ref, bf16[256,768]{1,0:T(8,128)(2,1)S(1)} %copy-done, bf16[256,768]{1,0:T(8,128)(2,1)S(1)} %collective-permute-done.3.refs_1_, ...), custom_call_target="tpu_custom_call" | custom-call | flops 400000000 | bytes 1000000 | tf_op jit(solution)/shard_map/far/pallas_call | solution.py:408
  23.7 1.0 %collective-permute-start.6 = (bf16[256,256]{1,0:T(8,128)(2,1)S(1)}, bf16[256,256]{1,0:T(8,128)(2,1)S(1)}, u32[]{:S(2)}, u32[]{:S(2)}) collective-permute-start(bf16[256,256]{1,0:T(8,128)(2,1)S(1)} %get-tuple-element.34), channel_id=1, source_target_pairs={{0,4},{1,5},{4,0},{5,1},{8,12},{9,13},{12,8},{13,9},{2,6},{3,7},{6... | collective-permute-start | bytes 393224 | tf_op jit(solution)/shard_map/ppermute | solution.py:301
  24.7 0.8 %near.1 = (bf16[256,256]{1,0:T(8,128)(2,1)S(1)}, bf16[256,256]{1,0:T(8,128)(2,1)S(1)}, f32[256,256]{1,0:T(8,128)S(1)}, bf16[256,256]{1,0:T(8,128)(2,1)S(1)}) custom-call(bf16[768,256]{1,0:T(8,128)(2,1)S(1)} %flux.2.flux0_ref.flux_ref, bf16[768,256]{1,0:T(8,128)(2,1)S(1)} %flux.3.flux1_ref.after.flux_ref, bf16[256,768]{1,0:T(8,128)(2,1)S(1)} %copy-done, ...), custom_call_target="tpu_custom_call" | custom-call | flops 400000000 | bytes 1000000 | tf_op jit(solution)/shard_map/near/pallas_call | solution.py:423
  25.5 1.2 %collective-permute-start.8 = (bf16[256,256]{1,0:T(8,128)(2,1)S(1)}, bf16[256,256]{1,0:T(8,128)(2,1)S(1)}, u32[]{:S(2)}, u32[]{:S(2)}) collective-permute-start(bf16[256,256]{1,0:T(8,128)(2,1)S(1)} %get-tuple-element.39), channel_id=1, source_target_pairs={{0,4},{1,5},{4,0},{5,1},{8,12},{9,13},{12,8},{13,9},{2,6},{3,7},{6... | collective-permute-start | bytes 393224 | tf_op jit(solution)/shard_map/ppermute | solution.py:301
  26.7 1.5 %collective-permute-done.10.far_ref = bf16[256,256]{1,0:T(8,128)(2,1)S(1)} collective-permute-done((bf16[256,256]{1,0:T(8,128)(2,1)S(1)}, bf16[256,256]{1,0:T(8,128)(2,1)S(1)}, u32[]{:S(2)}, u32[]{:S(2)}) %collective-permute-start.10) | collective-permute-done | bytes 131104 | tf_op jit(solution)/shard_map/ppermute | solution.py:301
  28.2 1.4 %collective-permute-start.11 = (bf16[256,256]{1,0:T(8,128)(2,1)S(1)}, bf16[256,256]{1,0:T(8,128)(2,1)S(1)}, u32[]{:S(2)}, u32[]{:S(2)}) collective-permute-start(bf16[256,256]{1,0:T(8,128)(2,1)S(1)} %add.3), channel_id=1, source_target_pairs={{0,8},{1,9},{4,12},{5,13},{8,0},{9,1},{12,4},{13,5},{2,10},{3,11},... | collective-permute-start | bytes 393224 | tf_op jit(solution)/shard_map/ppermute | solution.py:301
  29.6 2.8 %collective-permute-done.6.far_ref = bf16[256,256]{1,0:T(8,128)(2,1)S(1)} collective-permute-done((bf16[256,256]{1,0:T(8,128)(2,1)S(1)}, bf16[256,256]{1,0:T(8,128)(2,1)S(1)}, u32[]{:S(2)}, u32[]{:S(2)}) %collective-permute-start.6) | collective-permute-done | bytes 131104 | tf_op jit(solution)/shard_map/ppermute | solution.py:301
  32.5 0.1 collective-permute-start.12
  32.5 0.1 collective-permute-start.7
  32.6 2.5 %collective-permute-start.9 = (bf16[256,256]{1,0:T(8,128)(2,1)S(1)}, bf16[256,256]{1,0:T(8,128)(2,1)S(1)}, u32[]{:S(2)}, u32[]{:S(2)}) collective-permute-start(bf16[256,256]{1,0:T(8,128)(2,1)S(1)} %get-tuple-element.40), channel_id=1, source_target_pairs={{0,5},{1,4},{4,1},{5,0},{8,13},{9,12},{12,9},{13,8},{2,7},{3,6},{6... | collective-permute-start | bytes 393224 | tf_op jit(solution)/shard_map/ppermute | solution.py:301
  35.1 0.9 %collective-permute-done.8.refs_2_ = bf16[256,256]{1,0:T(8,128)(2,1)S(1)} collective-permute-done((bf16[256,256]{1,0:T(8,128)(2,1)S(1)}, bf16[256,256]{1,0:T(8,128)(2,1)S(1)}, u32[]{:S(2)}, u32[]{:S(2)}) %collective-permute-start.8) | collective-permute-done | bytes 131104 | tf_op jit(solution)/shard_map/ppermute | solution.py:301
  36.0 3.3 %collective-permute-done.11.refs_4_ = bf16[256,256]{1,0:T(8,128)(2,1)S(1)} collective-permute-done((bf16[256,256]{1,0:T(8,128)(2,1)S(1)}, bf16[256,256]{1,0:T(8,128)(2,1)S(1)}, u32[]{:S(2)}, u32[]{:S(2)}) %collective-permute-start.11) | collective-permute-done | bytes 131104 | tf_op jit(solution)/shard_map/ppermute | solution.py:301
  39.3 3.2 %collective-permute-done.12.refs_5_ = bf16[256,256]{1,0:T(8,128)(2,1)S(1)} collective-permute-done((bf16[256,256]{1,0:T(8,128)(2,1)S(1)}, bf16[256,256]{1,0:T(8,128)(2,1)S(1)}, u32[]{:S(2)}, u32[]{:S(2)}) %collective-permute-start.12) | collective-permute-done | bytes 131104 | tf_op jit(solution)/shard_map/ppermute | solution.py:301
  42.6 0.0 collective-permute-done.7.refs_1_
  42.6 0.0 collective-permute-done.9.refs_3_
  42.6 0.9 %total.1 = f32[1,256,512]{2,1,0:T(8,128)} custom-call(f32[256,256]{1,0:T(8,128)S(1)} %get-tuple-element.32.refs_0_, bf16[256,256]{1,0:T(8,128)(2,1)S(1)} %collective-permute-done.7.refs_1_, bf16[256,256]{1,0:T(8,128)(2,1)S(1)} %collective-permute-done.8.refs_2_, bf16[256,256]{1,0:T(8,128)(2,1)S(1)} %collective-permute-done.9.refs_3_, ...), custom_call_target="tpu_custom_call" | custom-call | tf_op jit(solution)/shard_map/total/pallas_call | solution.py:447
  (3 shorter events, 0.1 us)
Async XLA Ops:
  3.1 7.1 %collective-permute-start = (f32[1,16,256]{2,1,0:T(8,128)}, f32[1,16,256]{2,1,0:T(8,128)S(1)}, u32[]{:S(2)}, u32[]{:S(2)}) collective-permute-start(f32[1,16,256]{2,1,0:T(8,128)} %get-tuple-element.25), channel_id=1, source_target_pairs={{0,1},{1,0},{2,3},{3,2},{4,5},{5,4},{6,7},{7,6},{8,9},{9,8},{10,11... | collective-permute-start | bytes 49160 | tf_op jit(solution)/shard_map/ppermute | solution.py:293
  3.6 15.6 %collective-permute-start.4 = (bf16[256,768]{1,0:T(8,128)(2,1)}, bf16[256,768]{1,0:T(8,128)(2,1)S(1)}, u32[]{:S(2)}, u32[]{:S(2)}) collective-permute-start(bf16[256,768]{1,0:T(8,128)(2,1)} %get-tuple-element.26.turned_ref.refs_0_), channel_id=1, source_target_pairs={{0,2},{2,0},{1,3},{3,1},{4,6},{6,4},{5,7},{7,5},{8,10},{10,8},{9,1... | collective-permute-start | bytes 1179656 | tf_op jit(solution)/shard_map/ppermute | solution.py:293
  6.2 14.7 %collective-permute-start.3 = (bf16[256,768]{1,0:T(8,128)(2,1)}, bf16[256,768]{1,0:T(8,128)(2,1)S(1)}, u32[]{:S(2)}, u32[]{:S(2)}) collective-permute-start(bf16[256,768]{1,0:T(8,128)(2,1)} %get-tuple-element.26.turned_ref.refs_0_), channel_id=1, source_target_pairs={{0,1},{1,0},{2,3},{3,2},{4,5},{5,4},{6,7},{7,6},{8,9},{9,8},{10,11... | collective-permute-start | bytes 1179656 | tf_op jit(solution)/shard_map/ppermute | solution.py:293
  6.4 10.9 %collective-permute-start.1 = (bf16[384,256]{1,0:T(8,128)(2,1)}, bf16[384,256]{1,0:T(8,128)(2,1)S(1)}, u32[]{:S(2)}, u32[]{:S(2)}) collective-permute-start(bf16[384,256]{1,0:T(8,128)(2,1)} %get-tuple-element.30), channel_id=1, source_target_pairs={{0,4},{4,8},{8,12},{12,0},{1,5},{5,9},{9,13},{13,1},{2,6},{6,10},{... | collective-permute-start | bytes 589832 | tf_op jit(solution)/shard_map/ppermute | solution.py:293
  7.9 11.3 %collective-permute-start.2 = (bf16[384,256]{1,0:T(8,128)(2,1)}, bf16[384,256]{1,0:T(8,128)(2,1)S(1)}, u32[]{:S(2)}, u32[]{:S(2)}) collective-permute-start(bf16[384,256]{1,0:T(8,128)(2,1)} %get-tuple-element.31), channel_id=1, source_target_pairs={{0,12},{4,0},{8,4},{12,8},{1,13},{5,1},{9,5},{13,9},{2,14},{6,2},{... | collective-permute-start | bytes 589832 | tf_op jit(solution)/shard_map/ppermute | solution.py:293
  10.2 1.0 %copy-start = (bf16[256,768]{1,0:T(8,128)(2,1)S(1)}, bf16[256,768]{1,0:T(8,128)(2,1)}, u32[]{:S(2)}) copy-start(bf16[256,768]{1,0:T(8,128)(2,1)} %get-tuple-element.26.turned_ref.refs_0_) | copy-start | bytes 1179652
  11.2 0.9 %copy-start.1 = (f32[11,16,256]{2,1,0:T(8,128)S(1)}, f32[11,16,256]{2,1,0:T(8,128)}, u32[]{:S(2)}) copy-start(f32[11,16,256]{2,1,0:T(8,128)} %get-tuple-element.24.source_ref) | copy-start | bytes 540676
  19.3 1.8 %collective-permute-start.5 = (bf16[256,768]{1,0:T(8,128)(2,1)S(1)}, bf16[256,768]{1,0:T(8,128)(2,1)S(1)}, u32[]{:S(2)}, u32[]{:S(2)}) collective-permute-start(bf16[256,768]{1,0:T(8,128)(2,1)S(1)} %relay.1.refs_2_), channel_id=1, source_target_pairs={{0,1},{1,0},{2,3},{3,2},{4,5},{5,4},{6,7},{7,6},{8,9},{9,8},{10,11... | collective-permute-start | bytes 1179656 | tf_op jit(solution)/shard_map/ppermute | solution.py:293
  21.8 6.4 %collective-permute-start.10 = (bf16[256,256]{1,0:T(8,128)(2,1)S(1)}, bf16[256,256]{1,0:T(8,128)(2,1)S(1)}, u32[]{:S(2)}, u32[]{:S(2)}) collective-permute-start(bf16[256,256]{1,0:T(8,128)(2,1)S(1)} %get-tuple-element.33.after), channel_id=1, source_target_pairs={{0,4},{1,5},{4,0},{5,1},{8,12},{9,13},{12,8},{13,9},{2,6},{3,7},{6... | collective-permute-start | bytes 393224 | tf_op jit(solution)/shard_map/ppermute | solution.py:301
  23.7 8.7 %collective-permute-start.6 = (bf16[256,256]{1,0:T(8,128)(2,1)S(1)}, bf16[256,256]{1,0:T(8,128)(2,1)S(1)}, u32[]{:S(2)}, u32[]{:S(2)}) collective-permute-start(bf16[256,256]{1,0:T(8,128)(2,1)S(1)} %get-tuple-element.34), channel_id=1, source_target_pairs={{0,4},{1,5},{4,0},{5,1},{8,12},{9,13},{12,8},{13,9},{2,6},{3,7},{6... | collective-permute-start | bytes 393224 | tf_op jit(solution)/shard_map/ppermute | solution.py:301
  25.5 10.5 %collective-permute-start.8 = (bf16[256,256]{1,0:T(8,128)(2,1)S(1)}, bf16[256,256]{1,0:T(8,128)(2,1)S(1)}, u32[]{:S(2)}, u32[]{:S(2)}) collective-permute-start(bf16[256,256]{1,0:T(8,128)(2,1)S(1)} %get-tuple-element.39), channel_id=1, source_target_pairs={{0,4},{1,5},{4,0},{5,1},{8,12},{9,13},{12,8},{13,9},{2,6},{3,7},{6... | collective-permute-start | bytes 393224 | tf_op jit(solution)/shard_map/ppermute | solution.py:301
  28.2 11.1 %collective-permute-start.11 = (bf16[256,256]{1,0:T(8,128)(2,1)S(1)}, bf16[256,256]{1,0:T(8,128)(2,1)S(1)}, u32[]{:S(2)}, u32[]{:S(2)}) collective-permute-start(bf16[256,256]{1,0:T(8,128)(2,1)S(1)} %add.3), channel_id=1, source_target_pairs={{0,8},{1,9},{4,12},{5,13},{8,0},{9,1},{12,4},{13,5},{2,10},{3,11},... | collective-permute-start | bytes 393224 | tf_op jit(solution)/shard_map/ppermute | solution.py:301
  32.5 10.1 %collective-permute-start.12 = (bf16[256,256]{1,0:T(8,128)(2,1)S(1)}, bf16[256,256]{1,0:T(8,128)(2,1)S(1)}, u32[]{:S(2)}, u32[]{:S(2)}) collective-permute-start(bf16[256,256]{1,0:T(8,128)(2,1)S(1)} %get-tuple-element.42), channel_id=1, source_target_pairs={{0,9},{1,8},{4,13},{5,12},{8,1},{9,0},{12,5},{13,4},{2,11},{3,10},... | collective-permute-start | bytes 393224 | tf_op jit(solution)/shard_map/ppermute | solution.py:301
  32.5 10.1 %collective-permute-start.7 = (bf16[256,256]{1,0:T(8,128)(2,1)S(1)}, bf16[256,256]{1,0:T(8,128)(2,1)S(1)}, u32[]{:S(2)}, u32[]{:S(2)}) collective-permute-start(bf16[256,256]{1,0:T(8,128)(2,1)S(1)} %get-tuple-element.38), channel_id=1, source_target_pairs={{0,1},{1,0},{4,5},{5,4},{8,9},{9,8},{12,13},{13,12},{2,3},{3,2},{6... | collective-permute-start | bytes 393224 | tf_op jit(solution)/shard_map/ppermute | solution.py:301
  32.6 10.0 %collective-permute-start.9 = (bf16[256,256]{1,0:T(8,128)(2,1)S(1)}, bf16[256,256]{1,0:T(8,128)(2,1)S(1)}, u32[]{:S(2)}, u32[]{:S(2)}) collective-permute-start(bf16[256,256]{1,0:T(8,128)(2,1)S(1)} %get-tuple-element.40), channel_id=1, source_target_pairs={{0,5},{1,4},{4,1},{5,0},{8,13},{9,12},{12,9},{13,8},{2,7},{3,6},{6... | collective-permute-start | bytes 393224 | tf_op jit(solution)/shard_map/ppermute | solution.py:301

commit v8 on v7

--- a/solution.py
+++ b/solution.py
@@ -32,7 +32,7 @@
     v_hbm, low_hbm, high_hbm, force_hbm, bond_hbm, near_hbm,
     turned_hbm, send_low_hbm, send_high_hbm, source_hbm, bond_out_hbm,
     v_ref, low_ref, high_ref, near_ref, turned_ref, send_low_ref, send_high_ref,
-    source_ref, in_sems, out_sems,
+    source_ref, pick_ref, wide_ref, in_sems, out_sems,
 ):
     rows, half = v_ref.shape
     atoms = rows // 3
@@ -58,37 +58,35 @@
         copy.start()
         leaving.append(copy)
 
-    lane = lax.broadcasted_iota(jnp.int32, (atoms, rows), 1)
-    atom = lax.broadcasted_iota(jnp.int32, (atoms, rows), 0)
-    hot = [one_hot(lane == 3 * atom + b) for b in range(3)]
     for copy in arriving[1:]:
         copy.wait()
     source_ref[10] = near_ref[...].astype(F32)
     leave(source_ref.at[9:10], bond_out_hbm)
     leave(source_ref, source_hbm)
-    picks = []
-    for list_ref in (high_ref, low_ref):
+    for i, list_ref in enumerate((high_ref, low_ref)):
         count = list_ref.shape[1]
         named = jnp.broadcast_to(list_ref[...], (128, count)).T
         lane = lax.broadcasted_iota(jnp.int32, (count, 128), 1)
         for b in range(3):
             wanted = 3 * named + b
-            picks.append(
-                jnp.concatenate(
-                    [one_hot(lane + t * 128 == wanted) for t in range(rows // 128)], axis=1
+            at = (3 * i + b) * count
+            for t in range(rows // 128):
+                pick_ref[at : at + count, t * 128 : (t + 1) * 128] = one_hot(
+                    lane + t * 128 == wanted
                 )
-            )
     arriving[0].wait()
-    v = v_ref[...]
-    for b in range(3):
-        turned_ref[:, b * atoms : (b + 1) * atoms] = dot(hot[b], v).T.astype(BF16)
+    for t in range(half // 128):
+        columns = slice(t * 128, (t + 1) * 128)
+        wide_ref[t] = v_ref[:, columns].astype(F32)
+        for b in range(3):
+            part = wide_ref[t, pl.ds(b, atoms, stride=3), :]
+            turned_ref[columns, b * atoms : (b + 1) * atoms] = part.T.astype(BF16)
     leave(turned_ref, turned_hbm)
-    for i, (send_ref, send_hbm) in enumerate(
-        ((send_high_ref, send_high_hbm), (send_low_ref, send_low_hbm))
-    ):
-        for b in range(3):
-            send_ref[b * count : (b + 1) * count, :] = dot(picks[3 * i + b], v).astype(BF16)
-        leave(send_ref, send_hbm)
+    picked = dot(pick_ref[...], v_ref[...]).astype(BF16)
+    send_high_ref[...] = picked[: 3 * count]
+    leave(send_high_ref, send_high_hbm)
+    send_low_ref[...] = picked[3 * count :]
+    leave(send_low_ref, send_low_hbm)
     for copy in leaving:
         copy.wait()
 
@@ -168,8 +166,8 @@
 
     lax.fori_loop(0, groups // 4, several, 0)
     turned = turned_ref[...]
-    for part in range(6):
-        at = slice(part * atoms, (part + 1) * atoms)
+    for e in range(2):
+        at = slice(3 * e * atoms, 3 * (e + 1) * atoms)
         hi, lo = own_hi_ref[at, :], own_lo_ref[at, :]
         flux_ref[at, :] = dot(hi, turned, ((1,), (1,))) + dot(lo, turned, ((1,), (1,)))
 
@@ -187,10 +185,9 @@
         halo_ref[at + count : at + 2 * count] = above_ref[b * count : (b + 1) * count]
     atoms = flux_ref.shape[0] // 3
     halo = halo_ref[...]
-    for a in range(3):
-        at = slice((e * 3 + a) * atoms, (e * 3 + a + 1) * atoms)
-        flux = part_ref[at, :] + (dot(hi_ref[at, :], halo) + dot(lo_ref[at, :], halo))
-        flux_ref[a * atoms : (a + 1) * atoms, :] = flux.astype(BF16)
+    at = slice(3 * e * atoms, 3 * (e + 1) * atoms)
+    flux = part_ref[at, :] + (dot(hi_ref[at, :], halo) + dot(lo_ref[at, :], halo))
+    flux_ref[...] = flux.astype(BF16)
 
 
 def terms_of(quarter_refs, store, wanted=lambda tile: True):
@@ -339,6 +336,8 @@
             pltpu.VMEM(neighbours.shape, jnp.int32),
             *[pltpu.VMEM(like.shape, like.dtype) for like in prepared],
             pltpu.VMEM((11, *neighbours.shape), F32),
+            pltpu.VMEM((6 * count, rows), BF16),
+            pltpu.VMEM((half // 128, rows, 128), F32),
             pltpu.SemaphoreType.DMA((6,)),
             pltpu.SemaphoreType.DMA((5,)),
         ],

time: 43.7 us -> 43.4 us (level)
  no operation moved by 1% of the time
where the time goes in v8:
time: 43.4 us; the launch traced here: 43.2 us
  starting transfers between devices  14.5 us (33%)
  waiting for transfers between devices  13.9 us (32%)
  Pallas kernels  12.7 us (29%)
  local copies, waits for them, and re-layouts  1.92 us (4%)
    ppermute x7, waiting for transfers between devices, swap(): return lax.ppermute(value, ('dom', 'dir'), pairs)  11.8 us
    ppermute x7, starting transfers between devices, swap(): return lax.ppermute(value, ('dom', 'dir'), pairs)  7.39 us
    ppermute x6, starting transfers between devices, shift(): lax.ppermute(value, axis, [(i, (i + by) % length) for i in range(length)])  7.14 us
    pallas_call x1, Pallas kernels, per_device(): pl.pallas_call(weights_kernel, out_shape=(shape((2 * rows, half), F32), s...  5.13 us
    pallas_call x1, Pallas kernels, per_device(): pl.pallas_call(prep_kernel, out_shape=(*prepared, shape((11, *neighbours....  2.82 us
    ppermute x6, waiting for transfers between devices, shift(): lax.ppermute(value, axis, [(i, (i + by) % length) for i in range(length)])  2.14 us
    unnamed x4, local copies, waits for them, and re-layouts  1.92 us
    pallas_call x2, Pallas kernels, flux_of(): pl.pallas_call(functools.partial(flux_kernel, e), out_shape=shape((rows,...  1.54 us
  transfers between devices with their start and end apart: 13, of which 7 were waited for; matrix products, arithmetic and copies ran while one was open for 0% of the time, Pallas kernels for 19%

profile of v8, /device:TPU:0, one launch (start us, length us, event | category | flops | bytes accessed | tf_op | source)
XLA Modules:
  0.0 43.2 jit_solution(16673381129187338738)
XLA Ops:
  0.0 2.8 %prep.1 = (bf16[256,768]{1,0:T(8,128)(2,1)}, bf16[384,256]{1,0:T(8,128)(2,1)}, bf16[384,256]{1,0:T(8,128)(2,1)}, f32[11,16,256]{2,1,0:T(8,128)}, f32[1,16,256]{2,1,0:T(8,128)}) custom-call(bf16[768,512]{1,0:T(8,128)(2,1)} %v_hbm.1, s32[1,128]{1,0:T(1,128)} %bitcast.4, s32[1,128]{1,0:T(1,128)} %bitcast.5, f32[9,16,256]{2,1,0:T(8,128)} %bitcast.3, ...), custom_call_target="tpu_custom_call" | custom-call | tf_op jit(solution)/shard_map/prep/pallas_call | solution.py:323
  2.8 0.5 %collective-permute-start = (f32[1,16,256]{2,1,0:T(8,128)}, f32[1,16,256]{2,1,0:T(8,128)S(1)}, u32[]{:S(2)}, u32[]{:S(2)}) collective-permute-start(f32[1,16,256]{2,1,0:T(8,128)} %get-tuple-element.25), channel_id=1, source_target_pairs={{0,1},{1,0},{2,3},{3,2},{4,5},{5,4},{6,7},{7,6},{8,9},{9,8},{10,11... | collective-permute-start | bytes 49160 | tf_op jit(solution)/shard_map/ppermute | solution.py:290
  3.3 2.6 %collective-permute-start.4 = (bf16[256,768]{1,0:T(8,128)(2,1)}, bf16[256,768]{1,0:T(8,128)(2,1)S(1)}, u32[]{:S(2)}, u32[]{:S(2)}) collective-permute-start(bf16[256,768]{1,0:T(8,128)(2,1)} %get-tuple-element.26.turned_ref.refs_0_), channel_id=1, source_target_pairs={{0,2},{2,0},{1,3},{3,1},{4,6},{6,4},{5,7},{7,5},{8,10},{10,8},{9,1... | collective-permute-start | bytes 1179656 | tf_op jit(solution)/shard_map/ppermute | solution.py:290
  5.9 0.2 collective-permute-start.3
  6.1 1.6 %collective-permute-start.1 = (bf16[384,256]{1,0:T(8,128)(2,1)}, bf16[384,256]{1,0:T(8,128)(2,1)S(1)}, u32[]{:S(2)}, u32[]{:S(2)}) collective-permute-start(bf16[384,256]{1,0:T(8,128)(2,1)} %get-tuple-element.30), channel_id=1, source_target_pairs={{0,4},{4,8},{8,12},{12,0},{1,5},{5,9},{9,13},{13,1},{2,6},{6,10},{... | collective-permute-start | bytes 589832 | tf_op jit(solution)/shard_map/ppermute | solution.py:290
  7.7 2.2 %collective-permute-start.2 = (bf16[384,256]{1,0:T(8,128)(2,1)}, bf16[384,256]{1,0:T(8,128)(2,1)S(1)}, u32[]{:S(2)}, u32[]{:S(2)}) collective-permute-start(bf16[384,256]{1,0:T(8,128)(2,1)} %get-tuple-element.31), channel_id=1, source_target_pairs={{0,12},{4,0},{8,4},{12,8},{1,13},{5,1},{9,5},{13,9},{2,14},{6,2},{... | collective-permute-start | bytes 589832 | tf_op jit(solution)/shard_map/ppermute | solution.py:290
  9.9 0.0 collective-permute-done.other_ref
  9.9 0.0 copy-start
  9.9 1.0 %copy-done = bf16[256,768]{1,0:T(8,128)(2,1)S(1)} copy-done((bf16[256,768]{1,0:T(8,128)(2,1)S(1)}, bf16[256,768]{1,0:T(8,128)(2,1)}, u32[]{:S(2)}) %copy-start) | copy-done | bytes 393240
  10.9 0.0 copy-start.1
  10.9 0.9 %copy-done.1 = f32[11,16,256]{2,1,0:T(8,128)S(1)} copy-done((f32[11,16,256]{2,1,0:T(8,128)S(1)}, f32[11,16,256]{2,1,0:T(8,128)}, u32[]{:S(2)}) %copy-start.1) | copy-done | bytes 180248
  11.8 5.1 %weights.1 = (f32[1536,256]{1,0:T(8,128)S(1)}, bf16[1536,768]{1,0:T(8,128)(2,1)S(1)}, bf16[1536,768]{1,0:T(8,128)(2,1)S(1)}) custom-call(f32[11,16,256]{2,1,0:T(8,128)S(1)} %copy-done.1, f32[1,16,256]{2,1,0:T(8,128)S(1)} %collective-permute-done.other_ref, bf16[256,768]{1,0:T(8,128)(2,1)S(1)} %copy-done), custom_call_target="tpu_custom_call" | custom-call | flops 8000000000 | bytes 10000000 | tf_op jit(solution)/shard_map/weights/pallas_call | solution.py:353
  17.0 0.0 collective-permute-done.1.below_ref.below_hbm
  17.0 2.0 %collective-permute-done.2.above_ref.above_hbm = bf16[384,256]{1,0:T(8,128)(2,1)S(1)} collective-permute-done((bf16[384,256]{1,0:T(8,128)(2,1)}, bf16[384,256]{1,0:T(8,128)(2,1)S(1)}, u32[]{:S(2)}, u32[]{:S(2)}) %collective-permute-start.2) | collective-permute-done | bytes 196640 | tf_op jit(solution)/shard_map/ppermute | solution.py:290
  19.0 0.0 collective-permute-done.4.refs_0_
  19.0 0.1 collective-permute-start.5
  19.1 0.8 %flux.3.flux1_ref.after.flux_ref = bf16[768,256]{1,0:T(8,128)(2,1)S(1)} custom-call(f32[1536,256]{1,0:T(8,128)S(1)} %get-tuple-element.27.part_ref.part_hbm, bf16[1536,768]{1,0:T(8,128)(2,1)S(1)} %get-tuple-element.28.hi_ref, bf16[1536,768]{1,0:T(8,128)(2,1)S(1)} %get-tuple-element.29.lo_ref, ...), custom_call_target="tpu_custom_call" | custom-call | flops 1000000000 | bytes 1000000 | tf_op jit(solution)/shard_map/flux/pallas_call | solution.py:387
  19.8 0.8 %flux.2.flux0_ref.flux_ref = bf16[768,256]{1,0:T(8,128)(2,1)S(1)} custom-call(f32[1536,256]{1,0:T(8,128)S(1)} %get-tuple-element.27.part_ref.part_hbm, bf16[1536,768]{1,0:T(8,128)(2,1)S(1)} %get-tuple-element.28.hi_ref, bf16[1536,768]{1,0:T(8,128)(2,1)S(1)} %get-tuple-element.29.lo_ref, bf16[384,256]{1,0:T(8,128)(2,1)S(1)} %collective-permute-done.1.below_ref.below_hbm, ...), custom_call_target="tpu_custom_call" | custom-call | flops 1000000000 | bytes 1000000 | tf_op jit(solution)/shard_map/flux/pallas_call | solution.py:387
  20.6 0.0 collective-permute-done.3.refs_1_
  20.6 0.1 collective-permute-done.5.refs_3_
  20.8 0.7 %far.2 = (bf16[256,256]{1,0:T(8,128)(2,1)S(1)}, f32[256,256]{1,0:T(8,128)S(1)}) custom-call(bf16[768,256]{1,0:T(8,128)(2,1)S(1)} %flux.3.flux1_ref.after.flux_ref, bf16[768,256]{1,0:T(8,128)(2,1)S(1)} %flux.2.flux0_ref.flux_ref, bf16[256,768]{1,0:T(8,128)(2,1)S(1)} %copy-done, bf16[256,768]{1,0:T(8,128)(2,1)S(1)} %collective-permute-done.3.refs_1_, ...), custom_call_target="tpu_custom_call" | custom-call | flops 400000000 | bytes 1000000 | tf_op jit(solution)/shard_map/far/pallas_call | solution.py:407
  21.5 1.2 %collective-permute-start.10 = (bf16[256,256]{1,0:T(8,128)(2,1)S(1)}, bf16[256,256]{1,0:T(8,128)(2,1)S(1)}, u32[]{:S(2)}, u32[]{:S(2)}) collective-permute-start(bf16[256,256]{1,0:T(8,128)(2,1)S(1)} %get-tuple-element.33.after), channel_id=1, source_target_pairs={{0,4},{1,5},{4,0},{5,1},{8,12},{9,13},{12,8},{13,9},{2,6},{3,7},{6... | collective-permute-start | bytes 393224 | tf_op jit(solution)/shard_map/ppermute | solution.py:298
  22.7 0.7 %far.3 = (bf16[256,256]{1,0:T(8,128)(2,1)S(1)}, f32[256,256]{1,0:T(8,128)S(1)}) custom-call(bf16[256,256]{1,0:T(8,128)(2,1)S(1)} %get-tuple-element.33.after, bf16[768,256]{1,0:T(8,128)(2,1)S(1)} %flux.3.flux1_ref.after.flux_ref, bf16[256,768]{1,0:T(8,128)(2,1)S(1)} %copy-done, bf16[256,768]{1,0:T(8,128)(2,1)S(1)} %collective-permute-done.3.refs_1_, ...), custom_call_target="tpu_custom_call" | custom-call | flops 400000000 | bytes 1000000 | tf_op jit(solution)/shard_map/far/pallas_call | solution.py:407
  23.5 1.0 %collective-permute-start.6 = (bf16[256,256]{1,0:T(8,128)(2,1)S(1)}, bf16[256,256]{1,0:T(8,128)(2,1)S(1)}, u32[]{:S(2)}, u32[]{:S(2)}) collective-permute-start(bf16[256,256]{1,0:T(8,128)(2,1)S(1)} %get-tuple-element.34), channel_id=1, source_target_pairs={{0,4},{1,5},{4,0},{5,1},{8,12},{9,13},{12,8},{13,9},{2,6},{3,7},{6... | collective-permute-start | bytes 393224 | tf_op jit(solution)/shard_map/ppermute | solution.py:298
  24.4 0.8 %near.1 = (bf16[256,256]{1,0:T(8,128)(2,1)S(1)}, bf16[256,256]{1,0:T(8,128)(2,1)S(1)}, f32[256,256]{1,0:T(8,128)S(1)}, bf16[256,256]{1,0:T(8,128)(2,1)S(1)}) custom-call(bf16[768,256]{1,0:T(8,128)(2,1)S(1)} %flux.2.flux0_ref.flux_ref, bf16[768,256]{1,0:T(8,128)(2,1)S(1)} %flux.3.flux1_ref.after.flux_ref, bf16[256,768]{1,0:T(8,128)(2,1)S(1)} %copy-done, ...), custom_call_target="tpu_custom_call" | custom-call | flops 400000000 | bytes 1000000 | tf_op jit(solution)/shard_map/near/pallas_call | solution.py:422
  25.2 1.2 %collective-permute-start.8 = (bf16[256,256]{1,0:T(8,128)(2,1)S(1)}, bf16[256,256]{1,0:T(8,128)(2,1)S(1)}, u32[]{:S(2)}, u32[]{:S(2)}) collective-permute-start(bf16[256,256]{1,0:T(8,128)(2,1)S(1)} %get-tuple-element.39), channel_id=1, source_target_pairs={{0,4},{1,5},{4,0},{5,1},{8,12},{9,13},{12,8},{13,9},{2,6},{3,7},{6... | collective-permute-start | bytes 393224 | tf_op jit(solution)/shard_map/ppermute | solution.py:298
  26.4 1.5 %collective-permute-done.10.far_ref = bf16[256,256]{1,0:T(8,128)(2,1)S(1)} collective-permute-done((bf16[256,256]{1,0:T(8,128)(2,1)S(1)}, bf16[256,256]{1,0:T(8,128)(2,1)S(1)}, u32[]{:S(2)}, u32[]{:S(2)}) %collective-permute-start.10) | collective-permute-done | bytes 131104 | tf_op jit(solution)/shard_map/ppermute | solution.py:298
  27.9 1.4 %collective-permute-start.11 = (bf16[256,256]{1,0:T(8,128)(2,1)S(1)}, bf16[256,256]{1,0:T(8,128)(2,1)S(1)}, u32[]{:S(2)}, u32[]{:S(2)}) collective-permute-start(bf16[256,256]{1,0:T(8,128)(2,1)S(1)} %add.3), channel_id=1, source_target_pairs={{0,8},{1,9},{4,12},{5,13},{8,0},{9,1},{12,4},{13,5},{2,10},{3,11},... | collective-permute-start | bytes 393224 | tf_op jit(solution)/shard_map/ppermute | solution.py:298
  29.3 2.8 %collective-permute-done.6.far_ref = bf16[256,256]{1,0:T(8,128)(2,1)S(1)} collective-permute-done((bf16[256,256]{1,0:T(8,128)(2,1)S(1)}, bf16[256,256]{1,0:T(8,128)(2,1)S(1)}, u32[]{:S(2)}, u32[]{:S(2)}) %collective-permute-start.6) | collective-permute-done | bytes 131104 | tf_op jit(solution)/shard_map/ppermute | solution.py:298
  32.2 0.1 collective-permute-start.12
  32.2 0.1 collective-permute-start.7
  32.3 2.5 %collective-permute-start.9 = (bf16[256,256]{1,0:T(8,128)(2,1)S(1)}, bf16[256,256]{1,0:T(8,128)(2,1)S(1)}, u32[]{:S(2)}, u32[]{:S(2)}) collective-permute-start(bf16[256,256]{1,0:T(8,128)(2,1)S(1)} %get-tuple-element.40), channel_id=1, source_target_pairs={{0,5},{1,4},{4,1},{5,0},{8,13},{9,12},{12,9},{13,8},{2,7},{3,6},{6... | collective-permute-start | bytes 393224 | tf_op jit(solution)/shard_map/ppermute | solution.py:298
  34.8 0.9 %collective-permute-done.8.refs_2_ = bf16[256,256]{1,0:T(8,128)(2,1)S(1)} collective-permute-done((bf16[256,256]{1,0:T(8,128)(2,1)S(1)}, bf16[256,256]{1,0:T(8,128)(2,1)S(1)}, u32[]{:S(2)}, u32[]{:S(2)}) %collective-permute-start.8) | collective-permute-done | bytes 131104 | tf_op jit(solution)/shard_map/ppermute | solution.py:298
  35.7 3.3 %collective-permute-done.11.refs_4_ = bf16[256,256]{1,0:T(8,128)(2,1)S(1)} collective-permute-done((bf16[256,256]{1,0:T(8,128)(2,1)S(1)}, bf16[256,256]{1,0:T(8,128)(2,1)S(1)}, u32[]{:S(2)}, u32[]{:S(2)}) %collective-permute-start.11) | collective-permute-done | bytes 131104 | tf_op jit(solution)/shard_map/ppermute | solution.py:298
  39.0 3.3 %collective-permute-done.12.refs_5_ = bf16[256,256]{1,0:T(8,128)(2,1)S(1)} collective-permute-done((bf16[256,256]{1,0:T(8,128)(2,1)S(1)}, bf16[256,256]{1,0:T(8,128)(2,1)S(1)}, u32[]{:S(2)}, u32[]{:S(2)}) %collective-permute-start.12) | collective-permute-done | bytes 131104 | tf_op jit(solution)/shard_map/ppermute | solution.py:298
  42.3 0.0 collective-permute-done.7.refs_1_
  42.3 0.0 collective-permute-done.9.refs_3_
  42.3 0.9 %total.1 = f32[1,256,512]{2,1,0:T(8,128)} custom-call(f32[256,256]{1,0:T(8,128)S(1)} %get-tuple-element.32.refs_0_, bf16[256,256]{1,0:T(8,128)(2,1)S(1)} %collective-permute-done.7.refs_1_, bf16[256,256]{1,0:T(8,128)(2,1)S(1)} %collective-permute-done.8.refs_2_, bf16[256,256]{1,0:T(8,128)(2,1)S(1)} %collective-permute-done.9.refs_3_, ...), custom_call_target="tpu_custom_call" | custom-call | tf_op jit(solution)/shard_map/total/pallas_call | solution.py:446
  (3 shorter events, 0.1 us)
Async XLA Ops:
  2.8 7.1 %collective-permute-start = (f32[1,16,256]{2,1,0:T(8,128)}, f32[1,16,256]{2,1,0:T(8,128)S(1)}, u32[]{:S(2)}, u32[]{:S(2)}) collective-permute-start(f32[1,16,256]{2,1,0:T(8,128)} %get-tuple-element.25), channel_id=1, source_target_pairs={{0,1},{1,0},{2,3},{3,2},{4,5},{5,4},{6,7},{7,6},{8,9},{9,8},{10,11... | collective-permute-start | bytes 49160 | tf_op jit(solution)/shard_map/ppermute | solution.py:290
  3.3 15.6 %collective-permute-start.4 = (bf16[256,768]{1,0:T(8,128)(2,1)}, bf16[256,768]{1,0:T(8,128)(2,1)S(1)}, u32[]{:S(2)}, u32[]{:S(2)}) collective-permute-start(bf16[256,768]{1,0:T(8,128)(2,1)} %get-tuple-element.26.turned_ref.refs_0_), channel_id=1, source_target_pairs={{0,2},{2,0},{1,3},{3,1},{4,6},{6,4},{5,7},{7,5},{8,10},{10,8},{9,1... | collective-permute-start | bytes 1179656 | tf_op jit(solution)/shard_map/ppermute | solution.py:290
  5.9 14.7 %collective-permute-start.3 = (bf16[256,768]{1,0:T(8,128)(2,1)}, bf16[256,768]{1,0:T(8,128)(2,1)S(1)}, u32[]{:S(2)}, u32[]{:S(2)}) collective-permute-start(bf16[256,768]{1,0:T(8,128)(2,1)} %get-tuple-element.26.turned_ref.refs_0_), channel_id=1, source_target_pairs={{0,1},{1,0},{2,3},{3,2},{4,5},{5,4},{6,7},{7,6},{8,9},{9,8},{10,11... | collective-permute-start | bytes 1179656 | tf_op jit(solution)/shard_map/ppermute | solution.py:290
  6.1 10.9 %collective-permute-start.1 = (bf16[384,256]{1,0:T(8,128)(2,1)}, bf16[384,256]{1,0:T(8,128)(2,1)S(1)}, u32[]{:S(2)}, u32[]{:S(2)}) collective-permute-start(bf16[384,256]{1,0:T(8,128)(2,1)} %get-tuple-element.30), channel_id=1, source_target_pairs={{0,4},{4,8},{8,12},{12,0},{1,5},{5,9},{9,13},{13,1},{2,6},{6,10},{... | collective-permute-start | bytes 589832 | tf_op jit(solution)/shard_map/ppermute | solution.py:290
  7.7 11.3 %collective-permute-start.2 = (bf16[384,256]{1,0:T(8,128)(2,1)}, bf16[384,256]{1,0:T(8,128)(2,1)S(1)}, u32[]{:S(2)}, u32[]{:S(2)}) collective-permute-start(bf16[384,256]{1,0:T(8,128)(2,1)} %get-tuple-element.31), channel_id=1, source_target_pairs={{0,12},{4,0},{8,4},{12,8},{1,13},{5,1},{9,5},{13,9},{2,14},{6,2},{... | collective-permute-start | bytes 589832 | tf_op jit(solution)/shard_map/ppermute | solution.py:290
  9.9 1.0 %copy-start = (bf16[256,768]{1,0:T(8,128)(2,1)S(1)}, bf16[256,768]{1,0:T(8,128)(2,1)}, u32[]{:S(2)}) copy-start(bf16[256,768]{1,0:T(8,128)(2,1)} %get-tuple-element.26.turned_ref.refs_0_) | copy-start | bytes 1179652
  10.9 0.9 %copy-start.1 = (f32[11,16,256]{2,1,0:T(8,128)S(1)}, f32[11,16,256]{2,1,0:T(8,128)}, u32[]{:S(2)}) copy-start(f32[11,16,256]{2,1,0:T(8,128)} %get-tuple-element.24.source_ref) | copy-start | bytes 540676
  19.0 1.8 %collective-permute-start.5 = (bf16[256,768]{1,0:T(8,128)(2,1)S(1)}, bf16[256,768]{1,0:T(8,128)(2,1)S(1)}, u32[]{:S(2)}, u32[]{:S(2)}) collective-permute-start(bf16[256,768]{1,0:T(8,128)(2,1)S(1)} %relay.1.refs_2_), channel_id=1, source_target_pairs={{0,1},{1,0},{2,3},{3,2},{4,5},{5,4},{6,7},{7,6},{8,9},{9,8},{10,11... | collective-permute-start | bytes 1179656 | tf_op jit(solution)/shard_map/ppermute | solution.py:290
  21.5 6.4 %collective-permute-start.10 = (bf16[256,256]{1,0:T(8,128)(2,1)S(1)}, bf16[256,256]{1,0:T(8,128)(2,1)S(1)}, u32[]{:S(2)}, u32[]{:S(2)}) collective-permute-start(bf16[256,256]{1,0:T(8,128)(2,1)S(1)} %get-tuple-element.33.after), channel_id=1, source_target_pairs={{0,4},{1,5},{4,0},{5,1},{8,12},{9,13},{12,8},{13,9},{2,6},{3,7},{6... | collective-permute-start | bytes 393224 | tf_op jit(solution)/shard_map/ppermute | solution.py:298
  23.5 8.7 %collective-permute-start.6 = (bf16[256,256]{1,0:T(8,128)(2,1)S(1)}, bf16[256,256]{1,0:T(8,128)(2,1)S(1)}, u32[]{:S(2)}, u32[]{:S(2)}) collective-permute-start(bf16[256,256]{1,0:T(8,128)(2,1)S(1)} %get-tuple-element.34), channel_id=1, source_target_pairs={{0,4},{1,5},{4,0},{5,1},{8,12},{9,13},{12,8},{13,9},{2,6},{3,7},{6... | collective-permute-start | bytes 393224 | tf_op jit(solution)/shard_map/ppermute | solution.py:298
  25.2 10.5 %collective-permute-start.8 = (bf16[256,256]{1,0:T(8,128)(2,1)S(1)}, bf16[256,256]{1,0:T(8,128)(2,1)S(1)}, u32[]{:S(2)}, u32[]{:S(2)}) collective-permute-start(bf16[256,256]{1,0:T(8,128)(2,1)S(1)} %get-tuple-element.39), channel_id=1, source_target_pairs={{0,4},{1,5},{4,0},{5,1},{8,12},{9,13},{12,8},{13,9},{2,6},{3,7},{6... | collective-permute-start | bytes 393224 | tf_op jit(solution)/shard_map/ppermute | solution.py:298
  27.9 11.1 %collective-permute-start.11 = (bf16[256,256]{1,0:T(8,128)(2,1)S(1)}, bf16[256,256]{1,0:T(8,128)(2,1)S(1)}, u32[]{:S(2)}, u32[]{:S(2)}) collective-permute-start(bf16[256,256]{1,0:T(8,128)(2,1)S(1)} %add.3), channel_id=1, source_target_pairs={{0,8},{1,9},{4,12},{5,13},{8,0},{9,1},{12,4},{13,5},{2,10},{3,11},... | collective-permute-start | bytes 393224 | tf_op jit(solution)/shard_map/ppermute | solution.py:298
  32.2 10.1 %collective-permute-start.12 = (bf16[256,256]{1,0:T(8,128)(2,1)S(1)}, bf16[256,256]{1,0:T(8,128)(2,1)S(1)}, u32[]{:S(2)}, u32[]{:S(2)}) collective-permute-start(bf16[256,256]{1,0:T(8,128)(2,1)S(1)} %get-tuple-element.42), channel_id=1, source_target_pairs={{0,9},{1,8},{4,13},{5,12},{8,1},{9,0},{12,5},{13,4},{2,11},{3,10},... | collective-permute-start | bytes 393224 | tf_op jit(solution)/shard_map/ppermute | solution.py:298
  32.2 10.1 %collective-permute-start.7 = (bf16[256,256]{1,0:T(8,128)(2,1)S(1)}, bf16[256,256]{1,0:T(8,128)(2,1)S(1)}, u32[]{:S(2)}, u32[]{:S(2)}) collective-permute-start(bf16[256,256]{1,0:T(8,128)(2,1)S(1)} %get-tuple-element.38), channel_id=1, source_target_pairs={{0,1},{1,0},{4,5},{5,4},{8,9},{9,8},{12,13},{13,12},{2,3},{3,2},{6... | collective-permute-start | bytes 393224 | tf_op jit(solution)/shard_map/ppermute | solution.py:298
  32.3 10.0 %collective-permute-start.9 = (bf16[256,256]{1,0:T(8,128)(2,1)S(1)}, bf16[256,256]{1,0:T(8,128)(2,1)S(1)}, u32[]{:S(2)}, u32[]{:S(2)}) collective-permute-start(bf16[256,256]{1,0:T(8,128)(2,1)S(1)} %get-tuple-element.40), channel_id=1, source_target_pairs={{0,5},{1,4},{4,1},{5,0},{8,13},{9,12},{12,9},{13,8},{2,7},{3,6},{6... | collective-permute-start | bytes 393224 | tf_op jit(solution)/shard_map/ppermute | solution.py:298

commit v9 on v8

--- a/solution.py
+++ b/solution.py
@@ -32,7 +32,7 @@
     v_hbm, low_hbm, high_hbm, force_hbm, bond_hbm, near_hbm,
     turned_hbm, send_low_hbm, send_high_hbm, source_hbm, bond_out_hbm,
     v_ref, low_ref, high_ref, near_ref, turned_ref, send_low_ref, send_high_ref,
-    source_ref, pick_ref, wide_ref, in_sems, out_sems,
+    source_ref, pick_ref, wide_ref, v_sems, in_sems, out_sems,
 ):
     rows, half = v_ref.shape
     atoms = rows // 3
@@ -40,7 +40,6 @@
         pltpu.make_async_copy(source, target, in_sems.at[i])
         for i, (source, target) in enumerate(
             (
-                (v_hbm.at[:, my_columns(half)], v_ref),
                 (low_hbm, low_ref),
                 (high_hbm, high_ref),
                 (near_hbm, near_ref),
@@ -49,7 +48,14 @@
             )
         )
     ]
-    for copy in arriving:
+    quarter = rows // 4
+    v_in = [
+        pltpu.make_async_copy(
+            v_hbm.at[pl.ds(at, quarter), my_columns(half)], v_ref.at[pl.ds(at, quarter)], v_sems.at[i]
+        )
+        for i, at in enumerate(range(0, rows, quarter))
+    ]
+    for copy in arriving + v_in:
         copy.start()
     leaving = []
 
@@ -58,7 +64,7 @@
         copy.start()
         leaving.append(copy)
 
-    for copy in arriving[1:]:
+    for copy in arriving:
         copy.wait()
     source_ref[10] = near_ref[...].astype(F32)
     leave(source_ref.at[9:10], bond_out_hbm)
@@ -74,7 +80,8 @@
                 pick_ref[at : at + count, t * 128 : (t + 1) * 128] = one_hot(
                     lane + t * 128 == wanted
                 )
-    arriving[0].wait()
+    for copy in v_in:
+        copy.wait()
     for t in range(half // 128):
         columns = slice(t * 128, (t + 1) * 128)
         wide_ref[t] = v_ref[:, columns].astype(F32)
@@ -190,16 +197,13 @@
     flux_ref[...] = flux.astype(BF16)
 
 
-def terms_of(quarter_refs, store, wanted=lambda tile: True):
+def terms_of(quarter_refs, store):
     tiles = len(quarter_refs) // 2
     me, core = lax.axis_index("blk"), lax.axis_index("dir")
     for j in range(tiles):
         tile = lax.rem(me - j + tiles, tiles)
-
-        @pl.when(wanted(tile))
-        def _():
-            for s in range(2):
-                store(2 * tile + (core if s == 0 else 1 - core), quarter_refs[2 * j + s])
+        for s in range(2):
+            store(2 * tile + (core if s == 0 else 1 - core), quarter_refs[2 * j + s])
 
 
 def couple_kernel(flux0_ref, flux1_ref, *refs):
@@ -228,41 +232,31 @@
 
 
 def far_kernel(after, flux_ref, *refs):
-    *quarter_refs, far_ref, add_ref = refs
+    *quarter_refs, far_ref = refs
     home = lax.axis_index("dom")
 
     def store(quarter, turned_ref):
-        term = dot(turned_ref[...], flux_ref[...])
-
         @pl.when((quarter ^ home) == 3)
         def _():
-            far_ref[...] = term.astype(BF16)
-
-        @pl.when((quarter ^ home) == 2)
-        def _():
-            add_ref[...] = term
-
-    terms_of(quarter_refs, store, lambda tile: (tile ^ (home // 2)) == 1)
+            far_ref[...] = dot(turned_ref[...], flux_ref[...]).astype(BF16)
+
+    terms_of(quarter_refs, store)
 
 
 def near_kernel(flux0_ref, flux1_ref, *refs):
-    *quarter_refs, near0_ref, near1_ref, keep_ref, give_ref = refs
+    *quarter_refs, near0_ref, near1_ref, add0_ref, add1_ref, keep_ref, give_ref = refs
     home = lax.axis_index("dom")
+    outs = {0: (keep_ref, give_ref), 1: (near0_ref, near1_ref), 2: (add0_ref, add1_ref)}
 
     def store(quarter, turned_ref):
-        terms = [dot(turned_ref[...], ref[...]) for ref in (flux0_ref, flux1_ref)]
-
-        @pl.when((quarter ^ home) == 1)
-        def _():
-            near0_ref[...] = terms[0].astype(BF16)
-            near1_ref[...] = terms[1].astype(BF16)
-
-        @pl.when((quarter ^ home) == 0)
-        def _():
-            keep_ref[...] = terms[0]
-            give_ref[...] = terms[1].astype(BF16)
-
-    terms_of(quarter_refs, store, lambda tile: (tile ^ (home // 2)) == 0)
+        for away, out_refs in outs.items():
+
+            @pl.when((quarter ^ home) == away)
+            def _():
+                for flux_ref, out_ref in zip((flux0_ref, flux1_ref), out_refs):
+                    out_ref[...] = dot(turned_ref[...], flux_ref[...]).astype(out_ref.dtype)
+
+    terms_of(quarter_refs, store)
 
 
 def add_kernel(far_ref, add_ref, *refs):
@@ -272,17 +266,24 @@
         given_ref[...] = held_ref[...]
 
 
-def halving_sum_kernel(scale, keep_ref, give_ref, near0_ref, near1_ref, sum0_ref, sum1_ref, out_ref):
+def halving_sum_kernel(
+    scale, keep_ref, give_ref, near0_ref, near1_ref, sum0_ref, sum1_ref, out_hbm, total_ref, sems
+):
     half = keep_ref.shape[1]
     core = lax.axis_index("dir")
-    mine = pl.ds(pl.multiple_of(core * half, 128), half)
-    other = pl.ds(pl.multiple_of((1 - core) * half, 128), half)
-    for at, first, near, far in (
-        (mine, keep_ref, near0_ref, sum0_ref),
-        (other, give_ref, near1_ref, sum1_ref),
+    copies = []
+    for i, (owner, first, near, far) in enumerate(
+        ((core, keep_ref, near0_ref, sum0_ref), (1 - core, give_ref, near1_ref, sum1_ref))
     ):
         total = first[...].astype(F32) + near[...].astype(F32) + far[...].astype(F32)
-        out_ref[0, :, at] = total * scale
+        total_ref[i] = total * scale
+        columns = pl.ds(pl.multiple_of(owner * half, 128), half)
+        copies.append(
+            pltpu.make_async_copy(total_ref.at[i], out_hbm.at[0, :, columns], sems.at[i])
+        )
+        copies[i].start()
+    for copy in copies:
+        copy.wait()
 
 
 def shift(value, axis, by):
@@ -338,7 +339,8 @@
             pltpu.VMEM((11, *neighbours.shape), F32),
             pltpu.VMEM((6 * count, rows), BF16),
             pltpu.VMEM((half // 128, rows, 128), F32),
-            pltpu.SemaphoreType.DMA((6,)),
+            pltpu.SemaphoreType.DMA((4,)),
+            pltpu.SemaphoreType.DMA((5,)),
             pltpu.SemaphoreType.DMA((5,)),
         ],
         compiler_params=params(58),
@@ -404,26 +406,25 @@
         cost = pl.CostEstimate(flops=4 * 10**8, bytes_accessed=10**6, transcendentals=0)
 
         def far_of(flux, after):
-            far, add = pl.pallas_call(
+            return pl.pallas_call(
                 far_kernel,
-                out_shape=(sent, kept),
+                out_shape=sent,
                 in_specs=[anywhere] + [vmem] * (1 + len(given)),
-                out_specs=(vmem,) * 2,
+                out_specs=vmem,
                 compiler_params=params(16),
                 cost_estimate=cost,
                 name="far",
             )(after, flux, *given)
-            return far, add
 
         flux0, flux1 = flux_of(0), flux_of(1)
-        far0, add0 = far_of(flux0, flux1)
-        far1, add1 = far_of(flux1, far0)
+        far0 = far_of(flux0, flux1)
+        far1 = far_of(flux1, far0)
         far0, far1 = swap(far0, 1, 0), swap(far1, 1, 0)
-        near0, near1, keep, give = pl.pallas_call(
+        near0, near1, add0, add1, keep, give = pl.pallas_call(
             near_kernel,
-            out_shape=(sent, sent, kept, sent),
+            out_shape=(sent, sent, kept, kept, kept, sent),
             in_specs=[vmem] * (2 + len(given)),
-            out_specs=(vmem,) * 4,
+            out_specs=(vmem,) * 6,
             compiler_params=params(16),
             cost_estimate=cost,
             name="near",
@@ -447,7 +448,11 @@
             lambda *refs: halving_sum_kernel(scale, *refs),
             out_shape=result,
             in_specs=[vmem] * 6,
-            out_specs=vmem,
+            out_specs=hbm,
+            scratch_shapes=[
+                pltpu.VMEM((2, block, half), F32),
+                pltpu.SemaphoreType.DMA((2,)),
+            ],
             compiler_params=params(16),
             name="total",
         )(keep, give, near0, near1, sum0, sum1)

time: 43.4 us -> 42.9 us (0.988)
  starting transfers between devices: 14.5 us -> 16 us
  waiting for transfers between devices: 13.9 us -> 12.5 us
  Pallas kernels: 12.7 us -> 12.2 us
    ppermute x7, starting transfers between devices: 7.39 us -> 8.87 us  [swap(): return lax.ppermute(value, ('dom', 'dir'), pairs)]
    ppermute x7, waiting for transfers between devices: 11.8 us -> 10.4 us  [swap(): return lax.ppermute(value, ('dom', 'dir'), pairs)]
    pallas_call x3, Pallas kernels: 2.24 us -> 1.68 us  [the longest x1 1.15 us: per_device(): pl.pallas_call(near_kernel, out_shape=(sent, sent, kept, kept, kept, sent...]
where the time goes in v9:
time: 42.9 us; the launch traced here: 42.7 us
  starting transfers between devices  16 us (37%)
  waiting for transfers between devices  12.5 us (29%)
  Pallas kernels  12.2 us (28%)
  local copies, waits for them, and re-layouts  1.92 us (4%)
    ppermute x7, waiting for transfers between devices, swap(): return lax.ppermute(value, ('dom', 'dir'), pairs)  10.4 us
    ppermute x7, starting transfers between devices, swap(): return lax.ppermute(value, ('dom', 'dir'), pairs)  8.87 us
    ppermute x6, starting transfers between devices, shift(): lax.ppermute(value, axis, [(i, (i + by) % length) for i in range(length)])  7.14 us
    pallas_call x1, Pallas kernels, per_device(): pl.pallas_call(weights_kernel, out_shape=(shape((2 * rows, half), F32), s...  5.13 us
    pallas_call x1, Pallas kernels, per_device(): pl.pallas_call(prep_kernel, out_shape=(*prepared, shape((11, *neighbours....  2.85 us
    ppermute x6, waiting for transfers between devices, shift(): lax.ppermute(value, axis, [(i, (i + by) % length) for i in range(length)])  2.12 us
    unnamed x4, local copies, waits for them, and re-layouts  1.92 us
    pallas_call x2, Pallas kernels, flux_of(): pl.pallas_call(functools.partial(flux_kernel, e), out_shape=shape((rows,...  1.55 us
  transfers between devices with their start and end apart: 13, of which 7 were waited for; matrix products, arithmetic and copies ran while one was open for 0% of the time, Pallas kernels for 19%

profile of v9, /device:TPU:0, one launch (start us, length us, event | category | flops | bytes accessed | tf_op | source)
XLA Modules:
  0.0 42.7 jit_solution(15448173860802503733)
XLA Ops:
  0.0 2.9 %prep.1 = (bf16[256,768]{1,0:T(8,128)(2,1)}, bf16[384,256]{1,0:T(8,128)(2,1)}, bf16[384,256]{1,0:T(8,128)(2,1)}, f32[11,16,256]{2,1,0:T(8,128)}, f32[1,16,256]{2,1,0:T(8,128)}) custom-call(bf16[768,512]{1,0:T(8,128)(2,1)} %v_hbm.1, s32[1,128]{1,0:T(1,128)} %bitcast.4, s32[1,128]{1,0:T(1,128)} %bitcast.5, f32[9,16,256]{2,1,0:T(8,128)} %bitcast.3, ...), custom_call_target="tpu_custom_call" | custom-call | tf_op jit(solution)/shard_map/prep/pallas_call | solution.py:324
  2.9 0.5 %collective-permute-start = (f32[1,16,256]{2,1,0:T(8,128)}, f32[1,16,256]{2,1,0:T(8,128)S(1)}, u32[]{:S(2)}, u32[]{:S(2)}) collective-permute-start(f32[1,16,256]{2,1,0:T(8,128)} %get-tuple-element.23), channel_id=1, source_target_pairs={{0,1},{1,0},{2,3},{3,2},{4,5},{5,4},{6,7},{7,6},{8,9},{9,8},{10,11... | collective-permute-start | bytes 49160 | tf_op jit(solution)/shard_map/ppermute | solution.py:291
  3.4 2.6 %collective-permute-start.4 = (bf16[256,768]{1,0:T(8,128)(2,1)}, bf16[256,768]{1,0:T(8,128)(2,1)S(1)}, u32[]{:S(2)}, u32[]{:S(2)}) collective-permute-start(bf16[256,768]{1,0:T(8,128)(2,1)} %get-tuple-element.24.turned_ref.refs_0_), channel_id=1, source_target_pairs={{0,2},{2,0},{1,3},{3,1},{4,6},{6,4},{5,7},{7,5},{8,10},{10,8},{9,1... | collective-permute-start | bytes 1179656 | tf_op jit(solution)/shard_map/ppermute | solution.py:291
  5.9 0.2 collective-permute-start.3
  6.1 1.6 %collective-permute-start.1 = (bf16[384,256]{1,0:T(8,128)(2,1)}, bf16[384,256]{1,0:T(8,128)(2,1)S(1)}, u32[]{:S(2)}, u32[]{:S(2)}) collective-permute-start(bf16[384,256]{1,0:T(8,128)(2,1)} %get-tuple-element.28), channel_id=1, source_target_pairs={{0,4},{4,8},{8,12},{12,0},{1,5},{5,9},{9,13},{13,1},{2,6},{6,10},{... | collective-permute-start | bytes 589832 | tf_op jit(solution)/shard_map/ppermute | solution.py:291
  7.7 2.2 %collective-permute-start.2 = (bf16[384,256]{1,0:T(8,128)(2,1)}, bf16[384,256]{1,0:T(8,128)(2,1)S(1)}, u32[]{:S(2)}, u32[]{:S(2)}) collective-permute-start(bf16[384,256]{1,0:T(8,128)(2,1)} %get-tuple-element.29), channel_id=1, source_target_pairs={{0,12},{4,0},{8,4},{12,8},{1,13},{5,1},{9,5},{13,9},{2,14},{6,2},{... | collective-permute-start | bytes 589832 | tf_op jit(solution)/shard_map/ppermute | solution.py:291
  9.9 0.0 collective-permute-done.other_ref
  9.9 0.0 copy-start
  9.9 1.0 %copy-done = bf16[256,768]{1,0:T(8,128)(2,1)S(1)} copy-done((bf16[256,768]{1,0:T(8,128)(2,1)S(1)}, bf16[256,768]{1,0:T(8,128)(2,1)}, u32[]{:S(2)}) %copy-start) | copy-done | bytes 393240
  10.9 0.0 copy-start.1
  10.9 0.9 %copy-done.1 = f32[11,16,256]{2,1,0:T(8,128)S(1)} copy-done((f32[11,16,256]{2,1,0:T(8,128)S(1)}, f32[11,16,256]{2,1,0:T(8,128)}, u32[]{:S(2)}) %copy-start.1) | copy-done | bytes 180248
  11.9 5.1 %weights.1 = (f32[1536,256]{1,0:T(8,128)S(1)}, bf16[1536,768]{1,0:T(8,128)(2,1)S(1)}, bf16[1536,768]{1,0:T(8,128)(2,1)S(1)}) custom-call(f32[11,16,256]{2,1,0:T(8,128)S(1)} %copy-done.1, f32[1,16,256]{2,1,0:T(8,128)S(1)} %collective-permute-done.other_ref, bf16[256,768]{1,0:T(8,128)(2,1)S(1)} %copy-done), custom_call_target="tpu_custom_call" | custom-call | flops 8000000000 | bytes 10000000 | tf_op jit(solution)/shard_map/weights/pallas_call | solution.py:355
  17.0 0.0 collective-permute-done.1.below_ref.below_hbm
  17.0 2.0 %collective-permute-done.2.above_ref.above_hbm = bf16[384,256]{1,0:T(8,128)(2,1)S(1)} collective-permute-done((bf16[384,256]{1,0:T(8,128)(2,1)}, bf16[384,256]{1,0:T(8,128)(2,1)S(1)}, u32[]{:S(2)}, u32[]{:S(2)}) %collective-permute-start.2) | collective-permute-done | bytes 196640 | tf_op jit(solution)/shard_map/ppermute | solution.py:291
  19.0 0.0 collective-permute-done.4.refs_0_
  19.0 0.1 collective-permute-start.5
  19.1 0.8 %flux.3.flux1_ref.after.flux_ref = bf16[768,256]{1,0:T(8,128)(2,1)S(1)} custom-call(f32[1536,256]{1,0:T(8,128)S(1)} %get-tuple-element.25.part_ref.part_hbm, bf16[1536,768]{1,0:T(8,128)(2,1)S(1)} %get-tuple-element.26.hi_ref, bf16[1536,768]{1,0:T(8,128)(2,1)S(1)} %get-tuple-element.27.lo_ref, ...), custom_call_target="tpu_custom_call" | custom-call | flops 1000000000 | bytes 1000000 | tf_op jit(solution)/shard_map/flux/pallas_call | solution.py:389
  19.9 0.8 %flux.2.flux0_ref.flux_ref = bf16[768,256]{1,0:T(8,128)(2,1)S(1)} custom-call(f32[1536,256]{1,0:T(8,128)S(1)} %get-tuple-element.25.part_ref.part_hbm, bf16[1536,768]{1,0:T(8,128)(2,1)S(1)} %get-tuple-element.26.hi_ref, bf16[1536,768]{1,0:T(8,128)(2,1)S(1)} %get-tuple-element.27.lo_ref, bf16[384,256]{1,0:T(8,128)(2,1)S(1)} %collective-permute-done.1.below_ref.below_hbm, ...), custom_call_target="tpu_custom_call" | custom-call | flops 1000000000 | bytes 1000000 | tf_op jit(solution)/shard_map/flux/pallas_call | solution.py:389
  20.7 0.0 collective-permute-done.3.refs_1_
  20.7 0.1 collective-permute-done.5.refs_3_
  20.8 0.3 far.2.after
  21.1 1.2 %collective-permute-start.10 = (bf16[256,256]{1,0:T(8,128)(2,1)S(1)}, bf16[256,256]{1,0:T(8,128)(2,1)S(1)}, u32[]{:S(2)}, u32[]{:S(2)}) collective-permute-start(bf16[256,256]{1,0:T(8,128)(2,1)S(1)} %far.2.after), channel_id=1, source_target_pairs={{0,4},{1,5},{4,0},{5,1},{8,12},{9,13},{12,8},{13,9},{2,6},{3,7},{6... | collective-permute-start | bytes 393224 | tf_op jit(solution)/shard_map/ppermute | solution.py:299
  22.3 0.3 far.3
  22.6 0.9 %collective-permute-start.6 = (bf16[256,256]{1,0:T(8,128)(2,1)S(1)}, bf16[256,256]{1,0:T(8,128)(2,1)S(1)}, u32[]{:S(2)}, u32[]{:S(2)}) collective-permute-start(bf16[256,256]{1,0:T(8,128)(2,1)S(1)} %far.3), channel_id=1, source_target_pairs={{0,4},{1,5},{4,0},{5,1},{8,12},{9,13},{12,8},{13,9},{2,6},{3,7},{6... | collective-permute-start | bytes 393224 | tf_op jit(solution)/shard_map/ppermute | solution.py:299
  23.5 1.1 %near.1 = (bf16[256,256]{1,0:T(8,128)(2,1)S(1)}, bf16[256,256]{1,0:T(8,128)(2,1)S(1)}, f32[256,256]{1,0:T(8,128)S(1)}, f32[256,256]{1,0:T(8,128)S(1)}, f32[256,2...) custom-call(bf16[768,256]{1,0:T(8,128)(2,1)S(1)} %flux.2.flux0_ref.flux_ref, ...), custom_call_target="tpu_custom_call" | custom-call | flops 400000000 | bytes 1000000 | tf_op jit(solution)/shard_map/near/pallas_call | solution.py:423
  24.7 1.2 %collective-permute-start.8 = (bf16[256,256]{1,0:T(8,128)(2,1)S(1)}, bf16[256,256]{1,0:T(8,128)(2,1)S(1)}, u32[]{:S(2)}, u32[]{:S(2)}) collective-permute-start(bf16[256,256]{1,0:T(8,128)(2,1)S(1)} %get-tuple-element.35), channel_id=1, source_target_pairs={{0,4},{1,5},{4,0},{5,1},{8,12},{9,13},{12,8},{13,9},{2,6},{3,7},{6... | collective-permute-start | bytes 393224 | tf_op jit(solution)/shard_map/ppermute | solution.py:299
  25.9 1.6 %collective-permute-done.10.far_ref = bf16[256,256]{1,0:T(8,128)(2,1)S(1)} collective-permute-done((bf16[256,256]{1,0:T(8,128)(2,1)S(1)}, bf16[256,256]{1,0:T(8,128)(2,1)S(1)}, u32[]{:S(2)}, u32[]{:S(2)}) %collective-permute-start.10) | collective-permute-done | bytes 131104 | tf_op jit(solution)/shard_map/ppermute | solution.py:299
  27.5 1.4 %collective-permute-start.11 = (bf16[256,256]{1,0:T(8,128)(2,1)S(1)}, bf16[256,256]{1,0:T(8,128)(2,1)S(1)}, u32[]{:S(2)}, u32[]{:S(2)}) collective-permute-start(bf16[256,256]{1,0:T(8,128)(2,1)S(1)} %add.3), channel_id=1, source_target_pairs={{0,8},{1,9},{4,12},{5,13},{8,0},{9,1},{12,4},{13,5},{2,10},{3,11},... | collective-permute-start | bytes 393224 | tf_op jit(solution)/shard_map/ppermute | solution.py:299
  28.9 1.4 %collective-permute-done.6.far_ref = bf16[256,256]{1,0:T(8,128)(2,1)S(1)} collective-permute-done((bf16[256,256]{1,0:T(8,128)(2,1)S(1)}, bf16[256,256]{1,0:T(8,128)(2,1)S(1)}, u32[]{:S(2)}, u32[]{:S(2)}) %collective-permute-start.6) | collective-permute-done | bytes 131104 | tf_op jit(solution)/shard_map/ppermute | solution.py:299
  30.3 0.1 collective-permute-start.12
  30.4 1.4 %collective-permute-start.7 = (bf16[256,256]{1,0:T(8,128)(2,1)S(1)}, bf16[256,256]{1,0:T(8,128)(2,1)S(1)}, u32[]{:S(2)}, u32[]{:S(2)}) collective-permute-start(bf16[256,256]{1,0:T(8,128)(2,1)S(1)} %get-tuple-element.34), channel_id=1, source_target_pairs={{0,1},{1,0},{4,5},{5,4},{8,9},{9,8},{12,13},{13,12},{2,3},{3,2},{6... | collective-permute-start | bytes 393224 | tf_op jit(solution)/shard_map/ppermute | solution.py:299
  31.8 2.6 %collective-permute-start.9 = (bf16[256,256]{1,0:T(8,128)(2,1)S(1)}, bf16[256,256]{1,0:T(8,128)(2,1)S(1)}, u32[]{:S(2)}, u32[]{:S(2)}) collective-permute-start(bf16[256,256]{1,0:T(8,128)(2,1)S(1)} %get-tuple-element.36), channel_id=1, source_target_pairs={{0,5},{1,4},{4,1},{5,0},{8,13},{9,12},{12,9},{13,8},{2,7},{3,6},{6... | collective-permute-start | bytes 393224 | tf_op jit(solution)/shard_map/ppermute | solution.py:299
  34.4 1.0 %collective-permute-done.8.refs_2_ = bf16[256,256]{1,0:T(8,128)(2,1)S(1)} collective-permute-done((bf16[256,256]{1,0:T(8,128)(2,1)S(1)}, bf16[256,256]{1,0:T(8,128)(2,1)S(1)}, u32[]{:S(2)}, u32[]{:S(2)}) %collective-permute-start.8) | collective-permute-done | bytes 131104 | tf_op jit(solution)/shard_map/ppermute | solution.py:299
  35.4 3.2 %collective-permute-done.11.refs_4_ = bf16[256,256]{1,0:T(8,128)(2,1)S(1)} collective-permute-done((bf16[256,256]{1,0:T(8,128)(2,1)S(1)}, bf16[256,256]{1,0:T(8,128)(2,1)S(1)}, u32[]{:S(2)}, u32[]{:S(2)}) %collective-permute-start.11) | collective-permute-done | bytes 131104 | tf_op jit(solution)/shard_map/ppermute | solution.py:299
  38.5 3.3 %collective-permute-done.12.refs_5_ = bf16[256,256]{1,0:T(8,128)(2,1)S(1)} collective-permute-done((bf16[256,256]{1,0:T(8,128)(2,1)S(1)}, bf16[256,256]{1,0:T(8,128)(2,1)S(1)}, u32[]{:S(2)}, u32[]{:S(2)}) %collective-permute-start.12) | collective-permute-done | bytes 131104 | tf_op jit(solution)/shard_map/ppermute | solution.py:299
  41.8 0.0 collective-permute-done.7.refs_1_
  41.8 0.0 collective-permute-done.9.refs_3_
  41.8 0.9 %total.1 = f32[1,256,512]{2,1,0:T(8,128)} custom-call(f32[256,256]{1,0:T(8,128)S(1)} %get-tuple-element.30.refs_0_, bf16[256,256]{1,0:T(8,128)(2,1)S(1)} %collective-permute-done.7.refs_1_, bf16[256,256]{1,0:T(8,128)(2,1)S(1)} %collective-permute-done.8.refs_2_, bf16[256,256]{1,0:T(8,128)(2,1)S(1)} %collective-permute-done.9.refs_3_, ...), custom_call_target="tpu_custom_call" | custom-call | tf_op jit(solution)/shard_map/total/pallas_call | solution.py:447
  (3 shorter events, 0.1 us)
Async XLA Ops:
  2.9 7.1 %collective-permute-start = (f32[1,16,256]{2,1,0:T(8,128)}, f32[1,16,256]{2,1,0:T(8,128)S(1)}, u32[]{:S(2)}, u32[]{:S(2)}) collective-permute-start(f32[1,16,256]{2,1,0:T(8,128)} %get-tuple-element.23), channel_id=1, source_target_pairs={{0,1},{1,0},{2,3},{3,2},{4,5},{5,4},{6,7},{7,6},{8,9},{9,8},{10,11... | collective-permute-start | bytes 49160 | tf_op jit(solution)/shard_map/ppermute | solution.py:291
  3.4 15.6 %collective-permute-start.4 = (bf16[256,768]{1,0:T(8,128)(2,1)}, bf16[256,768]{1,0:T(8,128)(2,1)S(1)}, u32[]{:S(2)}, u32[]{:S(2)}) collective-permute-start(bf16[256,768]{1,0:T(8,128)(2,1)} %get-tuple-element.24.turned_ref.refs_0_), channel_id=1, source_target_pairs={{0,2},{2,0},{1,3},{3,1},{4,6},{6,4},{5,7},{7,5},{8,10},{10,8},{9,1... | collective-permute-start | bytes 1179656 | tf_op jit(solution)/shard_map/ppermute | solution.py:291
  5.9 14.7 %collective-permute-start.3 = (bf16[256,768]{1,0:T(8,128)(2,1)}, bf16[256,768]{1,0:T(8,128)(2,1)S(1)}, u32[]{:S(2)}, u32[]{:S(2)}) collective-permute-start(bf16[256,768]{1,0:T(8,128)(2,1)} %get-tuple-element.24.turned_ref.refs_0_), channel_id=1, source_target_pairs={{0,1},{1,0},{2,3},{3,2},{4,5},{5,4},{6,7},{7,6},{8,9},{9,8},{10,11... | collective-permute-start | bytes 1179656 | tf_op jit(solution)/shard_map/ppermute | solution.py:291
  6.1 10.9 %collective-permute-start.1 = (bf16[384,256]{1,0:T(8,128)(2,1)}, bf16[384,256]{1,0:T(8,128)(2,1)S(1)}, u32[]{:S(2)}, u32[]{:S(2)}) collective-permute-start(bf16[384,256]{1,0:T(8,128)(2,1)} %get-tuple-element.28), channel_id=1, source_target_pairs={{0,4},{4,8},{8,12},{12,0},{1,5},{5,9},{9,13},{13,1},{2,6},{6,10},{... | collective-permute-start | bytes 589832 | tf_op jit(solution)/shard_map/ppermute | solution.py:291
  7.7 11.3 %collective-permute-start.2 = (bf16[384,256]{1,0:T(8,128)(2,1)}, bf16[384,256]{1,0:T(8,128)(2,1)S(1)}, u32[]{:S(2)}, u32[]{:S(2)}) collective-permute-start(bf16[384,256]{1,0:T(8,128)(2,1)} %get-tuple-element.29), channel_id=1, source_target_pairs={{0,12},{4,0},{8,4},{12,8},{1,13},{5,1},{9,5},{13,9},{2,14},{6,2},{... | collective-permute-start | bytes 589832 | tf_op jit(solution)/shard_map/ppermute | solution.py:291
  9.9 1.0 %copy-start = (bf16[256,768]{1,0:T(8,128)(2,1)S(1)}, bf16[256,768]{1,0:T(8,128)(2,1)}, u32[]{:S(2)}) copy-start(bf16[256,768]{1,0:T(8,128)(2,1)} %get-tuple-element.24.turned_ref.refs_0_) | copy-start | bytes 1179652
  10.9 0.9 %copy-start.1 = (f32[11,16,256]{2,1,0:T(8,128)S(1)}, f32[11,16,256]{2,1,0:T(8,128)}, u32[]{:S(2)}) copy-start(f32[11,16,256]{2,1,0:T(8,128)} %get-tuple-element.22.source_ref) | copy-start | bytes 540676
  19.0 1.8 %collective-permute-start.5 = (bf16[256,768]{1,0:T(8,128)(2,1)S(1)}, bf16[256,768]{1,0:T(8,128)(2,1)S(1)}, u32[]{:S(2)}, u32[]{:S(2)}) collective-permute-start(bf16[256,768]{1,0:T(8,128)(2,1)S(1)} %relay.1.refs_2_), channel_id=1, source_target_pairs={{0,1},{1,0},{2,3},{3,2},{4,5},{5,4},{6,7},{7,6},{8,9},{9,8},{10,11... | collective-permute-start | bytes 1179656 | tf_op jit(solution)/shard_map/ppermute | solution.py:291
  21.1 6.4 %collective-permute-start.10 = (bf16[256,256]{1,0:T(8,128)(2,1)S(1)}, bf16[256,256]{1,0:T(8,128)(2,1)S(1)}, u32[]{:S(2)}, u32[]{:S(2)}) collective-permute-start(bf16[256,256]{1,0:T(8,128)(2,1)S(1)} %far.2.after), channel_id=1, source_target_pairs={{0,4},{1,5},{4,0},{5,1},{8,12},{9,13},{12,8},{13,9},{2,6},{3,7},{6... | collective-permute-start | bytes 393224 | tf_op jit(solution)/shard_map/ppermute | solution.py:299
  22.6 7.7 %collective-permute-start.6 = (bf16[256,256]{1,0:T(8,128)(2,1)S(1)}, bf16[256,256]{1,0:T(8,128)(2,1)S(1)}, u32[]{:S(2)}, u32[]{:S(2)}) collective-permute-start(bf16[256,256]{1,0:T(8,128)(2,1)S(1)} %far.3), channel_id=1, source_target_pairs={{0,4},{1,5},{4,0},{5,1},{8,12},{9,13},{12,8},{13,9},{2,6},{3,7},{6... | collective-permute-start | bytes 393224 | tf_op jit(solution)/shard_map/ppermute | solution.py:299
  24.7 10.7 %collective-permute-start.8 = (bf16[256,256]{1,0:T(8,128)(2,1)S(1)}, bf16[256,256]{1,0:T(8,128)(2,1)S(1)}, u32[]{:S(2)}, u32[]{:S(2)}) collective-permute-start(bf16[256,256]{1,0:T(8,128)(2,1)S(1)} %get-tuple-element.35), channel_id=1, source_target_pairs={{0,4},{1,5},{4,0},{5,1},{8,12},{9,13},{12,8},{13,9},{2,6},{3,7},{6... | collective-permute-start | bytes 393224 | tf_op jit(solution)/shard_map/ppermute | solution.py:299
  27.5 11.1 %collective-permute-start.11 = (bf16[256,256]{1,0:T(8,128)(2,1)S(1)}, bf16[256,256]{1,0:T(8,128)(2,1)S(1)}, u32[]{:S(2)}, u32[]{:S(2)}) collective-permute-start(bf16[256,256]{1,0:T(8,128)(2,1)S(1)} %add.3), channel_id=1, source_target_pairs={{0,8},{1,9},{4,12},{5,13},{8,0},{9,1},{12,4},{13,5},{2,10},{3,11},... | collective-permute-start | bytes 393224 | tf_op jit(solution)/shard_map/ppermute | solution.py:299
  30.3 11.5 %collective-permute-start.12 = (bf16[256,256]{1,0:T(8,128)(2,1)S(1)}, bf16[256,256]{1,0:T(8,128)(2,1)S(1)}, u32[]{:S(2)}, u32[]{:S(2)}) collective-permute-start(bf16[256,256]{1,0:T(8,128)(2,1)S(1)} %get-tuple-element.38), channel_id=1, source_target_pairs={{0,9},{1,8},{4,13},{5,12},{8,1},{9,0},{12,5},{13,4},{2,11},{3,10},... | collective-permute-start | bytes 393224 | tf_op jit(solution)/shard_map/ppermute | solution.py:299
  30.4 11.5 %collective-permute-start.7 = (bf16[256,256]{1,0:T(8,128)(2,1)S(1)}, bf16[256,256]{1,0:T(8,128)(2,1)S(1)}, u32[]{:S(2)}, u32[]{:S(2)}) collective-permute-start(bf16[256,256]{1,0:T(8,128)(2,1)S(1)} %get-tuple-element.34), channel_id=1, source_target_pairs={{0,1},{1,0},{4,5},{5,4},{8,9},{9,8},{12,13},{13,12},{2,3},{3,2},{6... | collective-permute-start | bytes 393224 | tf_op jit(solution)/shard_map/ppermute | solution.py:299
  31.8 10.0 %collective-permute-start.9 = (bf16[256,256]{1,0:T(8,128)(2,1)S(1)}, bf16[256,256]{1,0:T(8,128)(2,1)S(1)}, u32[]{:S(2)}, u32[]{:S(2)}) collective-permute-start(bf16[256,256]{1,0:T(8,128)(2,1)S(1)} %get-tuple-element.36), channel_id=1, source_target_pairs={{0,5},{1,4},{4,1},{5,0},{8,13},{9,12},{12,9},{13,8},{2,7},{3,6},{6... | collective-permute-start | bytes 393224 | tf_op jit(solution)/shard_map/ppermute | solution.py:299

commit v10 on v9

--- a/solution.py
+++ b/solution.py
@@ -7,6 +7,7 @@
 from jax.experimental.pallas import tpu as pltpu
 from jax.sharding import PartitionSpec as P
 
+PIECES = 2
 GROUP = 16
 BF16 = jnp.bfloat16
 F32 = jnp.float32
@@ -30,10 +31,11 @@
 
 def prep_kernel(
     v_hbm, low_hbm, high_hbm, force_hbm, bond_hbm, near_hbm,
-    turned_hbm, send_low_hbm, send_high_hbm, source_hbm, bond_out_hbm,
-    v_ref, low_ref, high_ref, near_ref, turned_ref, send_low_ref, send_high_ref,
-    source_ref, pick_ref, wide_ref, v_sems, in_sems, out_sems,
+    turned_hbm, send_low_hbm, send_high_hbm, source_hbm, bond_out_hbm, *refs
 ):
+    piece_hbms, scratch_refs = refs[:PIECES], refs[PIECES:]
+    v_ref, low_ref, high_ref, near_ref, turned_ref, send_low_ref, send_high_ref = scratch_refs[:7]
+    source_ref, pick_ref, wide_ref, v_sems, in_sems, out_sems = scratch_refs[7:]
     rows, half = v_ref.shape
     atoms = rows // 3
     arriving = [
@@ -89,6 +91,9 @@
             part = wide_ref[t, pl.ds(b, atoms, stride=3), :]
             turned_ref[columns, b * atoms : (b + 1) * atoms] = part.T.astype(BF16)
     leave(turned_ref, turned_hbm)
+    for i, piece_hbm in enumerate(piece_hbms):
+        length = piece_hbm.shape[0]
+        leave(turned_ref.at[pl.ds(i * length, length)], piece_hbm)
     picked = dot(pick_ref[...], v_ref[...]).astype(BF16)
     send_high_ref[...] = picked[: 3 * count]
     leave(send_high_ref, send_high_hbm)
@@ -180,8 +185,11 @@
 
 
 def relay_kernel(part_hbm, below_hbm, above_hbm, *refs):
-    for got_ref, given_ref in zip(refs[: len(refs) // 2], refs[len(refs) // 2 :]):
-        given_ref[...] = got_ref[...]
+    quarters = len(refs) // (PIECES + 1)
+    for t, given_ref in enumerate(refs[quarters * PIECES :]):
+        length = given_ref.shape[0] // PIECES
+        for i in range(PIECES):
+            given_ref[i * length : (i + 1) * length] = refs[t * PIECES + i][...]
 
 
 def flux_kernel(e, part_ref, hi_ref, lo_ref, below_ref, above_ref, flux_ref, halo_ref):
@@ -321,15 +329,16 @@
         shape((3 * count, half), BF16),
         shape((3 * count, half), BF16),
     )
-    turned, send_low, send_high, sources, bonds = pl.pallas_call(
+    turned, send_low, send_high, sources, bonds, *pieces = pl.pallas_call(
         prep_kernel,
         out_shape=(
             *prepared,
             shape((11, *neighbours.shape), F32),
             shape(bond_vectors.shape, F32),
-        ),
+        )
+        + (shape((half // PIECES, rows), BF16),) * PIECES,
         in_specs=[hbm] * 6,
-        out_specs=(hbm,) * 5,
+        out_specs=(hbm,) * (5 + PIECES),
         scratch_shapes=[
             pltpu.VMEM((rows, half), BF16),
             pltpu.VMEM((1, count), jnp.int32),
@@ -341,12 +350,12 @@
             pltpu.VMEM((half // 128, rows, 128), F32),
             pltpu.SemaphoreType.DMA((4,)),
             pltpu.SemaphoreType.DMA((5,)),
-            pltpu.SemaphoreType.DMA((5,)),
+            pltpu.SemaphoreType.DMA((5 + PIECES,)),
         ],
         compiler_params=params(58),
         name="prep",
     )(panel_vectors, *lists, forces, bond_vectors, neighbours)
-    quarters = [shift(turned, "blk", j) for j in range(1, tiles)]
+    quarters = [shift(piece, "blk", j) for j in range(1, tiles) for piece in pieces]
     turned_other = shift(turned, "dir", 1)
     other_bonds = shift(bonds, "dir", 1)
     below = shift(send_high, "dom", 1)

time: 42.9 us -> 43 us (level)
  starting transfers between devices: 16 us -> 14 us
  waiting for transfers between devices: 12.5 us -> 14.5 us
    ppermute x7, starting transfers between devices: 8.87 us -> 6.6 us  [swap(): return lax.ppermute(value, ('dom', 'dir'), pairs)]
    ppermute x7, waiting for transfers between devices: 10.4 us -> 12.1 us  [swap(): return lax.ppermute(value, ('dom', 'dir'), pairs)]
    ppermute x6 -> x7, waiting for transfers between devices: 2.12 us -> 2.37 us  [shift(): lax.ppermute(value, axis, [(i, (i + by) % length) for i in range(length)])]
    ppermute x6 -> x7, starting transfers between devices: 7.14 us -> 7.36 us  [shift(): lax.ppermute(value, axis, [(i, (i + by) % length) for i in range(length)])]
  transfers between devices with their start and end apart: 13 -> 14, of which waited for: 7 -> 9; matrix products, arithmetic and copies ran while one was open for 0% -> 0% of each run, Pallas kernels for 19% -> 19%
where the time goes in v10:
time: 43 us; the launch traced here: 42.8 us
  waiting for transfers between devices  14.5 us (34%)
  starting transfers between devices  14 us (33%)
  Pallas kernels  12.3 us (29%)
  local copies, waits for them, and re-layouts  1.92 us (4%)
    ppermute x7, waiting for transfers between devices, swap(): return lax.ppermute(value, ('dom', 'dir'), pairs)  12.1 us
    ppermute x7, starting transfers between devices, shift(): lax.ppermute(value, axis, [(i, (i + by) % length) for i in range(length)])  7.36 us
    ppermute x7, starting transfers between devices, swap(): return lax.ppermute(value, ('dom', 'dir'), pairs)  6.6 us
    pallas_call x1, Pallas kernels, per_device(): pl.pallas_call(weights_kernel, out_shape=(shape((2 * rows, half), F32), s...  5.13 us
    pallas_call x1, Pallas kernels, per_device(): pl.pallas_call(prep_kernel, out_shape=(*prepared, shape((11, *neighbours....  2.98 us
    ppermute x7, waiting for transfers between devices, shift(): lax.ppermute(value, axis, [(i, (i + by) % length) for i in range(length)])  2.37 us
    unnamed x4, local copies, waits for them, and re-layouts  1.92 us
    pallas_call x2, Pallas kernels, flux_of(): pl.pallas_call(functools.partial(flux_kernel, e), out_shape=shape((rows,...  1.54 us
  transfers between devices with their start and end apart: 14, of which 9 were waited for; matrix products, arithmetic and copies ran while one was open for 0% of the time, Pallas kernels for 19%

profile of v10, /device:TPU:0, one launch (start us, length us, event | category | flops | bytes accessed | tf_op | source)
XLA Modules:
  0.0 42.8 jit_solution(4556023747644532196)
XLA Ops:
  0.0 3.0 %prep.1 = (bf16[256,768]{1,0:T(8,128)(2,1)}, bf16[384,256]{1,0:T(8,128)(2,1)}, bf16[384,256]{1,0:T(8,128)(2,1)}, f32[11,16,256]{2,1,0:T(8,128)}, f32[1,16,256]{2...) custom-call(bf16[768,512]{1,0:T(8,128)(2,1)} %v_hbm.1, s32[1,128]{1,0:T(1,128)} %bitcast.4, ...), custom_call_target="tpu_custom_call" | custom-call | tf_op jit(solution)/shard_map/prep/pallas_call | solution.py:332
  3.0 0.5 %collective-permute-start = (f32[1,16,256]{2,1,0:T(8,128)}, f32[1,16,256]{2,1,0:T(8,128)S(1)}, u32[]{:S(2)}, u32[]{:S(2)}) collective-permute-start(f32[1,16,256]{2,1,0:T(8,128)} %get-tuple-element.25), channel_id=1, source_target_pairs={{0,1},{1,0},{2,3},{3,2},{4,5},{5,4},{6,7},{7,6},{8,9},{9,8},{10,11... | collective-permute-start | bytes 49160 | tf_op jit(solution)/shard_map/ppermute | solution.py:299
  3.5 2.6 %collective-permute-start.1 = (bf16[384,256]{1,0:T(8,128)(2,1)}, bf16[384,256]{1,0:T(8,128)(2,1)S(1)}, u32[]{:S(2)}, u32[]{:S(2)}) collective-permute-start(bf16[384,256]{1,0:T(8,128)(2,1)} %get-tuple-element.30), channel_id=1, source_target_pairs={{0,4},{4,8},{8,12},{12,0},{1,5},{5,9},{9,13},{13,1},{2,6},{6,10},{... | collective-permute-start | bytes 589832 | tf_op jit(solution)/shard_map/ppermute | solution.py:299
  6.1 2.1 %collective-permute-start.2 = (bf16[384,256]{1,0:T(8,128)(2,1)}, bf16[384,256]{1,0:T(8,128)(2,1)S(1)}, u32[]{:S(2)}, u32[]{:S(2)}) collective-permute-start(bf16[384,256]{1,0:T(8,128)(2,1)} %get-tuple-element.31), channel_id=1, source_target_pairs={{0,12},{4,0},{8,4},{12,8},{1,13},{5,1},{9,5},{13,9},{2,14},{6,2},{... | collective-permute-start | bytes 589832 | tf_op jit(solution)/shard_map/ppermute | solution.py:299
  8.3 1.6 %collective-permute-start.4 = (bf16[128,768]{1,0:T(8,128)(2,1)}, bf16[128,768]{1,0:T(8,128)(2,1)S(1)}, u32[]{:S(2)}, u32[]{:S(2)}) collective-permute-start(bf16[128,768]{1,0:T(8,128)(2,1)} %get-tuple-element.32), channel_id=1, source_target_pairs={{0,2},{2,0},{1,3},{3,1},{4,6},{6,4},{5,7},{7,5},{8,10},{10,8},{9,1... | collective-permute-start | bytes 589832 | tf_op jit(solution)/shard_map/ppermute | solution.py:299
  9.9 0.4 collective-permute-start.5
  10.3 0.0 collective-permute-done.other_ref
  10.3 0.0 collective-permute-start.3
  10.3 0.0 copy-start
  10.3 1.0 %copy-done = bf16[256,768]{1,0:T(8,128)(2,1)S(1)} copy-done((bf16[256,768]{1,0:T(8,128)(2,1)S(1)}, bf16[256,768]{1,0:T(8,128)(2,1)}, u32[]{:S(2)}) %copy-start) | copy-done | bytes 393240
  11.3 0.0 copy-start.1
  11.3 0.9 %copy-done.1 = f32[11,16,256]{2,1,0:T(8,128)S(1)} copy-done((f32[11,16,256]{2,1,0:T(8,128)S(1)}, f32[11,16,256]{2,1,0:T(8,128)}, u32[]{:S(2)}) %copy-start.1) | copy-done | bytes 180248
  12.2 5.1 %weights.1 = (f32[1536,256]{1,0:T(8,128)S(1)}, bf16[1536,768]{1,0:T(8,128)(2,1)S(1)}, bf16[1536,768]{1,0:T(8,128)(2,1)S(1)}) custom-call(f32[11,16,256]{2,1,0:T(8,128)S(1)} %copy-done.1, f32[1,16,256]{2,1,0:T(8,128)S(1)} %collective-permute-done.other_ref, bf16[256,768]{1,0:T(8,128)(2,1)S(1)} %copy-done), custom_call_target="tpu_custom_call" | custom-call | flops 8000000000 | bytes 10000000 | tf_op jit(solution)/shard_map/weights/pallas_call | solution.py:364
  17.3 0.0 collective-permute-done.1.below_ref.below_hbm
  17.3 0.2 collective-permute-done.2.above_ref.above_hbm
  17.5 0.0 collective-permute-done.4.refs_0_
  17.5 2.0 %collective-permute-done.5.refs_1_ = bf16[128,768]{1,0:T(8,128)(2,1)S(1)} collective-permute-done((bf16[128,768]{1,0:T(8,128)(2,1)}, bf16[128,768]{1,0:T(8,128)(2,1)S(1)}, u32[]{:S(2)}, u32[]{:S(2)}) %collective-permute-start.5) | collective-permute-done | bytes 196640 | tf_op jit(solution)/shard_map/ppermute | solution.py:299
  19.6 0.1 collective-permute-start.6
  19.7 0.8 %flux.3.flux1_ref.after.flux_ref = bf16[768,256]{1,0:T(8,128)(2,1)S(1)} custom-call(f32[1536,256]{1,0:T(8,128)S(1)} %get-tuple-element.27.part_ref.part_hbm, bf16[1536,768]{1,0:T(8,128)(2,1)S(1)} %get-tuple-element.28.hi_ref, bf16[1536,768]{1,0:T(8,128)(2,1)S(1)} %get-tuple-element.29.lo_ref, ...), custom_call_target="tpu_custom_call" | custom-call | flops 1000000000 | bytes 1000000 | tf_op jit(solution)/shard_map/flux/pallas_call | solution.py:398
  20.4 0.8 %flux.2.flux0_ref.flux_ref = bf16[768,256]{1,0:T(8,128)(2,1)S(1)} custom-call(f32[1536,256]{1,0:T(8,128)S(1)} %get-tuple-element.27.part_ref.part_hbm, bf16[1536,768]{1,0:T(8,128)(2,1)S(1)} %get-tuple-element.28.hi_ref, bf16[1536,768]{1,0:T(8,128)(2,1)S(1)} %get-tuple-element.29.lo_ref, bf16[384,256]{1,0:T(8,128)(2,1)S(1)} %collective-permute-done.1.below_ref.below_hbm, ...), custom_call_target="tpu_custom_call" | custom-call | flops 1000000000 | bytes 1000000 | tf_op jit(solution)/shard_map/flux/pallas_call | solution.py:398
  21.2 0.0 collective-permute-done.3.refs_1_
  21.2 0.1 collective-permute-done.6.refs_3_
  21.4 0.3 far.2.after
  21.7 0.1 collective-permute-start.11
  21.7 0.3 far.3
  22.0 2.0 %collective-permute-start.7 = (bf16[256,256]{1,0:T(8,128)(2,1)S(1)}, bf16[256,256]{1,0:T(8,128)(2,1)S(1)}, u32[]{:S(2)}, u32[]{:S(2)}) collective-permute-start(bf16[256,256]{1,0:T(8,128)(2,1)S(1)} %far.3), channel_id=1, source_target_pairs={{0,4},{1,5},{4,0},{5,1},{8,12},{9,13},{12,8},{13,9},{2,6},{3,7},{6... | collective-permute-start | bytes 393224 | tf_op jit(solution)/shard_map/ppermute | solution.py:307
  24.1 1.1 %near.1 = (bf16[256,256]{1,0:T(8,128)(2,1)S(1)}, bf16[256,256]{1,0:T(8,128)(2,1)S(1)}, f32[256,256]{1,0:T(8,128)S(1)}, f32[256,256]{1,0:T(8,128)S(1)}, f32[256,2...) custom-call(bf16[768,256]{1,0:T(8,128)(2,1)S(1)} %flux.2.flux0_ref.flux_ref, ...), custom_call_target="tpu_custom_call" | custom-call | flops 400000000 | bytes 1000000 | tf_op jit(solution)/shard_map/near/pallas_call | solution.py:432
  25.2 0.1 collective-permute-start.9
  25.4 2.7 %collective-permute-done.11.far_ref = bf16[256,256]{1,0:T(8,128)(2,1)S(1)} collective-permute-done((bf16[256,256]{1,0:T(8,128)(2,1)S(1)}, bf16[256,256]{1,0:T(8,128)(2,1)S(1)}, u32[]{:S(2)}, u32[]{:S(2)}) %collective-permute-start.11) | collective-permute-done | bytes 131104 | tf_op jit(solution)/shard_map/ppermute | solution.py:307
  28.1 0.9 %collective-permute-start.12 = (bf16[256,256]{1,0:T(8,128)(2,1)S(1)}, bf16[256,256]{1,0:T(8,128)(2,1)S(1)}, u32[]{:S(2)}, u32[]{:S(2)}) collective-permute-start(bf16[256,256]{1,0:T(8,128)(2,1)S(1)} %add.3), channel_id=1, source_target_pairs={{0,8},{1,9},{4,12},{5,13},{8,0},{9,1},{12,4},{13,5},{2,10},{3,11},... | collective-permute-start | bytes 393224 | tf_op jit(solution)/shard_map/ppermute | solution.py:307
  28.9 1.9 %collective-permute-done.7.far_ref = bf16[256,256]{1,0:T(8,128)(2,1)S(1)} collective-permute-done((bf16[256,256]{1,0:T(8,128)(2,1)S(1)}, bf16[256,256]{1,0:T(8,128)(2,1)S(1)}, u32[]{:S(2)}, u32[]{:S(2)}) %collective-permute-start.7) | collective-permute-done | bytes 131104 | tf_op jit(solution)/shard_map/ppermute | solution.py:307
  30.9 0.1 collective-permute-start.10
  31.0 3.5 %collective-permute-start.13 = (bf16[256,256]{1,0:T(8,128)(2,1)S(1)}, bf16[256,256]{1,0:T(8,128)(2,1)S(1)}, u32[]{:S(2)}, u32[]{:S(2)}) collective-permute-start(bf16[256,256]{1,0:T(8,128)(2,1)S(1)} %get-tuple-element.42), channel_id=1, source_target_pairs={{0,9},{1,8},{4,13},{5,12},{8,1},{9,0},{12,5},{13,4},{2,11},{3,10},... | collective-permute-start | bytes 393224 | tf_op jit(solution)/shard_map/ppermute | solution.py:307
  34.4 0.0 collective-permute-start.8
  34.4 1.6 %collective-permute-done.9.refs_2_ = bf16[256,256]{1,0:T(8,128)(2,1)S(1)} collective-permute-done((bf16[256,256]{1,0:T(8,128)(2,1)S(1)}, bf16[256,256]{1,0:T(8,128)(2,1)S(1)}, u32[]{:S(2)}, u32[]{:S(2)}) %collective-permute-start.9) | collective-permute-done | bytes 131104 | tf_op jit(solution)/shard_map/ppermute | solution.py:307
  36.0 1.4 %collective-permute-done.12.refs_4_ = bf16[256,256]{1,0:T(8,128)(2,1)S(1)} collective-permute-done((bf16[256,256]{1,0:T(8,128)(2,1)S(1)}, bf16[256,256]{1,0:T(8,128)(2,1)S(1)}, u32[]{:S(2)}, u32[]{:S(2)}) %collective-permute-start.12) | collective-permute-done | bytes 131104 | tf_op jit(solution)/shard_map/ppermute | solution.py:307
  37.4 3.1 %collective-permute-done.10.refs_3_ = bf16[256,256]{1,0:T(8,128)(2,1)S(1)} collective-permute-done((bf16[256,256]{1,0:T(8,128)(2,1)S(1)}, bf16[256,256]{1,0:T(8,128)(2,1)S(1)}, u32[]{:S(2)}, u32[]{:S(2)}) %collective-permute-start.10) | collective-permute-done | bytes 131104 | tf_op jit(solution)/shard_map/ppermute | solution.py:307
  40.6 1.4 %collective-permute-done.13.refs_5_ = bf16[256,256]{1,0:T(8,128)(2,1)S(1)} collective-permute-done((bf16[256,256]{1,0:T(8,128)(2,1)S(1)}, bf16[256,256]{1,0:T(8,128)(2,1)S(1)}, u32[]{:S(2)}, u32[]{:S(2)}) %collective-permute-start.13) | collective-permute-done | bytes 131104 | tf_op jit(solution)/shard_map/ppermute | solution.py:307
  41.9 0.0 collective-permute-done.8.refs_1_
  42.0 0.9 %total.1 = f32[1,256,512]{2,1,0:T(8,128)} custom-call(f32[256,256]{1,0:T(8,128)S(1)} %get-tuple-element.34.refs_0_, bf16[256,256]{1,0:T(8,128)(2,1)S(1)} %collective-permute-done.8.refs_1_, bf16[256,256]{1,0:T(8,128)(2,1)S(1)} %collective-permute-done.9.refs_2_, bf16[256,256]{1,0:T(8,128)(2,1)S(1)} %collective-permute-done.10.refs_3_, ...), custom_call_target="tpu_custom_call" | custom-call | tf_op jit(solution)/shard_map/total/pallas_call | solution.py:456
  (3 shorter events, 0.1 us)
Async XLA Ops:
  3.0 7.3 %collective-permute-start = (f32[1,16,256]{2,1,0:T(8,128)}, f32[1,16,256]{2,1,0:T(8,128)S(1)}, u32[]{:S(2)}, u32[]{:S(2)}) collective-permute-start(f32[1,16,256]{2,1,0:T(8,128)} %get-tuple-element.25), channel_id=1, source_target_pairs={{0,1},{1,0},{2,3},{3,2},{4,5},{5,4},{6,7},{7,6},{8,9},{9,8},{10,11... | collective-permute-start | bytes 49160 | tf_op jit(solution)/shard_map/ppermute | solution.py:299
  3.5 13.8 %collective-permute-start.1 = (bf16[384,256]{1,0:T(8,128)(2,1)}, bf16[384,256]{1,0:T(8,128)(2,1)S(1)}, u32[]{:S(2)}, u32[]{:S(2)}) collective-permute-start(bf16[384,256]{1,0:T(8,128)(2,1)} %get-tuple-element.30), channel_id=1, source_target_pairs={{0,4},{4,8},{8,12},{12,0},{1,5},{5,9},{9,13},{13,1},{2,6},{6,10},{... | collective-permute-start | bytes 589832 | tf_op jit(solution)/shard_map/ppermute | solution.py:299
  6.1 11.4 %collective-permute-start.2 = (bf16[384,256]{1,0:T(8,128)(2,1)}, bf16[384,256]{1,0:T(8,128)(2,1)S(1)}, u32[]{:S(2)}, u32[]{:S(2)}) collective-permute-start(bf16[384,256]{1,0:T(8,128)(2,1)} %get-tuple-element.31), channel_id=1, source_target_pairs={{0,12},{4,0},{8,4},{12,8},{1,13},{5,1},{9,5},{13,9},{2,14},{6,2},{... | collective-permute-start | bytes 589832 | tf_op jit(solution)/shard_map/ppermute | solution.py:299
  8.3 9.3 %collective-permute-start.4 = (bf16[128,768]{1,0:T(8,128)(2,1)}, bf16[128,768]{1,0:T(8,128)(2,1)S(1)}, u32[]{:S(2)}, u32[]{:S(2)}) collective-permute-start(bf16[128,768]{1,0:T(8,128)(2,1)} %get-tuple-element.32), channel_id=1, source_target_pairs={{0,2},{2,0},{1,3},{3,1},{4,6},{6,4},{5,7},{7,5},{8,10},{10,8},{9,1... | collective-permute-start | bytes 589832 | tf_op jit(solution)/shard_map/ppermute | solution.py:299
  9.9 9.7 %collective-permute-start.5 = (bf16[128,768]{1,0:T(8,128)(2,1)}, bf16[128,768]{1,0:T(8,128)(2,1)S(1)}, u32[]{:S(2)}, u32[]{:S(2)}) collective-permute-start(bf16[128,768]{1,0:T(8,128)(2,1)} %get-tuple-element.33), channel_id=1, source_target_pairs={{0,2},{2,0},{1,3},{3,1},{4,6},{6,4},{5,7},{7,5},{8,10},{10,8},{9,1... | collective-permute-start | bytes 589832 | tf_op jit(solution)/shard_map/ppermute | solution.py:299
  10.3 10.9 %collective-permute-start.3 = (bf16[256,768]{1,0:T(8,128)(2,1)}, bf16[256,768]{1,0:T(8,128)(2,1)S(1)}, u32[]{:S(2)}, u32[]{:S(2)}) collective-permute-start(bf16[256,768]{1,0:T(8,128)(2,1)} %get-tuple-element.26.turned_ref.refs_0_), channel_id=1, source_target_pairs={{0,1},{1,0},{2,3},{3,2},{4,5},{5,4},{6,7},{7,6},{8,9},{9,8},{10,11... | collective-permute-start | bytes 1179656 | tf_op jit(solution)/shard_map/ppermute | solution.py:299
  10.3 1.0 %copy-start = (bf16[256,768]{1,0:T(8,128)(2,1)S(1)}, bf16[256,768]{1,0:T(8,128)(2,1)}, u32[]{:S(2)}) copy-start(bf16[256,768]{1,0:T(8,128)(2,1)} %get-tuple-element.26.turned_ref.refs_0_) | copy-start | bytes 1179652
  11.3 0.9 %copy-start.1 = (f32[11,16,256]{2,1,0:T(8,128)S(1)}, f32[11,16,256]{2,1,0:T(8,128)}, u32[]{:S(2)}) copy-start(f32[11,16,256]{2,1,0:T(8,128)} %get-tuple-element.24.source_ref) | copy-start | bytes 540676
  19.6 1.8 %collective-permute-start.6 = (bf16[256,768]{1,0:T(8,128)(2,1)S(1)}, bf16[256,768]{1,0:T(8,128)(2,1)S(1)}, u32[]{:S(2)}, u32[]{:S(2)}) collective-permute-start(bf16[256,768]{1,0:T(8,128)(2,1)S(1)} %relay.1.refs_2_), channel_id=1, source_target_pairs={{0,1},{1,0},{2,3},{3,2},{4,5},{5,4},{6,7},{7,6},{8,9},{9,8},{10,11... | collective-permute-start | bytes 1179656 | tf_op jit(solution)/shard_map/ppermute | solution.py:299
  21.7 6.4 %collective-permute-start.11 = (bf16[256,256]{1,0:T(8,128)(2,1)S(1)}, bf16[256,256]{1,0:T(8,128)(2,1)S(1)}, u32[]{:S(2)}, u32[]{:S(2)}) collective-permute-start(bf16[256,256]{1,0:T(8,128)(2,1)S(1)} %far.2.after), channel_id=1, source_target_pairs={{0,4},{1,5},{4,0},{5,1},{8,12},{9,13},{12,8},{13,9},{2,6},{3,7},{6... | collective-permute-start | bytes 393224 | tf_op jit(solution)/shard_map/ppermute | solution.py:307
  22.0 8.8 %collective-permute-start.7 = (bf16[256,256]{1,0:T(8,128)(2,1)S(1)}, bf16[256,256]{1,0:T(8,128)(2,1)S(1)}, u32[]{:S(2)}, u32[]{:S(2)}) collective-permute-start(bf16[256,256]{1,0:T(8,128)(2,1)S(1)} %far.3), channel_id=1, source_target_pairs={{0,4},{1,5},{4,0},{5,1},{8,12},{9,13},{12,8},{13,9},{2,6},{3,7},{6... | collective-permute-start | bytes 393224 | tf_op jit(solution)/shard_map/ppermute | solution.py:307
  25.2 10.8 %collective-permute-start.9 = (bf16[256,256]{1,0:T(8,128)(2,1)S(1)}, bf16[256,256]{1,0:T(8,128)(2,1)S(1)}, u32[]{:S(2)}, u32[]{:S(2)}) collective-permute-start(bf16[256,256]{1,0:T(8,128)(2,1)S(1)} %get-tuple-element.39), channel_id=1, source_target_pairs={{0,4},{1,5},{4,0},{5,1},{8,12},{9,13},{12,8},{13,9},{2,6},{3,7},{6... | collective-permute-start | bytes 393224 | tf_op jit(solution)/shard_map/ppermute | solution.py:307
  28.1 9.3 %collective-permute-start.12 = (bf16[256,256]{1,0:T(8,128)(2,1)S(1)}, bf16[256,256]{1,0:T(8,128)(2,1)S(1)}, u32[]{:S(2)}, u32[]{:S(2)}) collective-permute-start(bf16[256,256]{1,0:T(8,128)(2,1)S(1)} %add.3), channel_id=1, source_target_pairs={{0,8},{1,9},{4,12},{5,13},{8,0},{9,1},{12,4},{13,5},{2,10},{3,11},... | collective-permute-start | bytes 393224 | tf_op jit(solution)/shard_map/ppermute | solution.py:307
  30.9 9.7 %collective-permute-start.10 = (bf16[256,256]{1,0:T(8,128)(2,1)S(1)}, bf16[256,256]{1,0:T(8,128)(2,1)S(1)}, u32[]{:S(2)}, u32[]{:S(2)}) collective-permute-start(bf16[256,256]{1,0:T(8,128)(2,1)S(1)} %get-tuple-element.40), channel_id=1, source_target_pairs={{0,5},{1,4},{4,1},{5,0},{8,13},{9,12},{12,9},{13,8},{2,7},{3,6},{6... | collective-permute-start | bytes 393224 | tf_op jit(solution)/shard_map/ppermute | solution.py:307
  31.0 11.0 %collective-permute-start.13 = (bf16[256,256]{1,0:T(8,128)(2,1)S(1)}, bf16[256,256]{1,0:T(8,128)(2,1)S(1)}, u32[]{:S(2)}, u32[]{:S(2)}) collective-permute-start(bf16[256,256]{1,0:T(8,128)(2,1)S(1)} %get-tuple-element.42), channel_id=1, source_target_pairs={{0,9},{1,8},{4,13},{5,12},{8,1},{9,0},{12,5},{13,4},{2,11},{3,10},... | collective-permute-start | bytes 393224 | tf_op jit(solution)/shard_map/ppermute | solution.py:307
  34.4 7.5 %collective-permute-start.8 = (bf16[256,256]{1,0:T(8,128)(2,1)S(1)}, bf16[256,256]{1,0:T(8,128)(2,1)S(1)}, u32[]{:S(2)}, u32[]{:S(2)}) collective-permute-start(bf16[256,256]{1,0:T(8,128)(2,1)S(1)} %get-tuple-element.38), channel_id=1, source_target_pairs={{0,1},{1,0},{4,5},{5,4},{8,9},{9,8},{12,13},{13,12},{2,3},{3,2},{6... | collective-permute-start | bytes 393224 | tf_op jit(solution)/shard_map/ppermute | solution.py:307

commit v11 on v9

--- a/solution.py
+++ b/solution.py
@@ -184,7 +184,7 @@
         given_ref[...] = got_ref[...]
 
 
-def flux_kernel(e, part_ref, hi_ref, lo_ref, below_ref, above_ref, flux_ref, halo_ref):
+def flux_kernel(e, part_ref, hi_ref, lo_ref, below_ref, above_ref, after, flux_ref, halo_ref):
     count = below_ref.shape[0] // 3
     for b in range(3):
         at = 2 * b * count
@@ -243,6 +243,18 @@
     terms_of(quarter_refs, store)
 
 
+def early_kernel(flux_ref, *refs):
+    *quarter_refs, far_ref = refs
+    home, me, core = lax.axis_index("dom"), lax.axis_index("blk"), lax.axis_index("dir")
+    owned = (me == home // 2, me != home // 2)
+    odd = ((core ^ home) & 1) == 1
+    for use, quarter_ref in zip(owned, (quarter_refs[1], quarter_refs[0])):
+
+        @pl.when(jnp.logical_and(use, odd))
+        def _():
+            far_ref[...] = dot(quarter_ref[...], flux_ref[...]).astype(BF16)
+
+
 def near_kernel(flux0_ref, flux1_ref, *refs):
     *quarter_refs, near0_ref, near1_ref, add0_ref, add1_ref, keep_ref, give_ref = refs
     home = lax.axis_index("dom")
@@ -257,6 +269,16 @@
                     out_ref[...] = dot(turned_ref[...], flux_ref[...]).astype(out_ref.dtype)
 
     terms_of(quarter_refs, store)
+
+
+def first_add_kernel(early_ref, late_ref, add_ref, sum_ref):
+    home, core = lax.axis_index("dom"), lax.axis_index("dir")
+    early = ((core ^ home) & 1) == 0
+    for came, far_ref in ((early, early_ref), (jnp.logical_not(early), late_ref)):
+
+        @pl.when(came)
+        def _():
+            sum_ref[...] = (add_ref[...] + far_ref[...].astype(F32)).astype(BF16)
 
 
 def add_kernel(far_ref, add_ref, *refs):
@@ -295,6 +317,14 @@
     domains = lax.axis_size("dom")
     pairs = [
         (2 * d + c, 2 * (d ^ away) + (c ^ other_core)) for d in range(domains) for c in range(2)
+    ]
+    return lax.ppermute(value, ("dom", "dir"), pairs)
+
+
+def swap_some(value, odd):
+    domains = lax.axis_size("dom")
+    pairs = [
+        (2 * d + c, 2 * (d ^ 1) + c) for d in range(domains) for c in range(2) if (c ^ d) & 1 == odd
     ]
     return lax.ppermute(value, ("dom", "dir"), pairs)
 
@@ -385,11 +415,11 @@
     for quarter in quarters:
         given += [quarter, shift(quarter, "dir", 1)]
 
-    def flux_of(e):
+    def flux_of(e, after):
         return pl.pallas_call(
             functools.partial(flux_kernel, e),
             out_shape=shape((rows, half), BF16),
-            in_specs=[vmem] * 5,
+            in_specs=[vmem] * 5 + [anywhere],
             out_specs=vmem,
             scratch_shapes=[pltpu.VMEM((6 * count, half), BF16)],
             compiler_params=params(16),
@@ -397,7 +427,7 @@
                 flops=10**9, bytes_accessed=10**6, transcendentals=0
             ),
             name="flux",
-        )(partial_flux, hi, lo, below, above)
+        )(partial_flux, hi, lo, below, above, after)
 
     scale = (3.0 * atoms * domains) ** (-0.5)
     result = shape((1, block, cols), F32)
@@ -416,10 +446,20 @@
                 name="far",
             )(after, flux, *given)
 
-        flux0, flux1 = flux_of(0), flux_of(1)
+        flux0 = flux_of(0, turned)
+        early = pl.pallas_call(
+            early_kernel,
+            out_shape=sent,
+            in_specs=[vmem] * 3,
+            out_specs=vmem,
+            compiler_params=params(16),
+            cost_estimate=cost,
+            name="early",
+        )(flux0, given[0], given[2])
+        flux1 = flux_of(1, early)
         far0 = far_of(flux0, flux1)
         far1 = far_of(flux1, far0)
-        far0, far1 = swap(far0, 1, 0), swap(far1, 1, 0)
+        early, late, far1 = swap_some(early, 1), swap_some(far0, 0), swap(far1, 1, 0)
         near0, near1, add0, add1, keep, give = pl.pallas_call(
             near_kernel,
             out_shape=(sent, sent, kept, kept, kept, sent),
@@ -441,7 +481,15 @@
             )(far, add, *handed_on)
 
         near0 = swap(near0, 1, 0)
-        sum0 = swap(sum_of(far0, add0)[0], 2, 0)
+        sum0 = pl.pallas_call(
+            first_add_kernel,
+            out_shape=sent,
+            in_specs=[vmem] * 3,
+            out_specs=vmem,
+            compiler_params=params(16),
+            name="add",
+        )(early, late, add0)
+        sum0 = swap(sum0, 2, 0)
         sum1, near1, give = sum_of(far1, add1, near1, give)
         sum1, near1, give = swap(sum1, 2, 1), swap(near1, 1, 1), swap(give, 0, 1)
         return pl.pallas_call(
@@ -464,7 +512,7 @@
         out_specs=vmem,
         compiler_params=params(16),
         name="couple",
-    )(flux_of(0), flux_of(1), *given)
+    )(flux_of(0, below), flux_of(1, below), *given)
     terms = lax.all_to_all(terms, ("dom", "dir"), split_axis=0, concat_axis=0, tiled=True)
     return pl.pallas_call(
         lambda *refs: sum_kernel(scale, *refs),

time: 42.9 us -> 46.1 us (1.075)
  waiting for transfers between devices: 12.5 us -> 14.1 us
  starting transfers between devices: 16 us -> 17.4 us
    ppermute x0 -> x2, starting transfers between devices: none -> 5.85 us  [swap_some(): return lax.ppermute(value, ('dom', 'dir'), pairs)]
    ppermute x7 -> x6, starting transfers between devices: 8.87 us -> 4.45 us  [swap(): return lax.ppermute(value, ('dom', 'dir'), pairs)]
    ppermute x7 -> x6, waiting for transfers between devices: 10.4 us -> 12.1 us  [swap(): return lax.ppermute(value, ('dom', 'dir'), pairs)]
  transfers between devices with their start and end apart: 13 -> 14, of which waited for: 7 -> 4; matrix products, arithmetic and copies ran while one was open for 0% -> 0% of each run, Pallas kernels for 19% -> 19%
where the time goes in v11:
time: 46.1 us; the launch traced here: 45.9 us
  starting transfers between devices  17.4 us (38%)
  waiting for transfers between devices  14.1 us (31%)
  Pallas kernels  12.3 us (27%)
  local copies, waits for them, and re-layouts  1.92 us (4%)
    ppermute x6, waiting for transfers between devices, swap(): return lax.ppermute(value, ('dom', 'dir'), pairs)  12.1 us
    ppermute x6, starting transfers between devices, shift(): lax.ppermute(value, axis, [(i, (i + by) % length) for i in range(length)])  7.14 us
    ppermute x2, starting transfers between devices, swap_some(): return lax.ppermute(value, ('dom', 'dir'), pairs)  5.85 us
    pallas_call x1, Pallas kernels, per_device(): pl.pallas_call(weights_kernel, out_shape=(shape((2 * rows, half), F32), s...  5.13 us
    ppermute x6, starting transfers between devices, swap(): return lax.ppermute(value, ('dom', 'dir'), pairs)  4.45 us
    pallas_call x1, Pallas kernels, per_device(): pl.pallas_call(prep_kernel, out_shape=(*prepared, shape((11, *neighbours....  2.84 us
    ppermute x6, waiting for transfers between devices, shift(): lax.ppermute(value, axis, [(i, (i + by) % length) for i in range(length)])  2 us
    unnamed x4, local copies, waits for them, and re-layouts  1.92 us
  transfers between devices with their start and end apart: 14, of which 4 were waited for; matrix products, arithmetic and copies ran while one was open for 0% of the time, Pallas kernels for 19%

profile of v11, /device:TPU:0, one launch (start us, length us, event | category | flops | bytes accessed | tf_op | source)
XLA Modules:
  0.0 45.9 jit_solution(8802489390330570427)
XLA Ops:
  0.0 2.8 %prep.1 = (bf16[256,768]{1,0:T(8,128)(2,1)}, bf16[384,256]{1,0:T(8,128)(2,1)}, bf16[384,256]{1,0:T(8,128)(2,1)}, f32[11,16,256]{2,1,0:T(8,128)}, f32[1,16,256]{2,1,0:T(8,128)}) custom-call(bf16[768,512]{1,0:T(8,128)(2,1)} %v_hbm.1, s32[1,128]{1,0:T(1,128)} %bitcast.4, s32[1,128]{1,0:T(1,128)} %bitcast.5, f32[9,16,256]{2,1,0:T(8,128)} %bitcast.3, ...), custom_call_target="tpu_custom_call" | custom-call | tf_op jit(solution)/shard_map/prep/pallas_call | solution.py:354
  2.8 0.5 %collective-permute-start = (f32[1,16,256]{2,1,0:T(8,128)}, f32[1,16,256]{2,1,0:T(8,128)S(1)}, u32[]{:S(2)}, u32[]{:S(2)}) collective-permute-start(f32[1,16,256]{2,1,0:T(8,128)} %get-tuple-element.23), channel_id=1, source_target_pairs={{0,1},{1,0},{2,3},{3,2},{4,5},{5,4},{6,7},{7,6},{8,9},{9,8},{10,11... | collective-permute-start | bytes 49160 | tf_op jit(solution)/shard_map/ppermute | solution.py:313
  3.4 2.6 %collective-permute-start.3 = (bf16[256,768]{1,0:T(8,128)(2,1)}, bf16[256,768]{1,0:T(8,128)(2,1)S(1)}, u32[]{:S(2)}, u32[]{:S(2)}) collective-permute-start(bf16[256,768]{1,0:T(8,128)(2,1)} %get-tuple-element.24.turned_ref.after.refs_0_), channel_id=1, source_target_pairs={{0,2},{2,0},{1,3},{3,1},{4,6},{6,4},{5,7},{7,5},{8,10},{10,8},{9,1... | collective-permute-start | bytes 1179656 | tf_op jit(solution)/shard_map/ppermute | solution.py:313
  5.9 0.2 collective-permute-start.4
  6.1 1.6 %collective-permute-start.1 = (bf16[384,256]{1,0:T(8,128)(2,1)}, bf16[384,256]{1,0:T(8,128)(2,1)S(1)}, u32[]{:S(2)}, u32[]{:S(2)}) collective-permute-start(bf16[384,256]{1,0:T(8,128)(2,1)} %get-tuple-element.28), channel_id=1, source_target_pairs={{0,4},{4,8},{8,12},{12,0},{1,5},{5,9},{9,13},{13,1},{2,6},{6,10},{... | collective-permute-start | bytes 589832 | tf_op jit(solution)/shard_map/ppermute | solution.py:313
  7.7 2.2 %collective-permute-start.2 = (bf16[384,256]{1,0:T(8,128)(2,1)}, bf16[384,256]{1,0:T(8,128)(2,1)S(1)}, u32[]{:S(2)}, u32[]{:S(2)}) collective-permute-start(bf16[384,256]{1,0:T(8,128)(2,1)} %get-tuple-element.29), channel_id=1, source_target_pairs={{0,12},{4,0},{8,4},{12,8},{1,13},{5,1},{9,5},{13,9},{2,14},{6,2},{... | collective-permute-start | bytes 589832 | tf_op jit(solution)/shard_map/ppermute | solution.py:313
  9.9 0.0 collective-permute-done.other_ref
  9.9 0.0 copy-start
  9.9 1.0 %copy-done = bf16[256,768]{1,0:T(8,128)(2,1)S(1)} copy-done((bf16[256,768]{1,0:T(8,128)(2,1)S(1)}, bf16[256,768]{1,0:T(8,128)(2,1)}, u32[]{:S(2)}) %copy-start) | copy-done | bytes 393240
  10.9 0.0 copy-start.1
  10.9 0.9 %copy-done.1 = f32[11,16,256]{2,1,0:T(8,128)S(1)} copy-done((f32[11,16,256]{2,1,0:T(8,128)S(1)}, f32[11,16,256]{2,1,0:T(8,128)}, u32[]{:S(2)}) %copy-start.1) | copy-done | bytes 180248
  11.8 5.1 %weights.1 = (f32[1536,256]{1,0:T(8,128)S(1)}, bf16[1536,768]{1,0:T(8,128)(2,1)S(1)}, bf16[1536,768]{1,0:T(8,128)(2,1)S(1)}) custom-call(f32[11,16,256]{2,1,0:T(8,128)S(1)} %copy-done.1, f32[1,16,256]{2,1,0:T(8,128)S(1)} %collective-permute-done.other_ref, bf16[256,768]{1,0:T(8,128)(2,1)S(1)} %copy-done), custom_call_target="tpu_custom_call" | custom-call | flops 8000000000 | bytes 10000000 | tf_op jit(solution)/shard_map/weights/pallas_call | solution.py:385
  17.0 0.0 collective-permute-done.1.below_ref.below_hbm
  17.0 2.0 %collective-permute-done.2.above_ref.above_hbm = bf16[384,256]{1,0:T(8,128)(2,1)S(1)} collective-permute-done((bf16[384,256]{1,0:T(8,128)(2,1)}, bf16[384,256]{1,0:T(8,128)(2,1)S(1)}, u32[]{:S(2)}, u32[]{:S(2)}) %collective-permute-start.2) | collective-permute-done | bytes 196640 | tf_op jit(solution)/shard_map/ppermute | solution.py:313
  19.0 0.0 collective-permute-done.3.refs_0_
  19.0 0.1 collective-permute-start.5
  19.1 0.8 %flux.2.flux_ref.flux0_ref = bf16[768,256]{1,0:T(8,128)(2,1)S(1)} custom-call(f32[1536,256]{1,0:T(8,128)S(1)} %get-tuple-element.25.part_ref.part_hbm, bf16[1536,768]{1,0:T(8,128)(2,1)S(1)} %get-tuple-element.26.hi_ref, bf16[1536,768]{1,0:T(8,128)(2,1)S(1)} %get-tuple-element.27.lo_ref, bf16[384,256]{1,0:T(8,128)(2,1)S(1)} %collective-permute-done.1.below_ref.below_hbm, ...), custom_call_target="tpu_custom_call" | custom-call | flops 1000000000 | bytes 1000000 | tf_op jit(solution)/shard_map/flux/pallas_call | solution.py:419
  19.9 1.3 %collective-permute-start.10 = (bf16[256,256]{1,0:T(8,128)(2,1)S(1)}, bf16[256,256]{1,0:T(8,128)(2,1)S(1)}, u32[]{:S(2)}, u32[]{:S(2)}) collective-permute-start(bf16[256,256]{1,0:T(8,128)(2,1)S(1)} %early.1.after), channel_id=1, source_target_pairs={{1,5},{4,0},{9,13},{12,8},{3,7},{6,2},{11,15},{14,10},{17,21},{20,... | collective-permute-start | bytes 393224 | tf_op jit(solution)/shard_map/ppermute | solution.py:329
  21.2 0.8 %flux.3.flux1_ref.after.flux_ref = bf16[768,256]{1,0:T(8,128)(2,1)S(1)} custom-call(f32[1536,256]{1,0:T(8,128)S(1)} %get-tuple-element.25.part_ref.part_hbm, bf16[1536,768]{1,0:T(8,128)(2,1)S(1)} %get-tuple-element.26.hi_ref, bf16[1536,768]{1,0:T(8,128)(2,1)S(1)} %get-tuple-element.27.lo_ref, ...), custom_call_target="tpu_custom_call" | custom-call | flops 1000000000 | bytes 1000000 | tf_op jit(solution)/shard_map/flux/pallas_call | solution.py:419
  22.0 0.0 collective-permute-done.4.refs_1_
  22.0 0.0 collective-permute-done.5.refs_3_
  22.0 0.3 far.2.after
  22.3 4.6 %collective-permute-start.11 = (bf16[256,256]{1,0:T(8,128)(2,1)S(1)}, bf16[256,256]{1,0:T(8,128)(2,1)S(1)}, u32[]{:S(2)}, u32[]{:S(2)}) collective-permute-start(bf16[256,256]{1,0:T(8,128)(2,1)S(1)} %far.2.after), channel_id=1, source_target_pairs={{0,4},{5,1},{8,12},{13,9},{2,6},{7,3},{10,14},{15,11},{16,20},{21,... | collective-permute-start | bytes 393224 | tf_op jit(solution)/shard_map/ppermute | solution.py:329
  26.9 0.3 far.3
  27.2 0.1 collective-permute-start.6
  27.3 1.2 %near.1 = (bf16[256,256]{1,0:T(8,128)(2,1)S(1)}, bf16[256,256]{1,0:T(8,128)(2,1)S(1)}, f32[256,256]{1,0:T(8,128)S(1)}, f32[256,256]{1,0:T(8,128)S(1)}, f32[256,2...) custom-call(bf16[768,256]{1,0:T(8,128)(2,1)S(1)} %flux.2.flux_ref.flux0_ref, ...), custom_call_target="tpu_custom_call" | custom-call | flops 400000000 | bytes 1000000 | tf_op jit(solution)/shard_map/near/pallas_call | solution.py:463
  28.4 2.1 %collective-permute-start.8 = (bf16[256,256]{1,0:T(8,128)(2,1)S(1)}, bf16[256,256]{1,0:T(8,128)(2,1)S(1)}, u32[]{:S(2)}, u32[]{:S(2)}) collective-permute-start(bf16[256,256]{1,0:T(8,128)(2,1)S(1)} %get-tuple-element.35), channel_id=1, source_target_pairs={{0,4},{1,5},{4,0},{5,1},{8,12},{9,13},{12,8},{13,9},{2,6},{3,7},{6... | collective-permute-start | bytes 393224 | tf_op jit(solution)/shard_map/ppermute | solution.py:321
  30.5 0.0 collective-permute-done.10.early_ref
  30.5 0.0 collective-permute-done.11.late_ref
  30.5 1.3 %collective-permute-start.12 = (bf16[256,256]{1,0:T(8,128)(2,1)S(1)}, bf16[256,256]{1,0:T(8,128)(2,1)S(1)}, u32[]{:S(2)}, u32[]{:S(2)}) collective-permute-start(bf16[256,256]{1,0:T(8,128)(2,1)S(1)} %add.3), channel_id=1, source_target_pairs={{0,8},{1,9},{4,12},{5,13},{8,0},{9,1},{12,4},{13,5},{2,10},{3,11},... | collective-permute-start | bytes 393224 | tf_op jit(solution)/shard_map/ppermute | solution.py:321
  31.9 3.3 %collective-permute-done.6.far_ref = bf16[256,256]{1,0:T(8,128)(2,1)S(1)} collective-permute-done((bf16[256,256]{1,0:T(8,128)(2,1)S(1)}, bf16[256,256]{1,0:T(8,128)(2,1)S(1)}, u32[]{:S(2)}, u32[]{:S(2)}) %collective-permute-start.6) | collective-permute-done | bytes 131104 | tf_op jit(solution)/shard_map/ppermute | solution.py:321
  35.2 0.1 collective-permute-start.13
  35.3 0.1 collective-permute-start.7
  35.4 0.8 %collective-permute-start.9 = (bf16[256,256]{1,0:T(8,128)(2,1)S(1)}, bf16[256,256]{1,0:T(8,128)(2,1)S(1)}, u32[]{:S(2)}, u32[]{:S(2)}) collective-permute-start(bf16[256,256]{1,0:T(8,128)(2,1)S(1)} %get-tuple-element.36), channel_id=1, source_target_pairs={{0,5},{1,4},{4,1},{5,0},{8,13},{9,12},{12,9},{13,8},{2,7},{3,6},{6... | collective-permute-start | bytes 393224 | tf_op jit(solution)/shard_map/ppermute | solution.py:321
  36.2 3.3 %collective-permute-done.8.refs_2_ = bf16[256,256]{1,0:T(8,128)(2,1)S(1)} collective-permute-done((bf16[256,256]{1,0:T(8,128)(2,1)S(1)}, bf16[256,256]{1,0:T(8,128)(2,1)S(1)}, u32[]{:S(2)}, u32[]{:S(2)}) %collective-permute-start.8) | collective-permute-done | bytes 131104 | tf_op jit(solution)/shard_map/ppermute | solution.py:321
  39.5 0.0 collective-permute-done.12.refs_4_
  39.5 5.5 %collective-permute-done.13.refs_5_ = bf16[256,256]{1,0:T(8,128)(2,1)S(1)} collective-permute-done((bf16[256,256]{1,0:T(8,128)(2,1)S(1)}, bf16[256,256]{1,0:T(8,128)(2,1)S(1)}, u32[]{:S(2)}, u32[]{:S(2)}) %collective-permute-start.13) | collective-permute-done | bytes 131104 | tf_op jit(solution)/shard_map/ppermute | solution.py:321
  45.1 0.0 collective-permute-done.7.refs_1_
  45.1 0.0 collective-permute-done.9.refs_3_
  45.1 0.9 %total.1 = f32[1,256,512]{2,1,0:T(8,128)} custom-call(f32[256,256]{1,0:T(8,128)S(1)} %get-tuple-element.30.refs_0_, bf16[256,256]{1,0:T(8,128)(2,1)S(1)} %collective-permute-done.7.refs_1_, bf16[256,256]{1,0:T(8,128)(2,1)S(1)} %collective-permute-done.8.refs_2_, bf16[256,256]{1,0:T(8,128)(2,1)S(1)} %collective-permute-done.9.refs_3_, ...), custom_call_target="tpu_custom_call" | custom-call | tf_op jit(solution)/shard_map/total/pallas_call | solution.py:495
  (4 shorter events, 0.1 us)
Async XLA Ops:
  2.8 7.1 %collective-permute-start = (f32[1,16,256]{2,1,0:T(8,128)}, f32[1,16,256]{2,1,0:T(8,128)S(1)}, u32[]{:S(2)}, u32[]{:S(2)}) collective-permute-start(f32[1,16,256]{2,1,0:T(8,128)} %get-tuple-element.23), channel_id=1, source_target_pairs={{0,1},{1,0},{2,3},{3,2},{4,5},{5,4},{6,7},{7,6},{8,9},{9,8},{10,11... | collective-permute-start | bytes 49160 | tf_op jit(solution)/shard_map/ppermute | solution.py:313
  3.4 15.6 %collective-permute-start.3 = (bf16[256,768]{1,0:T(8,128)(2,1)}, bf16[256,768]{1,0:T(8,128)(2,1)S(1)}, u32[]{:S(2)}, u32[]{:S(2)}) collective-permute-start(bf16[256,768]{1,0:T(8,128)(2,1)} %get-tuple-element.24.turned_ref.after.refs_0_), channel_id=1, source_target_pairs={{0,2},{2,0},{1,3},{3,1},{4,6},{6,4},{5,7},{7,5},{8,10},{10,8},{9,1... | collective-permute-start | bytes 1179656 | tf_op jit(solution)/shard_map/ppermute | solution.py:313
  5.9 16.0 %collective-permute-start.4 = (bf16[256,768]{1,0:T(8,128)(2,1)}, bf16[256,768]{1,0:T(8,128)(2,1)S(1)}, u32[]{:S(2)}, u32[]{:S(2)}) collective-permute-start(bf16[256,768]{1,0:T(8,128)(2,1)} %get-tuple-element.24.turned_ref.after.refs_0_), channel_id=1, source_target_pairs={{0,1},{1,0},{2,3},{3,2},{4,5},{5,4},{6,7},{7,6},{8,9},{9,8},{10,11... | collective-permute-start | bytes 1179656 | tf_op jit(solution)/shard_map/ppermute | solution.py:313
  6.1 10.9 %collective-permute-start.1 = (bf16[384,256]{1,0:T(8,128)(2,1)}, bf16[384,256]{1,0:T(8,128)(2,1)S(1)}, u32[]{:S(2)}, u32[]{:S(2)}) collective-permute-start(bf16[384,256]{1,0:T(8,128)(2,1)} %get-tuple-element.28), channel_id=1, source_target_pairs={{0,4},{4,8},{8,12},{12,0},{1,5},{5,9},{9,13},{13,1},{2,6},{6,10},{... | collective-permute-start | bytes 589832 | tf_op jit(solution)/shard_map/ppermute | solution.py:313
  7.7 11.3 %collective-permute-start.2 = (bf16[384,256]{1,0:T(8,128)(2,1)}, bf16[384,256]{1,0:T(8,128)(2,1)S(1)}, u32[]{:S(2)}, u32[]{:S(2)}) collective-permute-start(bf16[384,256]{1,0:T(8,128)(2,1)} %get-tuple-element.29), channel_id=1, source_target_pairs={{0,12},{4,0},{8,4},{12,8},{1,13},{5,1},{9,5},{13,9},{2,14},{6,2},{... | collective-permute-start | bytes 589832 | tf_op jit(solution)/shard_map/ppermute | solution.py:313
  9.9 1.0 %copy-start = (bf16[256,768]{1,0:T(8,128)(2,1)S(1)}, bf16[256,768]{1,0:T(8,128)(2,1)}, u32[]{:S(2)}) copy-start(bf16[256,768]{1,0:T(8,128)(2,1)} %get-tuple-element.24.turned_ref.after.refs_0_) | copy-start | bytes 1179652
  10.9 0.9 %copy-start.1 = (f32[11,16,256]{2,1,0:T(8,128)S(1)}, f32[11,16,256]{2,1,0:T(8,128)}, u32[]{:S(2)}) copy-start(f32[11,16,256]{2,1,0:T(8,128)} %get-tuple-element.22.source_ref) | copy-start | bytes 540676
  19.0 3.0 %collective-permute-start.5 = (bf16[256,768]{1,0:T(8,128)(2,1)S(1)}, bf16[256,768]{1,0:T(8,128)(2,1)S(1)}, u32[]{:S(2)}, u32[]{:S(2)}) collective-permute-start(bf16[256,768]{1,0:T(8,128)(2,1)S(1)} %relay.1.refs_1_.refs_2_), channel_id=1, source_target_pairs={{0,1},{1,0},{2,3},{3,2},{4,5},{5,4},{6,7},{7,6},{8,9},{9,8},{10,11... | collective-permute-start | bytes 1179656 | tf_op jit(solution)/shard_map/ppermute | solution.py:313
  19.9 10.6 %collective-permute-start.10 = (bf16[256,256]{1,0:T(8,128)(2,1)S(1)}, bf16[256,256]{1,0:T(8,128)(2,1)S(1)}, u32[]{:S(2)}, u32[]{:S(2)}) collective-permute-start(bf16[256,256]{1,0:T(8,128)(2,1)S(1)} %early.1.after), channel_id=1, source_target_pairs={{1,5},{4,0},{9,13},{12,8},{3,7},{6,2},{11,15},{14,10},{17,21},{20,... | collective-permute-start | bytes 393224 | tf_op jit(solution)/shard_map/ppermute | solution.py:329
  22.3 8.2 %collective-permute-start.11 = (bf16[256,256]{1,0:T(8,128)(2,1)S(1)}, bf16[256,256]{1,0:T(8,128)(2,1)S(1)}, u32[]{:S(2)}, u32[]{:S(2)}) collective-permute-start(bf16[256,256]{1,0:T(8,128)(2,1)S(1)} %far.2.after), channel_id=1, source_target_pairs={{0,4},{5,1},{8,12},{13,9},{2,6},{7,3},{10,14},{15,11},{16,20},{21,... | collective-permute-start | bytes 393224 | tf_op jit(solution)/shard_map/ppermute | solution.py:329
  27.2 8.0 %collective-permute-start.6 = (bf16[256,256]{1,0:T(8,128)(2,1)S(1)}, bf16[256,256]{1,0:T(8,128)(2,1)S(1)}, u32[]{:S(2)}, u32[]{:S(2)}) collective-permute-start(bf16[256,256]{1,0:T(8,128)(2,1)S(1)} %far.3), channel_id=1, source_target_pairs={{0,4},{1,5},{4,0},{5,1},{8,12},{9,13},{12,8},{13,9},{2,6},{3,7},{6... | collective-permute-start | bytes 393224 | tf_op jit(solution)/shard_map/ppermute | solution.py:321
  28.4 11.1 %collective-permute-start.8 = (bf16[256,256]{1,0:T(8,128)(2,1)S(1)}, bf16[256,256]{1,0:T(8,128)(2,1)S(1)}, u32[]{:S(2)}, u32[]{:S(2)}) collective-permute-start(bf16[256,256]{1,0:T(8,128)(2,1)S(1)} %get-tuple-element.35), channel_id=1, source_target_pairs={{0,4},{1,5},{4,0},{5,1},{8,12},{9,13},{12,8},{13,9},{2,6},{3,7},{6... | collective-permute-start | bytes 393224 | tf_op jit(solution)/shard_map/ppermute | solution.py:321
  30.5 9.0 %collective-permute-start.12 = (bf16[256,256]{1,0:T(8,128)(2,1)S(1)}, bf16[256,256]{1,0:T(8,128)(2,1)S(1)}, u32[]{:S(2)}, u32[]{:S(2)}) collective-permute-start(bf16[256,256]{1,0:T(8,128)(2,1)S(1)} %add.3), channel_id=1, source_target_pairs={{0,8},{1,9},{4,12},{5,13},{8,0},{9,1},{12,4},{13,5},{2,10},{3,11},... | collective-permute-start | bytes 393224 | tf_op jit(solution)/shard_map/ppermute | solution.py:321
  35.2 9.8 %collective-permute-start.13 = (bf16[256,256]{1,0:T(8,128)(2,1)S(1)}, bf16[256,256]{1,0:T(8,128)(2,1)S(1)}, u32[]{:S(2)}, u32[]{:S(2)}) collective-permute-start(bf16[256,256]{1,0:T(8,128)(2,1)S(1)} %get-tuple-element.38), channel_id=1, source_target_pairs={{0,9},{1,8},{4,13},{5,12},{8,1},{9,0},{12,5},{13,4},{2,11},{3,10},... | collective-permute-start | bytes 393224 | tf_op jit(solution)/shard_map/ppermute | solution.py:321
  35.3 9.8 %collective-permute-start.7 = (bf16[256,256]{1,0:T(8,128)(2,1)S(1)}, bf16[256,256]{1,0:T(8,128)(2,1)S(1)}, u32[]{:S(2)}, u32[]{:S(2)}) collective-permute-start(bf16[256,256]{1,0:T(8,128)(2,1)S(1)} %get-tuple-element.34), channel_id=1, source_target_pairs={{0,1},{1,0},{4,5},{5,4},{8,9},{9,8},{12,13},{13,12},{2,3},{3,2},{6... | collective-permute-start | bytes 393224 | tf_op jit(solution)/shard_map/ppermute | solution.py:321
  35.4 9.7 %collective-permute-start.9 = (bf16[256,256]{1,0:T(8,128)(2,1)S(1)}, bf16[256,256]{1,0:T(8,128)(2,1)S(1)}, u32[]{:S(2)}, u32[]{:S(2)}) collective-permute-start(bf16[256,256]{1,0:T(8,128)(2,1)S(1)} %get-tuple-element.36), channel_id=1, source_target_pairs={{0,5},{1,4},{4,1},{5,0},{8,13},{9,12},{12,9},{13,8},{2,7},{3,6},{6... | collective-permute-start | bytes 393224 | tf_op jit(solution)/shard_map/ppermute | solution.py:321

commit v12 on v9

--- a/solution.py
+++ b/solution.py
@@ -24,16 +24,18 @@
     return jnp.where(mask, 1.0, 0.0).astype(BF16)
 
 
-def my_columns(half):
-    return pl.ds(pl.multiple_of(lax.axis_index("dir") * half, 128), half)
+def core_columns(core, half, piece, i):
+    return pl.ds(pl.multiple_of(core * piece, 128) + i * 2 * piece, piece)
 
 
 def prep_kernel(
     v_hbm, low_hbm, high_hbm, force_hbm, bond_hbm, near_hbm,
-    turned_hbm, send_low_hbm, send_high_hbm, source_hbm, bond_out_hbm,
-    v_ref, low_ref, high_ref, near_ref, turned_ref, send_low_ref, send_high_ref,
-    source_ref, pick_ref, wide_ref, v_sems, in_sems, out_sems,
+    turned_hbm, send_low_hbm, send_high_hbm, source_hbm, bond_out_hbm, *refs
 ):
+    pieces = len(refs) - 13
+    piece_hbms, scratch_refs = refs[:pieces], refs[pieces:]
+    v_ref, low_ref, high_ref, near_ref, turned_ref, send_low_ref, send_high_ref = scratch_refs[:7]
+    source_ref, pick_ref, wide_ref, v_sems, in_sems, out_sems = scratch_refs[7:]
     rows, half = v_ref.shape
     atoms = rows // 3
     arriving = [
@@ -48,12 +50,14 @@
             )
         )
     ]
-    quarter = rows // 4
+    piece = half // pieces
     v_in = [
         pltpu.make_async_copy(
-            v_hbm.at[pl.ds(at, quarter), my_columns(half)], v_ref.at[pl.ds(at, quarter)], v_sems.at[i]
-        )
-        for i, at in enumerate(range(0, rows, quarter))
+            v_hbm.at[:, core_columns(lax.axis_index("dir"), half, piece, i)],
+            v_ref.at[:, pl.ds(i * piece, piece)],
+            v_sems.at[i],
+        )
+        for i in range(pieces)
     ]
     for copy in arriving + v_in:
         copy.start()
@@ -89,6 +93,9 @@
             part = wide_ref[t, pl.ds(b, atoms, stride=3), :]
             turned_ref[columns, b * atoms : (b + 1) * atoms] = part.T.astype(BF16)
     leave(turned_ref, turned_hbm)
+    for i, piece_hbm in enumerate(piece_hbms):
+        at = lax.rem(lax.axis_index("dom") + i + 1, 2) * piece if pieces == 2 else 0
+        leave(turned_ref.at[pl.ds(pl.multiple_of(at, 64), piece)], piece_hbm)
     picked = dot(pick_ref[...], v_ref[...]).astype(BF16)
     send_high_ref[...] = picked[: 3 * count]
     leave(send_high_ref, send_high_hbm)
@@ -179,7 +186,8 @@
         flux_ref[at, :] = dot(hi, turned, ((1,), (1,))) + dot(lo, turned, ((1,), (1,)))
 
 
-def relay_kernel(part_hbm, below_hbm, above_hbm, *refs):
+def relay_kernel(waited, *refs):
+    refs = refs[waited:]
     for got_ref, given_ref in zip(refs[: len(refs) // 2], refs[len(refs) // 2 :]):
         given_ref[...] = got_ref[...]
 
@@ -231,32 +239,39 @@
         out_ref[0, :, c * half : (c + 1) * half] = total * scale
 
 
-def far_kernel(after, flux_ref, *refs):
-    *quarter_refs, far_ref = refs
-    home = lax.axis_index("dom")
-
-    def store(quarter, turned_ref):
-        @pl.when((quarter ^ home) == 3)
-        def _():
-            far_ref[...] = dot(turned_ref[...], flux_ref[...]).astype(BF16)
-
-    terms_of(quarter_refs, store)
+def quarter_terms(this_half, parity, quarter_refs, flux_refs, out_refs):
+    mine_ref, other_ref, *got_refs = quarter_refs
+    home, core = lax.axis_index("dom"), lax.axis_index("dir")
+    piece = got_refs[0].shape[0]
+    here = (lax.axis_index("blk") == home // 2) == this_half
+    rows = pl.ds(pl.multiple_of(((home ^ parity) & 1) * piece, 128), piece)
+
+    def store(sources):
+        for owner, turned in zip((core, 1 - core), sources):
+            at = pl.ds(pl.multiple_of(owner * piece, 128), piece)
+            for flux_ref, out_ref in zip(flux_refs, out_refs):
+                out_ref[at, :] = dot(turned(), flux_ref[...]).astype(out_ref.dtype)
+
+    @pl.when(here)
+    def _():
+        store((lambda: mine_ref[rows, :], lambda: other_ref[rows, :]))
+
+    @pl.when(jnp.logical_not(here))
+    def _():
+        store((lambda: got_refs[0][...], lambda: got_refs[1][...]))
+
+
+def far_kernel(*refs):
+    quarter_terms(False, 1, refs[-5:-1], (refs[-6],), refs[-1:])
 
 
 def near_kernel(flux0_ref, flux1_ref, *refs):
-    *quarter_refs, near0_ref, near1_ref, add0_ref, add1_ref, keep_ref, give_ref = refs
-    home = lax.axis_index("dom")
-    outs = {0: (keep_ref, give_ref), 1: (near0_ref, near1_ref), 2: (add0_ref, add1_ref)}
-
-    def store(quarter, turned_ref):
-        for away, out_refs in outs.items():
-
-            @pl.when((quarter ^ home) == away)
-            def _():
-                for flux_ref, out_ref in zip((flux0_ref, flux1_ref), out_refs):
-                    out_ref[...] = dot(turned_ref[...], flux_ref[...]).astype(out_ref.dtype)
-
-    terms_of(quarter_refs, store)
+    quarter_terms(True, 1, refs[:4], (flux0_ref, flux1_ref), refs[4:])
+
+
+def even_kernel(flux0_ref, flux1_ref, *refs):
+    quarter_terms(False, 0, refs[:4], (flux0_ref, flux1_ref), refs[4:6])
+    quarter_terms(True, 0, refs[:4], (flux0_ref, flux1_ref), refs[6:])
 
 
 def add_kernel(far_ref, add_ref, *refs):
@@ -277,11 +292,15 @@
     ):
         total = first[...].astype(F32) + near[...].astype(F32) + far[...].astype(F32)
         total_ref[i] = total * scale
-        columns = pl.ds(pl.multiple_of(owner * half, 128), half)
-        copies.append(
-            pltpu.make_async_copy(total_ref.at[i], out_hbm.at[0, :, columns], sems.at[i])
-        )
-        copies[i].start()
+        for j in range(2):
+            piece = half // 2
+            copy = pltpu.make_async_copy(
+                total_ref.at[i, :, pl.ds(j * piece, piece)],
+                out_hbm.at[0, :, core_columns(owner, half, piece, j)],
+                sems.at[2 * i + j],
+            )
+            copy.start()
+            copies.append(copy)
     for copy in copies:
         copy.wait()
 
@@ -314,6 +333,8 @@
     hbm = pl.BlockSpec(memory_space=pltpu.HBM)
     anywhere = pl.BlockSpec(memory_space=pl.ANY)
 
+    halving = domains == 4 and block == half
+    pieces = 2 if halving else 1
     lists = [boundary_low.reshape(1, count), boundary_high.reshape(1, count)]
     forces = force_blocks.transpose(1, 0, 2)
     prepared = (
@@ -321,15 +342,16 @@
         shape((3 * count, half), BF16),
         shape((3 * count, half), BF16),
     )
-    turned, send_low, send_high, sources, bonds = pl.pallas_call(
+    turned, send_low, send_high, sources, bonds, *sent_pieces = pl.pallas_call(
         prep_kernel,
         out_shape=(
             *prepared,
             shape((11, *neighbours.shape), F32),
             shape(bond_vectors.shape, F32),
-        ),
+        )
+        + (shape((half // pieces, rows), BF16),) * pieces,
         in_specs=[hbm] * 6,
-        out_specs=(hbm,) * 5,
+        out_specs=(hbm,) * (5 + pieces),
         scratch_shapes=[
             pltpu.VMEM((rows, half), BF16),
             pltpu.VMEM((1, count), jnp.int32),
@@ -341,12 +363,12 @@
             pltpu.VMEM((half // 128, rows, 128), F32),
             pltpu.SemaphoreType.DMA((4,)),
             pltpu.SemaphoreType.DMA((5,)),
-            pltpu.SemaphoreType.DMA((5,)),
+            pltpu.SemaphoreType.DMA((5 + pieces,)),
         ],
         compiler_params=params(58),
         name="prep",
     )(panel_vectors, *lists, forces, bond_vectors, neighbours)
-    quarters = [shift(turned, "blk", j) for j in range(1, tiles)]
+    quarters = [shift(piece, "blk", j) for j in range(1, tiles) for piece in sent_pieces[::-1]][::-1]
     turned_other = shift(turned, "dir", 1)
     other_bonds = shift(bonds, "dir", 1)
     below = shift(send_high, "dom", 1)
@@ -373,17 +395,15 @@
         name="weights",
     )(sources, other_bonds, turned)
 
-    quarters = pl.pallas_call(
-        relay_kernel,
-        out_shape=[shape(turned.shape, BF16)] * (tiles - 1),
-        in_specs=[anywhere] * 3 + [vmem] * len(quarters),
-        out_specs=[vmem] * (tiles - 1),
-        compiler_params=params(16),
-        name="relay",
-    )(partial_flux, below, above, *quarters)
-    given = [turned, turned_other]
-    for quarter in quarters:
-        given += [quarter, shift(quarter, "dir", 1)]
+    def relay(after, *values):
+        return pl.pallas_call(
+            functools.partial(relay_kernel, len(after)),
+            out_shape=[shape(value.shape, value.dtype) for value in values],
+            in_specs=[anywhere] * len(after) + [vmem] * len(values),
+            out_specs=[vmem] * len(values),
+            compiler_params=params(16),
+            name="relay",
+        )(*after, *values)
 
     def flux_of(e):
         return pl.pallas_call(
@@ -401,34 +421,36 @@
 
     scale = (3.0 * atoms * domains) ** (-0.5)
     result = shape((1, block, cols), F32)
-    if domains == 4 and block == half:
+    if halving:
         sent, kept = shape((block, half), BF16), shape((block, half), F32)
         cost = pl.CostEstimate(flops=4 * 10**8, bytes_accessed=10**6, transcendentals=0)
 
-        def far_of(flux, after):
+        (first,) = relay((partial_flux, below, above), quarters[0])
+        odd = [turned, turned_other, first, shift(first, "dir", 1)]
+
+        def terms_of_quarters(kernel, name, after, fluxes, quarter_values, like):
             return pl.pallas_call(
-                far_kernel,
-                out_shape=sent,
-                in_specs=[anywhere] + [vmem] * (1 + len(given)),
-                out_specs=vmem,
+                kernel,
+                out_shape=like,
+                in_specs=[anywhere] * len(after) + [vmem] * (len(fluxes) + 4),
+                out_specs=[vmem] * len(like),
                 compiler_params=params(16),
                 cost_estimate=cost,
-                name="far",
-            )(after, flux, *given)
+                name=name,
+            )(*after, *fluxes, *quarter_values)
 
         flux0, flux1 = flux_of(0), flux_of(1)
-        far0 = far_of(flux0, flux1)
-        far1 = far_of(flux1, far0)
+        (second,) = relay((flux0, flux1), quarters[1])
+        (far0,) = terms_of_quarters(far_kernel, "far", (flux1, second), (flux0,), odd, [sent])
+        (far1,) = terms_of_quarters(far_kernel, "far", (far0,), (flux1,), odd, [sent])
+        even = [turned, turned_other, second, shift(second, "dir", 1)]
         far0, far1 = swap(far0, 1, 0), swap(far1, 1, 0)
-        near0, near1, add0, add1, keep, give = pl.pallas_call(
-            near_kernel,
-            out_shape=(sent, sent, kept, kept, kept, sent),
-            in_specs=[vmem] * (2 + len(given)),
-            out_specs=(vmem,) * 6,
-            compiler_params=params(16),
-            cost_estimate=cost,
-            name="near",
-        )(flux0, flux1, *given)
+        near0, near1 = terms_of_quarters(
+            near_kernel, "near", (), (flux0, flux1), odd, [sent, sent]
+        )
+        add0, add1, keep, give = terms_of_quarters(
+            even_kernel, "even", (), (flux0, flux1), even, [kept, kept, kept, sent]
+        )
 
         def sum_of(far, add, *handed_on):
             return pl.pallas_call(
@@ -451,12 +473,15 @@
             out_specs=hbm,
             scratch_shapes=[
                 pltpu.VMEM((2, block, half), F32),
-                pltpu.SemaphoreType.DMA((2,)),
+                pltpu.SemaphoreType.DMA((4,)),
             ],
             compiler_params=params(16),
             name="total",
         )(keep, give, near0, near1, sum0, sum1)
 
+    given = [turned, turned_other]
+    for quarter in relay((partial_flux, below, above), *quarters):
+        given += [quarter, shift(quarter, "dir", 1)]
     terms = pl.pallas_call(
         couple_kernel,
         out_shape=shape((2 * domains, block, half), BF16),

time: 42.9 us -> 43.6 us (1.016)
  waiting for transfers between devices: 12.5 us -> 16.3 us
  starting transfers between devices: 16 us -> 13.1 us
    ppermute x7, starting transfers between devices: 8.87 us -> 5.13 us  [swap(): return lax.ppermute(value, ('dom', 'dir'), pairs)]
    ppermute x7, waiting for transfers between devices: 10.4 us -> 14 us  [swap(): return lax.ppermute(value, ('dom', 'dir'), pairs)]
    ppermute x6 -> x8, starting transfers between devices: 7.14 us -> 7.93 us  [shift(): lax.ppermute(value, axis, [(i, (i + by) % length) for i in range(length)])]
    pallas_call x4 -> x6, Pallas kernels: 1.71 us -> 1.56 us  [the longest x4 1.53 us: terms_of_quarters(): pl.pallas_call(kernel, out_shape=like, in_specs=[anywhere] * len(after) +...]
    ppermute x6 -> x8, waiting for transfers between devices: 2.12 us -> 2.23 us  [shift(): lax.ppermute(value, axis, [(i, (i + by) % length) for i in range(length)])]
  transfers between devices with their start and end apart: 13 -> 15, of which waited for: 7 -> 8; matrix products, arithmetic and copies ran while one was open for 0% -> 0% of each run, Pallas kernels for 19% -> 19%
where the time goes in v12:
time: 43.6 us; the launch traced here: 43.4 us
  waiting for transfers between devices  16.3 us (37%)
  starting transfers between devices  13.1 us (30%)
  Pallas kernels  12 us (28%)
  local copies, waits for them, and re-layouts  1.92 us (4%)
    ppermute x7, waiting for transfers between devices, swap(): return lax.ppermute(value, ('dom', 'dir'), pairs)  14 us
    ppermute x8, starting transfers between devices, shift(): lax.ppermute(value, axis, [(i, (i + by) % length) for i in range(length)])  7.93 us
    ppermute x7, starting transfers between devices, swap(): return lax.ppermute(value, ('dom', 'dir'), pairs)  5.13 us
    pallas_call x1, Pallas kernels, per_device(): pl.pallas_call(weights_kernel, out_shape=(shape((2 * rows, half), F32), s...  5.13 us
    pallas_call x1, Pallas kernels, per_device(): pl.pallas_call(prep_kernel, out_shape=(*prepared, shape((11, *neighbours....  2.87 us
    ppermute x8, waiting for transfers between devices, shift(): lax.ppermute(value, axis, [(i, (i + by) % length) for i in range(length)])  2.23 us
    unnamed x4, local copies, waits for them, and re-layouts  1.92 us
    pallas_call x2, Pallas kernels, flux_of(): pl.pallas_call(functools.partial(flux_kernel, e), out_shape=shape((rows,...  1.54 us
  transfers between devices with their start and end apart: 15, of which 8 were waited for; matrix products, arithmetic and copies ran while one was open for 0% of the time, Pallas kernels for 19%

profile of v12, /device:TPU:0, one launch (start us, length us, event | category | flops | bytes accessed | tf_op | source)
XLA Modules:
  0.0 43.4 jit_solution(2471502178604434640)
XLA Ops:
  0.0 2.9 %prep.1 = (bf16[256,768]{1,0:T(8,128)(2,1)}, bf16[384,256]{1,0:T(8,128)(2,1)}, bf16[384,256]{1,0:T(8,128)(2,1)}, f32[11,16,256]{2,1,0:T(8,128)}, f32[1,16,256]{2...) custom-call(bf16[768,512]{1,0:T(8,128)(2,1)} %v_hbm.1, s32[1,128]{1,0:T(1,128)} %bitcast.4, ...), custom_call_target="tpu_custom_call" | custom-call | tf_op jit(solution)/shard_map/prep/pallas_call | solution.py:345
  2.9 0.5 %collective-permute-start = (f32[1,16,256]{2,1,0:T(8,128)}, f32[1,16,256]{2,1,0:T(8,128)S(1)}, u32[]{:S(2)}, u32[]{:S(2)}) collective-permute-start(f32[1,16,256]{2,1,0:T(8,128)} %get-tuple-element.25), channel_id=1, source_target_pairs={{0,1},{1,0},{2,3},{3,2},{4,5},{5,4},{6,7},{7,6},{8,9},{9,8},{10,11... | collective-permute-start | bytes 49160 | tf_op jit(solution)/shard_map/ppermute | solution.py:310
  3.4 2.6 %collective-permute-start.1 = (bf16[384,256]{1,0:T(8,128)(2,1)}, bf16[384,256]{1,0:T(8,128)(2,1)S(1)}, u32[]{:S(2)}, u32[]{:S(2)}) collective-permute-start(bf16[384,256]{1,0:T(8,128)(2,1)} %get-tuple-element.30), channel_id=1, source_target_pairs={{0,4},{4,8},{8,12},{12,0},{1,5},{5,9},{9,13},{13,1},{2,6},{6,10},{... | collective-permute-start | bytes 589832 | tf_op jit(solution)/shard_map/ppermute | solution.py:310
  6.0 2.1 %collective-permute-start.2 = (bf16[384,256]{1,0:T(8,128)(2,1)}, bf16[384,256]{1,0:T(8,128)(2,1)S(1)}, u32[]{:S(2)}, u32[]{:S(2)}) collective-permute-start(bf16[384,256]{1,0:T(8,128)(2,1)} %get-tuple-element.31), channel_id=1, source_target_pairs={{0,12},{4,0},{8,4},{12,8},{1,13},{5,1},{9,5},{13,9},{2,14},{6,2},{... | collective-permute-start | bytes 589832 | tf_op jit(solution)/shard_map/ppermute | solution.py:310
  8.1 1.6 %collective-permute-start.4 = (bf16[128,768]{1,0:T(8,128)(2,1)}, bf16[128,768]{1,0:T(8,128)(2,1)S(1)}, u32[]{:S(2)}, u32[]{:S(2)}) collective-permute-start(bf16[128,768]{1,0:T(8,128)(2,1)} %get-tuple-element.32), channel_id=1, source_target_pairs={{0,2},{2,0},{1,3},{3,1},{4,6},{6,4},{5,7},{7,5},{8,10},{10,8},{9,1... | collective-permute-start | bytes 589832 | tf_op jit(solution)/shard_map/ppermute | solution.py:310
  9.8 0.4 collective-permute-start.6
  10.2 0.0 collective-permute-done.other_ref
  10.2 0.0 collective-permute-start.3
  10.2 0.0 copy-start
  10.2 1.0 %copy-done = bf16[256,768]{1,0:T(8,128)(2,1)S(1)} copy-done((bf16[256,768]{1,0:T(8,128)(2,1)S(1)}, bf16[256,768]{1,0:T(8,128)(2,1)}, u32[]{:S(2)}) %copy-start) | copy-done | bytes 393240
  11.2 0.0 copy-start.1
  11.2 0.9 %copy-done.1 = f32[11,16,256]{2,1,0:T(8,128)S(1)} copy-done((f32[11,16,256]{2,1,0:T(8,128)S(1)}, f32[11,16,256]{2,1,0:T(8,128)}, u32[]{:S(2)}) %copy-start.1) | copy-done | bytes 180248
  12.1 5.1 %weights.1 = (f32[1536,256]{1,0:T(8,128)S(1)}, bf16[1536,768]{1,0:T(8,128)(2,1)S(1)}, bf16[1536,768]{1,0:T(8,128)(2,1)S(1)}) custom-call(f32[11,16,256]{2,1,0:T(8,128)S(1)} %copy-done.1, f32[1,16,256]{2,1,0:T(8,128)S(1)} %collective-permute-done.other_ref, bf16[256,768]{1,0:T(8,128)(2,1)S(1)} %copy-done), custom_call_target="tpu_custom_call" | custom-call | flops 8000000000 | bytes 10000000 | tf_op jit(solution)/shard_map/weights/pallas_call | solution.py:377
  17.2 0.0 collective-permute-done.1.below_ref.refs_1_
  17.2 0.2 collective-permute-done.2.above_ref.refs_2_
  17.4 2.0 %collective-permute-done.6.refs_3_ = bf16[128,768]{1,0:T(8,128)(2,1)S(1)} collective-permute-done((bf16[128,768]{1,0:T(8,128)(2,1)}, bf16[128,768]{1,0:T(8,128)(2,1)S(1)}, u32[]{:S(2)}, u32[]{:S(2)}) %collective-permute-start.6) | collective-permute-done | bytes 196640 | tf_op jit(solution)/shard_map/ppermute | solution.py:310
  19.5 0.1 collective-permute-start.7
  19.6 0.8 %flux.3.refs_1_.flux1_ref.refs_0_ = bf16[768,256]{1,0:T(8,128)(2,1)S(1)} custom-call(f32[1536,256]{1,0:T(8,128)S(1)} %get-tuple-element.27.part_ref.refs_0_, bf16[1536,768]{1,0:T(8,128)(2,1)S(1)} %get-tuple-element.28.hi_ref, bf16[1536,768]{1,0:T(8,128)(2,1)S(1)} %get-tuple-element.29.lo_ref, bf16[384,256]{1,0:T(8,128)(2,1)S(1)} %collective-permute-done.1.below_ref.refs_1_, ...), custom_call_target="tpu_custom_call" | custom-call | flops 1000000000 | bytes 1000000 | tf_op jit(solution)/shard_map/flux/pallas_call | solution.py:409
  20.3 0.8 %flux.2.refs_0_.flux0_ref.refs_2_ = bf16[768,256]{1,0:T(8,128)(2,1)S(1)} custom-call(f32[1536,256]{1,0:T(8,128)S(1)} %get-tuple-element.27.part_ref.refs_0_, bf16[1536,768]{1,0:T(8,128)(2,1)S(1)} %get-tuple-element.28.hi_ref, bf16[1536,768]{1,0:T(8,128)(2,1)S(1)} %get-tuple-element.29.lo_ref, bf16[384,256]{1,0:T(8,128)(2,1)S(1)} %collective-permute-done.1.below_ref.refs_1_, ...), custom_call_target="tpu_custom_call" | custom-call | flops 1000000000 | bytes 1000000 | tf_op jit(solution)/shard_map/flux/pallas_call | solution.py:409
  21.1 0.0 collective-permute-done.4.refs_2_
  21.1 0.6 %collective-permute-start.5 = (bf16[128,768]{1,0:T(8,128)(2,1)S(1)}, bf16[128,768]{1,0:T(8,128)(2,1)S(1)}, u32[]{:S(2)}, u32[]{:S(2)}) collective-permute-start(bf16[128,768]{1,0:T(8,128)(2,1)S(1)} %relay.2.refs_2_.refs_1_), channel_id=1, source_target_pairs={{0,1},{1,0},{2,3},{3,2},{4,5},{5,4},{6,7},{7,6},{8,9},{9,8},{10,11... | collective-permute-start | bytes 589832 | tf_op jit(solution)/shard_map/ppermute | solution.py:310
  21.7 0.0 collective-permute-done.7.refs_6_.refs_5_.refs_3_
  21.7 0.0 collective-permute-done.3.refs_1_.refs_4_.refs_3_
  21.7 0.3 far.2.refs_0_
  22.0 0.1 collective-permute-start.12
  22.1 0.3 far.3
  22.4 2.0 %collective-permute-start.8 = (bf16[256,256]{1,0:T(8,128)(2,1)S(1)}, bf16[256,256]{1,0:T(8,128)(2,1)S(1)}, u32[]{:S(2)}, u32[]{:S(2)}) collective-permute-start(bf16[256,256]{1,0:T(8,128)(2,1)S(1)} %far.3), channel_id=1, source_target_pairs={{0,4},{1,5},{4,0},{5,1},{8,12},{9,13},{12,8},{13,9},{2,6},{3,7},{6... | collective-permute-start | bytes 393224 | tf_op jit(solution)/shard_map/ppermute | solution.py:318
  24.4 0.4 near.1
  24.8 0.1 collective-permute-start.10
  24.9 0.0 collective-permute-done.5.refs_3_
  24.9 0.6 %even.1 = (f32[256,256]{1,0:T(8,128)S(1)}, f32[256,256]{1,0:T(8,128)S(1)}, f32[256,256]{1,0:T(8,128)S(1)}, bf16[256,256]{1,0:T(8,128)(2,1)S(1)}) custom-call(bf16[768,256]{1,0:T(8,128)(2,1)S(1)} %flux.2.refs_0_.flux0_ref.refs_2_, bf16[768,256]{1,0:T(8,128)(2,1)S(1)} %flux.3.refs_1_.flux1_ref.refs_0_, bf16[256,768]{1,0:T(8,128)(2,1)S(1)} %copy-done, ...), custom_call_target="tpu_custom_call" | custom-call | flops 400000000 | bytes 1000000 | tf_op jit(solution)/shard_map/even/pallas_call | solution.py:432
  25.5 2.9 %collective-permute-done.12.far_ref = bf16[256,256]{1,0:T(8,128)(2,1)S(1)} collective-permute-done((bf16[256,256]{1,0:T(8,128)(2,1)S(1)}, bf16[256,256]{1,0:T(8,128)(2,1)S(1)}, u32[]{:S(2)}, u32[]{:S(2)}) %collective-permute-start.12) | collective-permute-done | bytes 131104 | tf_op jit(solution)/shard_map/ppermute | solution.py:318
  28.4 0.8 %collective-permute-start.13 = (bf16[256,256]{1,0:T(8,128)(2,1)S(1)}, bf16[256,256]{1,0:T(8,128)(2,1)S(1)}, u32[]{:S(2)}, u32[]{:S(2)}) collective-permute-start(bf16[256,256]{1,0:T(8,128)(2,1)S(1)} %add.3), channel_id=1, source_target_pairs={{0,8},{1,9},{4,12},{5,13},{8,0},{9,1},{12,4},{13,5},{2,10},{3,11},... | collective-permute-start | bytes 393224 | tf_op jit(solution)/shard_map/ppermute | solution.py:318
  29.2 3.4 %collective-permute-done.8.far_ref = bf16[256,256]{1,0:T(8,128)(2,1)S(1)} collective-permute-done((bf16[256,256]{1,0:T(8,128)(2,1)S(1)}, bf16[256,256]{1,0:T(8,128)(2,1)S(1)}, u32[]{:S(2)}, u32[]{:S(2)}) %collective-permute-start.8) | collective-permute-done | bytes 131104 | tf_op jit(solution)/shard_map/ppermute | solution.py:318
  32.7 0.1 collective-permute-start.11
  32.7 2.0 %collective-permute-start.14 = (bf16[256,256]{1,0:T(8,128)(2,1)S(1)}, bf16[256,256]{1,0:T(8,128)(2,1)S(1)}, u32[]{:S(2)}, u32[]{:S(2)}) collective-permute-start(bf16[256,256]{1,0:T(8,128)(2,1)S(1)} %get-tuple-element.42), channel_id=1, source_target_pairs={{0,9},{1,8},{4,13},{5,12},{8,1},{9,0},{12,5},{13,4},{2,11},{3,10},... | collective-permute-start | bytes 393224 | tf_op jit(solution)/shard_map/ppermute | solution.py:318
  34.8 0.0 collective-permute-start.9
  34.8 0.5 %collective-permute-done.10.refs_2_ = bf16[256,256]{1,0:T(8,128)(2,1)S(1)} collective-permute-done((bf16[256,256]{1,0:T(8,128)(2,1)S(1)}, bf16[256,256]{1,0:T(8,128)(2,1)S(1)}, u32[]{:S(2)}, u32[]{:S(2)}) %collective-permute-start.10) | collective-permute-done | bytes 131104 | tf_op jit(solution)/shard_map/ppermute | solution.py:318
  35.3 1.5 %collective-permute-done.13.refs_4_ = bf16[256,256]{1,0:T(8,128)(2,1)S(1)} collective-permute-done((bf16[256,256]{1,0:T(8,128)(2,1)S(1)}, bf16[256,256]{1,0:T(8,128)(2,1)S(1)}, u32[]{:S(2)}, u32[]{:S(2)}) %collective-permute-start.13) | collective-permute-done | bytes 131104 | tf_op jit(solution)/shard_map/ppermute | solution.py:318
  36.7 4.1 %collective-permute-done.11.refs_3_ = bf16[256,256]{1,0:T(8,128)(2,1)S(1)} collective-permute-done((bf16[256,256]{1,0:T(8,128)(2,1)S(1)}, bf16[256,256]{1,0:T(8,128)(2,1)S(1)}, u32[]{:S(2)}, u32[]{:S(2)}) %collective-permute-start.11) | collective-permute-done | bytes 131104 | tf_op jit(solution)/shard_map/ppermute | solution.py:318
  40.8 1.8 %collective-permute-done.14.refs_5_ = bf16[256,256]{1,0:T(8,128)(2,1)S(1)} collective-permute-done((bf16[256,256]{1,0:T(8,128)(2,1)S(1)}, bf16[256,256]{1,0:T(8,128)(2,1)S(1)}, u32[]{:S(2)}, u32[]{:S(2)}) %collective-permute-start.14) | collective-permute-done | bytes 131104 | tf_op jit(solution)/shard_map/ppermute | solution.py:318
  42.5 0.0 collective-permute-done.9.refs_1_
  42.5 0.9 %total.1 = f32[1,256,512]{2,1,0:T(8,128)} custom-call(f32[256,256]{1,0:T(8,128)S(1)} %get-tuple-element.33.refs_0_, bf16[256,256]{1,0:T(8,128)(2,1)S(1)} %collective-permute-done.9.refs_1_, bf16[256,256]{1,0:T(8,128)(2,1)S(1)} %collective-permute-done.10.refs_2_, bf16[256,256]{1,0:T(8,128)(2,1)S(1)} %collective-permute-done.11.refs_3_, ...), custom_call_target="tpu_custom_call" | custom-call | tf_op jit(solution)/shard_map/total/pallas_call | solution.py:469
  (4 shorter events, 0.1 us)
Async XLA Ops:
  2.9 7.3 %collective-permute-start = (f32[1,16,256]{2,1,0:T(8,128)}, f32[1,16,256]{2,1,0:T(8,128)S(1)}, u32[]{:S(2)}, u32[]{:S(2)}) collective-permute-start(f32[1,16,256]{2,1,0:T(8,128)} %get-tuple-element.25), channel_id=1, source_target_pairs={{0,1},{1,0},{2,3},{3,2},{4,5},{5,4},{6,7},{7,6},{8,9},{9,8},{10,11... | collective-permute-start | bytes 49160 | tf_op jit(solution)/shard_map/ppermute | solution.py:310
  3.4 13.8 %collective-permute-start.1 = (bf16[384,256]{1,0:T(8,128)(2,1)}, bf16[384,256]{1,0:T(8,128)(2,1)S(1)}, u32[]{:S(2)}, u32[]{:S(2)}) collective-permute-start(bf16[384,256]{1,0:T(8,128)(2,1)} %get-tuple-element.30), channel_id=1, source_target_pairs={{0,4},{4,8},{8,12},{12,0},{1,5},{5,9},{9,13},{13,1},{2,6},{6,10},{... | collective-permute-start | bytes 589832 | tf_op jit(solution)/shard_map/ppermute | solution.py:310
  6.0 11.4 %collective-permute-start.2 = (bf16[384,256]{1,0:T(8,128)(2,1)}, bf16[384,256]{1,0:T(8,128)(2,1)S(1)}, u32[]{:S(2)}, u32[]{:S(2)}) collective-permute-start(bf16[384,256]{1,0:T(8,128)(2,1)} %get-tuple-element.31), channel_id=1, source_target_pairs={{0,12},{4,0},{8,4},{12,8},{1,13},{5,1},{9,5},{13,9},{2,14},{6,2},{... | collective-permute-start | bytes 589832 | tf_op jit(solution)/shard_map/ppermute | solution.py:310
  8.1 13.0 %collective-permute-start.4 = (bf16[128,768]{1,0:T(8,128)(2,1)}, bf16[128,768]{1,0:T(8,128)(2,1)S(1)}, u32[]{:S(2)}, u32[]{:S(2)}) collective-permute-start(bf16[128,768]{1,0:T(8,128)(2,1)} %get-tuple-element.32), channel_id=1, source_target_pairs={{0,2},{2,0},{1,3},{3,1},{4,6},{6,4},{5,7},{7,5},{8,10},{10,8},{9,1... | collective-permute-start | bytes 589832 | tf_op jit(solution)/shard_map/ppermute | solution.py:310
  9.8 9.7 %collective-permute-start.6 = (bf16[128,768]{1,0:T(8,128)(2,1)}, bf16[128,768]{1,0:T(8,128)(2,1)S(1)}, u32[]{:S(2)}, u32[]{:S(2)}) collective-permute-start(bf16[128,768]{1,0:T(8,128)(2,1)} %get-tuple-element.34), channel_id=1, source_target_pairs={{0,2},{2,0},{1,3},{3,1},{4,6},{6,4},{5,7},{7,5},{8,10},{10,8},{9,1... | collective-permute-start | bytes 589832 | tf_op jit(solution)/shard_map/ppermute | solution.py:310
  10.2 11.5 %collective-permute-start.3 = (bf16[256,768]{1,0:T(8,128)(2,1)}, bf16[256,768]{1,0:T(8,128)(2,1)S(1)}, u32[]{:S(2)}, u32[]{:S(2)}) collective-permute-start(bf16[256,768]{1,0:T(8,128)(2,1)} %get-tuple-element.26.turned_ref.refs_0_.refs_3_.refs_2_), channel_id=1, source_target_pairs={{0,1},{1,0},{2,3},{3,2},{4,5},{5,4},{6,7},{7,6},{8,9},{9,8},{10,11... | collective-permute-start | bytes 1179656 | tf_op jit(solution)/shard_map/ppermute | solution.py:310
  10.2 1.0 %copy-start = (bf16[256,768]{1,0:T(8,128)(2,1)S(1)}, bf16[256,768]{1,0:T(8,128)(2,1)}, u32[]{:S(2)}) copy-start(bf16[256,768]{1,0:T(8,128)(2,1)} %get-tuple-element.26.turned_ref.refs_0_.refs_3_.refs_2_) | copy-start | bytes 1179652
  11.2 0.9 %copy-start.1 = (f32[11,16,256]{2,1,0:T(8,128)S(1)}, f32[11,16,256]{2,1,0:T(8,128)}, u32[]{:S(2)}) copy-start(f32[11,16,256]{2,1,0:T(8,128)} %get-tuple-element.24.source_ref) | copy-start | bytes 540676
  19.5 2.2 %collective-permute-start.7 = (bf16[128,768]{1,0:T(8,128)(2,1)S(1)}, bf16[128,768]{1,0:T(8,128)(2,1)S(1)}, u32[]{:S(2)}, u32[]{:S(2)}) collective-permute-start(bf16[128,768]{1,0:T(8,128)(2,1)S(1)} %relay.3.refs_5_.refs_4_.refs_2_), channel_id=1, source_target_pairs={{0,1},{1,0},{2,3},{3,2},{4,5},{5,4},{6,7},{7,6},{8,9},{9,8},{10,11... | collective-permute-start | bytes 589832 | tf_op jit(solution)/shard_map/ppermute | solution.py:310
  21.1 3.8 %collective-permute-start.5 = (bf16[128,768]{1,0:T(8,128)(2,1)S(1)}, bf16[128,768]{1,0:T(8,128)(2,1)S(1)}, u32[]{:S(2)}, u32[]{:S(2)}) collective-permute-start(bf16[128,768]{1,0:T(8,128)(2,1)S(1)} %relay.2.refs_2_.refs_1_), channel_id=1, source_target_pairs={{0,1},{1,0},{2,3},{3,2},{4,5},{5,4},{6,7},{7,6},{8,9},{9,8},{10,11... | collective-permute-start | bytes 589832 | tf_op jit(solution)/shard_map/ppermute | solution.py:310
  22.0 6.4 %collective-permute-start.12 = (bf16[256,256]{1,0:T(8,128)(2,1)S(1)}, bf16[256,256]{1,0:T(8,128)(2,1)S(1)}, u32[]{:S(2)}, u32[]{:S(2)}) collective-permute-start(bf16[256,256]{1,0:T(8,128)(2,1)S(1)} %far.2.refs_0_), channel_id=1, source_target_pairs={{0,4},{1,5},{4,0},{5,1},{8,12},{9,13},{12,8},{13,9},{2,6},{3,7},{6... | collective-permute-start | bytes 393224 | tf_op jit(solution)/shard_map/ppermute | solution.py:318
  22.4 10.2 %collective-permute-start.8 = (bf16[256,256]{1,0:T(8,128)(2,1)S(1)}, bf16[256,256]{1,0:T(8,128)(2,1)S(1)}, u32[]{:S(2)}, u32[]{:S(2)}) collective-permute-start(bf16[256,256]{1,0:T(8,128)(2,1)S(1)} %far.3), channel_id=1, source_target_pairs={{0,4},{1,5},{4,0},{5,1},{8,12},{9,13},{12,8},{13,9},{2,6},{3,7},{6... | collective-permute-start | bytes 393224 | tf_op jit(solution)/shard_map/ppermute | solution.py:318
  24.8 10.4 %collective-permute-start.10 = (bf16[256,256]{1,0:T(8,128)(2,1)S(1)}, bf16[256,256]{1,0:T(8,128)(2,1)S(1)}, u32[]{:S(2)}, u32[]{:S(2)}) collective-permute-start(bf16[256,256]{1,0:T(8,128)(2,1)S(1)} %get-tuple-element.39), channel_id=1, source_target_pairs={{0,4},{1,5},{4,0},{5,1},{8,12},{9,13},{12,8},{13,9},{2,6},{3,7},{6... | collective-permute-start | bytes 393224 | tf_op jit(solution)/shard_map/ppermute | solution.py:318
  28.4 8.3 %collective-permute-start.13 = (bf16[256,256]{1,0:T(8,128)(2,1)S(1)}, bf16[256,256]{1,0:T(8,128)(2,1)S(1)}, u32[]{:S(2)}, u32[]{:S(2)}) collective-permute-start(bf16[256,256]{1,0:T(8,128)(2,1)S(1)} %add.3), channel_id=1, source_target_pairs={{0,8},{1,9},{4,12},{5,13},{8,0},{9,1},{12,4},{13,5},{2,10},{3,11},... | collective-permute-start | bytes 393224 | tf_op jit(solution)/shard_map/ppermute | solution.py:318
  32.7 8.1 %collective-permute-start.11 = (bf16[256,256]{1,0:T(8,128)(2,1)S(1)}, bf16[256,256]{1,0:T(8,128)(2,1)S(1)}, u32[]{:S(2)}, u32[]{:S(2)}) collective-permute-start(bf16[256,256]{1,0:T(8,128)(2,1)S(1)} %get-tuple-element.40), channel_id=1, source_target_pairs={{0,5},{1,4},{4,1},{5,0},{8,13},{9,12},{12,9},{13,8},{2,7},{3,6},{6... | collective-permute-start | bytes 393224 | tf_op jit(solution)/shard_map/ppermute | solution.py:318
  32.7 9.8 %collective-permute-start.14 = (bf16[256,256]{1,0:T(8,128)(2,1)S(1)}, bf16[256,256]{1,0:T(8,128)(2,1)S(1)}, u32[]{:S(2)}, u32[]{:S(2)}) collective-permute-start(bf16[256,256]{1,0:T(8,128)(2,1)S(1)} %get-tuple-element.42), channel_id=1, source_target_pairs={{0,9},{1,8},{4,13},{5,12},{8,1},{9,0},{12,5},{13,4},{2,11},{3,10},... | collective-permute-start | bytes 393224 | tf_op jit(solution)/shard_map/ppermute | solution.py:318
  34.8 7.8 %collective-permute-start.9 = (bf16[256,256]{1,0:T(8,128)(2,1)S(1)}, bf16[256,256]{1,0:T(8,128)(2,1)S(1)}, u32[]{:S(2)}, u32[]{:S(2)}) collective-permute-start(bf16[256,256]{1,0:T(8,128)(2,1)S(1)} %get-tuple-element.38), channel_id=1, source_target_pairs={{0,1},{1,0},{4,5},{5,4},{8,9},{9,8},{12,13},{13,12},{2,3},{3,2},{6... | collective-permute-start | bytes 393224 | tf_op jit(solution)/shard_map/ppermute | solution.py:318

commit v13 on v9

--- a/solution.py
+++ b/solution.py
@@ -82,18 +82,18 @@
                 )
     for copy in v_in:
         copy.wait()
+    picked = dot(pick_ref[...], v_ref[...]).astype(BF16)
+    send_high_ref[...] = picked[: 3 * count]
+    leave(send_high_ref, send_high_hbm)
+    send_low_ref[...] = picked[3 * count :]
+    leave(send_low_ref, send_low_hbm)
     for t in range(half // 128):
         columns = slice(t * 128, (t + 1) * 128)
         wide_ref[t] = v_ref[:, columns].astype(F32)
         for b in range(3):
             part = wide_ref[t, pl.ds(b, atoms, stride=3), :]
-            turned_ref[columns, b * atoms : (b + 1) * atoms] = part.T.astype(BF16)
+            turned_ref[columns, b * atoms : (b + 1) * atoms] = part.astype(BF16).T
     leave(turned_ref, turned_hbm)
-    picked = dot(pick_ref[...], v_ref[...]).astype(BF16)
-    send_high_ref[...] = picked[: 3 * count]
-    leave(send_high_ref, send_high_hbm)
-    send_low_ref[...] = picked[3 * count :]
-    leave(send_low_ref, send_low_hbm)
     for copy in leaving:
         copy.wait()
 

time: 42.9 us -> 42.9 us (level)
  no operation moved by 1% of the time
where the time goes in v13:
time: 42.9 us; the launch traced here: 42.7 us
  starting transfers between devices  16 us (37%)
  waiting for transfers between devices  12.5 us (29%)
  Pallas kernels  12.1 us (28%)
  local copies, waits for them, and re-layouts  1.92 us (4%)
    ppermute x7, waiting for transfers between devices, swap(): return lax.ppermute(value, ('dom', 'dir'), pairs)  10.4 us
    ppermute x7, starting transfers between devices, swap(): return lax.ppermute(value, ('dom', 'dir'), pairs)  8.88 us
    ppermute x6, starting transfers between devices, shift(): lax.ppermute(value, axis, [(i, (i + by) % length) for i in range(length)])  7.14 us
    pallas_call x1, Pallas kernels, per_device(): pl.pallas_call(weights_kernel, out_shape=(shape((2 * rows, half), F32), s...  5.13 us
    pallas_call x1, Pallas kernels, per_device(): pl.pallas_call(prep_kernel, out_shape=(*prepared, shape((11, *neighbours....  2.82 us
    ppermute x6, waiting for transfers between devices, shift(): lax.ppermute(value, axis, [(i, (i + by) % length) for i in range(length)])  2.14 us
    unnamed x4, local copies, waits for them, and re-layouts  1.92 us
    pallas_call x2, Pallas kernels, flux_of(): pl.pallas_call(functools.partial(flux_kernel, e), out_shape=shape((rows,...  1.54 us
  transfers between devices with their start and end apart: 13, of which 7 were waited for; matrix products, arithmetic and copies ran while one was open for 0% of the time, Pallas kernels for 19%

profile of v13, /device:TPU:0, one launch (start us, length us, event | category | flops | bytes accessed | tf_op | source)
XLA Modules:
  0.0 42.7 jit_solution(12384891458314163622)
XLA Ops:
  0.0 2.8 %prep.1 = (bf16[256,768]{1,0:T(8,128)(2,1)}, bf16[384,256]{1,0:T(8,128)(2,1)}, bf16[384,256]{1,0:T(8,128)(2,1)}, f32[11,16,256]{2,1,0:T(8,128)}, f32[1,16,256]{2,1,0:T(8,128)}) custom-call(bf16[768,512]{1,0:T(8,128)(2,1)} %v_hbm.1, s32[1,128]{1,0:T(1,128)} %bitcast.4, s32[1,128]{1,0:T(1,128)} %bitcast.5, f32[9,16,256]{2,1,0:T(8,128)} %bitcast.3, ...), custom_call_target="tpu_custom_call" | custom-call | tf_op jit(solution)/shard_map/prep/pallas_call | solution.py:324
  2.8 0.5 %collective-permute-start = (f32[1,16,256]{2,1,0:T(8,128)}, f32[1,16,256]{2,1,0:T(8,128)S(1)}, u32[]{:S(2)}, u32[]{:S(2)}) collective-permute-start(f32[1,16,256]{2,1,0:T(8,128)} %get-tuple-element.23), channel_id=1, source_target_pairs={{0,1},{1,0},{2,3},{3,2},{4,5},{5,4},{6,7},{7,6},{8,9},{9,8},{10,11... | collective-permute-start | bytes 49160 | tf_op jit(solution)/shard_map/ppermute | solution.py:291
  3.3 2.6 %collective-permute-start.4 = (bf16[256,768]{1,0:T(8,128)(2,1)}, bf16[256,768]{1,0:T(8,128)(2,1)S(1)}, u32[]{:S(2)}, u32[]{:S(2)}) collective-permute-start(bf16[256,768]{1,0:T(8,128)(2,1)} %get-tuple-element.24.turned_ref.refs_0_), channel_id=1, source_target_pairs={{0,2},{2,0},{1,3},{3,1},{4,6},{6,4},{5,7},{7,5},{8,10},{10,8},{9,1... | collective-permute-start | bytes 1179656 | tf_op jit(solution)/shard_map/ppermute | solution.py:291
  5.9 0.2 collective-permute-start.3
  6.1 1.6 %collective-permute-start.1 = (bf16[384,256]{1,0:T(8,128)(2,1)}, bf16[384,256]{1,0:T(8,128)(2,1)S(1)}, u32[]{:S(2)}, u32[]{:S(2)}) collective-permute-start(bf16[384,256]{1,0:T(8,128)(2,1)} %get-tuple-element.28), channel_id=1, source_target_pairs={{0,4},{4,8},{8,12},{12,0},{1,5},{5,9},{9,13},{13,1},{2,6},{6,10},{... | collective-permute-start | bytes 589832 | tf_op jit(solution)/shard_map/ppermute | solution.py:291
  7.7 2.2 %collective-permute-start.2 = (bf16[384,256]{1,0:T(8,128)(2,1)}, bf16[384,256]{1,0:T(8,128)(2,1)S(1)}, u32[]{:S(2)}, u32[]{:S(2)}) collective-permute-start(bf16[384,256]{1,0:T(8,128)(2,1)} %get-tuple-element.29), channel_id=1, source_target_pairs={{0,12},{4,0},{8,4},{12,8},{1,13},{5,1},{9,5},{13,9},{2,14},{6,2},{... | collective-permute-start | bytes 589832 | tf_op jit(solution)/shard_map/ppermute | solution.py:291
  9.9 0.0 collective-permute-done.other_ref
  9.9 0.0 copy-start
  9.9 1.0 %copy-done = bf16[256,768]{1,0:T(8,128)(2,1)S(1)} copy-done((bf16[256,768]{1,0:T(8,128)(2,1)S(1)}, bf16[256,768]{1,0:T(8,128)(2,1)}, u32[]{:S(2)}) %copy-start) | copy-done | bytes 393240
  10.9 0.0 copy-start.1
  10.9 0.9 %copy-done.1 = f32[11,16,256]{2,1,0:T(8,128)S(1)} copy-done((f32[11,16,256]{2,1,0:T(8,128)S(1)}, f32[11,16,256]{2,1,0:T(8,128)}, u32[]{:S(2)}) %copy-start.1) | copy-done | bytes 180248
  11.8 5.1 %weights.1 = (f32[1536,256]{1,0:T(8,128)S(1)}, bf16[1536,768]{1,0:T(8,128)(2,1)S(1)}, bf16[1536,768]{1,0:T(8,128)(2,1)S(1)}) custom-call(f32[11,16,256]{2,1,0:T(8,128)S(1)} %copy-done.1, f32[1,16,256]{2,1,0:T(8,128)S(1)} %collective-permute-done.other_ref, bf16[256,768]{1,0:T(8,128)(2,1)S(1)} %copy-done), custom_call_target="tpu_custom_call" | custom-call | flops 8000000000 | bytes 10000000 | tf_op jit(solution)/shard_map/weights/pallas_call | solution.py:355
  17.0 0.0 collective-permute-done.1.below_ref.below_hbm
  17.0 2.0 %collective-permute-done.2.above_ref.above_hbm = bf16[384,256]{1,0:T(8,128)(2,1)S(1)} collective-permute-done((bf16[384,256]{1,0:T(8,128)(2,1)}, bf16[384,256]{1,0:T(8,128)(2,1)S(1)}, u32[]{:S(2)}, u32[]{:S(2)}) %collective-permute-start.2) | collective-permute-done | bytes 196640 | tf_op jit(solution)/shard_map/ppermute | solution.py:291
  18.9 0.0 collective-permute-done.4.refs_0_
  19.0 0.1 collective-permute-start.5
  19.1 0.8 %flux.3.flux1_ref.after.flux_ref = bf16[768,256]{1,0:T(8,128)(2,1)S(1)} custom-call(f32[1536,256]{1,0:T(8,128)S(1)} %get-tuple-element.25.part_ref.part_hbm, bf16[1536,768]{1,0:T(8,128)(2,1)S(1)} %get-tuple-element.26.hi_ref, bf16[1536,768]{1,0:T(8,128)(2,1)S(1)} %get-tuple-element.27.lo_ref, ...), custom_call_target="tpu_custom_call" | custom-call | flops 1000000000 | bytes 1000000 | tf_op jit(solution)/shard_map/flux/pallas_call | solution.py:389
  19.8 0.8 %flux.2.flux0_ref.flux_ref = bf16[768,256]{1,0:T(8,128)(2,1)S(1)} custom-call(f32[1536,256]{1,0:T(8,128)S(1)} %get-tuple-element.25.part_ref.part_hbm, bf16[1536,768]{1,0:T(8,128)(2,1)S(1)} %get-tuple-element.26.hi_ref, bf16[1536,768]{1,0:T(8,128)(2,1)S(1)} %get-tuple-element.27.lo_ref, bf16[384,256]{1,0:T(8,128)(2,1)S(1)} %collective-permute-done.1.below_ref.below_hbm, ...), custom_call_target="tpu_custom_call" | custom-call | flops 1000000000 | bytes 1000000 | tf_op jit(solution)/shard_map/flux/pallas_call | solution.py:389
  20.6 0.0 collective-permute-done.3.refs_1_
  20.6 0.1 collective-permute-done.5.refs_3_
  20.8 0.3 far.2.after
  21.0 1.2 %collective-permute-start.10 = (bf16[256,256]{1,0:T(8,128)(2,1)S(1)}, bf16[256,256]{1,0:T(8,128)(2,1)S(1)}, u32[]{:S(2)}, u32[]{:S(2)}) collective-permute-start(bf16[256,256]{1,0:T(8,128)(2,1)S(1)} %far.2.after), channel_id=1, source_target_pairs={{0,4},{1,5},{4,0},{5,1},{8,12},{9,13},{12,8},{13,9},{2,6},{3,7},{6... | collective-permute-start | bytes 393224 | tf_op jit(solution)/shard_map/ppermute | solution.py:299
  22.3 0.3 far.3
  22.5 0.9 %collective-permute-start.6 = (bf16[256,256]{1,0:T(8,128)(2,1)S(1)}, bf16[256,256]{1,0:T(8,128)(2,1)S(1)}, u32[]{:S(2)}, u32[]{:S(2)}) collective-permute-start(bf16[256,256]{1,0:T(8,128)(2,1)S(1)} %far.3), channel_id=1, source_target_pairs={{0,4},{1,5},{4,0},{5,1},{8,12},{9,13},{12,8},{13,9},{2,6},{3,7},{6... | collective-permute-start | bytes 393224 | tf_op jit(solution)/shard_map/ppermute | solution.py:299
  23.5 1.1 %near.1 = (bf16[256,256]{1,0:T(8,128)(2,1)S(1)}, bf16[256,256]{1,0:T(8,128)(2,1)S(1)}, f32[256,256]{1,0:T(8,128)S(1)}, f32[256,256]{1,0:T(8,128)S(1)}, f32[256,2...) custom-call(bf16[768,256]{1,0:T(8,128)(2,1)S(1)} %flux.2.flux0_ref.flux_ref, ...), custom_call_target="tpu_custom_call" | custom-call | flops 400000000 | bytes 1000000 | tf_op jit(solution)/shard_map/near/pallas_call | solution.py:423
  24.6 1.2 %collective-permute-start.8 = (bf16[256,256]{1,0:T(8,128)(2,1)S(1)}, bf16[256,256]{1,0:T(8,128)(2,1)S(1)}, u32[]{:S(2)}, u32[]{:S(2)}) collective-permute-start(bf16[256,256]{1,0:T(8,128)(2,1)S(1)} %get-tuple-element.35), channel_id=1, source_target_pairs={{0,4},{1,5},{4,0},{5,1},{8,12},{9,13},{12,8},{13,9},{2,6},{3,7},{6... | collective-permute-start | bytes 393224 | tf_op jit(solution)/shard_map/ppermute | solution.py:299
  25.9 1.6 %collective-permute-done.10.far_ref = bf16[256,256]{1,0:T(8,128)(2,1)S(1)} collective-permute-done((bf16[256,256]{1,0:T(8,128)(2,1)S(1)}, bf16[256,256]{1,0:T(8,128)(2,1)S(1)}, u32[]{:S(2)}, u32[]{:S(2)}) %collective-permute-start.10) | collective-permute-done | bytes 131104 | tf_op jit(solution)/shard_map/ppermute | solution.py:299
  27.4 1.4 %collective-permute-start.11 = (bf16[256,256]{1,0:T(8,128)(2,1)S(1)}, bf16[256,256]{1,0:T(8,128)(2,1)S(1)}, u32[]{:S(2)}, u32[]{:S(2)}) collective-permute-start(bf16[256,256]{1,0:T(8,128)(2,1)S(1)} %add.3), channel_id=1, source_target_pairs={{0,8},{1,9},{4,12},{5,13},{8,0},{9,1},{12,4},{13,5},{2,10},{3,11},... | collective-permute-start | bytes 393224 | tf_op jit(solution)/shard_map/ppermute | solution.py:299
  28.9 1.4 %collective-permute-done.6.far_ref = bf16[256,256]{1,0:T(8,128)(2,1)S(1)} collective-permute-done((bf16[256,256]{1,0:T(8,128)(2,1)S(1)}, bf16[256,256]{1,0:T(8,128)(2,1)S(1)}, u32[]{:S(2)}, u32[]{:S(2)}) %collective-permute-start.6) | collective-permute-done | bytes 131104 | tf_op jit(solution)/shard_map/ppermute | solution.py:299
  30.3 0.1 collective-permute-start.12
  30.4 1.4 %collective-permute-start.7 = (bf16[256,256]{1,0:T(8,128)(2,1)S(1)}, bf16[256,256]{1,0:T(8,128)(2,1)S(1)}, u32[]{:S(2)}, u32[]{:S(2)}) collective-permute-start(bf16[256,256]{1,0:T(8,128)(2,1)S(1)} %get-tuple-element.34), channel_id=1, source_target_pairs={{0,1},{1,0},{4,5},{5,4},{8,9},{9,8},{12,13},{13,12},{2,3},{3,2},{6... | collective-permute-start | bytes 393224 | tf_op jit(solution)/shard_map/ppermute | solution.py:299
  31.8 2.6 %collective-permute-start.9 = (bf16[256,256]{1,0:T(8,128)(2,1)S(1)}, bf16[256,256]{1,0:T(8,128)(2,1)S(1)}, u32[]{:S(2)}, u32[]{:S(2)}) collective-permute-start(bf16[256,256]{1,0:T(8,128)(2,1)S(1)} %get-tuple-element.36), channel_id=1, source_target_pairs={{0,5},{1,4},{4,1},{5,0},{8,13},{9,12},{12,9},{13,8},{2,7},{3,6},{6... | collective-permute-start | bytes 393224 | tf_op jit(solution)/shard_map/ppermute | solution.py:299
  34.4 1.0 %collective-permute-done.8.refs_2_ = bf16[256,256]{1,0:T(8,128)(2,1)S(1)} collective-permute-done((bf16[256,256]{1,0:T(8,128)(2,1)S(1)}, bf16[256,256]{1,0:T(8,128)(2,1)S(1)}, u32[]{:S(2)}, u32[]{:S(2)}) %collective-permute-start.8) | collective-permute-done | bytes 131104 | tf_op jit(solution)/shard_map/ppermute | solution.py:299
  35.4 3.1 %collective-permute-done.11.refs_4_ = bf16[256,256]{1,0:T(8,128)(2,1)S(1)} collective-permute-done((bf16[256,256]{1,0:T(8,128)(2,1)S(1)}, bf16[256,256]{1,0:T(8,128)(2,1)S(1)}, u32[]{:S(2)}, u32[]{:S(2)}) %collective-permute-start.11) | collective-permute-done | bytes 131104 | tf_op jit(solution)/shard_map/ppermute | solution.py:299
  38.5 3.3 %collective-permute-done.12.refs_5_ = bf16[256,256]{1,0:T(8,128)(2,1)S(1)} collective-permute-done((bf16[256,256]{1,0:T(8,128)(2,1)S(1)}, bf16[256,256]{1,0:T(8,128)(2,1)S(1)}, u32[]{:S(2)}, u32[]{:S(2)}) %collective-permute-start.12) | collective-permute-done | bytes 131104 | tf_op jit(solution)/shard_map/ppermute | solution.py:299
  41.8 0.0 collective-permute-done.7.refs_1_
  41.8 0.0 collective-permute-done.9.refs_3_
  41.8 0.9 %total.1 = f32[1,256,512]{2,1,0:T(8,128)} custom-call(f32[256,256]{1,0:T(8,128)S(1)} %get-tuple-element.30.refs_0_, bf16[256,256]{1,0:T(8,128)(2,1)S(1)} %collective-permute-done.7.refs_1_, bf16[256,256]{1,0:T(8,128)(2,1)S(1)} %collective-permute-done.8.refs_2_, bf16[256,256]{1,0:T(8,128)(2,1)S(1)} %collective-permute-done.9.refs_3_, ...), custom_call_target="tpu_custom_call" | custom-call | tf_op jit(solution)/shard_map/total/pallas_call | solution.py:447
  (3 shorter events, 0.1 us)
Async XLA Ops:
  2.8 7.1 %collective-permute-start = (f32[1,16,256]{2,1,0:T(8,128)}, f32[1,16,256]{2,1,0:T(8,128)S(1)}, u32[]{:S(2)}, u32[]{:S(2)}) collective-permute-start(f32[1,16,256]{2,1,0:T(8,128)} %get-tuple-element.23), channel_id=1, source_target_pairs={{0,1},{1,0},{2,3},{3,2},{4,5},{5,4},{6,7},{7,6},{8,9},{9,8},{10,11... | collective-permute-start | bytes 49160 | tf_op jit(solution)/shard_map/ppermute | solution.py:291
  3.3 15.6 %collective-permute-start.4 = (bf16[256,768]{1,0:T(8,128)(2,1)}, bf16[256,768]{1,0:T(8,128)(2,1)S(1)}, u32[]{:S(2)}, u32[]{:S(2)}) collective-permute-start(bf16[256,768]{1,0:T(8,128)(2,1)} %get-tuple-element.24.turned_ref.refs_0_), channel_id=1, source_target_pairs={{0,2},{2,0},{1,3},{3,1},{4,6},{6,4},{5,7},{7,5},{8,10},{10,8},{9,1... | collective-permute-start | bytes 1179656 | tf_op jit(solution)/shard_map/ppermute | solution.py:291
  5.9 14.7 %collective-permute-start.3 = (bf16[256,768]{1,0:T(8,128)(2,1)}, bf16[256,768]{1,0:T(8,128)(2,1)S(1)}, u32[]{:S(2)}, u32[]{:S(2)}) collective-permute-start(bf16[256,768]{1,0:T(8,128)(2,1)} %get-tuple-element.24.turned_ref.refs_0_), channel_id=1, source_target_pairs={{0,1},{1,0},{2,3},{3,2},{4,5},{5,4},{6,7},{7,6},{8,9},{9,8},{10,11... | collective-permute-start | bytes 1179656 | tf_op jit(solution)/shard_map/ppermute | solution.py:291
  6.1 10.9 %collective-permute-start.1 = (bf16[384,256]{1,0:T(8,128)(2,1)}, bf16[384,256]{1,0:T(8,128)(2,1)S(1)}, u32[]{:S(2)}, u32[]{:S(2)}) collective-permute-start(bf16[384,256]{1,0:T(8,128)(2,1)} %get-tuple-element.28), channel_id=1, source_target_pairs={{0,4},{4,8},{8,12},{12,0},{1,5},{5,9},{9,13},{13,1},{2,6},{6,10},{... | collective-permute-start | bytes 589832 | tf_op jit(solution)/shard_map/ppermute | solution.py:291
  7.7 11.3 %collective-permute-start.2 = (bf16[384,256]{1,0:T(8,128)(2,1)}, bf16[384,256]{1,0:T(8,128)(2,1)S(1)}, u32[]{:S(2)}, u32[]{:S(2)}) collective-permute-start(bf16[384,256]{1,0:T(8,128)(2,1)} %get-tuple-element.29), channel_id=1, source_target_pairs={{0,12},{4,0},{8,4},{12,8},{1,13},{5,1},{9,5},{13,9},{2,14},{6,2},{... | collective-permute-start | bytes 589832 | tf_op jit(solution)/shard_map/ppermute | solution.py:291
  9.9 1.0 %copy-start = (bf16[256,768]{1,0:T(8,128)(2,1)S(1)}, bf16[256,768]{1,0:T(8,128)(2,1)}, u32[]{:S(2)}) copy-start(bf16[256,768]{1,0:T(8,128)(2,1)} %get-tuple-element.24.turned_ref.refs_0_) | copy-start | bytes 1179652
  10.9 0.9 %copy-start.1 = (f32[11,16,256]{2,1,0:T(8,128)S(1)}, f32[11,16,256]{2,1,0:T(8,128)}, u32[]{:S(2)}) copy-start(f32[11,16,256]{2,1,0:T(8,128)} %get-tuple-element.22.source_ref) | copy-start | bytes 540676
  19.0 1.8 %collective-permute-start.5 = (bf16[256,768]{1,0:T(8,128)(2,1)S(1)}, bf16[256,768]{1,0:T(8,128)(2,1)S(1)}, u32[]{:S(2)}, u32[]{:S(2)}) collective-permute-start(bf16[256,768]{1,0:T(8,128)(2,1)S(1)} %relay.1.refs_2_), channel_id=1, source_target_pairs={{0,1},{1,0},{2,3},{3,2},{4,5},{5,4},{6,7},{7,6},{8,9},{9,8},{10,11... | collective-permute-start | bytes 1179656 | tf_op jit(solution)/shard_map/ppermute | solution.py:291
  21.0 6.4 %collective-permute-start.10 = (bf16[256,256]{1,0:T(8,128)(2,1)S(1)}, bf16[256,256]{1,0:T(8,128)(2,1)S(1)}, u32[]{:S(2)}, u32[]{:S(2)}) collective-permute-start(bf16[256,256]{1,0:T(8,128)(2,1)S(1)} %far.2.after), channel_id=1, source_target_pairs={{0,4},{1,5},{4,0},{5,1},{8,12},{9,13},{12,8},{13,9},{2,6},{3,7},{6... | collective-permute-start | bytes 393224 | tf_op jit(solution)/shard_map/ppermute | solution.py:299
  22.5 7.7 %collective-permute-start.6 = (bf16[256,256]{1,0:T(8,128)(2,1)S(1)}, bf16[256,256]{1,0:T(8,128)(2,1)S(1)}, u32[]{:S(2)}, u32[]{:S(2)}) collective-permute-start(bf16[256,256]{1,0:T(8,128)(2,1)S(1)} %far.3), channel_id=1, source_target_pairs={{0,4},{1,5},{4,0},{5,1},{8,12},{9,13},{12,8},{13,9},{2,6},{3,7},{6... | collective-permute-start | bytes 393224 | tf_op jit(solution)/shard_map/ppermute | solution.py:299
  24.6 10.7 %collective-permute-start.8 = (bf16[256,256]{1,0:T(8,128)(2,1)S(1)}, bf16[256,256]{1,0:T(8,128)(2,1)S(1)}, u32[]{:S(2)}, u32[]{:S(2)}) collective-permute-start(bf16[256,256]{1,0:T(8,128)(2,1)S(1)} %get-tuple-element.35), channel_id=1, source_target_pairs={{0,4},{1,5},{4,0},{5,1},{8,12},{9,13},{12,8},{13,9},{2,6},{3,7},{6... | collective-permute-start | bytes 393224 | tf_op jit(solution)/shard_map/ppermute | solution.py:299
  27.4 11.1 %collective-permute-start.11 = (bf16[256,256]{1,0:T(8,128)(2,1)S(1)}, bf16[256,256]{1,0:T(8,128)(2,1)S(1)}, u32[]{:S(2)}, u32[]{:S(2)}) collective-permute-start(bf16[256,256]{1,0:T(8,128)(2,1)S(1)} %add.3), channel_id=1, source_target_pairs={{0,8},{1,9},{4,12},{5,13},{8,0},{9,1},{12,4},{13,5},{2,10},{3,11},... | collective-permute-start | bytes 393224 | tf_op jit(solution)/shard_map/ppermute | solution.py:299
  30.3 11.5 %collective-permute-start.12 = (bf16[256,256]{1,0:T(8,128)(2,1)S(1)}, bf16[256,256]{1,0:T(8,128)(2,1)S(1)}, u32[]{:S(2)}, u32[]{:S(2)}) collective-permute-start(bf16[256,256]{1,0:T(8,128)(2,1)S(1)} %get-tuple-element.38), channel_id=1, source_target_pairs={{0,9},{1,8},{4,13},{5,12},{8,1},{9,0},{12,5},{13,4},{2,11},{3,10},... | collective-permute-start | bytes 393224 | tf_op jit(solution)/shard_map/ppermute | solution.py:299
  30.4 11.5 %collective-permute-start.7 = (bf16[256,256]{1,0:T(8,128)(2,1)S(1)}, bf16[256,256]{1,0:T(8,128)(2,1)S(1)}, u32[]{:S(2)}, u32[]{:S(2)}) collective-permute-start(bf16[256,256]{1,0:T(8,128)(2,1)S(1)} %get-tuple-element.34), channel_id=1, source_target_pairs={{0,1},{1,0},{4,5},{5,4},{8,9},{9,8},{12,13},{13,12},{2,3},{3,2},{6... | collective-permute-start | bytes 393224 | tf_op jit(solution)/shard_map/ppermute | solution.py:299
  31.8 10.0 %collective-permute-start.9 = (bf16[256,256]{1,0:T(8,128)(2,1)S(1)}, bf16[256,256]{1,0:T(8,128)(2,1)S(1)}, u32[]{:S(2)}, u32[]{:S(2)}) collective-permute-start(bf16[256,256]{1,0:T(8,128)(2,1)S(1)} %get-tuple-element.36), channel_id=1, source_target_pairs={{0,5},{1,4},{4,1},{5,0},{8,13},{9,12},{12,9},{13,8},{2,7},{3,6},{6... | collective-permute-start | bytes 393224 | tf_op jit(solution)/shard_map/ppermute | solution.py:299

commit v14 on v13

--- a/solution.py
+++ b/solution.py
@@ -55,7 +55,7 @@
         )
         for i, at in enumerate(range(0, rows, quarter))
     ]
-    for copy in arriving + v_in:
+    for copy in v_in + arriving:
         copy.start()
     leaving = []
 
@@ -64,11 +64,8 @@
         copy.start()
         leaving.append(copy)
 
-    for copy in arriving:
+    for copy in arriving[:2]:
         copy.wait()
-    source_ref[10] = near_ref[...].astype(F32)
-    leave(source_ref.at[9:10], bond_out_hbm)
-    leave(source_ref, source_hbm)
     for i, list_ref in enumerate((high_ref, low_ref)):
         count = list_ref.shape[1]
         named = jnp.broadcast_to(list_ref[...], (128, count)).T
@@ -87,6 +84,11 @@
     leave(send_high_ref, send_high_hbm)
     send_low_ref[...] = picked[3 * count :]
     leave(send_low_ref, send_low_hbm)
+    for copy in arriving[2:]:
+        copy.wait()
+    source_ref[10] = near_ref[...].astype(F32)
+    leave(source_ref.at[9:10], bond_out_hbm)
+    leave(source_ref, source_hbm)
     for t in range(half // 128):
         columns = slice(t * 128, (t + 1) * 128)
         wide_ref[t] = v_ref[:, columns].astype(F32)

time: 42.9 us -> 42.7 us (level)
  no operation moved by 1% of the time
where the time goes in v14:
time: 42.7 us; the launch traced here: 42.5 us
  starting transfers between devices  16 us (37%)
  waiting for transfers between devices  12.5 us (29%)
  Pallas kernels  12 us (28%)
  local copies, waits for them, and re-layouts  1.92 us (4%)
    ppermute x7, waiting for transfers between devices, swap(): return lax.ppermute(value, ('dom', 'dir'), pairs)  10.4 us
    ppermute x7, starting transfers between devices, swap(): return lax.ppermute(value, ('dom', 'dir'), pairs)  8.87 us
    ppermute x6, starting transfers between devices, shift(): lax.ppermute(value, axis, [(i, (i + by) % length) for i in range(length)])  7.14 us
    pallas_call x1, Pallas kernels, per_device(): pl.pallas_call(weights_kernel, out_shape=(shape((2 * rows, half), F32), s...  5.13 us
    pallas_call x1, Pallas kernels, per_device(): pl.pallas_call(prep_kernel, out_shape=(*prepared, shape((11, *neighbours....  2.68 us
    ppermute x6, waiting for transfers between devices, shift(): lax.ppermute(value, axis, [(i, (i + by) % length) for i in range(length)])  2.13 us
    unnamed x4, local copies, waits for them, and re-layouts  1.92 us
    pallas_call x2, Pallas kernels, flux_of(): pl.pallas_call(functools.partial(flux_kernel, e), out_shape=shape((rows,...  1.54 us
  transfers between devices with their start and end apart: 13, of which 7 were waited for; matrix products, arithmetic and copies ran while one was open for 0% of the time, Pallas kernels for 19%

profile of v14, /device:TPU:0, one launch (start us, length us, event | category | flops | bytes accessed | tf_op | source)
XLA Modules:
  0.0 42.5 jit_solution(9107218304275758051)
XLA Ops:
  0.0 2.7 %prep.1 = (bf16[256,768]{1,0:T(8,128)(2,1)}, bf16[384,256]{1,0:T(8,128)(2,1)}, bf16[384,256]{1,0:T(8,128)(2,1)}, f32[11,16,256]{2,1,0:T(8,128)}, f32[1,16,256]{2,1,0:T(8,128)}) custom-call(bf16[768,512]{1,0:T(8,128)(2,1)} %v_hbm.1, s32[1,128]{1,0:T(1,128)} %bitcast.4, s32[1,128]{1,0:T(1,128)} %bitcast.5, f32[9,16,256]{2,1,0:T(8,128)} %bitcast.3, ...), custom_call_target="tpu_custom_call" | custom-call | tf_op jit(solution)/shard_map/prep/pallas_call | solution.py:326
  2.7 0.5 %collective-permute-start = (f32[1,16,256]{2,1,0:T(8,128)}, f32[1,16,256]{2,1,0:T(8,128)S(1)}, u32[]{:S(2)}, u32[]{:S(2)}) collective-permute-start(f32[1,16,256]{2,1,0:T(8,128)} %get-tuple-element.23), channel_id=1, source_target_pairs={{0,1},{1,0},{2,3},{3,2},{4,5},{5,4},{6,7},{7,6},{8,9},{9,8},{10,11... | collective-permute-start | bytes 49160 | tf_op jit(solution)/shard_map/ppermute | solution.py:293
  3.2 2.6 %collective-permute-start.4 = (bf16[256,768]{1,0:T(8,128)(2,1)}, bf16[256,768]{1,0:T(8,128)(2,1)S(1)}, u32[]{:S(2)}, u32[]{:S(2)}) collective-permute-start(bf16[256,768]{1,0:T(8,128)(2,1)} %get-tuple-element.24.turned_ref.refs_0_), channel_id=1, source_target_pairs={{0,2},{2,0},{1,3},{3,1},{4,6},{6,4},{5,7},{7,5},{8,10},{10,8},{9,1... | collective-permute-start | bytes 1179656 | tf_op jit(solution)/shard_map/ppermute | solution.py:293
  5.8 0.2 collective-permute-start.3
  5.9 1.6 %collective-permute-start.1 = (bf16[384,256]{1,0:T(8,128)(2,1)}, bf16[384,256]{1,0:T(8,128)(2,1)S(1)}, u32[]{:S(2)}, u32[]{:S(2)}) collective-permute-start(bf16[384,256]{1,0:T(8,128)(2,1)} %get-tuple-element.28), channel_id=1, source_target_pairs={{0,4},{4,8},{8,12},{12,0},{1,5},{5,9},{9,13},{13,1},{2,6},{6,10},{... | collective-permute-start | bytes 589832 | tf_op jit(solution)/shard_map/ppermute | solution.py:293
  7.5 2.2 %collective-permute-start.2 = (bf16[384,256]{1,0:T(8,128)(2,1)}, bf16[384,256]{1,0:T(8,128)(2,1)S(1)}, u32[]{:S(2)}, u32[]{:S(2)}) collective-permute-start(bf16[384,256]{1,0:T(8,128)(2,1)} %get-tuple-element.29), channel_id=1, source_target_pairs={{0,12},{4,0},{8,4},{12,8},{1,13},{5,1},{9,5},{13,9},{2,14},{6,2},{... | collective-permute-start | bytes 589832 | tf_op jit(solution)/shard_map/ppermute | solution.py:293
  9.8 0.0 collective-permute-done.other_ref
  9.8 0.0 copy-start
  9.8 1.0 %copy-done = bf16[256,768]{1,0:T(8,128)(2,1)S(1)} copy-done((bf16[256,768]{1,0:T(8,128)(2,1)S(1)}, bf16[256,768]{1,0:T(8,128)(2,1)}, u32[]{:S(2)}) %copy-start) | copy-done | bytes 393240
  10.8 0.0 copy-start.1
  10.8 0.9 %copy-done.1 = f32[11,16,256]{2,1,0:T(8,128)S(1)} copy-done((f32[11,16,256]{2,1,0:T(8,128)S(1)}, f32[11,16,256]{2,1,0:T(8,128)}, u32[]{:S(2)}) %copy-start.1) | copy-done | bytes 180248
  11.7 5.1 %weights.1 = (f32[1536,256]{1,0:T(8,128)S(1)}, bf16[1536,768]{1,0:T(8,128)(2,1)S(1)}, bf16[1536,768]{1,0:T(8,128)(2,1)S(1)}) custom-call(f32[11,16,256]{2,1,0:T(8,128)S(1)} %copy-done.1, f32[1,16,256]{2,1,0:T(8,128)S(1)} %collective-permute-done.other_ref, bf16[256,768]{1,0:T(8,128)(2,1)S(1)} %copy-done), custom_call_target="tpu_custom_call" | custom-call | flops 8000000000 | bytes 10000000 | tf_op jit(solution)/shard_map/weights/pallas_call | solution.py:357
  16.8 0.0 collective-permute-done.1.below_ref.below_hbm
  16.8 2.0 %collective-permute-done.2.above_ref.above_hbm = bf16[384,256]{1,0:T(8,128)(2,1)S(1)} collective-permute-done((bf16[384,256]{1,0:T(8,128)(2,1)}, bf16[384,256]{1,0:T(8,128)(2,1)S(1)}, u32[]{:S(2)}, u32[]{:S(2)}) %collective-permute-start.2) | collective-permute-done | bytes 196640 | tf_op jit(solution)/shard_map/ppermute | solution.py:293
  18.8 0.0 collective-permute-done.4.refs_0_
  18.8 0.1 collective-permute-start.5
  18.9 0.8 %flux.3.flux1_ref.after.flux_ref = bf16[768,256]{1,0:T(8,128)(2,1)S(1)} custom-call(f32[1536,256]{1,0:T(8,128)S(1)} %get-tuple-element.25.part_ref.part_hbm, bf16[1536,768]{1,0:T(8,128)(2,1)S(1)} %get-tuple-element.26.hi_ref, bf16[1536,768]{1,0:T(8,128)(2,1)S(1)} %get-tuple-element.27.lo_ref, ...), custom_call_target="tpu_custom_call" | custom-call | flops 1000000000 | bytes 1000000 | tf_op jit(solution)/shard_map/flux/pallas_call | solution.py:391
  19.7 0.8 %flux.2.flux0_ref.flux_ref = bf16[768,256]{1,0:T(8,128)(2,1)S(1)} custom-call(f32[1536,256]{1,0:T(8,128)S(1)} %get-tuple-element.25.part_ref.part_hbm, bf16[1536,768]{1,0:T(8,128)(2,1)S(1)} %get-tuple-element.26.hi_ref, bf16[1536,768]{1,0:T(8,128)(2,1)S(1)} %get-tuple-element.27.lo_ref, bf16[384,256]{1,0:T(8,128)(2,1)S(1)} %collective-permute-done.1.below_ref.below_hbm, ...), custom_call_target="tpu_custom_call" | custom-call | flops 1000000000 | bytes 1000000 | tf_op jit(solution)/shard_map/flux/pallas_call | solution.py:391
  20.5 0.0 collective-permute-done.3.refs_1_
  20.5 0.1 collective-permute-done.5.refs_3_
  20.6 0.3 far.2.after
  20.9 1.2 %collective-permute-start.10 = (bf16[256,256]{1,0:T(8,128)(2,1)S(1)}, bf16[256,256]{1,0:T(8,128)(2,1)S(1)}, u32[]{:S(2)}, u32[]{:S(2)}) collective-permute-start(bf16[256,256]{1,0:T(8,128)(2,1)S(1)} %far.2.after), channel_id=1, source_target_pairs={{0,4},{1,5},{4,0},{5,1},{8,12},{9,13},{12,8},{13,9},{2,6},{3,7},{6... | collective-permute-start | bytes 393224 | tf_op jit(solution)/shard_map/ppermute | solution.py:301
  22.1 0.3 far.3
  22.4 0.9 %collective-permute-start.6 = (bf16[256,256]{1,0:T(8,128)(2,1)S(1)}, bf16[256,256]{1,0:T(8,128)(2,1)S(1)}, u32[]{:S(2)}, u32[]{:S(2)}) collective-permute-start(bf16[256,256]{1,0:T(8,128)(2,1)S(1)} %far.3), channel_id=1, source_target_pairs={{0,4},{1,5},{4,0},{5,1},{8,12},{9,13},{12,8},{13,9},{2,6},{3,7},{6... | collective-permute-start | bytes 393224 | tf_op jit(solution)/shard_map/ppermute | solution.py:301
  23.3 1.1 %near.1 = (bf16[256,256]{1,0:T(8,128)(2,1)S(1)}, bf16[256,256]{1,0:T(8,128)(2,1)S(1)}, f32[256,256]{1,0:T(8,128)S(1)}, f32[256,256]{1,0:T(8,128)S(1)}, f32[256,2...) custom-call(bf16[768,256]{1,0:T(8,128)(2,1)S(1)} %flux.2.flux0_ref.flux_ref, ...), custom_call_target="tpu_custom_call" | custom-call | flops 400000000 | bytes 1000000 | tf_op jit(solution)/shard_map/near/pallas_call | solution.py:425
  24.5 1.2 %collective-permute-start.8 = (bf16[256,256]{1,0:T(8,128)(2,1)S(1)}, bf16[256,256]{1,0:T(8,128)(2,1)S(1)}, u32[]{:S(2)}, u32[]{:S(2)}) collective-permute-start(bf16[256,256]{1,0:T(8,128)(2,1)S(1)} %get-tuple-element.35), channel_id=1, source_target_pairs={{0,4},{1,5},{4,0},{5,1},{8,12},{9,13},{12,8},{13,9},{2,6},{3,7},{6... | collective-permute-start | bytes 393224 | tf_op jit(solution)/shard_map/ppermute | solution.py:301
  25.7 1.6 %collective-permute-done.10.far_ref = bf16[256,256]{1,0:T(8,128)(2,1)S(1)} collective-permute-done((bf16[256,256]{1,0:T(8,128)(2,1)S(1)}, bf16[256,256]{1,0:T(8,128)(2,1)S(1)}, u32[]{:S(2)}, u32[]{:S(2)}) %collective-permute-start.10) | collective-permute-done | bytes 131104 | tf_op jit(solution)/shard_map/ppermute | solution.py:301
  27.3 1.4 %collective-permute-start.11 = (bf16[256,256]{1,0:T(8,128)(2,1)S(1)}, bf16[256,256]{1,0:T(8,128)(2,1)S(1)}, u32[]{:S(2)}, u32[]{:S(2)}) collective-permute-start(bf16[256,256]{1,0:T(8,128)(2,1)S(1)} %add.3), channel_id=1, source_target_pairs={{0,8},{1,9},{4,12},{5,13},{8,0},{9,1},{12,4},{13,5},{2,10},{3,11},... | collective-permute-start | bytes 393224 | tf_op jit(solution)/shard_map/ppermute | solution.py:301
  28.7 1.4 %collective-permute-done.6.far_ref = bf16[256,256]{1,0:T(8,128)(2,1)S(1)} collective-permute-done((bf16[256,256]{1,0:T(8,128)(2,1)S(1)}, bf16[256,256]{1,0:T(8,128)(2,1)S(1)}, u32[]{:S(2)}, u32[]{:S(2)}) %collective-permute-start.6) | collective-permute-done | bytes 131104 | tf_op jit(solution)/shard_map/ppermute | solution.py:301
  30.1 0.1 collective-permute-start.12
  30.2 1.4 %collective-permute-start.7 = (bf16[256,256]{1,0:T(8,128)(2,1)S(1)}, bf16[256,256]{1,0:T(8,128)(2,1)S(1)}, u32[]{:S(2)}, u32[]{:S(2)}) collective-permute-start(bf16[256,256]{1,0:T(8,128)(2,1)S(1)} %get-tuple-element.34), channel_id=1, source_target_pairs={{0,1},{1,0},{4,5},{5,4},{8,9},{9,8},{12,13},{13,12},{2,3},{3,2},{6... | collective-permute-start | bytes 393224 | tf_op jit(solution)/shard_map/ppermute | solution.py:301
  31.6 2.6 %collective-permute-start.9 = (bf16[256,256]{1,0:T(8,128)(2,1)S(1)}, bf16[256,256]{1,0:T(8,128)(2,1)S(1)}, u32[]{:S(2)}, u32[]{:S(2)}) collective-permute-start(bf16[256,256]{1,0:T(8,128)(2,1)S(1)} %get-tuple-element.36), channel_id=1, source_target_pairs={{0,5},{1,4},{4,1},{5,0},{8,13},{9,12},{12,9},{13,8},{2,7},{3,6},{6... | collective-permute-start | bytes 393224 | tf_op jit(solution)/shard_map/ppermute | solution.py:301
  34.2 1.0 %collective-permute-done.8.refs_2_ = bf16[256,256]{1,0:T(8,128)(2,1)S(1)} collective-permute-done((bf16[256,256]{1,0:T(8,128)(2,1)S(1)}, bf16[256,256]{1,0:T(8,128)(2,1)S(1)}, u32[]{:S(2)}, u32[]{:S(2)}) %collective-permute-start.8) | collective-permute-done | bytes 131104 | tf_op jit(solution)/shard_map/ppermute | solution.py:301
  35.2 3.2 %collective-permute-done.11.refs_4_ = bf16[256,256]{1,0:T(8,128)(2,1)S(1)} collective-permute-done((bf16[256,256]{1,0:T(8,128)(2,1)S(1)}, bf16[256,256]{1,0:T(8,128)(2,1)S(1)}, u32[]{:S(2)}, u32[]{:S(2)}) %collective-permute-start.11) | collective-permute-done | bytes 131104 | tf_op jit(solution)/shard_map/ppermute | solution.py:301
  38.4 3.3 %collective-permute-done.12.refs_5_ = bf16[256,256]{1,0:T(8,128)(2,1)S(1)} collective-permute-done((bf16[256,256]{1,0:T(8,128)(2,1)S(1)}, bf16[256,256]{1,0:T(8,128)(2,1)S(1)}, u32[]{:S(2)}, u32[]{:S(2)}) %collective-permute-start.12) | collective-permute-done | bytes 131104 | tf_op jit(solution)/shard_map/ppermute | solution.py:301
  41.7 0.0 collective-permute-done.7.refs_1_
  41.7 0.0 collective-permute-done.9.refs_3_
  41.7 0.9 %total.1 = f32[1,256,512]{2,1,0:T(8,128)} custom-call(f32[256,256]{1,0:T(8,128)S(1)} %get-tuple-element.30.refs_0_, bf16[256,256]{1,0:T(8,128)(2,1)S(1)} %collective-permute-done.7.refs_1_, bf16[256,256]{1,0:T(8,128)(2,1)S(1)} %collective-permute-done.8.refs_2_, bf16[256,256]{1,0:T(8,128)(2,1)S(1)} %collective-permute-done.9.refs_3_, ...), custom_call_target="tpu_custom_call" | custom-call | tf_op jit(solution)/shard_map/total/pallas_call | solution.py:449
  (3 shorter events, 0.1 us)
Async XLA Ops:
  2.7 7.1 %collective-permute-start = (f32[1,16,256]{2,1,0:T(8,128)}, f32[1,16,256]{2,1,0:T(8,128)S(1)}, u32[]{:S(2)}, u32[]{:S(2)}) collective-permute-start(f32[1,16,256]{2,1,0:T(8,128)} %get-tuple-element.23), channel_id=1, source_target_pairs={{0,1},{1,0},{2,3},{3,2},{4,5},{5,4},{6,7},{7,6},{8,9},{9,8},{10,11... | collective-permute-start | bytes 49160 | tf_op jit(solution)/shard_map/ppermute | solution.py:293
  3.2 15.6 %collective-permute-start.4 = (bf16[256,768]{1,0:T(8,128)(2,1)}, bf16[256,768]{1,0:T(8,128)(2,1)S(1)}, u32[]{:S(2)}, u32[]{:S(2)}) collective-permute-start(bf16[256,768]{1,0:T(8,128)(2,1)} %get-tuple-element.24.turned_ref.refs_0_), channel_id=1, source_target_pairs={{0,2},{2,0},{1,3},{3,1},{4,6},{6,4},{5,7},{7,5},{8,10},{10,8},{9,1... | collective-permute-start | bytes 1179656 | tf_op jit(solution)/shard_map/ppermute | solution.py:293
  5.8 14.7 %collective-permute-start.3 = (bf16[256,768]{1,0:T(8,128)(2,1)}, bf16[256,768]{1,0:T(8,128)(2,1)S(1)}, u32[]{:S(2)}, u32[]{:S(2)}) collective-permute-start(bf16[256,768]{1,0:T(8,128)(2,1)} %get-tuple-element.24.turned_ref.refs_0_), channel_id=1, source_target_pairs={{0,1},{1,0},{2,3},{3,2},{4,5},{5,4},{6,7},{7,6},{8,9},{9,8},{10,11... | collective-permute-start | bytes 1179656 | tf_op jit(solution)/shard_map/ppermute | solution.py:293
  5.9 10.9 %collective-permute-start.1 = (bf16[384,256]{1,0:T(8,128)(2,1)}, bf16[384,256]{1,0:T(8,128)(2,1)S(1)}, u32[]{:S(2)}, u32[]{:S(2)}) collective-permute-start(bf16[384,256]{1,0:T(8,128)(2,1)} %get-tuple-element.28), channel_id=1, source_target_pairs={{0,4},{4,8},{8,12},{12,0},{1,5},{5,9},{9,13},{13,1},{2,6},{6,10},{... | collective-permute-start | bytes 589832 | tf_op jit(solution)/shard_map/ppermute | solution.py:293
  7.5 11.3 %collective-permute-start.2 = (bf16[384,256]{1,0:T(8,128)(2,1)}, bf16[384,256]{1,0:T(8,128)(2,1)S(1)}, u32[]{:S(2)}, u32[]{:S(2)}) collective-permute-start(bf16[384,256]{1,0:T(8,128)(2,1)} %get-tuple-element.29), channel_id=1, source_target_pairs={{0,12},{4,0},{8,4},{12,8},{1,13},{5,1},{9,5},{13,9},{2,14},{6,2},{... | collective-permute-start | bytes 589832 | tf_op jit(solution)/shard_map/ppermute | solution.py:293
  9.8 1.0 %copy-start = (bf16[256,768]{1,0:T(8,128)(2,1)S(1)}, bf16[256,768]{1,0:T(8,128)(2,1)}, u32[]{:S(2)}) copy-start(bf16[256,768]{1,0:T(8,128)(2,1)} %get-tuple-element.24.turned_ref.refs_0_) | copy-start | bytes 1179652
  10.8 0.9 %copy-start.1 = (f32[11,16,256]{2,1,0:T(8,128)S(1)}, f32[11,16,256]{2,1,0:T(8,128)}, u32[]{:S(2)}) copy-start(f32[11,16,256]{2,1,0:T(8,128)} %get-tuple-element.22.source_ref) | copy-start | bytes 540676
  18.8 1.8 %collective-permute-start.5 = (bf16[256,768]{1,0:T(8,128)(2,1)S(1)}, bf16[256,768]{1,0:T(8,128)(2,1)S(1)}, u32[]{:S(2)}, u32[]{:S(2)}) collective-permute-start(bf16[256,768]{1,0:T(8,128)(2,1)S(1)} %relay.1.refs_2_), channel_id=1, source_target_pairs={{0,1},{1,0},{2,3},{3,2},{4,5},{5,4},{6,7},{7,6},{8,9},{9,8},{10,11... | collective-permute-start | bytes 1179656 | tf_op jit(solution)/shard_map/ppermute | solution.py:293
  20.9 6.4 %collective-permute-start.10 = (bf16[256,256]{1,0:T(8,128)(2,1)S(1)}, bf16[256,256]{1,0:T(8,128)(2,1)S(1)}, u32[]{:S(2)}, u32[]{:S(2)}) collective-permute-start(bf16[256,256]{1,0:T(8,128)(2,1)S(1)} %far.2.after), channel_id=1, source_target_pairs={{0,4},{1,5},{4,0},{5,1},{8,12},{9,13},{12,8},{13,9},{2,6},{3,7},{6... | collective-permute-start | bytes 393224 | tf_op jit(solution)/shard_map/ppermute | solution.py:301
  22.4 7.7 %collective-permute-start.6 = (bf16[256,256]{1,0:T(8,128)(2,1)S(1)}, bf16[256,256]{1,0:T(8,128)(2,1)S(1)}, u32[]{:S(2)}, u32[]{:S(2)}) collective-permute-start(bf16[256,256]{1,0:T(8,128)(2,1)S(1)} %far.3), channel_id=1, source_target_pairs={{0,4},{1,5},{4,0},{5,1},{8,12},{9,13},{12,8},{13,9},{2,6},{3,7},{6... | collective-permute-start | bytes 393224 | tf_op jit(solution)/shard_map/ppermute | solution.py:301
  24.5 10.7 %collective-permute-start.8 = (bf16[256,256]{1,0:T(8,128)(2,1)S(1)}, bf16[256,256]{1,0:T(8,128)(2,1)S(1)}, u32[]{:S(2)}, u32[]{:S(2)}) collective-permute-start(bf16[256,256]{1,0:T(8,128)(2,1)S(1)} %get-tuple-element.35), channel_id=1, source_target_pairs={{0,4},{1,5},{4,0},{5,1},{8,12},{9,13},{12,8},{13,9},{2,6},{3,7},{6... | collective-permute-start | bytes 393224 | tf_op jit(solution)/shard_map/ppermute | solution.py:301
  27.3 11.1 %collective-permute-start.11 = (bf16[256,256]{1,0:T(8,128)(2,1)S(1)}, bf16[256,256]{1,0:T(8,128)(2,1)S(1)}, u32[]{:S(2)}, u32[]{:S(2)}) collective-permute-start(bf16[256,256]{1,0:T(8,128)(2,1)S(1)} %add.3), channel_id=1, source_target_pairs={{0,8},{1,9},{4,12},{5,13},{8,0},{9,1},{12,4},{13,5},{2,10},{3,11},... | collective-permute-start | bytes 393224 | tf_op jit(solution)/shard_map/ppermute | solution.py:301
  30.1 11.5 %collective-permute-start.12 = (bf16[256,256]{1,0:T(8,128)(2,1)S(1)}, bf16[256,256]{1,0:T(8,128)(2,1)S(1)}, u32[]{:S(2)}, u32[]{:S(2)}) collective-permute-start(bf16[256,256]{1,0:T(8,128)(2,1)S(1)} %get-tuple-element.38), channel_id=1, source_target_pairs={{0,9},{1,8},{4,13},{5,12},{8,1},{9,0},{12,5},{13,4},{2,11},{3,10},... | collective-permute-start | bytes 393224 | tf_op jit(solution)/shard_map/ppermute | solution.py:301
  30.2 11.5 %collective-permute-start.7 = (bf16[256,256]{1,0:T(8,128)(2,1)S(1)}, bf16[256,256]{1,0:T(8,128)(2,1)S(1)}, u32[]{:S(2)}, u32[]{:S(2)}) collective-permute-start(bf16[256,256]{1,0:T(8,128)(2,1)S(1)} %get-tuple-element.34), channel_id=1, source_target_pairs={{0,1},{1,0},{4,5},{5,4},{8,9},{9,8},{12,13},{13,12},{2,3},{3,2},{6... | collective-permute-start | bytes 393224 | tf_op jit(solution)/shard_map/ppermute | solution.py:301
  31.6 10.0 %collective-permute-start.9 = (bf16[256,256]{1,0:T(8,128)(2,1)S(1)}, bf16[256,256]{1,0:T(8,128)(2,1)S(1)}, u32[]{:S(2)}, u32[]{:S(2)}) collective-permute-start(bf16[256,256]{1,0:T(8,128)(2,1)S(1)} %get-tuple-element.36), channel_id=1, source_target_pairs={{0,5},{1,4},{4,1},{5,0},{8,13},{9,12},{12,9},{13,8},{2,7},{3,6},{6... | collective-permute-start | bytes 393224 | tf_op jit(solution)/shard_map/ppermute | solution.py:301

commit v15 on v13

--- a/solution.py
+++ b/solution.py
@@ -418,8 +418,7 @@
 
         flux0, flux1 = flux_of(0), flux_of(1)
         far0 = far_of(flux0, flux1)
-        far1 = far_of(flux1, far0)
-        far0, far1 = swap(far0, 1, 0), swap(far1, 1, 0)
+        far0 = swap(far0, 1, 0)
         near0, near1, add0, add1, keep, give = pl.pallas_call(
             near_kernel,
             out_shape=(sent, sent, kept, kept, kept, sent),
@@ -429,6 +428,7 @@
             cost_estimate=cost,
             name="near",
         )(flux0, flux1, *given)
+        far1 = swap(far_of(flux1, near0), 1, 0)
 
         def sum_of(far, add, *handed_on):
             return pl.pallas_call(

time: 42.9 us -> 42.8 us (level)
    ppermute x7, starting transfers between devices: 8.88 us -> 8.42 us  [swap(): return lax.ppermute(value, ('dom', 'dir'), pairs)]
  transfers between devices with their start and end apart: 13 -> 13, of which waited for: 7 -> 6; matrix products, arithmetic and copies ran while one was open for 0% -> 0% of each run, Pallas kernels for 19% -> 19%
where the time goes in v15:
time: 42.8 us; the launch traced here: 42.6 us
  starting transfers between devices  15.6 us (36%)
  waiting for transfers between devices  12.9 us (30%)
  Pallas kernels  12.1 us (28%)
  local copies, waits for them, and re-layouts  1.92 us (4%)
    ppermute x7, waiting for transfers between devices, swap(): return lax.ppermute(value, ('dom', 'dir'), pairs)  10.7 us
    ppermute x7, starting transfers between devices, swap(): return lax.ppermute(value, ('dom', 'dir'), pairs)  8.42 us
    ppermute x6, starting transfers between devices, shift(): lax.ppermute(value, axis, [(i, (i + by) % length) for i in range(length)])  7.14 us
    pallas_call x1, Pallas kernels, per_device(): pl.pallas_call(weights_kernel, out_shape=(shape((2 * rows, half), F32), s...  5.13 us
    pallas_call x1, Pallas kernels, per_device(): pl.pallas_call(prep_kernel, out_shape=(*prepared, shape((11, *neighbours....  2.82 us
    ppermute x6, waiting for transfers between devices, shift(): lax.ppermute(value, axis, [(i, (i + by) % length) for i in range(length)])  2.14 us
    unnamed x4, local copies, waits for them, and re-layouts  1.92 us
    pallas_call x2, Pallas kernels, flux_of(): pl.pallas_call(functools.partial(flux_kernel, e), out_shape=shape((rows,...  1.54 us
  transfers between devices with their start and end apart: 13, of which 6 were waited for; matrix products, arithmetic and copies ran while one was open for 0% of the time, Pallas kernels for 19%

profile of v15, /device:TPU:0, one launch (start us, length us, event | category | flops | bytes accessed | tf_op | source)
XLA Modules:
  0.0 42.6 jit_solution(8172633197155253697)
XLA Ops:
  0.0 2.8 %prep.1 = (bf16[256,768]{1,0:T(8,128)(2,1)}, bf16[384,256]{1,0:T(8,128)(2,1)}, bf16[384,256]{1,0:T(8,128)(2,1)}, f32[11,16,256]{2,1,0:T(8,128)}, f32[1,16,256]{2,1,0:T(8,128)}) custom-call(bf16[768,512]{1,0:T(8,128)(2,1)} %v_hbm.1, s32[1,128]{1,0:T(1,128)} %bitcast.4, s32[1,128]{1,0:T(1,128)} %bitcast.5, f32[9,16,256]{2,1,0:T(8,128)} %bitcast.3, ...), custom_call_target="tpu_custom_call" | custom-call | tf_op jit(solution)/shard_map/prep/pallas_call | solution.py:324
  2.8 0.5 %collective-permute-start = (f32[1,16,256]{2,1,0:T(8,128)}, f32[1,16,256]{2,1,0:T(8,128)S(1)}, u32[]{:S(2)}, u32[]{:S(2)}) collective-permute-start(f32[1,16,256]{2,1,0:T(8,128)} %get-tuple-element.23), channel_id=1, source_target_pairs={{0,1},{1,0},{2,3},{3,2},{4,5},{5,4},{6,7},{7,6},{8,9},{9,8},{10,11... | collective-permute-start | bytes 49160 | tf_op jit(solution)/shard_map/ppermute | solution.py:291
  3.3 2.6 %collective-permute-start.4 = (bf16[256,768]{1,0:T(8,128)(2,1)}, bf16[256,768]{1,0:T(8,128)(2,1)S(1)}, u32[]{:S(2)}, u32[]{:S(2)}) collective-permute-start(bf16[256,768]{1,0:T(8,128)(2,1)} %get-tuple-element.24.turned_ref.refs_0_), channel_id=1, source_target_pairs={{0,2},{2,0},{1,3},{3,1},{4,6},{6,4},{5,7},{7,5},{8,10},{10,8},{9,1... | collective-permute-start | bytes 1179656 | tf_op jit(solution)/shard_map/ppermute | solution.py:291
  5.9 0.2 collective-permute-start.3
  6.1 1.6 %collective-permute-start.1 = (bf16[384,256]{1,0:T(8,128)(2,1)}, bf16[384,256]{1,0:T(8,128)(2,1)S(1)}, u32[]{:S(2)}, u32[]{:S(2)}) collective-permute-start(bf16[384,256]{1,0:T(8,128)(2,1)} %get-tuple-element.28), channel_id=1, source_target_pairs={{0,4},{4,8},{8,12},{12,0},{1,5},{5,9},{9,13},{13,1},{2,6},{6,10},{... | collective-permute-start | bytes 589832 | tf_op jit(solution)/shard_map/ppermute | solution.py:291
  7.7 2.2 %collective-permute-start.2 = (bf16[384,256]{1,0:T(8,128)(2,1)}, bf16[384,256]{1,0:T(8,128)(2,1)S(1)}, u32[]{:S(2)}, u32[]{:S(2)}) collective-permute-start(bf16[384,256]{1,0:T(8,128)(2,1)} %get-tuple-element.29), channel_id=1, source_target_pairs={{0,12},{4,0},{8,4},{12,8},{1,13},{5,1},{9,5},{13,9},{2,14},{6,2},{... | collective-permute-start | bytes 589832 | tf_op jit(solution)/shard_map/ppermute | solution.py:291
  9.9 0.0 collective-permute-done.other_ref
  9.9 0.0 copy-start
  9.9 1.0 %copy-done = bf16[256,768]{1,0:T(8,128)(2,1)S(1)} copy-done((bf16[256,768]{1,0:T(8,128)(2,1)S(1)}, bf16[256,768]{1,0:T(8,128)(2,1)}, u32[]{:S(2)}) %copy-start) | copy-done | bytes 393240
  10.9 0.0 copy-start.1
  10.9 0.9 %copy-done.1 = f32[11,16,256]{2,1,0:T(8,128)S(1)} copy-done((f32[11,16,256]{2,1,0:T(8,128)S(1)}, f32[11,16,256]{2,1,0:T(8,128)}, u32[]{:S(2)}) %copy-start.1) | copy-done | bytes 180248
  11.8 5.1 %weights.1 = (f32[1536,256]{1,0:T(8,128)S(1)}, bf16[1536,768]{1,0:T(8,128)(2,1)S(1)}, bf16[1536,768]{1,0:T(8,128)(2,1)S(1)}) custom-call(f32[11,16,256]{2,1,0:T(8,128)S(1)} %copy-done.1, f32[1,16,256]{2,1,0:T(8,128)S(1)} %collective-permute-done.other_ref, bf16[256,768]{1,0:T(8,128)(2,1)S(1)} %copy-done), custom_call_target="tpu_custom_call" | custom-call | flops 8000000000 | bytes 10000000 | tf_op jit(solution)/shard_map/weights/pallas_call | solution.py:355
  17.0 0.0 collective-permute-done.1.below_ref.below_hbm
  17.0 2.0 %collective-permute-done.2.above_ref.above_hbm = bf16[384,256]{1,0:T(8,128)(2,1)S(1)} collective-permute-done((bf16[384,256]{1,0:T(8,128)(2,1)}, bf16[384,256]{1,0:T(8,128)(2,1)S(1)}, u32[]{:S(2)}, u32[]{:S(2)}) %collective-permute-start.2) | collective-permute-done | bytes 196640 | tf_op jit(solution)/shard_map/ppermute | solution.py:291
  18.9 0.0 collective-permute-done.4.refs_0_
  19.0 0.1 collective-permute-start.5
  19.1 0.8 %flux.3.flux1_ref.flux_ref.after = bf16[768,256]{1,0:T(8,128)(2,1)S(1)} custom-call(f32[1536,256]{1,0:T(8,128)S(1)} %get-tuple-element.25.part_ref.part_hbm, bf16[1536,768]{1,0:T(8,128)(2,1)S(1)} %get-tuple-element.26.hi_ref, bf16[1536,768]{1,0:T(8,128)(2,1)S(1)} %get-tuple-element.27.lo_ref, ...), custom_call_target="tpu_custom_call" | custom-call | flops 1000000000 | bytes 1000000 | tf_op jit(solution)/shard_map/flux/pallas_call | solution.py:389
  19.8 0.8 %flux.2.flux0_ref.flux_ref = bf16[768,256]{1,0:T(8,128)(2,1)S(1)} custom-call(f32[1536,256]{1,0:T(8,128)S(1)} %get-tuple-element.25.part_ref.part_hbm, bf16[1536,768]{1,0:T(8,128)(2,1)S(1)} %get-tuple-element.26.hi_ref, bf16[1536,768]{1,0:T(8,128)(2,1)S(1)} %get-tuple-element.27.lo_ref, bf16[384,256]{1,0:T(8,128)(2,1)S(1)} %collective-permute-done.1.below_ref.below_hbm, ...), custom_call_target="tpu_custom_call" | custom-call | flops 1000000000 | bytes 1000000 | tf_op jit(solution)/shard_map/flux/pallas_call | solution.py:389
  20.6 0.0 collective-permute-done.3.refs_1_
  20.6 0.1 collective-permute-done.5.refs_3_
  20.8 0.3 far.3
  21.0 1.2 %collective-permute-start.10 = (bf16[256,256]{1,0:T(8,128)(2,1)S(1)}, bf16[256,256]{1,0:T(8,128)(2,1)S(1)}, u32[]{:S(2)}, u32[]{:S(2)}) collective-permute-start(bf16[256,256]{1,0:T(8,128)(2,1)S(1)} %far.3), channel_id=1, source_target_pairs={{0,4},{1,5},{4,0},{5,1},{8,12},{9,13},{12,8},{13,9},{2,6},{3,7},{6... | collective-permute-start | bytes 393224 | tf_op jit(solution)/shard_map/ppermute | solution.py:299
  22.3 1.1 %near.1 = (bf16[256,256]{1,0:T(8,128)(2,1)S(1)}, bf16[256,256]{1,0:T(8,128)(2,1)S(1)}, f32[256,256]{1,0:T(8,128)S(1)}, f32[256,256]{1,0:T(8,128)S(1)}, f32[256,2...) custom-call(bf16[768,256]{1,0:T(8,128)(2,1)S(1)} %flux.2.flux0_ref.flux_ref, ...), custom_call_target="tpu_custom_call" | custom-call | flops 400000000 | bytes 1000000 | tf_op jit(solution)/shard_map/near/pallas_call | solution.py:422
  23.4 0.3 far.2
  23.7 0.9 %collective-permute-start.6 = (bf16[256,256]{1,0:T(8,128)(2,1)S(1)}, bf16[256,256]{1,0:T(8,128)(2,1)S(1)}, u32[]{:S(2)}, u32[]{:S(2)}) collective-permute-start(bf16[256,256]{1,0:T(8,128)(2,1)S(1)} %far.2), channel_id=1, source_target_pairs={{0,4},{1,5},{4,0},{5,1},{8,12},{9,13},{12,8},{13,9},{2,6},{3,7},{6... | collective-permute-start | bytes 393224 | tf_op jit(solution)/shard_map/ppermute | solution.py:299
  24.7 1.2 %collective-permute-start.8 = (bf16[256,256]{1,0:T(8,128)(2,1)S(1)}, bf16[256,256]{1,0:T(8,128)(2,1)S(1)}, u32[]{:S(2)}, u32[]{:S(2)}) collective-permute-start(bf16[256,256]{1,0:T(8,128)(2,1)S(1)} %get-tuple-element.31.after), channel_id=1, source_target_pairs={{0,4},{1,5},{4,0},{5,1},{8,12},{9,13},{12,8},{13,9},{2,6},{3,7},{6... | collective-permute-start | bytes 393224 | tf_op jit(solution)/shard_map/ppermute | solution.py:299
  25.8 1.5 %collective-permute-done.10.far_ref = bf16[256,256]{1,0:T(8,128)(2,1)S(1)} collective-permute-done((bf16[256,256]{1,0:T(8,128)(2,1)S(1)}, bf16[256,256]{1,0:T(8,128)(2,1)S(1)}, u32[]{:S(2)}, u32[]{:S(2)}) %collective-permute-start.10) | collective-permute-done | bytes 131104 | tf_op jit(solution)/shard_map/ppermute | solution.py:299
  27.4 0.9 %collective-permute-start.11 = (bf16[256,256]{1,0:T(8,128)(2,1)S(1)}, bf16[256,256]{1,0:T(8,128)(2,1)S(1)}, u32[]{:S(2)}, u32[]{:S(2)}) collective-permute-start(bf16[256,256]{1,0:T(8,128)(2,1)S(1)} %add.3), channel_id=1, source_target_pairs={{0,8},{1,9},{4,12},{5,13},{8,0},{9,1},{12,4},{13,5},{2,10},{3,11},... | collective-permute-start | bytes 393224 | tf_op jit(solution)/shard_map/ppermute | solution.py:299
  28.3 1.9 %collective-permute-done.6.far_ref = bf16[256,256]{1,0:T(8,128)(2,1)S(1)} collective-permute-done((bf16[256,256]{1,0:T(8,128)(2,1)S(1)}, bf16[256,256]{1,0:T(8,128)(2,1)S(1)}, u32[]{:S(2)}, u32[]{:S(2)}) %collective-permute-start.6) | collective-permute-done | bytes 131104 | tf_op jit(solution)/shard_map/ppermute | solution.py:299
  30.2 0.1 collective-permute-start.12
  30.3 1.8 %collective-permute-start.7 = (bf16[256,256]{1,0:T(8,128)(2,1)S(1)}, bf16[256,256]{1,0:T(8,128)(2,1)S(1)}, u32[]{:S(2)}, u32[]{:S(2)}) collective-permute-start(bf16[256,256]{1,0:T(8,128)(2,1)S(1)} %get-tuple-element.35), channel_id=1, source_target_pairs={{0,1},{1,0},{4,5},{5,4},{8,9},{9,8},{12,13},{13,12},{2,3},{3,2},{6... | collective-permute-start | bytes 393224 | tf_op jit(solution)/shard_map/ppermute | solution.py:299
  32.1 2.3 %collective-permute-start.9 = (bf16[256,256]{1,0:T(8,128)(2,1)S(1)}, bf16[256,256]{1,0:T(8,128)(2,1)S(1)}, u32[]{:S(2)}, u32[]{:S(2)}) collective-permute-start(bf16[256,256]{1,0:T(8,128)(2,1)S(1)} %get-tuple-element.36), channel_id=1, source_target_pairs={{0,5},{1,4},{4,1},{5,0},{8,13},{9,12},{12,9},{13,8},{2,7},{3,6},{6... | collective-permute-start | bytes 393224 | tf_op jit(solution)/shard_map/ppermute | solution.py:299
  34.4 1.1 %collective-permute-done.8.refs_2_ = bf16[256,256]{1,0:T(8,128)(2,1)S(1)} collective-permute-done((bf16[256,256]{1,0:T(8,128)(2,1)S(1)}, bf16[256,256]{1,0:T(8,128)(2,1)S(1)}, u32[]{:S(2)}, u32[]{:S(2)}) %collective-permute-start.8) | collective-permute-done | bytes 131104 | tf_op jit(solution)/shard_map/ppermute | solution.py:299
  35.4 0.0 collective-permute-done.11.refs_4_
  35.4 6.3 %collective-permute-done.12.refs_5_ = bf16[256,256]{1,0:T(8,128)(2,1)S(1)} collective-permute-done((bf16[256,256]{1,0:T(8,128)(2,1)S(1)}, bf16[256,256]{1,0:T(8,128)(2,1)S(1)}, u32[]{:S(2)}, u32[]{:S(2)}) %collective-permute-start.12) | collective-permute-done | bytes 131104 | tf_op jit(solution)/shard_map/ppermute | solution.py:299
  41.7 0.0 collective-permute-done.7.refs_1_
  41.7 0.0 collective-permute-done.9.refs_3_
  41.7 0.9 %total.1 = f32[1,256,512]{2,1,0:T(8,128)} custom-call(f32[256,256]{1,0:T(8,128)S(1)} %get-tuple-element.30.refs_0_, bf16[256,256]{1,0:T(8,128)(2,1)S(1)} %collective-permute-done.7.refs_1_, bf16[256,256]{1,0:T(8,128)(2,1)S(1)} %collective-permute-done.8.refs_2_, bf16[256,256]{1,0:T(8,128)(2,1)S(1)} %collective-permute-done.9.refs_3_, ...), custom_call_target="tpu_custom_call" | custom-call | tf_op jit(solution)/shard_map/total/pallas_call | solution.py:447
  (3 shorter events, 0.1 us)
Async XLA Ops:
  2.8 7.1 %collective-permute-start = (f32[1,16,256]{2,1,0:T(8,128)}, f32[1,16,256]{2,1,0:T(8,128)S(1)}, u32[]{:S(2)}, u32[]{:S(2)}) collective-permute-start(f32[1,16,256]{2,1,0:T(8,128)} %get-tuple-element.23), channel_id=1, source_target_pairs={{0,1},{1,0},{2,3},{3,2},{4,5},{5,4},{6,7},{7,6},{8,9},{9,8},{10,11... | collective-permute-start | bytes 49160 | tf_op jit(solution)/shard_map/ppermute | solution.py:291
  3.3 15.6 %collective-permute-start.4 = (bf16[256,768]{1,0:T(8,128)(2,1)}, bf16[256,768]{1,0:T(8,128)(2,1)S(1)}, u32[]{:S(2)}, u32[]{:S(2)}) collective-permute-start(bf16[256,768]{1,0:T(8,128)(2,1)} %get-tuple-element.24.turned_ref.refs_0_), channel_id=1, source_target_pairs={{0,2},{2,0},{1,3},{3,1},{4,6},{6,4},{5,7},{7,5},{8,10},{10,8},{9,1... | collective-permute-start | bytes 1179656 | tf_op jit(solution)/shard_map/ppermute | solution.py:291
  5.9 14.7 %collective-permute-start.3 = (bf16[256,768]{1,0:T(8,128)(2,1)}, bf16[256,768]{1,0:T(8,128)(2,1)S(1)}, u32[]{:S(2)}, u32[]{:S(2)}) collective-permute-start(bf16[256,768]{1,0:T(8,128)(2,1)} %get-tuple-element.24.turned_ref.refs_0_), channel_id=1, source_target_pairs={{0,1},{1,0},{2,3},{3,2},{4,5},{5,4},{6,7},{7,6},{8,9},{9,8},{10,11... | collective-permute-start | bytes 1179656 | tf_op jit(solution)/shard_map/ppermute | solution.py:291
  6.1 10.9 %collective-permute-start.1 = (bf16[384,256]{1,0:T(8,128)(2,1)}, bf16[384,256]{1,0:T(8,128)(2,1)S(1)}, u32[]{:S(2)}, u32[]{:S(2)}) collective-permute-start(bf16[384,256]{1,0:T(8,128)(2,1)} %get-tuple-element.28), channel_id=1, source_target_pairs={{0,4},{4,8},{8,12},{12,0},{1,5},{5,9},{9,13},{13,1},{2,6},{6,10},{... | collective-permute-start | bytes 589832 | tf_op jit(solution)/shard_map/ppermute | solution.py:291
  7.7 11.3 %collective-permute-start.2 = (bf16[384,256]{1,0:T(8,128)(2,1)}, bf16[384,256]{1,0:T(8,128)(2,1)S(1)}, u32[]{:S(2)}, u32[]{:S(2)}) collective-permute-start(bf16[384,256]{1,0:T(8,128)(2,1)} %get-tuple-element.29), channel_id=1, source_target_pairs={{0,12},{4,0},{8,4},{12,8},{1,13},{5,1},{9,5},{13,9},{2,14},{6,2},{... | collective-permute-start | bytes 589832 | tf_op jit(solution)/shard_map/ppermute | solution.py:291
  9.9 1.0 %copy-start = (bf16[256,768]{1,0:T(8,128)(2,1)S(1)}, bf16[256,768]{1,0:T(8,128)(2,1)}, u32[]{:S(2)}) copy-start(bf16[256,768]{1,0:T(8,128)(2,1)} %get-tuple-element.24.turned_ref.refs_0_) | copy-start | bytes 1179652
  10.9 0.9 %copy-start.1 = (f32[11,16,256]{2,1,0:T(8,128)S(1)}, f32[11,16,256]{2,1,0:T(8,128)}, u32[]{:S(2)}) copy-start(f32[11,16,256]{2,1,0:T(8,128)} %get-tuple-element.22.source_ref) | copy-start | bytes 540676
  19.0 1.8 %collective-permute-start.5 = (bf16[256,768]{1,0:T(8,128)(2,1)S(1)}, bf16[256,768]{1,0:T(8,128)(2,1)S(1)}, u32[]{:S(2)}, u32[]{:S(2)}) collective-permute-start(bf16[256,768]{1,0:T(8,128)(2,1)S(1)} %relay.1.refs_2_), channel_id=1, source_target_pairs={{0,1},{1,0},{2,3},{3,2},{4,5},{5,4},{6,7},{7,6},{8,9},{9,8},{10,11... | collective-permute-start | bytes 1179656 | tf_op jit(solution)/shard_map/ppermute | solution.py:291
  21.0 6.3 %collective-permute-start.10 = (bf16[256,256]{1,0:T(8,128)(2,1)S(1)}, bf16[256,256]{1,0:T(8,128)(2,1)S(1)}, u32[]{:S(2)}, u32[]{:S(2)}) collective-permute-start(bf16[256,256]{1,0:T(8,128)(2,1)S(1)} %far.3), channel_id=1, source_target_pairs={{0,4},{1,5},{4,0},{5,1},{8,12},{9,13},{12,8},{13,9},{2,6},{3,7},{6... | collective-permute-start | bytes 393224 | tf_op jit(solution)/shard_map/ppermute | solution.py:299
  23.7 6.4 %collective-permute-start.6 = (bf16[256,256]{1,0:T(8,128)(2,1)S(1)}, bf16[256,256]{1,0:T(8,128)(2,1)S(1)}, u32[]{:S(2)}, u32[]{:S(2)}) collective-permute-start(bf16[256,256]{1,0:T(8,128)(2,1)S(1)} %far.2), channel_id=1, source_target_pairs={{0,4},{1,5},{4,0},{5,1},{8,12},{9,13},{12,8},{13,9},{2,6},{3,7},{6... | collective-permute-start | bytes 393224 | tf_op jit(solution)/shard_map/ppermute | solution.py:299
  24.7 10.8 %collective-permute-start.8 = (bf16[256,256]{1,0:T(8,128)(2,1)S(1)}, bf16[256,256]{1,0:T(8,128)(2,1)S(1)}, u32[]{:S(2)}, u32[]{:S(2)}) collective-permute-start(bf16[256,256]{1,0:T(8,128)(2,1)S(1)} %get-tuple-element.31.after), channel_id=1, source_target_pairs={{0,4},{1,5},{4,0},{5,1},{8,12},{9,13},{12,8},{13,9},{2,6},{3,7},{6... | collective-permute-start | bytes 393224 | tf_op jit(solution)/shard_map/ppermute | solution.py:299
  27.4 8.1 %collective-permute-start.11 = (bf16[256,256]{1,0:T(8,128)(2,1)S(1)}, bf16[256,256]{1,0:T(8,128)(2,1)S(1)}, u32[]{:S(2)}, u32[]{:S(2)}) collective-permute-start(bf16[256,256]{1,0:T(8,128)(2,1)S(1)} %add.3), channel_id=1, source_target_pairs={{0,8},{1,9},{4,12},{5,13},{8,0},{9,1},{12,4},{13,5},{2,10},{3,11},... | collective-permute-start | bytes 393224 | tf_op jit(solution)/shard_map/ppermute | solution.py:299
  30.2 11.5 %collective-permute-start.12 = (bf16[256,256]{1,0:T(8,128)(2,1)S(1)}, bf16[256,256]{1,0:T(8,128)(2,1)S(1)}, u32[]{:S(2)}, u32[]{:S(2)}) collective-permute-start(bf16[256,256]{1,0:T(8,128)(2,1)S(1)} %get-tuple-element.38), channel_id=1, source_target_pairs={{0,9},{1,8},{4,13},{5,12},{8,1},{9,0},{12,5},{13,4},{2,11},{3,10},... | collective-permute-start | bytes 393224 | tf_op jit(solution)/shard_map/ppermute | solution.py:299
  30.3 11.5 %collective-permute-start.7 = (bf16[256,256]{1,0:T(8,128)(2,1)S(1)}, bf16[256,256]{1,0:T(8,128)(2,1)S(1)}, u32[]{:S(2)}, u32[]{:S(2)}) collective-permute-start(bf16[256,256]{1,0:T(8,128)(2,1)S(1)} %get-tuple-element.35), channel_id=1, source_target_pairs={{0,1},{1,0},{4,5},{5,4},{8,9},{9,8},{12,13},{13,12},{2,3},{3,2},{6... | collective-permute-start | bytes 393224 | tf_op jit(solution)/shard_map/ppermute | solution.py:299
  32.1 9.6 %collective-permute-start.9 = (bf16[256,256]{1,0:T(8,128)(2,1)S(1)}, bf16[256,256]{1,0:T(8,128)(2,1)S(1)}, u32[]{:S(2)}, u32[]{:S(2)}) collective-permute-start(bf16[256,256]{1,0:T(8,128)(2,1)S(1)} %get-tuple-element.36), channel_id=1, source_target_pairs={{0,5},{1,4},{4,1},{5,0},{8,13},{9,12},{12,9},{13,8},{2,7},{3,6},{6... | collective-permute-start | bytes 393224 | tf_op jit(solution)/shard_map/ppermute | solution.py:299
